TPU v7x, 32 devices: a whole 2x2x4 slice. The times are simulated.
32 devices in a mesh: dp: 4 (over z), mp: 8 (over y, x, core).
Axes of the slice: x: 2, y: 2, z: 4, core: 2. Of those that a mesh axis runs over, the one named last changes fastest.
Arguments:
- inputs: bfloat16 [8192, 2048], P(('dp', 'mp')), may hold values from -6 to 6
- out_grad: bfloat16 [8192, 2048], P(('dp', 'mp')), may hold values from -6 to 6
- project_weight: float32 [2, 2048, 3, 2048], P(None, 'dp', None, 'mp'), may hold values from -0.125 to 0.125
- dense_weight: float32 [2, 2048, 2048], P(None, 'mp', 'dp'), may hold values from -0.5 to 0.5
- up_weight: float32 [2, 2048, 8192], P(None, 'dp', 'mp'), may hold values from -0.125 to 0.125
- down_weight: float32 [2, 8192, 2048], P(None, 'mp', 'dp'), may hold values from -0.09375 to 0.09375
- project_bias: float32 [2, 2, 2048], P(None, None, 'mp'), may hold values from -3 to 3
- up_bias: float32 [2, 8192], P(None, 'mp'), may hold values from -3 to 3
- norm_gain: float32 [2, 2, 2048], replicated, may hold values from 0.1 to 1.9
- norm_bias: float32 [2, 2, 2048], replicated, may hold values from -3 to 3
- output_bias: float32 [2, 2, 2048], replicated, may hold values from -3 to 3
Outputs:
- outputs: bfloat16 [8192, 2048], P(('dp', 'mp'))
- input_grad: float32 [8192, 2048], P(('dp', 'mp'))
- project_grad: float32 [2, 2048, 3, 2048], P(None, 'dp', None, 'mp')
- dense_grad: float32 [2, 2048, 2048], P(None, 'mp', 'dp')
- up_grad: float32 [2, 2048, 8192], P(None, 'dp', 'mp')
- down_grad: float32 [2, 8192, 2048], P(None, 'mp', 'dp')
- project_bias_grad: float32 [2, 2, 2048], P(None, None, 'mp')
- up_bias_grad: float32 [2, 8192], P(None, 'mp')
- gain_grad: float32 [2, 2, 2048], replicated
- norm_bias_grad: float32 [2, 2, 2048], replicated
- output_bias_grad: float32 [2, 2, 2048], replicated
All inputs are finite; a program needn't handle non-finite values.
Results may differ from a plain program's by a relative error of at most 0.029.
Values may be sent and summed in bfloat16 or wider, within the bound.
A program may use at most 256 MiB of HBM per device.

v0:
```python
import jax
import jax.numpy as jnp
from jax import lax
from jax.sharding import PartitionSpec as P

N_HEADS = 16
BLOCK = 256


norm_eps = 1e-05


def layer_norm(values, scale_row, shift_row):
    centre = jnp.mean(values, axis=-1, keepdims=True)
    centred = values - centre
    spread = jnp.mean(centred * centred, axis=-1, keepdims=True)
    return centred * lax.rsqrt(spread + norm_eps) * scale_row + shift_row


def gelu_tanh(values):
    return (
        0.5
        * values
        * (1.0 + jnp.tanh(0.7978845608028654 * (values + 0.044715 * values * values * values)))
    )


def alibi_scores(query_block, keys, offset, slopes):
    block_rows = query_block.shape[0]
    length = keys.shape[0]
    scores = jnp.einsum(
        "qhd,khd->hqk", query_block, keys, preferred_element_type=jnp.float32
    ) * query_block.shape[2] ** (-0.5)
    query_pos = offset + lax.iota(jnp.int32, block_rows)
    key_pos = lax.iota(jnp.int32, length)
    distance = jnp.abs(query_pos[:, None] - key_pos[None, :]).astype(jnp.float32)
    allowed = key_pos[None, :] // BLOCK <= query_pos[:, None] // BLOCK
    scores = scores - slopes[:, None, None] * distance[None]
    return jnp.where(allowed[None], scores, -1e30)


def attend_forward(queries, keys, values, slopes):
    length = queries.shape[0]
    block_rows = min(512, length)

    def one_block(block_index):
        offset = block_index * block_rows
        query_block = lax.dynamic_slice_in_dim(queries, offset, block_rows, 0)
        scores = alibi_scores(query_block, keys, offset, slopes)
        highest = jnp.max(scores, axis=-1, keepdims=True)
        weights = jnp.exp(scores - highest)
        denominator = jnp.sum(weights, axis=-1, keepdims=True)
        weights_low = (weights / denominator).astype(jnp.bfloat16)
        context = jnp.einsum(
            "hqk,khd->qhd", weights_low, values, preferred_element_type=jnp.float32
        )
        return (context.astype(jnp.bfloat16), (highest + jnp.log(denominator))[:, :, 0])

    return lax.map(one_block, jnp.arange(length // block_rows, dtype=jnp.int32))


def attend_backward(queries, keys, values, log_norms, grad_context, slopes):
    length = queries.shape[0]
    block_rows = min(512, length)
    factor = queries.shape[2] ** (-0.5)

    def one_block(carry, block_index):
        grad_keys, grad_values = carry
        offset = block_index * block_rows
        query_block = lax.dynamic_slice_in_dim(queries, offset, block_rows, 0)
        grad_block = lax.dynamic_slice_in_dim(grad_context, offset, block_rows, 0)
        scores = alibi_scores(query_block, keys, offset, slopes)
        weights = jnp.exp(scores - log_norms[block_index][:, :, None])
        grad_weights = jnp.einsum(
            "qhd,khd->hqk", grad_block, values, preferred_element_type=jnp.float32
        )
        inner_sum = jnp.sum(weights * grad_weights, axis=-1, keepdims=True)
        grad_scores = (weights * (grad_weights - inner_sum)).astype(jnp.bfloat16)
        grad_query = (
            jnp.einsum("hqk,khd->qhd", grad_scores, keys, preferred_element_type=jnp.float32)
            * factor
        )
        grad_keys = (
            grad_keys
            + jnp.einsum(
                "hqk,qhd->khd", grad_scores, query_block, preferred_element_type=jnp.float32
            )
            * factor
        )
        grad_values = grad_values + jnp.einsum(
            "hqk,qhd->khd",
            weights.astype(jnp.bfloat16),
            grad_block,
            preferred_element_type=jnp.float32,
        )
        return ((grad_keys, grad_values), grad_query)

    empty = jnp.zeros(keys.shape, jnp.float32)
    (grad_keys, grad_values), grad_query = lax.scan(
        one_block, (empty, empty), jnp.arange(length // block_rows, dtype=jnp.int32)
    )
    return (grad_query.reshape(keys.shape), grad_keys, grad_values)


def shards(
    inputs,
    out_grad,
    project_weight,
    dense_weight,
    up_weight,
    down_weight,
    project_bias,
    up_bias,
    norm_gain,
    norm_bias,
    output_bias,
):
    tensor_size = lax.axis_size("mp")
    tensor_rank = lax.axis_index("mp")
    row_count = inputs.shape[0]
    total_rows = row_count * tensor_size
    model_width = inputs.shape[1]
    inner_width = project_weight.shape[3]
    hidden_width = up_weight.shape[2]
    heads_here = N_HEADS // tensor_size
    head_width = inner_width // heads_here
    layer_count = project_weight.shape[0]
    slopes = 2.0 ** (
        -8.0
        * (tensor_rank * heads_here + lax.iota(jnp.int32, heads_here) + 1).astype(jnp.float32)
        / N_HEADS
    )
    stream = inputs.astype(jnp.float32)
    stored = []
    saved_weights = []
    for layer_index in range(layer_count):
        gathered = (
            lax.all_gather(
                project_weight[layer_index].astype(jnp.bfloat16), "dp", axis=0, tiled=True
            ),
            lax.all_gather(
                dense_weight[layer_index].astype(jnp.bfloat16), "dp", axis=1, tiled=True
            ),
            lax.all_gather(up_weight[layer_index].astype(jnp.bfloat16), "dp", axis=0, tiled=True),
            lax.all_gather(down_weight[layer_index].astype(jnp.bfloat16), "dp", axis=1, tiled=True),
        )
        saved_weights.append(gathered)
        w_project, w_dense, w_up, w_down = gathered
        normed = layer_norm(stream, norm_gain[layer_index, 0], norm_bias[layer_index, 0]).astype(
            jnp.bfloat16
        )
        normed_all = lax.all_gather(normed, "mp", axis=0, tiled=True)
        project = jnp.dot(
            normed_all,
            w_project.reshape(model_width, 3 * inner_width),
            preferred_element_type=jnp.float32,
        ).reshape(total_rows, 3, inner_width)
        shifts = jnp.stack(
            [
                project_bias[layer_index, 0],
                jnp.zeros((inner_width,), jnp.float32),
                project_bias[layer_index, 1],
            ]
        )
        project_low = (project + shifts).astype(jnp.bfloat16)
        queries = project_low[:, 0].reshape(total_rows, heads_here, head_width)
        keys = project_low[:, 1].reshape(total_rows, heads_here, head_width)
        values = project_low[:, 2].reshape(total_rows, heads_here, head_width)
        context, log_norms = attend_forward(queries, keys, values, slopes)
        context_low = context.reshape(total_rows, inner_width)
        partial_sum = jnp.dot(context_low, w_dense, preferred_element_type=jnp.float32)
        attn_rows = lax.psum_scatter(
            partial_sum.astype(jnp.bfloat16), "mp", scatter_dimension=0, tiled=True
        ).astype(jnp.float32)
        middle = stream + attn_rows + output_bias[layer_index, 0]
        normed2 = layer_norm(middle, norm_gain[layer_index, 1], norm_bias[layer_index, 1]).astype(
            jnp.bfloat16
        )
        normed2_all = lax.all_gather(normed2, "mp", axis=0, tiled=True)
        hidden = (
            jnp.dot(normed2_all, w_up, preferred_element_type=jnp.float32) + up_bias[layer_index]
        )
        active = gelu_tanh(hidden).astype(jnp.bfloat16)
        down_part = jnp.dot(active, w_down, preferred_element_type=jnp.float32)
        stored.append(
            (
                stream,
                normed_all,
                queries,
                keys,
                values,
                log_norms,
                context_low,
                middle,
                normed2_all,
                hidden,
            )
        )
        stream = (
            middle
            + lax.psum_scatter(
                down_part.astype(jnp.bfloat16), "mp", scatter_dimension=0, tiled=True
            ).astype(jnp.float32)
            + output_bias[layer_index, 1]
        )
    outputs = stream.astype(jnp.bfloat16)
    grad = out_grad.astype(jnp.float32)
    project_grads = [None] * layer_count
    dense_grads = [None] * layer_count
    up_grads = [None] * layer_count
    down_grads = [None] * layer_count
    gain_parts = [None] * layer_count
    shift_parts = [None] * layer_count
    outbias_parts = [None] * layer_count
    project_bias_parts = [None] * layer_count
    up_bias_parts = [None] * layer_count
    for layer_index in reversed(range(layer_count)):
        w_project, w_dense, w_up, w_down = (
            lax.all_gather(
                project_weight[layer_index].astype(jnp.bfloat16), "dp", axis=0, tiled=True
            ),
            lax.all_gather(
                dense_weight[layer_index].astype(jnp.bfloat16), "dp", axis=1, tiled=True
            ),
            lax.all_gather(up_weight[layer_index].astype(jnp.bfloat16), "dp", axis=0, tiled=True),
            lax.all_gather(down_weight[layer_index].astype(jnp.bfloat16), "dp", axis=1, tiled=True),
        )
        (
            stream_in,
            normed_all,
            queries,
            keys,
            values,
            log_norms,
            context_low,
            middle,
            normed2_all,
            hidden,
        ) = stored[layer_index]
        down_bias_grad = jnp.sum(grad, axis=0)
        grad_down = lax.all_gather(grad.astype(jnp.bfloat16), "mp", axis=0, tiled=True)
        active = gelu_tanh(hidden).astype(jnp.bfloat16)
        down_grad_local = jnp.einsum(
            "tf,td->fd", active, grad_down, preferred_element_type=jnp.float32
        )
        grad_active = jnp.einsum("td,fd->tf", grad_down, w_down, preferred_element_type=jnp.float32)
        grad_hidden = jax.vjp(gelu_tanh, hidden)[1](grad_active)[0].astype(jnp.bfloat16)
        up_bias_parts[layer_index] = jnp.sum(grad_hidden.astype(jnp.float32), axis=0)
        up_grad_local = jnp.einsum(
            "td,tf->df", normed2_all, grad_hidden, preferred_element_type=jnp.float32
        )
        grad_normed2 = lax.psum_scatter(
            jnp.einsum("tf,df->td", grad_hidden, w_up, preferred_element_type=jnp.float32).astype(
                jnp.bfloat16
            ),
            "mp",
            scatter_dimension=0,
            tiled=True,
        ).astype(jnp.float32)
        norm_back = jax.vjp(
            layer_norm, middle, norm_gain[layer_index, 1], norm_bias[layer_index, 1]
        )[1]
        grad_from_norm, gain_second, shift_second = norm_back(grad_normed2)
        grad_middle = grad + grad_from_norm
        dense_bias_grad = jnp.sum(grad_middle, axis=0)
        grad_branch = lax.all_gather(grad_middle.astype(jnp.bfloat16), "mp", axis=0, tiled=True)
        dense_grad_local = jnp.einsum(
            "ti,td->id", context_low, grad_branch, preferred_element_type=jnp.float32
        )
        grad_context = jnp.einsum(
            "td,id->ti", grad_branch, w_dense, preferred_element_type=jnp.float32
        ).astype(jnp.bfloat16)
        grad_context = grad_context.reshape(total_rows, heads_here, head_width)
        grad_query, grad_keys, grad_values = attend_backward(
            queries, keys, values, log_norms, grad_context, slopes
        )
        grad_project = (
            jnp.stack([grad_query, grad_keys, grad_values], axis=1)
            .reshape(total_rows, 3, inner_width)
            .astype(jnp.bfloat16)
        )
        column_sums = jnp.sum(grad_project.astype(jnp.float32), axis=0)
        project_bias_parts[layer_index] = jnp.stack([column_sums[0], column_sums[2]])
        project_grad_local = jnp.einsum(
            "td,tsi->dsi", normed_all, grad_project, preferred_element_type=jnp.float32
        )
        grad_normed = lax.psum_scatter(
            jnp.einsum(
                "tsi,dsi->td", grad_project, w_project, preferred_element_type=jnp.float32
            ).astype(jnp.bfloat16),
            "mp",
            scatter_dimension=0,
            tiled=True,
        ).astype(jnp.float32)
        norm_back = jax.vjp(
            layer_norm, stream_in, norm_gain[layer_index, 0], norm_bias[layer_index, 0]
        )[1]
        grad_from_norm, gain_first, shift_first = norm_back(grad_normed)
        grad = grad_middle + grad_from_norm
        reduced = (
            lax.psum_scatter(
                project_grad_local.astype(jnp.bfloat16), "dp", scatter_dimension=0, tiled=True
            ).astype(jnp.float32),
            lax.psum_scatter(
                dense_grad_local.astype(jnp.bfloat16), "dp", scatter_dimension=1, tiled=True
            ).astype(jnp.float32),
            lax.psum_scatter(
                up_grad_local.astype(jnp.bfloat16), "dp", scatter_dimension=0, tiled=True
            ).astype(jnp.float32),
            lax.psum_scatter(
                down_grad_local.astype(jnp.bfloat16), "dp", scatter_dimension=1, tiled=True
            ).astype(jnp.float32),
        )
        project_grads[layer_index] = reduced[0]
        dense_grads[layer_index] = reduced[1]
        up_grads[layer_index] = reduced[2]
        down_grads[layer_index] = reduced[3]
        gain_parts[layer_index] = jnp.stack([gain_first, gain_second])
        shift_parts[layer_index] = jnp.stack([shift_first, shift_second])
        outbias_parts[layer_index] = jnp.stack([dense_bias_grad, down_bias_grad])
    project_slots = lax.dynamic_update_slice_in_dim(
        jnp.zeros((layer_count, 2, model_width), jnp.float32),
        jnp.stack(project_bias_parts),
        tensor_rank * inner_width,
        2,
    )
    up_slots = lax.dynamic_update_slice_in_dim(
        jnp.zeros((layer_count, hidden_width * tensor_size), jnp.float32),
        jnp.stack(up_bias_parts),
        tensor_rank * hidden_width,
        1,
    )
    summed = lax.psum(
        (
            jnp.stack(gain_parts),
            jnp.stack(shift_parts),
            jnp.stack(outbias_parts),
            project_slots,
            up_slots,
        ),
        ("dp", "mp"),
    )
    project_bias_grad = lax.dynamic_slice_in_dim(
        summed[3], tensor_rank * inner_width, inner_width, 2
    )
    up_bias_grad = lax.dynamic_slice_in_dim(summed[4], tensor_rank * hidden_width, hidden_width, 1)
    return (
        outputs,
        grad,
        jnp.stack(project_grads),
        jnp.stack(dense_grads),
        jnp.stack(up_grads),
        jnp.stack(down_grads),
        project_bias_grad,
        up_bias_grad,
        summed[0],
        summed[1],
        summed[2],
    )


def solution(mesh):
    in_specs = (
        P(("dp", "mp"), None),
        P(("dp", "mp"), None),
        P(None, "dp", None, "mp"),
        P(None, "mp", "dp"),
        P(None, "dp", "mp"),
        P(None, "mp", "dp"),
        P(None, None, "mp"),
        P(None, "mp"),
        P(),
        P(),
        P(),
    )
    out_specs = (
        P(("dp", "mp"), None),
        P(("dp", "mp"), None),
        P(None, "dp", None, "mp"),
        P(None, "mp", "dp"),
        P(None, "dp", "mp"),
        P(None, "mp", "dp"),
        P(None, None, "mp"),
        P(None, "mp"),
        P(),
        P(),
        P(),
    )
    return jax.shard_map(shards, mesh=mesh, in_specs=in_specs, out_specs=out_specs, check_vma=False)
```

profile of v0, /device:TPU:0, one launch (start us, length us, event | category | flops | bytes accessed | tf_op | source)
XLA Modules:
  0.0 2695.3 jit_solution(386089861362678171)
XLA Ops:
  16.5 60.5 %all-gather.41.cloned.1.call-done = bf16[1,2048,3,256]{3,1,2,0:T(8,128)(2,1)} async-done(((bf16[1,512,3,256]{3,1,2,0:T(8,128)(2,1)}), bf16[1,2048,3,256]{3,1,2,0:T(8,128)(2,1)}) %all-gather.41.cloned.1.call-update) | async-done | bytes 3145744 | tf_op jit(solution)/shard_map/all_gather | solution.py:138
  80.2 52.4 %all-gather.25.cloned.1.call-done = bf16[2048,2048]{1,0:T(8,128)(2,1)} async-done(((bf16[256,2048]{1,0:T(8,128)(2,1)}), bf16[2048,2048]{1,0:T(8,128)(2,1)}) %all-gather.25.cloned.1.call-update) | async-done | bytes 8388624 | tf_op jit(solution)/shard_map/all_gather | solution.py:152
  132.6 9.1 add_convert_fusion.1
  146.4 58.0 %while.68 = (s32[]{:T(128)}, bf16[4,512,2,128]{3,2,1,0:T(2,128)(2,1)S(1)}, f32[4,2,512]{2,1,0:T(2,128)S(1)}, s32[4]{0:T(128)S(1)}, bf16[2048,2,128]{2,0,1:T(8,12...) while((s32[]{:T(128)}, ...), condition=%wide.region_5.6_spmd.clone, body=%wide.region_2.5_spmd.clone.sunk | while | flops 1115839488 | bytes 49340648 | solution.py:59
  204.5 7.3 convolution_convert_fusion.5
  217.0 66.2 %reduce-scatter.17.cloned.1.call-done = bf16[256,2048]{1,0:T(8,128)(2,1)} async-done(((bf16[2048,2048]{1,0:T(8,128)(2,1)}), bf16[256,2048]{1,0:T(8,128)(2,1)}) %reduce-scatter.17.cloned.1.call-update) | async-done | bytes 1048592 | tf_op jit(solution)/shard_map/reduce_scatter | solution.py:172
  293.2 72.9 %all-gather.45.cloned.1.call-done = bf16[1,2048,1024]{2,1,0:T(8,128)(2,1)} async-done(((bf16[1,512,1024]{2,1,0:T(8,128)(2,1)}), bf16[1,2048,1024]{2,1,0:T(8,128)(2,1)}) %all-gather.45.cloned.1.call-update) | async-done | bytes 4194320 | tf_op jit(solution)/shard_map/all_gather | solution.py:144
  366.1 55.4 %all-gather.27.cloned.1.call-done = bf16[2048,2048]{1,0:T(8,128)(2,1)} async-done(((bf16[256,2048]{1,0:T(8,128)(2,1)}), bf16[2048,2048]{1,0:T(8,128)(2,1)}) %all-gather.27.cloned.1.call-update) | async-done | bytes 8388624 | tf_op jit(solution)/shard_map/all_gather | solution.py:179
  421.5 14.4 fusion.128
  435.9 68.6 %all-gather.47.cloned.1.call-done = bf16[1,1024,2048]{2,1,0:T(8,128)(2,1)} async-done(((bf16[1,1024,512]{2,1,0:T(8,128)(2,1)}), bf16[1,1024,2048]{2,1,0:T(8,128)(2,1)}) %all-gather.47.cloned.1.call-update) | async-done | bytes 4194320 | tf_op jit(solution)/shard_map/all_gather | solution.py:145
  504.5 15.4 convolution_convert_fusion.4
  520.8 69.2 %reduce-scatter.19.cloned.1.call-done = bf16[256,2048]{1,0:T(8,128)(2,1)} async-done(((bf16[2048,2048]{1,0:T(8,128)(2,1)}), bf16[256,2048]{1,0:T(8,128)(2,1)}) %reduce-scatter.19.cloned.1.call-update) | async-done | bytes 1048592 | tf_op jit(solution)/shard_map/reduce_scatter | solution.py:201
  595.6 59.4 %all-gather.49.cloned.1.call-done = bf16[1,2048,3,256]{3,1,2,0:T(8,128)(2,1)} async-done(((bf16[1,512,3,256]{3,1,2,0:T(8,128)(2,1)}), bf16[1,2048,3,256]{3,1,2,0:T(8,128)(2,1)}) %all-gather.49.cloned.1.call-update) | async-done | bytes 3145744 | tf_op jit(solution)/shard_map/all_gather | solution.py:138
  659.8 50.6 %all-gather.29.cloned.1.call-done = bf16[2048,2048]{1,0:T(8,128)(2,1)} async-done(((bf16[256,2048]{1,0:T(8,128)(2,1)}), bf16[2048,2048]{1,0:T(8,128)(2,1)}) %all-gather.29.cloned.1.call-update) | async-done | bytes 8388624 | tf_op jit(solution)/shard_map/all_gather | solution.py:152
  710.4 10.1 add_convert_fusion
  728.6 58.2 %while.69 = (s32[]{:T(128)}, bf16[4,512,2,128]{3,2,1,0:T(2,128)(2,1)S(1)}, f32[4,2,512]{2,1,0:T(2,128)S(1)}, s32[4]{0:T(128)S(1)}, bf16[2048,2,128]{2,0,1:T(8,12...) while((s32[]{:T(128)}, ...), condition=%wide.region_15.16_spmd.clone, body=%wide.region_12.15_spmd.clone.sunk | while | flops 1115839488 | bytes 49340648 | solution.py:59
  786.8 7.2 convolution_convert_fusion.3
  794.9 70.6 %reduce-scatter.21.cloned.1.call-done = bf16[256,2048]{1,0:T(8,128)(2,1)} async-done(((bf16[2048,2048]{1,0:T(8,128)(2,1)}), bf16[256,2048]{1,0:T(8,128)(2,1)}) %reduce-scatter.21.cloned.1.call-update) | async-done | bytes 1048592 | tf_op jit(solution)/shard_map/reduce_scatter | solution.py:172
  871.1 77.4 %all-gather.53.cloned.1.call-done = bf16[1,2048,1024]{2,1,0:T(8,128)(2,1)} async-done(((bf16[1,512,1024]{2,1,0:T(8,128)(2,1)}), bf16[1,2048,1024]{2,1,0:T(8,128)(2,1)}) %all-gather.53.cloned.1.call-update) | async-done | bytes 4194320 | tf_op jit(solution)/shard_map/all_gather | solution.py:144
  948.5 55.4 %all-gather.31.cloned.1.call-done = bf16[2048,2048]{1,0:T(8,128)(2,1)} async-done(((bf16[256,2048]{1,0:T(8,128)(2,1)}), bf16[2048,2048]{1,0:T(8,128)(2,1)}) %all-gather.31.cloned.1.call-update) | async-done | bytes 8388624 | tf_op jit(solution)/shard_map/all_gather | solution.py:179
  1004.0 14.4 fusion.120
  1018.4 68.4 %all-gather.55.cloned.1.call-done = bf16[1,1024,2048]{2,1,0:T(8,128)(2,1)} async-done(((bf16[1,1024,512]{2,1,0:T(8,128)(2,1)}), bf16[1,1024,2048]{2,1,0:T(8,128)(2,1)}) %all-gather.55.cloned.1.call-update) | async-done | bytes 4194320 | tf_op jit(solution)/shard_map/all_gather | solution.py:145
  1086.8 54.8 %all-gather.33.cloned.1.call-done = bf16[2048,2048]{1,0:T(8,128)(2,1)} async-done(((bf16[256,2048]{1,0:T(8,128)(2,1)}), bf16[2048,2048]{1,0:T(8,128)(2,1)}) %all-gather.33.cloned.1.call-update) | async-done | bytes 8388624 | tf_op jit(solution)/shard_map/all_gather | solution.py:241
  1141.7 20.6 convert_reduce_fusion
  1164.2 11.1 convolution_convert_fusion.1
  1175.4 15.5 convolution_convert_fusion.2
  1191.0 55.8 %reduce-scatter.25.cloned.1.call-done = bf16[256,2048]{1,0:T(8,128)(2,1)} async-done(((bf16[2048,2048]{1,0:T(8,128)(2,1)}), bf16[256,2048]{1,0:T(8,128)(2,1)}) %reduce-scatter.25.cloned.1.call-update) | async-done | bytes 1048592 | tf_op jit(solution)/shard_map/reduce_scatter | solution.py:252
  1249.4 72.0 %reduce-scatter.23.cloned.1.call-done = bf16[256,2048]{1,0:T(8,128)(2,1)} async-done(((bf16[2048,2048]{1,0:T(8,128)(2,1)}), bf16[256,2048]{1,0:T(8,128)(2,1)}) %reduce-scatter.23.cloned.1.call-update) | async-done | bytes 1048592 | tf_op jit(solution)/shard_map/reduce_scatter | solution.py:201
  1328.3 54.5 %all-gather.35.cloned.1.call-done = bf16[2048,2048]{1,0:T(8,128)(2,1)} async-done(((bf16[256,2048]{1,0:T(8,128)(2,1)}), bf16[2048,2048]{1,0:T(8,128)(2,1)}) %all-gather.35.cloned.1.call-update) | async-done | bytes 8388624 | tf_op jit(solution)/shard_map/all_gather | solution.py:266
  1390.6 137.1 %while.70 = (s32[]{:T(128)}, f32[2048,2,128]{0,2,1:T(8,128)}, f32[2048,2,128]{0,2,1:T(8,128)}, bf16[4,512,2,128]{3,1,2,0:T(8,128)(2,1)}, s32[4]{0:T(128)S(1)}, /...) while((s32[]{:T(128)}, f32[2048,2,128]{0,2,1:T(8,128)}, ...), condition=%wide.region_25.26_spmd.clone, body=%wide.region_23.25_spmd.clone.sunk | while | flops 2714393600 | bytes 145273296 | solution.py:99
  1397.8 8.2 multiply_reduce_fusion.7
  1431.5 8.2 multiply_reduce_fusion.7
  1465.9 8.2 multiply_reduce_fusion.7
  1500.3 8.2 multiply_reduce_fusion.7
  1535.3 11.5 bitcast_convert_fusion.1
  1546.9 71.4 %reduce-scatter.27.cloned.1.call-done = bf16[256,2048]{1,0:T(8,128)(2,1)} async-done(((bf16[2048,2048]{1,0:T(8,128)(2,1)}), bf16[256,2048]{1,0:T(8,128)(2,1)}) %reduce-scatter.27.cloned.1.call-update) | async-done | bytes 1048592 | tf_op jit(solution)/shard_map/reduce_scatter | solution.py:287
  1627.9 54.5 %all-gather.37.cloned.1.call-done = bf16[2048,2048]{1,0:T(8,128)(2,1)} async-done(((bf16[256,2048]{1,0:T(8,128)(2,1)}), bf16[2048,2048]{1,0:T(8,128)(2,1)}) %all-gather.37.cloned.1.call-update) | async-done | bytes 8388624 | tf_op jit(solution)/shard_map/all_gather | solution.py:241
  1682.4 20.1 convert_reduce_fusion.1
  1704.6 11.0 convolution_convert_fusion
  1715.9 71.1 %reduce-scatter.29.cloned.1.call-done = bf16[256,2048]{1,0:T(8,128)(2,1)} async-done(((bf16[2048,2048]{1,0:T(8,128)(2,1)}), bf16[256,2048]{1,0:T(8,128)(2,1)}) %reduce-scatter.29.cloned.1.call-update) | async-done | bytes 1048592 | tf_op jit(solution)/shard_map/reduce_scatter | solution.py:252
  1797.9 16.7 convolution_convert_fusion.6
  1815.1 16.5 convolution_convert_fusion.7
  1831.7 14.1 convolution_convert_fusion.8
  1846.0 14.0 convolution_convert_fusion.9
  1868.2 6.8 convolution_convert_fusion.11
  1875.1 10.8 fusion.137
  1886.2 6.8 convolution_convert_fusion.12
  1894.2 141.9 %while.71 = (s32[]{:T(128)}, f32[2048,2,128]{0,2,1:T(8,128)}, f32[2048,2,128]{0,2,1:T(8,128)}, bf16[4,512,2,128]{3,1,2,0:T(8,128)(2,1)}, s32[4]{0:T(128)S(1)}, /...) while((s32[]{:T(128)}, f32[2048,2,128]{0,2,1:T(8,128)}, ...), condition=%wide.region_34.35_spmd.clone, body=%wide.region_32.34_spmd.clone.sunk | while | flops 2714393600 | bytes 145273296 | solution.py:99
  1902.1 8.2 multiply_reduce_fusion.8
  1937.0 8.2 multiply_reduce_fusion.8
  1972.3 8.2 multiply_reduce_fusion.8
  1980.5 7.3 multiply_convert_fusion.11
  2008.5 8.2 multiply_reduce_fusion.8
  2044.5 12.7 fusion.134
  2057.2 10.9 bitcast_convert_fusion
  2071.8 63.3 %reduce-scatter.45.cloned.1.call-done = bf16[1024,512]{1,0:T(8,128)(2,1)} async-done(((bf16[1024,2048]{1,0:T(8,128)(2,1)}), bf16[1024,512]{1,0:T(8,128)(2,1)}) %reduce-scatter.45.cloned.1.call-update) | async-done | bytes 1048592 | tf_op jit(solution)/shard_map/reduce_scatter | solution.py:310
  2138.9 76.3 %reduce-scatter.43.cloned.1.call-done = bf16[512,1024]{1,0:T(8,128)(2,1)} async-done(((bf16[2048,1024]{1,0:T(8,128)(2,1)}), bf16[512,1024]{1,0:T(8,128)(2,1)}) %reduce-scatter.43.cloned.1.call-update) | async-done | bytes 1048592 | tf_op jit(solution)/shard_map/reduce_scatter | solution.py:307
  2215.2 79.6 %reduce-scatter.41.cloned.1.call-done = bf16[512,1024]{1,0:T(8,128)(2,1)} async-done(((bf16[2048,1024]{1,0:T(8,128)(2,1)}), bf16[512,1024]{1,0:T(8,128)(2,1)}) %reduce-scatter.41.cloned.1.call-update) | async-done | bytes 1048592 | tf_op jit(solution)/shard_map/reduce_scatter | solution.py:307
  2301.1 23.7 reduce-scatter.39.cloned.1.call-done
  2324.8 28.0 %reduce-scatter.37.cloned.1.call-done = bf16[256,512]{1,0:T(8,128)(2,1)} async-done(((bf16[256,2048]{1,0:T(8,128)(2,1)}), bf16[256,512]{1,0:T(8,128)(2,1)}) %reduce-scatter.37.cloned.1.call-update) | async-done | bytes 262160 | tf_op jit(solution)/shard_map/reduce_scatter | solution.py:304
  2354.9 59.8 %reduce-scatter.35.cloned.1.call-done = bf16[512,3,256]{2,0,1:T(8,128)(2,1)} async-done(((bf16[2048,3,256]{2,0,1:T(8,128)(2,1)}), bf16[512,3,256]{2,0,1:T(8,128)(2,1)}) %reduce-scatter.35.cloned.1.call-update) | async-done | bytes 786448 | tf_op jit(solution)/shard_map/reduce_scatter | solution.py:301
  2414.8 62.7 %reduce-scatter.33.cloned.1.call-done = bf16[512,3,256]{2,0,1:T(8,128)(2,1)} async-done(((bf16[2048,3,256]{2,0,1:T(8,128)(2,1)}), bf16[512,3,256]{2,0,1:T(8,128)(2,1)}) %reduce-scatter.33.cloned.1.call-update) | async-done | bytes 786448 | tf_op jit(solution)/shard_map/reduce_scatter | solution.py:301
  2480.9 71.6 %reduce-scatter.31.cloned.1.call-done = bf16[256,2048]{1,0:T(8,128)(2,1)} async-done(((bf16[2048,2048]{1,0:T(8,128)(2,1)}), bf16[256,2048]{1,0:T(8,128)(2,1)}) %reduce-scatter.31.cloned.1.call-update) | async-done | bytes 1048592 | tf_op jit(solution)/shard_map/reduce_scatter | solution.py:287
  2561.5 121.1 %all-reduce.6.cloned.1.call-done = (f32[2,2,2048]{2,1,0:T(2,128)}, f32[2,2,2048]{2,1,0:T(2,128)}, f32[2,2,2048]{2,1,0:T(2,128)}, f32[2,2,2048]{2,1,0:T(2,128)}) async-done(((f32[2,2,2048]{2,1,0:T(2,128)}, f32[2,2,2048]{2,1,0:T(2,128)}, f32[2,2,2048]{2,1,0:T(2,128)}, f32[2,2,2048]{2,1,0:T(2,128)}), (f32[2,2,2048]{2,1,0:T(2,128)}, f32[2,2,2048]{2,1,0:T(2,128)}, f32[2,2,2048]{2,1,0:T(2,128)}, ...) | async-done | bytes 131088 | tf_op jit(solution)/shard_map/psum | solution.py:333
  (659 shorter events, 455.1 us)
Async XLA Ops:
  7.2 69.8 %all-gather.41.cloned.1.call-start = ((), (), s32[]{:S(2)}) async-start(), calls=%async_computation.41 | async-start | bytes 3932160 | tf_op jit(solution)/shard_map/all_gather | solution.py:138
  10.7 121.9 %all-gather.25.cloned.1.call-start = ((), (), s32[]{:S(2)}) async-start(), calls=%async_computation.16 | async-start | bytes 9437184 | tf_op jit(solution)/shard_map/all_gather | solution.py:152
  14.7 189.8 %all-gather.43.cloned.1.call-start = ((), (), s32[]{:S(2)}) async-start(), calls=%async_computation.42 | async-start | bytes 1310720 | tf_op jit(solution)/shard_map/all_gather | solution.py:141
  15.7 267.5 %reduce-scatter.17.cloned.1.call-start = ((), (), s32[]{:S(2)}) async-start(), calls=%async_computation.17 | async-start | bytes 9437184 | tf_op jit(solution)/shard_map/reduce_scatter | solution.py:172
  211.8 154.3 %all-gather.45.cloned.1.call-start = ((), (), s32[]{:S(2)}) async-start(), calls=%async_computation.43 | async-start | bytes 5242880 | tf_op jit(solution)/shard_map/all_gather | solution.py:144
  215.9 205.6 %all-gather.27.cloned.1.call-start = ((), (), s32[]{:S(2)}) async-start(), calls=%async_computation.18 | async-start | bytes 9437184 | tf_op jit(solution)/shard_map/all_gather | solution.py:179
  217.0 372.9 %copy-start.50 = (f32[1,1,2048]{2,1,0:T(1,128)}, f32[1,1,2048]{2,1,0:T(1,128)S(1)}, u32[]{:S(2)}) copy-start(f32[1,1,2048]{2,1,0:T(1,128)S(1)} %get-tuple-element.948) | copy-start | bytes 24580
  288.5 216.0 %all-gather.47.cloned.1.call-start = ((), (), s32[]{:S(2)}) async-start(), calls=%async_computation.44 | async-start | bytes 5242880 | tf_op jit(solution)/shard_map/all_gather | solution.py:145
  292.5 297.4 %reduce-scatter.19.cloned.1.call-start = ((), (), s32[]{:S(2)}) async-start(), calls=%async_computation.19 | async-start | bytes 9437184 | tf_op jit(solution)/shard_map/reduce_scatter | solution.py:201
  293.2 211.3 %copy-start.103 = (f32[1,1024]{1,0:T(1,128)}, f32[1,1024]{1,0:T(1,128)S(1)}, u32[]{:S(2)}) copy-start(f32[1,1024]{1,0:T(1,128)S(1)} %get-tuple-element.959) | copy-start | bytes 12292
  520.0 135.0 %all-gather.49.cloned.1.call-start = ((), (), s32[]{:S(2)}) async-start(), calls=%async_computation.45 | async-start | bytes 3932160 | tf_op jit(solution)/shard_map/all_gather | solution.py:138
  520.7 189.7 %all-gather.29.cloned.1.call-start = ((), (), s32[]{:S(2)}) async-start(), calls=%async_computation.20 | async-start | bytes 9437184 | tf_op jit(solution)/shard_map/all_gather | solution.py:152
  592.1 273.4 %copy-start.6 = (f32[256,2048]{1,0:T(8,128)}, f32[256,2048]{1,0:T(8,128)S(1)}, u32[]{:S(2)}) copy-start(f32[256,2048]{1,0:T(8,128)S(1)} %get-tuple-element.913) | copy-start | bytes 6291460
  594.8 115.7 %copy-start.101 = (f32[3,256]{1,0:T(4,128)S(1)}, f32[3,256]{1,0:T(4,128)}, u32[]{:S(2)}) copy-start(f32[3,256]{1,0:T(4,128)} %get-tuple-element.968) | copy-start | bytes 9220
  594.8 192.0 %all-gather.51.cloned.1.call-start = ((), (), s32[]{:S(2)}) async-start(), calls=%async_computation.46 | async-start | bytes 1310720 | tf_op jit(solution)/shard_map/all_gather | solution.py:141
  595.5 270.0 %reduce-scatter.21.cloned.1.call-start = ((), (), s32[]{:S(2)}) async-start(), calls=%async_computation.21 | async-start | bytes 9437184 | tf_op jit(solution)/shard_map/reduce_scatter | solution.py:172
  794.1 154.4 %all-gather.53.cloned.1.call-start = ((), (), s32[]{:S(2)}) async-start(), calls=%async_computation.47 | async-start | bytes 5242880 | tf_op jit(solution)/shard_map/all_gather | solution.py:144
  794.8 209.1 %all-gather.31.cloned.1.call-start = ((), (), s32[]{:S(2)}) async-start(), calls=%async_computation.22 | async-start | bytes 9437184 | tf_op jit(solution)/shard_map/all_gather | solution.py:179
  869.9 216.9 %all-gather.55.cloned.1.call-start = ((), (), s32[]{:S(2)}) async-start(), calls=%async_computation.48 | async-start | bytes 5242880 | tf_op jit(solution)/shard_map/all_gather | solution.py:145
  870.5 271.2 %all-gather.33.cloned.1.call-start = ((), (), s32[]{:S(2)}) async-start(), calls=%async_computation.24 | async-start | bytes 9437184 | tf_op jit(solution)/shard_map/all_gather | solution.py:241
  871.1 270.6 %copy-start.105 = (f32[1,1024]{1,0:T(1,128)S(1)}, f32[1,1024]{1,0:T(1,128)}, u32[]{:S(2)}) copy-start(f32[1,1024]{1,0:T(1,128)} %get-tuple-element.958) | copy-start | bytes 12292
  871.1 375.8 %reduce-scatter.25.cloned.1.call-start = ((), (), s32[]{:S(2)}) async-start(), calls=%async_computation.25 | async-start | bytes 9437184 | tf_op jit(solution)/shard_map/reduce_scatter | solution.py:252
  1175.4 146.0 %reduce-scatter.23.cloned.1.call-start = ((), (), s32[]{:S(2)}) async-start(), calls=%async_computation.23 | async-start | bytes 9437184 | tf_op jit(solution)/shard_map/reduce_scatter | solution.py:201
  1190.9 130.5 %copy-start.77 = (f32[1,1,2048]{2,1,0:T(1,128)S(1)}, f32[1,1,2048]{2,1,0:T(1,128)}, u32[]{:S(2)}) copy-start(f32[1,1,2048]{2,1,0:T(1,128)} %get-tuple-element.946) | copy-start | bytes 24580
  1190.9 191.8 %all-gather.35.cloned.1.call-start = ((), (), s32[]{:S(2)}) async-start(), calls=%async_computation.26 | async-start | bytes 9437184 | tf_op jit(solution)/shard_map/all_gather | solution.py:266
  1249.4 76.7 %copy-start.28 = (bf16[256,2048]{1,0:T(8,128)(2,1)S(1)}, bf16[256,2048]{1,0:T(8,128)(2,1)}, u32[]{:S(2)}) copy-start(bf16[256,2048]{1,0:T(8,128)(2,1)} %param.20) | copy-start | bytes 3145732
  1328.2 290.1 %reduce-scatter.27.cloned.1.call-start = ((), (), s32[]{:S(2)}) async-start(), calls=%async_computation.27 | async-start | bytes 9437184 | tf_op jit(solution)/shard_map/reduce_scatter | solution.py:287
  1546.9 76.9 %copy-start.29 = (bf16[256,2048]{1,0:T(8,128)(2,1)S(1)}, bf16[256,2048]{1,0:T(8,128)(2,1)}, u32[]{:S(2)}) copy-start(bf16[256,2048]{1,0:T(8,128)(2,1)} %param.20) | copy-start | bytes 3145732
  1546.9 76.9 %copy-start.97 = (f32[256]{0:T(256)S(1)}, f32[256]{0:T(256)}, u32[]{:S(2)}) copy-start(f32[256]{0:T(256)} %copy-done.96) | copy-start | bytes 3076
  1546.9 135.5 %all-gather.37.cloned.1.call-start = ((), (), s32[]{:S(2)}) async-start(), calls=%async_computation.28 | async-start | bytes 9437184 | tf_op jit(solution)/shard_map/all_gather | solution.py:241
  1627.9 159.2 %reduce-scatter.29.cloned.1.call-start = ((), (), s32[]{:S(2)}) async-start(), calls=%async_computation.29 | async-start | bytes 9437184 | tf_op jit(solution)/shard_map/reduce_scatter | solution.py:252
  1715.6 74.3 %copy-start.93 = (f32[256]{0:T(256)S(1)}, f32[256]{0:T(256)}, u32[]{:S(2)}) copy-start(f32[256]{0:T(256)} %copy-done.92) | copy-start | bytes 3076
  1715.6 74.3 %copy-start.91 = (f32[256]{0:T(256)S(1)}, f32[256]{0:T(256)}, u32[]{:S(2)}) copy-start(f32[256]{0:T(256)} %copy-done.90) | copy-start | bytes 3076
  1715.6 152.5 %all-gather.39.cloned.1.call-start = ((), (), s32[]{:S(2)}) async-start(), calls=%async_computation.30 | async-start | bytes 9437184 | tf_op jit(solution)/shard_map/all_gather | solution.py:266
  1797.1 273.3 %all-reduce.4.cloned.1.call-start = ((), (), s32[]{:S(2)}) async-start(), calls=%async_computation.40 | async-start | bytes 131072 | tf_op jit(solution)/shard_map/psum | solution.py:333
  1797.9 273.9 %reduce-scatter.47.cloned.1.call-start = ((), (), s32[]{:S(2)}) async-start(), calls=%async_computation.39 | async-start | bytes 5242880 | tf_op jit(solution)/shard_map/reduce_scatter | solution.py:310
  1814.6 320.4 %reduce-scatter.45.cloned.1.call-start = ((), (), s32[]{:S(2)}) async-start(), calls=%async_computation.38 | async-start | bytes 5242880 | tf_op jit(solution)/shard_map/reduce_scatter | solution.py:310
  1831.6 383.5 %reduce-scatter.43.cloned.1.call-start = ((), (), s32[]{:S(2)}) async-start(), calls=%async_computation.37 | async-start | bytes 5242880 | tf_op jit(solution)/shard_map/reduce_scatter | solution.py:307
  1845.8 448.9 %reduce-scatter.41.cloned.1.call-start = ((), (), s32[]{:S(2)}) async-start(), calls=%async_computation.36 | async-start | bytes 5242880 | tf_op jit(solution)/shard_map/reduce_scatter | solution.py:307
  1860.1 464.7 %reduce-scatter.39.cloned.1.call-start = ((), (), s32[]{:S(2)}) async-start(), calls=%async_computation.35 | async-start | bytes 1310720 | tf_op jit(solution)/shard_map/reduce_scatter | solution.py:304
  1868.1 484.8 %reduce-scatter.37.cloned.1.call-start = ((), (), s32[]{:S(2)}) async-start(), calls=%async_computation.34 | async-start | bytes 1310720 | tf_op jit(solution)/shard_map/reduce_scatter | solution.py:304
  1875.1 539.7 %reduce-scatter.35.cloned.1.call-start = ((), (), s32[]{:S(2)}) async-start(), calls=%async_computation.33 | async-start | bytes 3932160 | tf_op jit(solution)/shard_map/reduce_scatter | solution.py:301
  1886.0 591.5 %reduce-scatter.33.cloned.1.call-start = ((), (), s32[]{:S(2)}) async-start(), calls=%async_computation.32 | async-start | bytes 3932160 | tf_op jit(solution)/shard_map/reduce_scatter | solution.py:301
  2057.2 495.4 %reduce-scatter.31.cloned.1.call-start = ((), (), s32[]{:S(2)}) async-start(), calls=%async_computation.31 | async-start | bytes 9437184 | tf_op jit(solution)/shard_map/reduce_scatter | solution.py:287
  2068.1 614.5 %all-reduce.6.cloned.1.call-start = ((), (), s32[]{:S(2)}) async-start(), calls=%async_computation.49 | async-start | bytes 262144 | tf_op jit(solution)/shard_map/psum | solution.py:333
  2138.9 159.7 %copy-start.70 = (f32[2048]{0:T(1024)S(1)}, f32[2048]{0:T(1024)}, u32[]{:S(2)}) copy-start(f32[2048]{0:T(1024)} %get-tuple-element.815) | copy-start | bytes 24580
  2138.9 159.7 %copy-start.71 = (f32[2048]{0:T(1024)S(1)}, f32[2048]{0:T(1024)}, u32[]{:S(2)}) copy-start(f32[2048]{0:T(1024)} %get-tuple-element.816) | copy-start | bytes 24580
  2138.9 159.7 %copy-start.84 = (f32[2048]{0:T(1024)S(1)}, f32[2048]{0:T(1024)}, u32[]{:S(2)}) copy-start(f32[2048]{0:T(1024)} %get-tuple-element.906) | copy-start | bytes 24580
  2138.9 159.7 %copy-start.85 = (f32[2048]{0:T(1024)S(1)}, f32[2048]{0:T(1024)}, u32[]{:S(2)}) copy-start(f32[2048]{0:T(1024)} %get-tuple-element.904) | copy-start | bytes 24580
  2138.9 160.4 %copy-start.39 = (bf16[2048,1,256]{2,0,1:T(8,128)(2,1)S(1)}, bf16[2048,1,256]{2,0,1:T(8,128)(2,1)}, u32[]{:S(2)}) copy-start(bf16[2048,1,256]{2,0,1:T(8,128)(2,1)} %stack.179) | copy-start | bytes 3145732
  2138.9 160.4 %copy-start.41 = (bf16[2048,1,256]{2,0,1:T(8,128)(2,1)S(1)}, bf16[2048,1,256]{2,0,1:T(8,128)(2,1)}, u32[]{:S(2)}) copy-start(bf16[2048,1,256]{2,0,1:T(8,128)(2,1)} %copy.86) | copy-start | bytes 3145732
  2299.3 253.3 %copy-start.5 = (bf16[256,2048]{1,0:T(8,128)(2,1)S(1)}, bf16[256,2048]{1,0:T(8,128)(2,1)}, u32[]{:S(2)}) copy-start(bf16[256,2048]{1,0:T(8,128)(2,1)} %param.19) | copy-start | bytes 3145732
  2299.3 253.3 %copy-start.54 = (f32[1,1,2048]{2,1,0:T(1,128)S(1)}, f32[1,1,2048]{2,1,0:T(1,128)}, u32[]{:S(2)}) copy-start(f32[1,1,2048]{2,1,0:T(1,128)} %copy-done.53) | copy-start | bytes 24580
  2299.3 253.3 %copy-start.65 = (f32[256]{0:T(256)S(1)}, f32[256]{0:T(256)}, u32[]{:S(2)}) copy-start(f32[256]{0:T(256)} %copy-done.64) | copy-start | bytes 3076
  2301.1 253.3 %copy-start.60 = (f32[2,2,2048]{2,1,0:T(2,128)}, f32[2,2,2048]{2,1,0:T(2,128)S(1)}, u32[]{:S(2)}) copy-start(f32[2,2,2048]{2,1,0:T(2,128)S(1)} %maximum_dynamic-update-slice_fusion.1) | copy-start | bytes 98308
  2352.8 201.6 %copy-start.99 = (f32[256]{0:T(256)S(1)}, f32[256]{0:T(256)}, u32[]{:S(2)}) copy-start(f32[256]{0:T(256)} %copy-done.98) | copy-start | bytes 3076
  2352.8 201.6 %copy-start.89 = (f32[256]{0:T(256)S(1)}, f32[256]{0:T(256)}, u32[]{:S(2)}) copy-start(f32[256]{0:T(256)} %copy-done.88) | copy-start | bytes 3076
  2477.5 79.3 %copy-start.69 = (f32[2048]{0:T(1024)S(1)}, f32[2048]{0:T(1024)}, u32[]{:S(2)}) copy-start(f32[2048]{0:T(1024)} %get-tuple-element.823) | copy-start | bytes 24580
  2477.5 79.3 %copy-start.73 = (f32[2048]{0:T(1024)S(1)}, f32[2048]{0:T(1024)}, u32[]{:S(2)}) copy-start(f32[2048]{0:T(1024)} %get-tuple-element.821) | copy-start | bytes 24580
  2477.5 79.3 %copy-start.76 = (f32[2048]{0:T(1024)S(1)}, f32[2048]{0:T(1024)}, u32[]{:S(2)}) copy-start(f32[2048]{0:T(1024)} %get-tuple-element.819) | copy-start | bytes 24580
  2477.5 80.0 %copy-start.68 = (f32[2048]{0:T(1024)S(1)}, f32[2048]{0:T(1024)}, u32[]{:S(2)}) copy-start(f32[2048]{0:T(1024)} %get-tuple-element.811) | copy-start | bytes 24580
  2477.5 80.0 %copy-start.72 = (f32[2048]{0:T(1024)S(1)}, f32[2048]{0:T(1024)}, u32[]{:S(2)}) copy-start(f32[2048]{0:T(1024)} %get-tuple-element.809) | copy-start | bytes 24580
  2477.5 80.0 %copy-start.75 = (f32[2048]{0:T(1024)S(1)}, f32[2048]{0:T(1024)}, u32[]{:S(2)}) copy-start(f32[2048]{0:T(1024)} %get-tuple-element.807) | copy-start | bytes 24580
  2477.5 80.6 %copy-start.21 = (f32[256,2048]{1,0:T(8,128)S(1)}, f32[256,2048]{1,0:T(8,128)}, u32[]{:S(2)}) copy-start(f32[256,2048]{1,0:T(8,128)} %copy-done.20) | copy-start | bytes 6291460
  (112 other events, 2089.8 us)
Sparse Core Ops, SparseCore 0:
  10.8 66.1 all-gather.40
  79.4 53.0 all-gather.24
  134.7 27.9 all-gather.42
  211.9 71.2 reduce-scatter.16
  285.3 80.7 all-gather.44
  368.5 52.9 all-gather.26
  423.7 80.7 all-gather.46
  520.1 69.7 reduce-scatter.18
  591.5 63.4 all-gather.48
  657.3 53.0 all-gather.28
  712.0 27.9 all-gather.50
  794.2 71.2 reduce-scatter.20
  867.7 80.7 all-gather.52
  951.0 52.9 all-gather.30
  1006.0 80.7 all-gather.54
  1088.7 52.9 all-gather.32
  1175.5 71.2 reduce-scatter.24
  1250.1 71.2 reduce-scatter.22
  1328.3 54.3 all-gather.34
  1547.0 71.2 reduce-scatter.26
  1628.0 54.3 all-gather.36
  1715.8 71.2 reduce-scatter.28
  1797.2 54.3 all-gather.38
  1858.0 117.5 all-reduce.3
  1978.0 77.5 reduce-scatter.46
  2057.7 77.2 reduce-scatter.44
  2137.9 77.2 reduce-scatter.42
  2217.4 77.2 reduce-scatter.40
  2297.2 27.6 reduce-scatter.38
  2327.0 25.8 reduce-scatter.36
  2355.8 58.8 reduce-scatter.34
  2417.2 60.2 reduce-scatter.32
  2481.2 71.2 reduce-scatter.30
  2559.0 123.5 all-reduce.5
where the time goes:
time: 2700 us
  waiting for transfers between devices  1850 us (69%)
  matrix products  531 us (20%)
  other arithmetic  178 us (7%)
  local copies, waits for them, and re-layouts  88.7 us (3%)
  loops' own time  27.1 us (1%)
    reduce_scatter x2, waiting for transfers between devices, shards(): lax.psum_scatter(up_grad_local.astype(jnp.bfloat16), 'dp', scatter_dimens...  156 us
    all_gather x2, waiting for transfers between devices, shards(): lax.all_gather(up_weight[layer_index].astype(jnp.bfloat16), 'dp', axis=0,...  150 us
    reduce_scatter x2, waiting for transfers between devices, shards(): lax.psum_scatter(jnp.einsum('tsi,dsi->td', grad_project, w_project, prefe...  143 us
    reduce_scatter x2, waiting for transfers between devices, shards(): lax.psum_scatter(down_part.astype(jnp.bfloat16), 'mp', scatter_dimension=...  141 us
    all_gather x2, waiting for transfers between devices, shards(): lax.all_gather(down_weight[layer_index].astype(jnp.bfloat16), 'dp', axis=...  137 us
    reduce_scatter x2, waiting for transfers between devices, shards(): lax.psum_scatter(partial_sum.astype(jnp.bfloat16), 'mp', scatter_dimensio...  137 us
    reduce_scatter x2, waiting for transfers between devices, shards(): lax.psum_scatter(jnp.einsum('tf,df->td', grad_hidden, w_up, preferred_ele...  127 us
    reduce_scatter x2, waiting for transfers between devices, shards(): lax.psum_scatter(project_grad_local.astype(jnp.bfloat16), 'dp', scatter_d...  123 us
  transfers between devices with their start and end apart: 34, of which 29 were waited for; matrix products, arithmetic and copies ran while one was open for 18% of the time, Pallas kernels for 0%

commit v1 on v0

v1 whole, which is shorter than its diff:
```python
import functools

import jax
import jax.numpy as jnp
from jax import lax
from jax.experimental import pallas as pl
from jax.experimental.pallas import tpu as pltpu
from jax.sharding import PartitionSpec as P

N_HEADS = 16
BLOCK = 256
LOG2E = 1.4426950408889634
MESH = pl.DeviceIdType.MESH
NT_DIMS = (((1,), (1,)), ((), ()))
norm_eps = 1e-05


def nt(a, b):
    return lax.dot_general(a, b, NT_DIMS, preferred_element_type=jnp.float32)


def nn(a, b):
    return jnp.dot(a, b, preferred_element_type=jnp.float32)


def bias_tile(slope, first_key, first_query, keys, queries):
    kp = first_key + lax.broadcasted_iota(jnp.int32, (keys, queries), 0)
    qp = first_query + lax.broadcasted_iota(jnp.int32, (keys, queries), 1)
    return (jnp.abs(qp - kp).astype(jnp.float32)) * (-slope * LOG2E)

def scores_t(q, k, slope, i, B):
    L = (i+1)*B
    factor = q.shape[1] ** (-0.5) * LOG2E
    st = nt(k, q) * factor
    key = lax.broadcasted_iota(jnp.int32, (L, 1), 0)
    if i > 0:
        m = i * B
        kp = lax.broadcasted_iota(jnp.int32, (m, 1), 0).astype(jnp.float32)
        qp = (m + lax.broadcasted_iota(jnp.int32, (1, B), 1)).astype(jnp.float32)
        head = st[:m] - (qp - kp) * (slope * LOG2E)
        tail = st[m:] + bias_tile(slope, 0, 0, B, B)
        return head, tail
    return None, st + bias_tile(slope, 0, 0, B, B)

def attend_fwd_kernel(slope_ref, q_ref, k_ref, v_ref, ctx_ref, lse_ref, vt_ref):
    B = BLOCK
    slope = slope_ref[pl.program_id(0)]
    T = q_ref.shape[0]
    vt_ref[...] = v_ref[...].T
    for i in range(T // B):
        L = (i+1)*B
        head, tail = scores_t(q_ref[i*B:L, :], k_ref[:L, :], slope, i, B)
        top = jnp.max(tail, axis=0, keepdims=True)
        if head is not None:
            top = jnp.maximum(top, jnp.max(head, axis=0, keepdims=True))
        pt = jnp.exp2(tail - top)
        den = jnp.sum(pt, axis=0, keepdims=True)
        ct = nn(vt_ref[:, i*B:L], pt.astype(jnp.bfloat16))
        if head is not None:
            ph = jnp.exp2(head - top)
            den = den + jnp.sum(ph, axis=0, keepdims=True)
            ct = ct + nn(vt_ref[:, :i*B], ph.astype(jnp.bfloat16))
        ctx_ref[i*B:L, :] = (ct / den).T.astype(ctx_ref.dtype)
        lse_ref[0, i:i+1, :] = top + jnp.log2(den)

def attend_bwd_kernel(slope_ref, q_ref, k_ref, v_ref, g_ref, c_ref, lse_ref, out_ref, sums_ref, kt_ref, dk_ref, dv_ref):
    B = BLOCK
    slope = slope_ref[pl.program_id(0)]
    T = q_ref.shape[0]
    W = q_ref.shape[1]
    factor = W ** (-0.5)
    kt_ref[...] = k_ref[...].T
    qsum = jnp.zeros((1, W), jnp.float32)
    n = T // B
    for i in reversed(range(n)):
        L = (i+1)*B
        q = q_ref[i*B:L, :]
        g = g_ref[i*B:L, :]
        head, tail = scores_t(q, k_ref[:L, :], slope, i, B)
        prod = g.astype(jnp.float32) * c_ref[i*B:L, :].astype(jnp.float32)
        inner = lax.dot_general(jnp.ones((8, W), jnp.float32), prod, NT_DIMS, preferred_element_type=jnp.float32, precision=lax.Precision.HIGHEST)[:1]
        lse = lse_ref[0, i:i+1, :]
        dpt = nt(v_ref[:L, :], g)
        dqt = None
        for part, lo, hi in ((head, 0, i*B), (tail, i*B, L)):
            if part is None:
                continue
            pt = jnp.exp2(part - lse)
            ds = (pt * (dpt[lo:hi] - inner)).astype(jnp.bfloat16)
            pt = pt.astype(jnp.bfloat16)
            dk = nn(ds, q)
            dv = nn(pt, g)
            if i == n - 1:
                dk_ref[lo:hi, :] = dk
                dv_ref[lo:hi, :] = dv
            else:
                dk_ref[lo:hi, :] += dk
                dv_ref[lo:hi, :] += dv
            t = nn(kt_ref[:, lo:hi], ds)
            dqt = t if dqt is None else dqt + t
        dq = (dqt * factor).T.astype(jnp.bfloat16)
        out_ref[0, i*B:L, :] = dq
        qsum += jnp.sum(dq.astype(jnp.float32), axis=0, keepdims=True)
    out_ref[1] = (dk_ref[...] * factor).astype(jnp.bfloat16)
    dv = dv_ref[...].astype(jnp.bfloat16)
    out_ref[2] = dv
    sums_ref[0:1, :] = qsum
    sums_ref[1:2, :] = jnp.sum(dv.astype(jnp.float32), axis=0, keepdims=True)

def attend_fwd(project, slopes):
    T, W = project.shape
    H = W // 384
    col = lambda part: pl.BlockSpec((T, 128), lambda h, part=part: (0, part * H + h))
    return pl.pallas_call(
        attend_fwd_kernel, grid=(H,),
        out_shape=(jax.ShapeDtypeStruct((T, H*128), jnp.bfloat16), jax.ShapeDtypeStruct((H, T//BLOCK, BLOCK), jnp.float32)),
        in_specs=[pl.BlockSpec(memory_space=pltpu.SMEM), col(0), col(1), col(2)],
        out_specs=(pl.BlockSpec((T,128), lambda h: (0,h)), pl.BlockSpec((1, T//BLOCK, BLOCK), lambda h: (h,0,0))),
        scratch_shapes=[pltpu.VMEM((128, T), jnp.bfloat16)],
        compiler_params=pltpu.CompilerParams(vmem_limit_bytes=48<<20),
        cost_estimate=pl.CostEstimate(flops=4*T*T*128*H//2, bytes_accessed=8*T*H*128, transcendentals=T*T*H//2),
        name="attend_fwd")(slopes, project, project, project)

def attend_bwd(project, grad_context, context, lse, slopes):
    T, W = project.shape
    H = W // 384
    col = lambda part: pl.BlockSpec((T, 128), lambda h, part=part: (0, part * H + h))
    return pl.pallas_call(
        attend_bwd_kernel, grid=(H,),
        out_shape=(jax.ShapeDtypeStruct((3, T, H*128), jnp.bfloat16), jax.ShapeDtypeStruct((2, H*128), jnp.float32)),
        in_specs=[pl.BlockSpec(memory_space=pltpu.SMEM), col(0), col(1), col(2), col(0), col(0), pl.BlockSpec((1, T//BLOCK, BLOCK), lambda h: (h,0,0))],
        out_specs=(pl.BlockSpec((3, T,128), lambda h: (0, 0,h)), pl.BlockSpec((2,128), lambda h: (0,h))),
        scratch_shapes=[pltpu.VMEM((128, T), jnp.bfloat16), pltpu.VMEM((T,128), jnp.float32), pltpu.VMEM((T,128), jnp.float32)],
        compiler_params=pltpu.CompilerParams(vmem_limit_bytes=56<<20),
        cost_estimate=pl.CostEstimate(flops=10*T*T*128*H//2, bytes_accessed=16*T*H*128, transcendentals=T*T*H//2),
        name="attend_bwd")(slopes, project, project, project, grad_context, context, lse)


def peers():
    me = lax.axis_index("mp")
    core = me % 2
    bx = (me // 2) % 2
    by = me // 4
    return me, core, bx, by, me + 1 - 2 * core, me + 2 - 4 * bx, me + 4 - 8 * by


def owner(rel, core, bx, by):
    c = core if rel % 2 == 0 else 1 - core
    x = bx if (rel // 2) % 2 == 0 else 1 - bx
    y = by if rel // 4 == 0 else 1 - by
    return y * 4 + x * 2 + c


def enter(partner, xn, yn):
    barrier = pltpu.get_barrier_semaphore()
    for n in (partner, xn, yn):
        pl.semaphore_signal(barrier, inc=1, device_id={"mp": n}, device_id_type=MESH)
    pl.semaphore_wait(barrier, 3)


def gather_kernel(C, n_in, n_out, body, *refs):
    x_ref, ins = refs[0], refs[1 : 1 + n_in]
    full_ref, outs = refs[1 + n_in], refs[2 + n_in : 2 + n_in + n_out]
    buf, send, recv, loc = refs[2 + n_in + n_out :]
    R, D = x_ref.shape
    rc = R // C
    me, core, bx, by, partner, xn, yn = peers()
    enter(partner, xn, yn)

    def copy(src, rel, k, target, sidx):
        rows = pl.ds(k * rc, rc)
        return pltpu.make_async_remote_copy(
            src_ref=src.at[rows, :],
            dst_ref=buf.at[rel, rows, :],
            send_sem=send.at[sidx, k],
            recv_sem=recv.at[rel, k],
            device_id={"mp": target},
            device_id_type=MESH,
        )

    def arrive(rel, k):
        copy(x_ref, rel, k, partner, 0).wait_recv()

    sent = []
    for k in range(C):
        for rel, target, s in ((2, xn, 1), (4, yn, 2), (1, partner, 0)):
            c = copy(x_ref, rel, k, target, s)
            c.start()
            sent.append(c)

    def block(rel):
        src = x_ref if rel == 0 else buf.at[rel]
        start = pl.multiple_of(owner(rel, core, bx, by) * R, R)
        rows = pl.ds(start, R)
        lc = pltpu.make_async_copy(src, full_ref.at[rows, :], loc.at[rel])
        lc.start()
        body(rel == 0, src, rows, ins, outs)
        return lc

    locs = [block(0)]
    dl = 4 - 2 * core
    fwd_target = jnp.where(core == 0, xn, yn)
    for k in range(C):
        arrive(2, k)
        arrive(4, k)
        for c in (
            copy(buf.at[dl], 6, k, fwd_target, 3),
            copy(buf.at[2], 3, k, partner, 4),
            copy(buf.at[4], 5, k, partner, 5),
        ):
            c.start()
            sent.append(c)
        if k == 0:
            for kk in range(C):
                arrive(1, kk)
            locs.append(block(1))
        if k >= 1:
            arrive(6, k - 1)
            c = copy(buf.at[6], 7, k - 1, partner, 6)
            c.start()
            sent.append(c)
    locs.append(block(2))
    locs.append(block(4))
    arrive(6, C - 1)
    c = copy(buf.at[6], 7, C - 1, partner, 6)
    c.start()
    sent.append(c)
    for k in range(C):
        arrive(3, k)
        arrive(5, k)
    locs.append(block(3))
    locs.append(block(5))
    locs.append(block(6))
    for k in range(C):
        arrive(7, k)
    locs.append(block(7))
    for c in sent:
        c.wait_send()
    for c in locs:
        c.wait()


def gather_call(name, cid, x, ins, outs, body, C=4):
    R, D = x.shape
    vmem = pl.BlockSpec(memory_space=pltpu.VMEM)
    flops = 2 * 8 * R * D * outs[0].shape[1]
    return pl.pallas_call(
        functools.partial(gather_kernel, C, len(ins), len(outs), body),
        out_shape=(jax.ShapeDtypeStruct((8 * R, D), x.dtype), *outs),
        in_specs=[vmem] * (1 + len(ins)),
        out_specs=(pl.BlockSpec(memory_space=pl.ANY),) + (vmem,) * len(outs),
        scratch_shapes=[
            pltpu.VMEM((8, R, D), x.dtype),
            pltpu.SemaphoreType.DMA((7, C)),
            pltpu.SemaphoreType.DMA((8, C)),
            pltpu.SemaphoreType.DMA((8,)),
        ],
        compiler_params=pltpu.CompilerParams(
            collective_id=cid, has_side_effects=True, vmem_limit_bytes=60 << 20
        ),
        cost_estimate=pl.CostEstimate(flops=flops, bytes_accessed=32 * R * D, transcendentals=0),
        name=name,
    )(x, *ins)


def tiles(n, step, f):
    step = min(step, n)

    @pl.loop(0, n // step)
    def _(j):
        f(pl.ds(pl.multiple_of(j * step, step), step))


def project_body(first, src, rows, ins, outs):
    w, shift = ins

    def f(cols):
        outs[0][rows, cols] = (nn(src[...], w[:, cols]) + shift[:, cols]).astype(jnp.bfloat16)

    tiles(w.shape[1], 256, f)


def up_body(first, src, rows, ins, outs):
    w, shift = ins

    def f(cols):
        v = nn(src[...], w[:, cols]) + shift[:, cols]
        t = jnp.tanh(0.7978845608028654 * (v + 0.044715 * v * v * v))
        outs[0][rows, cols] = (0.5 * v * (1.0 + t)).astype(jnp.bfloat16)
        d = 0.5 * (1.0 + t) + 0.5 * v * (1.0 - t * t) * (
            0.7978845608028654 * (1.0 + 3 * 0.044715 * v * v)
        )
        outs[1][rows, cols] = d.astype(jnp.bfloat16)

    tiles(w.shape[1], 256, f)


def wide_nt(src, w, cols):
    Z, _, d = w.shape
    total = None
    for z in range(Z):
        t = nt(src[:, z * d : (z + 1) * d], w[z, cols, :])
        total = t if total is None else total + t
    return total


def down_back_body(first, src, rows, ins, outs):
    w, slope = ins

    def f(cols):
        g = wide_nt(src, w, cols) * slope[rows, cols].astype(jnp.float32)
        g = g.astype(jnp.bfloat16)
        outs[0][rows, cols] = g
        sums = jnp.sum(g.astype(jnp.float32), axis=0, keepdims=True)
        if first:
            outs[1][:, cols] = sums
        else:
            outs[1][:, cols] += sums

    tiles(w.shape[1], 256, f)


def dense_back_body(first, src, rows, ins, outs):
    (w,) = ins

    def f(cols):
        outs[0][rows, cols] = wide_nt(src, w, cols).astype(jnp.bfloat16)

    tiles(w.shape[1], 256, f)


def scatter_kernel(C, n_in, body, *refs):
    ins, out_ref = refs[:n_in], refs[n_in]
    pbuf, rbuf, send, recv = refs[n_in + 1 :]
    R, D = out_ref.shape
    rc = R // C
    me, core, bx, by, partner, xn, yn = peers()
    enter(partner, xn, yn)
    dn = jnp.where(core == 0, yn, xn)
    fn = jnp.where(core == 0, xn, yn)

    def copy(src, slot, k, target):
        rows = pl.ds(k * rc, rc)
        return pltpu.make_async_remote_copy(
            src_ref=src.at[rows, :],
            dst_ref=rbuf.at[slot, rows, :],
            send_sem=send.at[slot, k],
            recv_sem=recv.at[slot, k],
            device_id={"mp": target},
            device_id_type=MESH,
        )

    sent = []

    def send_one(src, slot, target, k):
        c = copy(src, slot, k, target)
        c.start()
        sent.append(c)

    def arrive(slot, k):
        copy(pbuf.at[0], slot, k, partner).wait_recv()

    def dest_rank(which, c):
        if which == "diag":
            return (1 - by) * 4 + (1 - bx) * 2 + c
        if which == "me":
            return by * 4 + bx * 2 + c
        flip_y = (1 - c) if which == "direct" else c
        y = by + flip_y * (1 - 2 * by)
        x = bx + (1 - flip_y) * (1 - 2 * bx)
        return y * 4 + x * 2 + c

    def compute(which, c, slot):
        rows = pl.ds(pl.multiple_of(dest_rank(which, c) * R, R), R)
        body(rows, ins, pbuf.at[slot])

    def add(slot, rslot, k):
        @pl.loop(0, rc // 16)
        def _(i):
            rows = pl.ds(pl.multiple_of(k * rc + i * 16, 16), 16)
            pbuf[slot, rows, :] = (
                pbuf[slot, rows, :].astype(jnp.float32) + rbuf[rslot, rows, :].astype(jnp.float32)
            ).astype(pbuf.dtype)

    for i, which in enumerate(("diag", "direct", "onward", "me")):
        compute(which, 1 - core, i)
        for k in range(C):
            send_one(pbuf.at[i], i, partner, k)
        compute(which, core, 4 + i)
        for k in range(C):
            arrive(i, k)
            add(4 + i, i, k)
            if i == 0:
                send_one(pbuf.at[4], 4, dn, k)
            if i == 1:
                send_one(pbuf.at[5], 5, dn, k)
            if i == 2:
                arrive(4, k)
                add(6, 4, k)
                send_one(pbuf.at[6], 6, fn, k)
    for k in range(C):
        arrive(5, k)
        arrive(6, k)

        @pl.loop(0, rc // 16)
        def _(i):
            rows = pl.ds(pl.multiple_of(k * rc + i * 16, 16), 16)
            out_ref[rows, :] = (
                pbuf[7, rows, :].astype(jnp.float32)
                + rbuf[5, rows, :].astype(jnp.float32)
                + rbuf[6, rows, :].astype(jnp.float32)
            )
    for c in sent:
        c.wait_send()


def scatter_call(name, cid, T, D, ins, body, C=4):
    R = T // 8
    vmem = pl.BlockSpec(memory_space=pltpu.VMEM)
    return pl.pallas_call(
        functools.partial(scatter_kernel, C, len(ins), body),
        out_shape=jax.ShapeDtypeStruct((R, D), jnp.float32),
        in_specs=[vmem] * len(ins),
        out_specs=vmem,
        scratch_shapes=[
            pltpu.VMEM((8, R, D), jnp.bfloat16),
            pltpu.VMEM((7, R, D), jnp.bfloat16),
            pltpu.SemaphoreType.DMA((7, C)),
            pltpu.SemaphoreType.DMA((7, C)),
        ],
        compiler_params=pltpu.CompilerParams(
            collective_id=cid, has_side_effects=True, vmem_limit_bytes=60 << 20
        ),
        cost_estimate=pl.CostEstimate(flops=2 * T * D * 1024, bytes_accessed=32 * R * D, transcendentals=0),
        name=name,
    )(*ins)


def row_split_body(rows, ins, out):
    a, w = ins
    Z, _, d = w.shape
    for z in range(Z):
        out[:, z * d : (z + 1) * d] = nn(a[rows, :], w[z]).astype(out.dtype)


def up_back_body(rows, ins, out):
    a, w = ins

    def f(cols):
        out[:, cols] = nt(a[rows, :], w[cols, :]).astype(out.dtype)

    tiles(w.shape[0], 512, f)


def project_back_body(rows, ins, out):
    a, w = ins
    S, _, width = a.shape

    def f(cols):
        total = None
        for s in range(S):
            t = nt(a[s, rows, :], w[cols, s * width : (s + 1) * width])
            total = t if total is None else total + t
        out[:, cols] = total.astype(out.dtype)

    tiles(w.shape[0], 512, f)


def layer_norm(values, scale_row, shift_row):
    centre = jnp.mean(values, axis=-1, keepdims=True)
    centred = values - centre
    spread = jnp.mean(centred * centred, axis=-1, keepdims=True)
    return centred * lax.rsqrt(spread + norm_eps) * scale_row + shift_row


def gather_project(cid, normed, w, shift):
    if lax.axis_size("mp") == 8:
        out = jax.ShapeDtypeStruct((8 * normed.shape[0], w.shape[1]), jnp.bfloat16)
        return gather_call("gather_project", cid, normed, (w, shift[None]), (out,), project_body)
    full = lax.all_gather(normed, "mp", axis=0, tiled=True)
    return full, (nn(full, w) + shift).astype(jnp.bfloat16)


def gather_up(cid, normed, w, shift):
    if lax.axis_size("mp") == 8:
        out = jax.ShapeDtypeStruct((8 * normed.shape[0], w.shape[1]), jnp.bfloat16)
        return gather_call("gather_up", cid, normed, (w, shift[None]), (out, out), up_body)
    full = lax.all_gather(normed, "mp", axis=0, tiled=True)
    v = nn(full, w) + shift
    t = jnp.tanh(0.7978845608028654 * (v + 0.044715 * v * v * v))
    d = 0.5 * (1.0 + t) + 0.5 * v * (1.0 - t * t) * (
        0.7978845608028654 * (1.0 + 3 * 0.044715 * v * v)
    )
    return full, (0.5 * v * (1.0 + t)).astype(jnp.bfloat16), d.astype(jnp.bfloat16)


def gather_down_back(cid, grad, w, slope):
    if lax.axis_size("mp") == 8:
        outs = (
            jax.ShapeDtypeStruct(slope.shape, jnp.bfloat16),
            jax.ShapeDtypeStruct((1, slope.shape[1]), jnp.float32),
        )
        return gather_call("gather_down_back", cid, grad, (w, slope), outs, down_back_body)
    full = lax.all_gather(grad, "mp", axis=0, tiled=True)
    g = (wide_nt(full, w, slice(None)) * slope.astype(jnp.float32)).astype(jnp.bfloat16)
    return full, g, jnp.sum(g.astype(jnp.float32), axis=0, keepdims=True)


def gather_dense_back(cid, grad, w):
    if lax.axis_size("mp") == 8:
        out = jax.ShapeDtypeStruct((8 * grad.shape[0], w.shape[1]), jnp.bfloat16)
        return gather_call("gather_dense_back", cid, grad, (w,), (out,), dense_back_body)
    full = lax.all_gather(grad, "mp", axis=0, tiled=True)
    return full, wide_nt(full, w, slice(None)).astype(jnp.bfloat16)


def scatter(name, cid, T, D, ins, body):
    if lax.axis_size("mp") == 8:
        return scatter_call(name, cid, T, D, ins, body)
    a, w = ins
    if body is row_split_body:
        part = jnp.concatenate([nn(a, w[z]) for z in range(w.shape[0])], axis=1)
    elif body is up_back_body:
        part = nt(a, w)
    else:
        width = a.shape[2]
        part = sum(nt(a[s], w[:, s * width : (s + 1) * width]) for s in range(a.shape[0]))
    return lax.psum_scatter(
        part.astype(jnp.bfloat16), "mp", scatter_dimension=0, tiled=True
    ).astype(jnp.float32)


def shards(
    inputs,
    out_grad,
    project_weight,
    dense_weight,
    up_weight,
    down_weight,
    project_bias,
    up_bias,
    norm_gain,
    norm_bias,
    output_bias,
):
    tensor_size = lax.axis_size("mp")
    data_size = lax.axis_size("dp")
    tensor_rank = lax.axis_index("mp")
    row_count, model_width = inputs.shape
    total_rows = row_count * tensor_size
    inner_width = project_weight.shape[3]
    heads_here = N_HEADS // tensor_size
    layer_count = project_weight.shape[0]
    slopes = 2.0 ** (
        -8.0
        * (tensor_rank * heads_here + lax.iota(jnp.int32, heads_here) + 1).astype(jnp.float32)
        / N_HEADS
    )
    low = jnp.bfloat16
    gathered = []
    for l in range(layer_count):
        gathered.append(
            (
                lax.all_gather(
                    project_weight[l].reshape(-1, 3 * inner_width).astype(low),
                    "dp",
                    axis=0,
                    tiled=True,
                ),
                lax.all_gather(dense_weight[l].astype(low), "dp", axis=0),
                lax.all_gather(up_weight[l].astype(low), "dp", axis=0, tiled=True),
                lax.all_gather(down_weight[l].astype(low), "dp", axis=0),
            )
        )
    stream = inputs.astype(jnp.float32)
    stored = []
    for l in range(layer_count):
        w_project, w_dense, w_up, w_down = gathered[l]
        normed = layer_norm(stream, norm_gain[l, 0], norm_bias[l, 0]).astype(low)
        shift = jnp.concatenate(
            [project_bias[l, 0], jnp.zeros((inner_width,), jnp.float32), project_bias[l, 1]]
        )
        normed_all, project = gather_project(10 * l, normed, w_project, shift)
        context, log_norms = attend_fwd(project, slopes)
        attn_rows = scatter(
            "dense_scatter", 10 * l + 1, total_rows, model_width, (context, w_dense), row_split_body
        )
        middle = stream + attn_rows + output_bias[l, 0]
        normed2 = layer_norm(middle, norm_gain[l, 1], norm_bias[l, 1]).astype(low)
        normed2_all, active, slope = gather_up(10 * l + 2, normed2, w_up, up_bias[l])
        down_rows = scatter(
            "down_scatter", 10 * l + 3, total_rows, model_width, (active, w_down), row_split_body
        )
        stored.append(
            (stream, normed_all, project, log_norms, context, middle, normed2_all, active, slope)
        )
        stream = middle + down_rows + output_bias[l, 1]
    outputs = stream.astype(low)
    grad = out_grad.astype(jnp.float32)
    project_grads = [None] * layer_count
    dense_grads = [None] * layer_count
    up_grads = [None] * layer_count
    down_grads = [None] * layer_count
    copied = [None] * layer_count
    split = [None] * layer_count

    def reduce_dp(part):
        return lax.psum_scatter(part.astype(low), "dp", scatter_dimension=0, tiled=True).astype(
            jnp.float32
        )

    for l in reversed(range(layer_count)):
        w_project, w_dense, w_up, w_down = gathered[l]
        stream_in, normed_all, project, log_norms, context, middle, normed2_all, active, slope = (
            stored[l]
        )
        down_bias_grad = jnp.sum(grad, axis=0)
        grad_down, grad_hidden, up_bias_part = gather_down_back(
            10 * l + 4, grad.astype(low), w_down, slope
        )
        down_grads[l] = reduce_dp(
            jnp.einsum(
                "tf,tzd->zfd",
                active,
                grad_down.reshape(total_rows, data_size, -1),
                preferred_element_type=jnp.float32,
            )
        )[0]
        grad_normed2 = scatter(
            "up_back_scatter",
            10 * l + 5,
            total_rows,
            model_width,
            (grad_hidden, w_up),
            up_back_body,
        )
        up_grads[l] = reduce_dp(
            jnp.einsum("td,tf->df", normed2_all, grad_hidden, preferred_element_type=jnp.float32)
        )
        norm_back = jax.vjp(layer_norm, middle, norm_gain[l, 1], norm_bias[l, 1])[1]
        grad_from_norm, gain_second, shift_second = norm_back(grad_normed2)
        grad_middle = grad + grad_from_norm
        dense_bias_grad = jnp.sum(grad_middle, axis=0)
        grad_branch, grad_context = gather_dense_back(10 * l + 6, grad_middle.astype(low), w_dense)
        dense_grads[l] = reduce_dp(
            jnp.einsum(
                "ti,tzd->zid",
                context,
                grad_branch.reshape(total_rows, data_size, -1),
                preferred_element_type=jnp.float32,
            )
        )[0]
        grad_project, project_bias_part = attend_bwd(
            project, grad_context, context, log_norms, slopes
        )
        grad_normed = scatter(
            "project_back_scatter",
            10 * l + 7,
            total_rows,
            model_width,
            (grad_project, w_project),
            project_back_body,
        )
        project_grads[l] = reduce_dp(
            jnp.einsum(
                "td,sti->dsi", normed_all, grad_project, preferred_element_type=jnp.float32
            )
        )
        norm_back = jax.vjp(layer_norm, stream_in, norm_gain[l, 0], norm_bias[l, 0])[1]
        grad_from_norm, gain_first, shift_first = norm_back(grad_normed)
        grad = grad_middle + grad_from_norm
        copied[l] = lax.psum(
            jnp.stack(
                [gain_first, gain_second, shift_first, shift_second, dense_bias_grad, down_bias_grad]
            ),
            ("dp", "mp"),
        )
        split[l] = lax.psum(
            jnp.concatenate([project_bias_part.reshape(-1), up_bias_part.reshape(-1)]), "dp"
        )
    copied = jnp.stack(copied)
    split = jnp.stack(split)
    return (
        outputs,
        grad,
        jnp.stack(project_grads),
        jnp.stack(dense_grads),
        jnp.stack(up_grads),
        jnp.stack(down_grads),
        split[:, : 2 * inner_width].reshape(layer_count, 2, inner_width),
        split[:, 2 * inner_width :],
        copied[:, 0:2],
        copied[:, 2:4],
        copied[:, 4:6],
    )


def solution(mesh):
    rows = P(("dp", "mp"), None)
    specs = (P(None, "dp", None, "mp"), P(None, "mp", "dp"), P(None, "dp", "mp"), P(None, "mp", "dp"))
    biases = (P(None, None, "mp"), P(None, "mp"), P(), P(), P())
    return jax.shard_map(
        shards,
        mesh=mesh,
        in_specs=(rows, rows, *specs, *biases),
        out_specs=(rows, rows, *specs, *biases),
        check_vma=False,
    )
```

time: 2700 us -> 1660 us (0.61)
  waiting for transfers between devices: 1850 us -> 568 us
  Pallas kernels: 0 us -> 815 us
  matrix products: 531 us -> 92.4 us
  other arithmetic: 178 us -> 57.5 us
  loops' own time: 27.1 us -> 0 us
    pallas_call x0 -> x20, Pallas kernels: none -> 815 us  [the longest x8 391 us: gather_call(): pl.pallas_call(functools.partial(gather_kernel, C, len(ins), len(outs), b...]
    all_gather x16 -> x8, waiting for transfers between devices: 785 us -> 114 us  [the longest x2 61.3 us: shards(): lax.all_gather(project_weight[l].reshape(-1, 3 * inner_width).astype(low)...]
    reduce_scatter x16 -> x8, waiting for transfers between devices: 941 us -> 452 us  [reduce_dp(): lax.psum_scatter(part.astype(low), 'dp', scatter_dimension=0, tiled=True)]
    dot_general x78 -> x6, matrix products: 503 us -> 64.2 us  [the longest x2 27.6 us: shards(): jnp.einsum('tf,tzd->zfd', active, grad_down.reshape(total_rows, data_size...]
    psum x2 -> x1, waiting for transfers between devices: 121 us -> 0.01 us  [shards(): lax.psum(jnp.stack([gain_first, gain_second, shift_first, shift_second, d...]
    convert_element_type x30 -> x7, other arithmetic: 73.4 us -> 9.22 us  [the longest x2 2.86 us: shards(): normed = layer_norm(stream, norm_gain[l, 0], norm_bias[l, 0]).astype(low)]
    reshape x0 -> x5, local copies, waits for them, and re-layouts: none -> 49 us  [the longest x2 24.5 us: shards(): grad_branch.reshape(total_rows, data_size, -1)]
    reduce_sum x10 -> x0, other arithmetic: 28.2 us -> none  [the longest x8 26 us: one_block(): denominator = jnp.sum(weights, axis=-1, keepdims=True)]
  transfers between devices with their start and end apart: 34 -> 17, of which waited for: 29 -> 12; matrix products, arithmetic and copies ran while one was open for 18% -> 11% of each run, Pallas kernels for 0% -> 22%
where the time goes in v1:
time: 1660 us; the launch traced here: 1650 us
  Pallas kernels  815 us (49%)
  waiting for transfers between devices  568 us (34%)
  matrix products  92.4 us (6%)
  local copies, waits for them, and re-layouts  86.7 us (5%)
  other arithmetic  57.5 us (3%)
  blocking collectives  17.5 us (1%)
    reduce_scatter x8, waiting for transfers between devices, reduce_dp(): lax.psum_scatter(part.astype(low), 'dp', scatter_dimension=0, tiled=True)  452 us
    pallas_call x8, Pallas kernels, gather_call(): pl.pallas_call(functools.partial(gather_kernel, C, len(ins), len(outs), b...  391 us
    pallas_call x8, Pallas kernels, scatter_call(): pl.pallas_call(functools.partial(scatter_kernel, C, len(ins), body), out_...  362 us
    all_gather x2, waiting for transfers between devices, shards(): lax.all_gather(project_weight[l].reshape(-1, 3 * inner_width).astype(low)...  61.3 us
    all_gather x2, waiting for transfers between devices, shards(): lax.all_gather(down_weight[l].astype(low), 'dp', axis=0)  52.6 us
    pallas_call x2, Pallas kernels, attend_bwd(): pl.pallas_call(attend_bwd_kernel, grid=(H,), out_shape=(jax.ShapeDtypeStr...  35.8 us
  transfers between devices with their start and end apart: 17, of which 12 were waited for; matrix products, arithmetic and copies ran while one was open for 11% of the time, Pallas kernels for 22%

profile of v1, /device:TPU:0, one launch (start us, length us, event | category | flops | bytes accessed | tf_op | source)
XLA Modules:
  0.0 1652.9 jit_solution(975185570076516299)
XLA Ops:
  7.2 2.2 copy.43
  11.8 2.5 convert.26
  14.3 1.5 fusion.54
  15.9 2.5 convert.27
  18.3 1.5 fusion.53
  28.3 48.8 %all-gather.11.cloned.1.call-done.refs_1_ = bf16[2048,768]{1,0:T(8,128)(2,1)} async-done(((bf16[512,768]{1,0:T(8,128)(2,1)}), bf16[2048,768]{1,0:T(8,128)(2,1)}) %all-gather.11.cloned.1.call-update) | async-done | bytes 3145744 | tf_op jit(solution)/shard_map/all_gather | solution.py:564
  77.1 47.3 %gather_project.2 = (bf16[2048,2048]{1,0:T(8,128)(2,1)}, bf16[2048,768]{1,0:T(8,128)(2,1)}) custom-call(bf16[256,2048]{1,0:T(8,128)(2,1)} %fusion.25.refs_0_, bf16[2048,768]{1,0:T(8,128)(2,1)} %all-gather.11.cloned.1.call-done.refs_1_, f32[1,768]{1,0:T(1,128)} %broadcast_in_dim.20.refs_2_), custom_call_target="tpu_custom_call" | custom-call | flops 6442450944 | bytes 16777216 | tf_op jit(solution)/shard_map/gather_project/pallas_call | solution.py:247
  124.4 1.9 copy-done
  126.3 13.1 attend_fwd.2
  140.9 42.6 %dense_scatter.2 = f32[256,2048]{1,0:T(8,128)} custom-call(bf16[2048,256]{1,0:T(8,128)(2,1)} %copy-done.3, bf16[4,256,512]{2,1,0:T(8,128)(2,1)} %all-gather.13.cloned.1.call-done.refs_1_), custom_call_target="tpu_custom_call" | custom-call | flops 8589934592 | bytes 16777216 | tf_op jit(solution)/shard_map/dense_scatter/pallas_call | solution.py:420
  183.5 2.0 fusion.51
  187.7 55.0 %gather_up.2 = (bf16[2048,2048]{1,0:T(8,128)(2,1)}, bf16[2048,1024]{1,0:T(8,128)(2,1)}, bf16[2048,1024]{1,0:T(8,128)(2,1)}) custom-call(bf16[256,2048]{1,0:T(8,128)(2,1)} %add_convert_fusion.3.refs_0_, bf16[2048,1024]{1,0:T(8,128)(2,1)} %bitcast.147, f32[1,1024]{1,0:T(1,128)} %get-tuple-element.162.refs_2_), custom_call_target="tpu_custom_call" | custom-call | flops 8589934592 | bytes 16777216 | tf_op jit(solution)/shard_map/gather_up/pallas_call | solution.py:247
  242.8 26.3 %all-gather.15.cloned.1.call-done.refs_1_ = bf16[4,1024,512]{2,1,0:T(8,128)(2,1)} async-done(((bf16[1,1024,512]{2,1,0:T(8,128)(2,1)}), bf16[4,1024,512]{2,1,0:T(8,128)(2,1)}) %all-gather.15.cloned.1.call-update) | async-done | bytes 4194320 | tf_op jit(solution)/shard_map/all_gather | solution.py:572
  269.1 46.3 %down_scatter.2 = f32[256,2048]{1,0:T(8,128)} custom-call(bf16[2048,1024]{1,0:T(8,128)(2,1)} %get-tuple-element.41.refs_0_, bf16[4,1024,512]{2,1,0:T(8,128)(2,1)} %all-gather.15.cloned.1.call-done.refs_1_), custom_call_target="tpu_custom_call" | custom-call | flops 8589934592 | bytes 16777216 | tf_op jit(solution)/shard_map/down_scatter/pallas_call | solution.py:420
  315.4 1.9 fusion.50
  320.1 12.5 all-gather.17.cloned.1.call-done.refs_1_
  332.5 47.1 %gather_project.3 = (bf16[2048,2048]{1,0:T(8,128)(2,1)}, bf16[2048,768]{1,0:T(8,128)(2,1)}) custom-call(bf16[256,2048]{1,0:T(8,128)(2,1)} %add_convert_fusion.2.refs_0_, bf16[2048,768]{1,0:T(8,128)(2,1)} %all-gather.17.cloned.1.call-done.refs_1_, f32[1,768]{1,0:T(1,128)} %broadcast_in_dim.21.refs_2_), custom_call_target="tpu_custom_call" | custom-call | flops 6442450944 | bytes 16777216 | tf_op jit(solution)/shard_map/gather_project/pallas_call | solution.py:247
  379.6 1.9 copy-done.1
  381.5 13.3 attend_fwd.3
  396.4 42.2 %dense_scatter.3 = f32[256,2048]{1,0:T(8,128)} custom-call(bf16[2048,256]{1,0:T(8,128)(2,1)} %copy-done.5, bf16[4,256,512]{2,1,0:T(8,128)(2,1)} %all-gather.19.cloned.1.call-done.refs_1_), custom_call_target="tpu_custom_call" | custom-call | flops 8589934592 | bytes 16777216 | tf_op jit(solution)/shard_map/dense_scatter/pallas_call | solution.py:420
  438.6 2.6 fusion.49
  443.9 54.4 %gather_up.3 = (bf16[2048,2048]{1,0:T(8,128)(2,1)}, bf16[2048,1024]{1,0:T(8,128)(2,1)}, bf16[2048,1024]{1,0:T(8,128)(2,1)}) custom-call(bf16[256,2048]{1,0:T(8,128)(2,1)} %add_convert_fusion.1.refs_0_, bf16[2048,1024]{1,0:T(8,128)(2,1)} %bitcast.149, f32[1,1024]{1,0:T(1,128)} %get-tuple-element.161.refs_2_), custom_call_target="tpu_custom_call" | custom-call | flops 8589934592 | bytes 16777216 | tf_op jit(solution)/shard_map/gather_up/pallas_call | solution.py:247
  498.3 26.3 %all-gather.21.cloned.1.call-done.refs_1_ = bf16[4,1024,512]{2,1,0:T(8,128)(2,1)} async-done(((bf16[1,1024,512]{2,1,0:T(8,128)(2,1)}), bf16[4,1024,512]{2,1,0:T(8,128)(2,1)}) %all-gather.21.cloned.1.call-update) | async-done | bytes 4194320 | tf_op jit(solution)/shard_map/all_gather | solution.py:572
  524.5 52.4 %gather_down_back.2 = (bf16[2048,2048]{1,0:T(8,128)(2,1)}, bf16[2048,1024]{1,0:T(8,128)(2,1)}, f32[1,1024]{1,0:T(1,128)}) custom-call(bf16[256,2048]{1,0:T(8,128)(2,1)} %refs_0_, bf16[4,1024,512]{2,1,0:T(8,128)(2,1)} %all-gather.21.cloned.1.call-done.refs_1_, bf16[2048,1024]{1,0:T(8,128)(2,1)} %get-tuple-element.45.refs_2_), custom_call_target="tpu_custom_call" | custom-call | flops 8589934592 | bytes 16777216 | tf_op jit(solution)/shard_map/gather_down_back/pallas_call | solution.py:247
  577.0 47.0 %up_back_scatter.2 = f32[256,2048]{1,0:T(8,128)} custom-call(bf16[2048,1024]{1,0:T(8,128)(2,1)} %get-tuple-element.46.refs_0_, bf16[2048,1024]{1,0:T(8,128)(2,1)} %bitcast.150), custom_call_target="tpu_custom_call" | custom-call | flops 8589934592 | bytes 16777216 | tf_op jit(solution)/shard_map/up_back_scatter/pallas_call | solution.py:420
  624.0 2.9 multiply_reduce_fusion
  626.9 45.5 %down_scatter.3 = f32[256,2048]{1,0:T(8,128)} custom-call(bf16[2048,1024]{1,0:T(8,128)(2,1)} %get-tuple-element.44.refs_0_, bf16[4,1024,512]{2,1,0:T(8,128)(2,1)} %all-gather.21.cloned.1.call-done.refs_1_), custom_call_target="tpu_custom_call" | custom-call | flops 8589934592 | bytes 16777216 | tf_op jit(solution)/shard_map/down_scatter/pallas_call | solution.py:420
  672.5 4.7 fusion.48
  679.7 41.5 %gather_dense_back.2 = (bf16[2048,2048]{1,0:T(8,128)(2,1)}, bf16[2048,256]{1,0:T(8,128)(2,1)}) custom-call(bf16[256,2048]{1,0:T(8,128)(2,1)} %fusion.41.refs_0_, bf16[4,256,512]{2,1,0:T(8,128)(2,1)} %all-gather.19.cloned.1.call-done.refs_1_), custom_call_target="tpu_custom_call" | custom-call | flops 2147483648 | bytes 16777216 | tf_op jit(solution)/shard_map/gather_dense_back/pallas_call | solution.py:247
  721.3 17.9 %attend_bwd.2 = (bf16[3,2048,256]{2,1,0:T(8,128)(2,1)}, f32[2,256]{1,0:T(2,128)}) custom-call(f32[2]{0:T(128)} %copy-done.2, bf16[2048,768]{1,0:T(8,128)(2,1)} %get-tuple-element.42.q_ref.k_ref.v_ref, bf16[2048,768]{1,0:T(8,128)(2,1)} %get-tuple-element.42.q_ref.k_ref.v_ref, bf16[2048,768]{1,0:T(8,128)(2,1)} %get-tuple-element.42.q_ref.k_ref.v_ref, ...), custom_call_target="tpu_custom_call" | custom-call | flops 5368709120 | bytes 8388608 | tf_op jit(solution)/shard_map/attend_bwd/pallas_call | solution.py:128
  739.2 45.4 %project_back_scatter.2 = f32[256,2048]{1,0:T(8,128)} custom-call(bf16[3,2048,256]{2,1,0:T(8,128)(2,1)} %get-tuple-element.49.refs_0_, bf16[2048,768]{1,0:T(8,128)(2,1)} %all-gather.17.cloned.1.call-done.refs_1_), custom_call_target="tpu_custom_call" | custom-call | flops 8589934592 | bytes 16777216 | tf_op jit(solution)/shard_map/project_back_scatter/pallas_call | solution.py:420
  784.6 3.1 multiply_reduce_fusion.1
  793.2 51.5 %gather_down_back.3 = (bf16[2048,2048]{1,0:T(8,128)(2,1)}, bf16[2048,1024]{1,0:T(8,128)(2,1)}, f32[1,1024]{1,0:T(1,128)}) custom-call(bf16[256,2048]{1,0:T(8,128)(2,1)} %convert_element_type.115.refs_0_, bf16[4,1024,512]{2,1,0:T(8,128)(2,1)} %all-gather.15.cloned.1.call-done.refs_1_, bf16[2048,1024]{1,0:T(8,128)(2,1)} %get-tuple-element.50.refs_2_), custom_call_target="tpu_custom_call" | custom-call | flops 8589934592 | bytes 16777216 | tf_op jit(solution)/shard_map/gather_down_back/pallas_call | solution.py:247
  844.6 47.0 %up_back_scatter.3 = f32[256,2048]{1,0:T(8,128)} custom-call(bf16[2048,1024]{1,0:T(8,128)(2,1)} %get-tuple-element.51.refs_0_, bf16[2048,1024]{1,0:T(8,128)(2,1)} %bitcast.148), custom_call_target="tpu_custom_call" | custom-call | flops 8589934592 | bytes 16777216 | tf_op jit(solution)/shard_map/up_back_scatter/pallas_call | solution.py:420
  891.6 2.5 multiply_reduce_fusion.2
  898.5 41.5 %gather_dense_back.3 = (bf16[2048,2048]{1,0:T(8,128)(2,1)}, bf16[2048,256]{1,0:T(8,128)(2,1)}) custom-call(bf16[256,2048]{1,0:T(8,128)(2,1)} %convert_element_type.116.refs_0_, bf16[4,256,512]{2,1,0:T(8,128)(2,1)} %all-gather.13.cloned.1.call-done.refs_1_), custom_call_target="tpu_custom_call" | custom-call | flops 2147483648 | bytes 16777216 | tf_op jit(solution)/shard_map/gather_dense_back/pallas_call | solution.py:247
  939.9 17.9 %attend_bwd.3 = (bf16[3,2048,256]{2,1,0:T(8,128)(2,1)}, f32[2,256]{1,0:T(2,128)}) custom-call(f32[2]{0:T(128)} %copy-done.2, bf16[2048,768]{1,0:T(8,128)(2,1)} %get-tuple-element.39.q_ref.k_ref.v_ref, bf16[2048,768]{1,0:T(8,128)(2,1)} %get-tuple-element.39.q_ref.k_ref.v_ref, bf16[2048,768]{1,0:T(8,128)(2,1)} %get-tuple-element.39.q_ref.k_ref.v_ref, ...), custom_call_target="tpu_custom_call" | custom-call | flops 5368709120 | bytes 8388608 | tf_op jit(solution)/shard_map/attend_bwd/pallas_call | solution.py:128
  957.9 45.8 %project_back_scatter.3 = f32[256,2048]{1,0:T(8,128)} custom-call(bf16[3,2048,256]{2,1,0:T(8,128)(2,1)} %get-tuple-element.54.refs_0_, bf16[2048,768]{1,0:T(8,128)(2,1)} %all-gather.11.cloned.1.call-done.refs_1_), custom_call_target="tpu_custom_call" | custom-call | flops 8589934592 | bytes 16777216 | tf_op jit(solution)/shard_map/project_back_scatter/pallas_call | solution.py:420
  1003.7 2.3 fusion.43
  1007.0 12.4 copy.58
  1020.9 6.8 fusion.30
  1027.8 12.1 copy.59
  1039.8 6.7 fusion.31
  1046.6 11.7 fusion.11
  1058.4 11.4 fusion.8
  1069.9 11.8 copy.61
  1081.7 13.8 convert_bitcast_fusion
  1095.5 12.0 copy.60
  1107.6 13.8 convert_bitcast_fusion.1
  1121.4 14.0 convolution_convert_fusion
  1135.5 14.3 convolution_convert_fusion.1
  1150.6 17.5 %all-reduce.1 = (f32[1,1536]{1,0:T(1,128)S(1)}, f32[1,1536]{1,0:T(1,128)S(1)}) all-reduce(f32[1,1536]{1,0:T(1,128)S(1)} %stack.97, f32[1,1536]{1,0:T(1,128)S(1)} %stack.96), channel_id=1, replica_groups=mesh['dp'=4,'mp'=8] {'dp'}, use_global_device_ids=true, to_apply=%region_25.0 | all-reduce | flops 3072 | bytes 24576 | tf_op jit(solution)/shard_map/psum | solution.py:678
  1169.3 3.7 add_add_fusion.4
  1175.3 23.7 %reduce-scatter.15.cloned.1.call-done = bf16[1,256,512]{1,2,0:T(8,128)(2,1)} async-done(((bf16[4,256,512]{1,2,0:T(8,128)(2,1)}), bf16[1,256,512]{1,2,0:T(8,128)(2,1)}) %reduce-scatter.15.cloned.1.call-update) | async-done | bytes 262160 | tf_op jit(solution)/shard_map/reduce_scatter | solution.py:608
  1201.4 58.7 %reduce-scatter.11.cloned.1.call-done = bf16[512,3,256]{2,0,1:T(8,128)(2,1)} async-done(((bf16[2048,3,256]{2,0,1:T(8,128)(2,1)}), bf16[512,3,256]{2,0,1:T(8,128)(2,1)}) %reduce-scatter.11.cloned.1.call-update) | async-done | bytes 786448 | tf_op jit(solution)/shard_map/reduce_scatter | solution.py:608
  1260.1 63.2 %reduce-scatter.9.cloned.1.call-done = bf16[512,3,256]{2,0,1:T(8,128)(2,1)} async-done(((bf16[2048,3,256]{2,0,1:T(8,128)(2,1)}), bf16[512,3,256]{2,0,1:T(8,128)(2,1)}) %reduce-scatter.9.cloned.1.call-update) | async-done | bytes 786448 | tf_op jit(solution)/shard_map/reduce_scatter | solution.py:608
  1323.4 3.2 maximum_convert_fusion.2
  1326.6 76.3 %reduce-scatter.23.cloned.1.call-done = bf16[1,1024,512]{1,2,0:T(8,128)(2,1)} async-done(((bf16[4,1024,512]{1,2,0:T(8,128)(2,1)}), bf16[1,1024,512]{1,2,0:T(8,128)(2,1)}) %reduce-scatter.23.cloned.1.call-update) | async-done | bytes 1048592 | tf_op jit(solution)/shard_map/reduce_scatter | solution.py:608
  1402.9 79.6 %reduce-scatter.21.cloned.1.call-done = bf16[1,1024,512]{1,2,0:T(8,128)(2,1)} async-done(((bf16[4,1024,512]{1,2,0:T(8,128)(2,1)}), bf16[1,1024,512]{1,2,0:T(8,128)(2,1)}) %reduce-scatter.21.cloned.1.call-update) | async-done | bytes 1048592 | tf_op jit(solution)/shard_map/reduce_scatter | solution.py:608
  1482.4 3.8 maximum_convert_fusion.1
  1486.2 5.4 copy.53
  1491.6 70.9 %reduce-scatter.19.cloned.1.call-done = bf16[512,1024]{1,0:T(8,128)(2,1)} async-done(((bf16[2048,1024]{1,0:T(8,128)(2,1)}), bf16[512,1024]{1,0:T(8,128)(2,1)}) %reduce-scatter.19.cloned.1.call-update) | async-done | bytes 1048592 | tf_op jit(solution)/shard_map/reduce_scatter | solution.py:608
  1562.4 79.6 %reduce-scatter.17.cloned.1.call-done = bf16[512,1024]{1,0:T(8,128)(2,1)} async-done(((bf16[2048,1024]{1,0:T(8,128)(2,1)}), bf16[512,1024]{1,0:T(8,128)(2,1)}) %reduce-scatter.17.cloned.1.call-update) | async-done | bytes 1048592 | tf_op jit(solution)/shard_map/reduce_scatter | solution.py:608
  1642.0 3.8 maximum_convert_fusion
  (186 shorter events, 43.5 us)
Async XLA Ops:
  7.2 69.9 %all-gather.11.cloned.1.call-start = ((), (), s32[]{:S(2)}) async-start(), calls=%async_computation.8 | async-start | bytes 3932160 | tf_op jit(solution)/shard_map/all_gather | solution.py:564
  9.6 1.3 copy-start.24
  10.7 130.2 %all-gather.13.cloned.1.call-start = ((), (), s32[]{:S(2)}) async-start(), calls=%async_computation.9 | async-start | bytes 1310720 | tf_op jit(solution)/shard_map/all_gather | solution.py:570
  11.7 176.0 %all-gather.23.cloned.1.call-start = ((), (), s32[]{:S(2)}) async-start(), calls=%async_computation.22 | async-start | bytes 5242880 | tf_op jit(solution)/shard_map/all_gather | solution.py:571
  15.8 253.2 %all-gather.15.cloned.1.call-start = ((), (), s32[]{:S(2)}) async-start(), calls=%async_computation.10 | async-start | bytes 5242880 | tf_op jit(solution)/shard_map/all_gather | solution.py:572
  19.8 312.7 %all-gather.17.cloned.1.call-start = ((), (), s32[]{:S(2)}) async-start(), calls=%async_computation.11 | async-start | bytes 3932160 | tf_op jit(solution)/shard_map/all_gather | solution.py:564
  19.9 3.4 copy-start.12
  21.1 375.3 %all-gather.19.cloned.1.call-start = ((), (), s32[]{:S(2)}) async-start(), calls=%async_computation.12 | async-start | bytes 1310720 | tf_op jit(solution)/shard_map/all_gather | solution.py:570
  21.6 422.2 %all-gather.25.cloned.1.call-start = ((), (), s32[]{:S(2)}) async-start(), calls=%async_computation.23 | async-start | bytes 5242880 | tf_op jit(solution)/shard_map/all_gather | solution.py:571
  21.7 2.2 copy-start.39
  21.7 3.9 copy-start.36
  21.7 4.5 copy-start.29
  21.7 4.6 copy-start.30
  21.7 4.6 copy-start.31
  22.4 502.1 %all-gather.21.cloned.1.call-start = ((), (), s32[]{:S(2)}) async-start(), calls=%async_computation.13 | async-start | bytes 5242880 | tf_op jit(solution)/shard_map/all_gather | solution.py:572
  23.1 1149.8 %all-reduce.4.cloned.1.call-start = ((), (), s32[]{:S(2)}) async-start(), calls=%async_computation.24 | async-start | bytes 262144 | tf_op jit(solution)/shard_map/psum | solution.py:672
  23.2 356.4 %copy-start.2 = (f32[2]{0:T(128)}, f32[2]{0:T(128)S(1)}, u32[]{:S(2)}) copy-start(f32[2]{0:T(128)S(1)} %multiply_power_fusion.slope_ref) | copy-start | bytes 28
  23.5 2.9 copy-start.27
  23.9 0.6 copy-start.34
  23.9 100.5 %copy-start.32 = (f32[256]{0:T(256)}, f32[256]{0:T(256)S(1)}, u32[]{:S(2)}) copy-start(f32[256]{0:T(256)S(1)} %fusion.36) | copy-start | bytes 3076
  26.3 0.6 copy-start.25
  124.4 1.9 copy-start
  139.4 1.0 copy-start.3
  140.3 0.6 copy-start.7
  317.3 1.3 copy-start.9
  379.6 1.9 copy-start.1
  394.8 1.0 copy-start.5
  395.8 0.6 copy-start.8
  441.1 1.3 copy-start.11
  672.5 6.0 copy-start.22
  677.1 1.3 copy-start.13
  784.6 3.1 copy-start.10
  784.6 3.5 copy-start.20
  788.1 1.6 copy-start.14
  788.1 1.9 copy-start.23
  790.7 1.3 copy-start.15
  891.6 2.5 copy-start.21
  894.1 1.6 copy-start.16
  896.0 1.3 copy-start.19
  957.8 45.8 %copy-start.26 = (f32[1,1,2048]{2,1,0:T(1,128)S(1)}, f32[1,1,2048]{2,1,0:T(1,128)}, u32[]{:S(2)}) copy-start(f32[1,1,2048]{2,1,0:T(1,128)} %copy-done.25) | copy-start | bytes 24580
  957.9 45.8 %copy-start.28 = (f32[256]{0:T(256)S(1)}, f32[256]{0:T(256)}, u32[]{:S(2)}) copy-start(f32[256]{0:T(256)} %copy-done.27) | copy-start | bytes 3076
  1003.7 2.3 copy-start.35
  1003.7 2.3 copy-start.17
  1003.7 2.3 copy-start.33
  1007.0 13.9 copy-start.4
  1020.8 154.5 %reduce-scatter.13.cloned.1.call-start = ((), (), s32[]{:S(2)}) async-start(), calls=%async_computation.16 | async-start | bytes 1310720 | tf_op jit(solution)/shard_map/reduce_scatter | solution.py:608
  1027.7 171.3 %reduce-scatter.15.cloned.1.call-start = ((), (), s32[]{:S(2)}) async-start(), calls=%async_computation.17 | async-start | bytes 1310720 | tf_op jit(solution)/shard_map/reduce_scatter | solution.py:608
  1027.7 12.1 copy-start.6
  1046.6 213.5 %reduce-scatter.11.cloned.1.call-start = ((), (), s32[]{:S(2)}) async-start(), calls=%async_computation.15 | async-start | bytes 3932160 | tf_op jit(solution)/shard_map/reduce_scatter | solution.py:608
  1058.3 265.0 %reduce-scatter.9.cloned.1.call-start = ((), (), s32[]{:S(2)}) async-start(), calls=%async_computation.14 | async-start | bytes 3932160 | tf_op jit(solution)/shard_map/reduce_scatter | solution.py:608
  1069.8 333.1 %reduce-scatter.23.cloned.1.call-start = ((), (), s32[]{:S(2)}) async-start(), calls=%async_computation.21 | async-start | bytes 5242880 | tf_op jit(solution)/shard_map/reduce_scatter | solution.py:608
  1095.5 387.0 %reduce-scatter.21.cloned.1.call-start = ((), (), s32[]{:S(2)}) async-start(), calls=%async_computation.20 | async-start | bytes 5242880 | tf_op jit(solution)/shard_map/reduce_scatter | solution.py:608
  1121.4 441.1 %reduce-scatter.19.cloned.1.call-start = ((), (), s32[]{:S(2)}) async-start(), calls=%async_computation.19 | async-start | bytes 5242880 | tf_op jit(solution)/shard_map/reduce_scatter | solution.py:608
  1135.5 506.6 %reduce-scatter.17.cloned.1.call-start = ((), (), s32[]{:S(2)}) async-start(), calls=%async_computation.18 | async-start | bytes 5242880 | tf_op jit(solution)/shard_map/reduce_scatter | solution.py:608
  1149.8 0.7 copy-start.40
  1149.8 0.7 copy-start.37
  1149.8 0.7 copy-start.41
  1149.8 0.7 copy-start.38
  1149.8 19.5 %copy-start.18 = (f32[256,2048]{1,0:T(8,128)S(1)}, f32[256,2048]{1,0:T(8,128)}, u32[]{:S(2)}) copy-start(f32[256,2048]{1,0:T(8,128)} %project_back_scatter.3) | copy-start | bytes 6291460
Sparse Core Ops, SparseCore 0:
  10.9 66.1 all-gather.10
  78.7 26.5 all-gather.12
  107.4 80.2 all-gather.22
  189.7 79.2 all-gather.14
  270.5 62.0 all-gather.16
  334.0 26.5 all-gather.18
  362.7 80.2 all-gather.24
  445.2 79.3 all-gather.20
  1021.0 120.3 all-reduce.3
  1143.5 26.6 reduce-scatter.12
  1173.2 25.7 reduce-scatter.14
  1201.2 58.8 reduce-scatter.10
  1263.0 60.2 reduce-scatter.8
  1326.1 76.7 reduce-scatter.22
  1405.1 77.2 reduce-scatter.20
  1485.2 77.2 reduce-scatter.18
  1564.7 77.2 reduce-scatter.16

commit v2 on v1

v2 whole, which is shorter than its diff:
```python
import functools

import jax
import jax.numpy as jnp
from jax import lax
from jax.experimental import pallas as pl
from jax.experimental.pallas import tpu as pltpu
from jax.sharding import PartitionSpec as P

N_HEADS = 16
BLOCK = 256
LOG2E = 1.4426950408889634
MESH = pl.DeviceIdType.MESH
NT_DIMS = (((1,), (1,)), ((), ()))
norm_eps = 1e-05


def nt(a, b):
    return lax.dot_general(a, b, NT_DIMS, preferred_element_type=jnp.float32)


def nn(a, b):
    return jnp.dot(a, b, preferred_element_type=jnp.float32)


def bias_tile(slope, first_key, first_query, keys, queries):
    kp = first_key + lax.broadcasted_iota(jnp.int32, (keys, queries), 0)
    qp = first_query + lax.broadcasted_iota(jnp.int32, (keys, queries), 1)
    return (jnp.abs(qp - kp).astype(jnp.float32)) * (-slope * LOG2E)

def scores_t(q, k, slope, i, B):
    L = (i+1)*B
    factor = q.shape[1] ** (-0.5) * LOG2E
    st = nt(k, q) * factor
    key = lax.broadcasted_iota(jnp.int32, (L, 1), 0)
    if i > 0:
        m = i * B
        kp = lax.broadcasted_iota(jnp.int32, (m, 1), 0).astype(jnp.float32)
        qp = (m + lax.broadcasted_iota(jnp.int32, (1, B), 1)).astype(jnp.float32)
        head = st[:m] - (qp - kp) * (slope * LOG2E)
        tail = st[m:] + bias_tile(slope, 0, 0, B, B)
        return head, tail
    return None, st + bias_tile(slope, 0, 0, B, B)

def attend_fwd_kernel(slope_ref, q_ref, k_ref, v_ref, ctx_ref, lse_ref, vt_ref):
    B = BLOCK
    slope = slope_ref[pl.program_id(0)]
    T = q_ref.shape[0]
    vt_ref[...] = v_ref[...].T
    for i in range(T // B):
        L = (i+1)*B
        head, tail = scores_t(q_ref[i*B:L, :], k_ref[:L, :], slope, i, B)
        top = jnp.max(tail, axis=0, keepdims=True)
        if head is not None:
            top = jnp.maximum(top, jnp.max(head, axis=0, keepdims=True))
        pt = jnp.exp2(tail - top)
        den = jnp.sum(pt, axis=0, keepdims=True)
        ct = nn(vt_ref[:, i*B:L], pt.astype(jnp.bfloat16))
        if head is not None:
            ph = jnp.exp2(head - top)
            den = den + jnp.sum(ph, axis=0, keepdims=True)
            ct = ct + nn(vt_ref[:, :i*B], ph.astype(jnp.bfloat16))
        ctx_ref[i*B:L, :] = (ct / den).T.astype(ctx_ref.dtype)
        lse_ref[0, i:i+1, :] = top + jnp.log2(den)

def attend_bwd_kernel(slope_ref, q_ref, k_ref, v_ref, g_ref, c_ref, lse_ref, out_ref, sums_ref, kt_ref, dk_ref, dv_ref):
    B = BLOCK
    slope = slope_ref[pl.program_id(0)]
    T = q_ref.shape[0]
    W = q_ref.shape[1]
    factor = W ** (-0.5)
    kt_ref[...] = k_ref[...].T
    qsum = jnp.zeros((1, W), jnp.float32)
    n = T // B
    for i in reversed(range(n)):
        L = (i+1)*B
        q = q_ref[i*B:L, :]
        g = g_ref[i*B:L, :]
        head, tail = scores_t(q, k_ref[:L, :], slope, i, B)
        prod = g.astype(jnp.float32) * c_ref[i*B:L, :].astype(jnp.float32)
        inner = lax.dot_general(jnp.ones((8, W), jnp.float32), prod, NT_DIMS, preferred_element_type=jnp.float32, precision=lax.Precision.HIGHEST)[:1]
        lse = lse_ref[0, i:i+1, :]
        dpt = nt(v_ref[:L, :], g)
        dqt = None
        for part, lo, hi in ((head, 0, i*B), (tail, i*B, L)):
            if part is None:
                continue
            pt = jnp.exp2(part - lse)
            ds = (pt * (dpt[lo:hi] - inner)).astype(jnp.bfloat16)
            pt = pt.astype(jnp.bfloat16)
            dk = nn(ds, q)
            dv = nn(pt, g)
            if i == n - 1:
                dk_ref[lo:hi, :] = dk
                dv_ref[lo:hi, :] = dv
            else:
                dk_ref[lo:hi, :] += dk
                dv_ref[lo:hi, :] += dv
            t = nn(kt_ref[:, lo:hi], ds)
            dqt = t if dqt is None else dqt + t
        dq = (dqt * factor).T.astype(jnp.bfloat16)
        out_ref[0, i*B:L, :] = dq
        qsum += jnp.sum(dq.astype(jnp.float32), axis=0, keepdims=True)
    out_ref[1] = (dk_ref[...] * factor).astype(jnp.bfloat16)
    dv = dv_ref[...].astype(jnp.bfloat16)
    out_ref[2] = dv
    sums_ref[0:1, :] = qsum
    sums_ref[1:2, :] = jnp.sum(dv.astype(jnp.float32), axis=0, keepdims=True)

def attend_fwd(project, slopes):
    T, W = project.shape
    H = W // 384
    col = lambda part: pl.BlockSpec((T, 128), lambda h, part=part: (0, part * H + h))
    return pl.pallas_call(
        attend_fwd_kernel, grid=(H,),
        out_shape=(jax.ShapeDtypeStruct((T, H*128), jnp.bfloat16), jax.ShapeDtypeStruct((H, T//BLOCK, BLOCK), jnp.float32)),
        in_specs=[pl.BlockSpec(memory_space=pltpu.SMEM), col(0), col(1), col(2)],
        out_specs=(pl.BlockSpec((T,128), lambda h: (0,h)), pl.BlockSpec((1, T//BLOCK, BLOCK), lambda h: (h,0,0))),
        scratch_shapes=[pltpu.VMEM((128, T), jnp.bfloat16)],
        compiler_params=pltpu.CompilerParams(vmem_limit_bytes=48<<20),
        cost_estimate=cost(1 << 20),
        name="attend_fwd")(slopes, project, project, project)

def attend_bwd(project, grad_context, context, lse, slopes):
    T, W = project.shape
    H = W // 384
    col = lambda part: pl.BlockSpec((T, 128), lambda h, part=part: (0, part * H + h))
    return pl.pallas_call(
        attend_bwd_kernel, grid=(H,),
        out_shape=(jax.ShapeDtypeStruct((3, T, H*128), jnp.bfloat16), jax.ShapeDtypeStruct((2, H*128), jnp.float32)),
        in_specs=[pl.BlockSpec(memory_space=pltpu.SMEM), col(0), col(1), col(2), col(0), col(0), pl.BlockSpec((1, T//BLOCK, BLOCK), lambda h: (h,0,0))],
        out_specs=(pl.BlockSpec((3, T,128), lambda h: (0, 0,h)), pl.BlockSpec((2,128), lambda h: (0,h))),
        scratch_shapes=[pltpu.VMEM((128, T), jnp.bfloat16), pltpu.VMEM((T,128), jnp.float32), pltpu.VMEM((T,128), jnp.float32)],
        compiler_params=pltpu.CompilerParams(vmem_limit_bytes=56<<20),
        cost_estimate=cost(1 << 20),
        name="attend_bwd")(slopes, project, project, project, grad_context, context, lse)


def peers():
    me = lax.axis_index("mp")
    core = me % 2
    bx = (me // 2) % 2
    by = me // 4
    return me, core, bx, by, me + 1 - 2 * core, me + 2 - 4 * bx, me + 4 - 8 * by


def owner(rel, core, bx, by):
    c = core if rel % 2 == 0 else 1 - core
    x = bx if (rel // 2) % 2 == 0 else 1 - bx
    y = by if rel // 4 == 0 else 1 - by
    return y * 4 + x * 2 + c


def z_peers():
    z = lax.axis_index("dp")
    z1 = z + 1 - 2 * (z % 2)
    return z, z1, (z + 2) % 4, (z1 + 2) % 4


def enter(partner, xn, yn, z=False):
    barrier = pltpu.get_barrier_semaphore()
    for n in (partner, xn, yn):
        pl.semaphore_signal(barrier, inc=1, device_id={"mp": n}, device_id_type=MESH)
    if z:
        _, z1, z2, _ = z_peers()
        for n in (z1, z2):
            pl.semaphore_signal(barrier, inc=1, device_id={"dp": n}, device_id_type=MESH)
    pl.semaphore_wait(barrier, 5 if z else 3)


ZR = 128


def z_scratch(n, w):
    return (
        pltpu.VMEM((3, n, ZR, w), jnp.bfloat16),
        pltpu.VMEM((2, n, ZR, w), jnp.bfloat16),
        pltpu.SemaphoreType.DMA((3, n)),
        pltpu.SemaphoreType.DMA((3, n)),
        pltpu.SemaphoreType.DMA((2, n)),
    )


class ZSum:
    def __init__(self, plan, srcs, out, scratch):
        self.plan, self.srcs, self.out = plan, srcs, out
        self.recv, self.own, self.send_sem, self.recv_sem, self.loc = scratch
        self.z, self.z1, self.z2, self.z3 = z_peers()
        self.sent = []
        self.events = [functools.partial(self.event, c) for c in range(len(plan))]

    def block(self, c, z):
        i, row = self.plan[c]
        return self.srcs[i].at[z, pl.ds(row, ZR), :]

    def remote(self, src, kind, c, target):
        return pltpu.make_async_remote_copy(
            src_ref=src,
            dst_ref=self.recv.at[kind, c],
            send_sem=self.send_sem.at[kind, c],
            recv_sem=self.recv_sem.at[kind, c],
            device_id={"dp": target},
            device_id_type=MESH,
        )

    def push(self, *args):
        c = self.remote(*args)
        c.start()
        self.sent.append(c)

    def here(self, kind, c):
        return pltpu.make_async_copy(
            self.block(c, self.z2 if kind else self.z), self.own.at[kind, c], self.loc.at[kind, c]
        )

    def arrive(self, kind, c):
        self.remote(self.own.at[0, c], kind, c, self.z1).wait_recv()

    def start(self):
        for c in range(len(self.plan)):
            self.push(self.block(c, self.z3), 1, c, self.z1)
        for c in range(len(self.plan)):
            self.here(1, c).start()
            self.here(0, c).start()

    def event(self, c):
        self.arrive(1, c)
        self.here(1, c).wait()

        @pl.loop(0, ZR // 16)
        def _(i):
            rows = pl.ds(pl.multiple_of(i * 16, 16), 16)
            self.own[1, c, rows, :] = (
                self.own[1, c, rows, :].astype(jnp.float32)
                + self.recv[1, c, rows, :].astype(jnp.float32)
            ).astype(jnp.bfloat16)

        self.push(self.own.at[1, c], 2, c, self.z2)
        self.push(self.block(c, self.z1), 0, c, self.z1)

    def tick(self, n=1):
        for _ in range(min(n, len(self.events))):
            self.events.pop(0)()

    def finish(self):
        self.tick(len(self.events))
        for c in range(len(self.plan)):
            self.here(0, c).wait()
            self.arrive(0, c)
            self.arrive(2, c)

            @pl.loop(0, ZR // 16)
            def _(i):
                rows = pl.ds(pl.multiple_of(i * 16, 16), 16)
                to = pl.ds(pl.multiple_of(c * ZR + i * 16, 16), 16)
                self.out[to, :] = (
                    self.own[0, c, rows, :].astype(jnp.float32)
                    + self.recv[0, c, rows, :].astype(jnp.float32)
                    + self.recv[2, c, rows, :].astype(jnp.float32)
                )

        for c in self.sent:
            c.wait_send()


class NoZ:
    def start(self):
        pass

    def tick(self, n=1):
        pass

    def finish(self):
        pass


def z_task(plan, srcs, outs, scratch):
    return ZSum(plan, srcs, outs[0], scratch) if plan else NoZ()


def z_parts(z):
    if z is None or not z.plan:
        return (), (), ()
    w = z.arrays[0].shape[2]
    n = len(z.plan)
    return tuple(z.arrays), (jax.ShapeDtypeStruct((n * ZR, w), jnp.float32),), z_scratch(n, w)


def cost(flops):
    return pl.CostEstimate(flops=flops, bytes_accessed=1 << 16, transcendentals=0)


def gather_kernel(C, n_in, n_out, body, plan, n_src, *refs):
    x_ref, ins, refs = refs[0], refs[1 : 1 + n_in], refs[1 + n_in :]
    srcs, refs = refs[:n_src], refs[n_src:]
    full_ref, outs, refs = refs[0], refs[1 : 1 + n_out], refs[1 + n_out :]
    z_out, refs = (refs[:1], refs[1:]) if plan else ((), refs)
    buf, send, recv, loc = refs[:4]
    R, D = x_ref.shape
    rc = R // C
    me, core, bx, by, partner, xn, yn = peers()
    z = z_task(plan, srcs, z_out, refs[4:])
    enter(partner, xn, yn, bool(plan))
    z.start()
    sent = []

    def copy(src, rel, k, target, sidx):
        return pltpu.make_async_remote_copy(
            src_ref=src,
            dst_ref=buf.at[k, rel],
            send_sem=send.at[sidx, k],
            recv_sem=recv.at[rel, k],
            device_id={"mp": target},
            device_id_type=MESH,
        )

    def push(src, rel, k, target, sidx):
        c = copy(src, rel, k, target, sidx)
        c.start()
        sent.append(c)

    def arrive(rel, k):
        copy(buf.at[k, 0], rel, k, partner, 0).wait_recv()

    kept = []

    def keep(src, start, size, k, rel):
        c = pltpu.make_async_copy(src, full_ref.at[pl.ds(start, size), :], loc.at[k, rel])
        c.start()
        kept.append(c)

    def run(k, lo, hi):
        starts = []
        for rel in range(lo, hi):
            start = pl.multiple_of(owner(rel, core, bx, by) * R + k * rc, rc)
            keep(buf.at[k, rel], start, rc, k, rel)
            starts.append(start)
        body(
            False,
            lambda lo_=lo, hi_=hi: buf[k, lo_:hi_].reshape((hi_ - lo_) * rc, D),
            [pl.ds(s, rc) for s in starts],
            ins,
            outs,
        )

    for k in range(C):
        own = x_ref.at[pl.ds(k * rc, rc), :]
        push(own, 2, k, xn, 1)
        push(own, 4, k, yn, 2)
        push(own, 1, k, partner, 0)
    start = pl.multiple_of(me * R, R)
    keep(x_ref, start, R, 0, 0)
    body(True, lambda: x_ref[...], [pl.ds(start, R)], ins, outs)
    across = jnp.where(core == 0, xn, yn)
    for k in range(C + 2):
        if k < C:
            arrive(2, k)
            arrive(4, k)
            push(buf.at[k, 4 - 2 * core], 6, k, across, 3)
            push(buf.at[k, 2], 3, k, partner, 4)
            push(buf.at[k, 4], 5, k, partner, 5)
        if k == 0:
            starts = []
            other = owner(1, core, bx, by) * R
            for j in range(C):
                arrive(1, j)
                starts.append(pl.multiple_of(other + j * rc, rc))
                keep(buf.at[j, 1], starts[-1], rc, j, 1)
            body(
                False,
                lambda: buf[:, 1].reshape(R, D),
                [pl.ds(s, rc) for s in starts],
                ins,
                outs,
            )
        if 1 <= k <= C:
            arrive(3, k - 1)
            arrive(5, k - 1)
            run(k - 1, 2, 6)
            arrive(6, k - 1)
            push(buf.at[k - 1, 6], 7, k - 1, partner, 6)
        if k >= 2:
            arrive(7, k - 2)
            run(k - 2, 6, 8)
        if k >= 1:
            z.tick(-(-len(plan) // C))
    z.finish()
    for c in sent:
        c.wait_send()
    for c in kept:
        c.wait()


def gather_call(name, cid, x, ins, outs, body, z=None, C=4):
    R, D = x.shape
    vmem = pl.BlockSpec(memory_space=pltpu.VMEM)
    anywhere = pl.BlockSpec(memory_space=pl.ANY)
    srcs, z_out, more_scratch = z_parts(z)
    plan = tuple(z.plan) if z else ()
    out = pl.pallas_call(
        functools.partial(gather_kernel, C, len(ins), len(outs), body, plan, len(srcs)),
        out_shape=(jax.ShapeDtypeStruct((8 * R, D), x.dtype), *outs, *z_out),
        in_specs=[vmem] * (1 + len(ins)) + [anywhere] * len(srcs),
        out_specs=(anywhere,) + (vmem,) * (len(outs) + len(z_out)),
        scratch_shapes=[
            pltpu.VMEM((C, 8, R // C, D), x.dtype),
            pltpu.SemaphoreType.DMA((7, C)),
            pltpu.SemaphoreType.DMA((8, C)),
            pltpu.SemaphoreType.DMA((C, 8)),
            *more_scratch,
        ],
        compiler_params=pltpu.CompilerParams(
            collective_id=cid, has_side_effects=True, vmem_limit_bytes=60 << 20
        ),
        cost_estimate=cost(1 << 20),
        name=name,
    )(x, *ins, *srcs)
    if plan:
        z.done(out[-1])
        out = out[:-1]
    return out


def gather_only_kernel(C, n, *refs):
    xs, fulls = refs[:n], refs[n : 2 * n]
    send, recv, loc = refs[2 * n :]
    R, D = xs[0].shape
    rc = R // C
    me, core, bx, by, partner, xn, yn = peers()
    enter(partner, xn, yn)
    sent = []

    def copy(src, a, k, target, rel, sidx, whose):
        rows = pl.ds(pl.multiple_of(whose * R + k * rc, rc), rc)
        return pltpu.make_async_remote_copy(
            src_ref=fulls[a].at[rows, :] if src is None else src,
            dst_ref=fulls[a].at[rows, :],
            send_sem=send.at[a, sidx, k],
            recv_sem=recv.at[a, rel, k],
            device_id={"mp": target},
            device_id_type=MESH,
        )

    def push(*args):
        c = copy(*args)
        c.start()
        sent.append(c)

    def arrive(a, k, rel):
        copy(None, a, k, partner, rel, 0, owner(rel, core, bx, by)).wait_recv()

    kept = []
    for a in range(n):
        for k in range(C):
            own = xs[a].at[pl.ds(k * rc, rc), :]
            push(own, a, k, xn, 2, 1, me)
            push(own, a, k, yn, 4, 2, me)
            push(own, a, k, partner, 1, 0, me)
        c = pltpu.make_async_copy(
            xs[a], fulls[a].at[pl.ds(pl.multiple_of(me * R, R), R), :], loc.at[a]
        )
        c.start()
        kept.append(c)
    across = jnp.where(core == 0, xn, yn)
    x_core = owner(2, core, bx, by)
    y_core = owner(4, core, bx, by)
    through = jnp.where(core == 0, y_core, x_core)
    steps = [(a, k) for a in range(n) for k in range(C)]
    for i in range(len(steps) + 1):
        if i < len(steps):
            a, k = steps[i]
            arrive(a, k, 2)
            arrive(a, k, 4)
            push(None, a, k, across, 6, 3, through)
            push(None, a, k, partner, 3, 4, x_core)
            push(None, a, k, partner, 5, 5, y_core)
        if i >= 1:
            a, k = steps[i - 1]
            arrive(a, k, 6)
            push(None, a, k, partner, 7, 6, owner(6, core, bx, by))
    for a, k in steps:
        for rel in (1, 3, 5, 7):
            arrive(a, k, rel)
    for c in sent:
        c.wait_send()
    for c in kept:
        c.wait()


def gather_only(cid, *xs, C=4):
    R, D = xs[0].shape
    n = len(xs)
    anywhere = pl.BlockSpec(memory_space=pl.ANY)
    return pl.pallas_call(
        functools.partial(gather_only_kernel, C, n),
        out_shape=tuple(jax.ShapeDtypeStruct((8 * R, D), x.dtype) for x in xs),
        in_specs=[anywhere] * n,
        out_specs=(anywhere,) * n,
        scratch_shapes=[
            pltpu.SemaphoreType.DMA((n, 7, C)),
            pltpu.SemaphoreType.DMA((n, 8, C)),
            pltpu.SemaphoreType.DMA((n,)),
        ],
        compiler_params=pltpu.CompilerParams(collective_id=cid, has_side_effects=True),
        cost_estimate=cost(1 << 20),
        name="gather_rows",
    )(*xs)


def tiles(n, step, f):
    step = min(step, n)

    @pl.loop(0, n // step)
    def _(j):
        f(pl.ds(pl.multiple_of(j * step, step), step))


def put(ref, pieces, cols, value):
    at = 0
    for rows in pieces:
        ref[rows, cols] = value[at : at + rows.size]
        at += rows.size


def take(ref, pieces, cols):
    parts = [ref[rows, cols] for rows in pieces]
    return parts[0] if len(parts) == 1 else jnp.concatenate(parts, axis=0)


def project_body(first, lhs, pieces, ins, outs):
    w, shift = ins

    def f(cols):
        put(outs[0], pieces, cols, (nn(lhs(), w[:, cols]) + shift[:, cols]).astype(jnp.bfloat16))

    tiles(w.shape[1], 256, f)


def gelu_both(v):
    t = jnp.tanh(0.7978845608028654 * (v + 0.044715 * v * v * v))
    d = 0.5 * (1.0 + t) + 0.5 * v * (1.0 - t * t) * (
        0.7978845608028654 * (1.0 + 3 * 0.044715 * v * v)
    )
    return (0.5 * v * (1.0 + t)).astype(jnp.bfloat16), d.astype(jnp.bfloat16)


def up_body(first, lhs, pieces, ins, outs):
    w, shift = ins

    def f(cols):
        active, slope = gelu_both(nn(lhs(), w[:, cols]) + shift[:, cols])
        put(outs[0], pieces, cols, active)
        put(outs[1], pieces, cols, slope)

    tiles(w.shape[1], 256, f)


def wide_nt(src, w, cols):
    Z, _, d = w.shape
    total = None
    for z in range(Z):
        t = nt(src[:, z * d : (z + 1) * d], w[z, cols, :])
        total = t if total is None else total + t
    return total


def down_back_body(first, lhs, pieces, ins, outs):
    w, slope = ins

    def f(cols):
        g = wide_nt(lhs(), w, cols) * take(slope, pieces, cols).astype(jnp.float32)
        g = g.astype(jnp.bfloat16)
        put(outs[0], pieces, cols, g)
        sums = jnp.sum(g.astype(jnp.float32), axis=0, keepdims=True)
        if first:
            outs[1][:, cols] = sums
        else:
            outs[1][:, cols] += sums

    tiles(w.shape[1], 256, f)


def down_back_kernel(g_ref, w_ref, slope_ref, out_ref, sum_ref):
    def f(cols):
        g = wide_nt(g_ref[...], w_ref, cols) * slope_ref[:, cols].astype(jnp.float32)
        g = g.astype(jnp.bfloat16)
        out_ref[:, cols] = g
        sums = jnp.sum(g.astype(jnp.float32), axis=0, keepdims=True)

        @pl.when(pl.program_id(0) == 0)
        def _():
            sum_ref[:, cols] = sums

        @pl.when(pl.program_id(0) > 0)
        def _():
            sum_ref[:, cols] += sums

    tiles(w_ref.shape[1], 256, f)


def down_back_here(grad, w, slope):
    T, F = slope.shape
    D = grad.shape[1]
    return pl.pallas_call(
        down_back_kernel,
        grid=(T // BLOCK,),
        out_shape=(
            jax.ShapeDtypeStruct((T, F), jnp.bfloat16),
            jax.ShapeDtypeStruct((1, F), jnp.float32),
        ),
        in_specs=[
            pl.BlockSpec((BLOCK, D), lambda i: (i, 0)),
            pl.BlockSpec(w.shape, lambda i: (0, 0, 0)),
            pl.BlockSpec((BLOCK, F), lambda i: (i, 0)),
        ],
        out_specs=(pl.BlockSpec((BLOCK, F), lambda i: (i, 0)), pl.BlockSpec((1, F), lambda i: (0, 0))),
        compiler_params=pltpu.CompilerParams(vmem_limit_bytes=40 << 20),
        cost_estimate=cost(1 << 20),
        name="down_back",
    )(grad, w, slope)


def dense_back_body(first, lhs, pieces, ins, outs):
    (w,) = ins

    def f(cols):
        put(outs[0], pieces, cols, wide_nt(lhs(), w, cols).astype(jnp.bfloat16))

    tiles(w.shape[1], 256, f)


def scatter_kernel(C, n_in, n_more, n_more_out, body, filler, plan, n_src, n_scratch, *refs):
    ins, more = refs[:n_in], refs[n_in : n_in + n_more]
    srcs, rest = refs[n_in + n_more :][:n_src], refs[n_in + n_more + n_src :]
    out_ref, more_out, rest = rest[0], rest[1 : 1 + n_more_out], rest[1 + n_more_out :]
    z_out, rest = (rest[:1], rest[1:]) if plan else ((), rest)
    pbuf, rbuf, send, recv = rest[:4]
    scratch = rest[4 : 4 + n_scratch]
    z = z_task(plan, srcs, z_out, rest[4 + n_scratch :])
    R, D = out_ref.shape
    rc = R // C
    me, core, bx, by, partner, xn, yn = peers()
    steps = filler(ins, more, more_out, scratch) if filler else []
    enter(partner, xn, yn, bool(plan))
    z.start()
    dn = jnp.where(core == 0, yn, xn)
    fn = jnp.where(core == 0, xn, yn)
    sent = []

    def fill(n):
        for _ in range(min(n, len(steps))):
            steps.pop(0)()
            z.tick()

    def copy(src, slot, k, target):
        rows = pl.ds(k * rc, rc)
        return pltpu.make_async_remote_copy(
            src_ref=src.at[rows, :],
            dst_ref=rbuf.at[slot, rows, :],
            send_sem=send.at[slot, k],
            recv_sem=recv.at[slot, k],
            device_id={"mp": target},
            device_id_type=MESH,
        )

    def push(slot, to, target, k):
        c = copy(pbuf.at[slot], to, k, target)
        c.start()
        sent.append(c)

    def arrive(slot, k):
        copy(pbuf.at[0], slot, k, partner).wait_recv()

    def dest_rank(which, c):
        if which == 0:
            return (1 - by) * 4 + (1 - bx) * 2 + c
        if which == 3:
            return by * 4 + bx * 2 + c
        flip_y = (1 - c) if which == 1 else c
        y = by + flip_y * (1 - 2 * by)
        x = bx + (1 - flip_y) * (1 - 2 * bx)
        return y * 4 + x * 2 + c

    def compute(which, c, slot):
        rows = pl.ds(pl.multiple_of(dest_rank(which, c) * R, R), R)
        body(rows, ins, pbuf.at[slot])

    def theirs(which):
        compute(which, 1 - core, which)
        for k in range(C):
            push(which, which, partner, k)

    def add(slot, rslot, k):
        @pl.loop(0, rc // 16)
        def _(i):
            rows = pl.ds(pl.multiple_of(k * rc + i * 16, 16), 16)
            pbuf[slot, rows, :] = (
                pbuf[slot, rows, :].astype(jnp.float32) + rbuf[rslot, rows, :].astype(jnp.float32)
            ).astype(pbuf.dtype)

    def join(which):
        for k in range(C):
            arrive(which, k)
            add(4 + which, which, k)
            if which < 2:
                push(4 + which, 4 + which, dn, k)

    theirs(0)
    compute(0, core, 4)
    theirs(1)
    join(0)
    compute(1, core, 5)
    theirs(2)
    join(1)
    z.tick()
    compute(2, core, 6)
    theirs(3)
    join(2)
    z.tick()
    compute(3, core, 7)
    join(3)
    z.tick()
    fill(2)
    for k in range(C):
        arrive(4, k)
        add(6, 4, k)
        push(6, 6, fn, k)
        z.tick()
        fill(2)
    fill(len(steps))
    for k in range(C):
        arrive(5, k)
        arrive(6, k)

        @pl.loop(0, rc // 16)
        def _(i):
            rows = pl.ds(pl.multiple_of(k * rc + i * 16, 16), 16)
            out_ref[rows, :] = (
                pbuf[7, rows, :].astype(jnp.float32)
                + rbuf[5, rows, :].astype(jnp.float32)
                + rbuf[6, rows, :].astype(jnp.float32)
            )
    z.finish()
    for c in sent:
        c.wait_send()


def scatter_call(
    name, cid, T, D, ins, body, more=(), more_out=(), scratch=(), filler=None, z=None, C=4
):
    R = T // 8
    vmem = pl.BlockSpec(memory_space=pltpu.VMEM)
    anywhere = pl.BlockSpec(memory_space=pl.ANY)
    srcs, z_out, more_scratch = z_parts(z)
    plan = tuple(z.plan) if z else ()
    out = pl.pallas_call(
        functools.partial(
            scatter_kernel,
            C,
            len(ins),
            len(more),
            len(more_out),
            body,
            filler,
            plan,
            len(srcs),
            len(scratch),
        ),
        out_shape=(jax.ShapeDtypeStruct((R, D), jnp.float32), *more_out, *z_out),
        in_specs=[vmem] * len(ins) + [anywhere] * (len(more) + len(srcs)),
        out_specs=(vmem,) + (anywhere,) * len(more_out) + (vmem,) * len(z_out),
        scratch_shapes=[
            pltpu.VMEM((8, R, D), jnp.bfloat16),
            pltpu.VMEM((7, R, D), jnp.bfloat16),
            pltpu.SemaphoreType.DMA((7, C)),
            pltpu.SemaphoreType.DMA((7, C)),
            *scratch,
            *more_scratch,
        ],
        compiler_params=pltpu.CompilerParams(
            collective_id=cid, has_side_effects=True, vmem_limit_bytes=60 << 20
        ),
        cost_estimate=cost(1 << 20),
        name=name,
    )(*ins, *more, *srcs)
    if plan:
        z.done(out[-1])
        out = out[:-1]
    return out if more_out else out[0]


def row_split_body(rows, ins, out):
    a, w = ins
    Z, _, d = w.shape
    for z in range(Z):
        out[:, z * d : (z + 1) * d] = nn(a[rows, :], w[z]).astype(out.dtype)


def up_back_body(rows, ins, out):
    a, w = ins

    def f(cols):
        out[:, cols] = nt(a[rows, :], w[cols, :]).astype(out.dtype)

    tiles(w.shape[0], 512, f)


def project_back_body(rows, ins, out):
    a, w = ins
    S, _, width = a.shape

    def f(cols):
        total = None
        for s in range(S):
            t = nt(a[s, rows, :], w[cols, s * width : (s + 1) * width])
            total = t if total is None else total + t
        out[:, cols] = total.astype(out.dtype)

    tiles(w.shape[0], 512, f)


class Stream:
    def __init__(self, chunks, buf, sems, stage, out_sems):
        self.chunks, self.buf, self.sems = chunks, buf, sems
        self.stage, self.out_sems = stage, out_sems
        self.turn, self.flying = 0, [[], []]

    def fetch(self, i):
        src, j = self.chunks[i]
        w = self.buf.shape[2]
        return pltpu.make_async_copy(
            src.at[:, pl.ds(j * w, w)], self.buf.at[i % 2], self.sems.at[i % 2]
        )

    def get(self, i):
        self.fetch(i).wait()
        if i + 1 < len(self.chunks):
            self.fetch(i + 1).start()
        return self.buf.at[i % 2]

    def result(self, make, targets):
        slot = self.turn % 2
        self.turn += 1
        for c in self.flying[slot]:
            c.wait()
        make(self.stage.at[slot])
        self.flying[slot] = []
        for n, (lo, width, dest) in enumerate(targets):
            c = pltpu.make_async_copy(
                self.stage.at[slot, :, pl.ds(lo, width)], dest, self.out_sems.at[slot, n]
            )
            c.start()
            self.flying[slot].append(c)

    def drain(self):
        for slot in range(2):
            for c in self.flying[slot]:
                c.wait()


STREAM_SCRATCH = (
    pltpu.VMEM((2, 2048, 256), jnp.bfloat16),
    pltpu.SemaphoreType.DMA((2,)),
    pltpu.VMEM((2, 256, 1024), jnp.bfloat16),
    pltpu.SemaphoreType.DMA((2, 4)),
    pltpu.VMEM((256, 2048), jnp.bfloat16),
)


def ffn_filler(ins, more, more_out, scratch):
    hidden = ins[0]
    active, normed, grad = more
    (out,) = more_out
    buf, sems, stage, out_sems, turned, held, held_sem = scratch
    T, F = hidden.shape
    D = grad.shape[1]
    Z, _, d = out.shape
    w = buf.shape[2]
    half = stage.shape[2]
    stream = Stream(
        [(active, j) for j in range(F // w)] + [(normed, j) for j in range(D // w)],
        buf,
        sems,
        stage,
        out_sems,
    )
    held_copy = pltpu.make_async_copy(grad, held, held_sem)
    stream.fetch(0).start()
    held_copy.start()

    def product(right, lo):
        def make(tile):
            def f(cols):
                at = pl.ds(pl.multiple_of(lo + cols.start, 256), cols.size)
                tile[:, cols] = nn(turned[...], right[:, at]).astype(tile.dtype)

            tiles(half, 256, f)

        return make

    steps = []

    def down(j, h):
        def step():
            if h == 0:
                turned[...] = stream.get(j)[...].T
            if j == 0 and h == 0:
                held_copy.wait()
            targets = [
                (b * d, d, out.at[h * (half // d) + b, pl.ds(j * w, w), :]) for b in range(half // d)
            ]
            stream.result(product(held, h * half), targets)

        return step

    def up(j):
        def step():
            turned[...] = stream.get(F // w + j)[...].T
            z, r = (j * w) // d, (j * w) % d
            targets = [(b * d, d, out.at[z, pl.ds(F + b * d + r, w), :]) for b in range(F // d)]
            stream.result(product(hidden, 0), targets)

        return step

    for j in range(F // w):
        for h in range(D // half):
            steps.append(down(j, h))
    for j in range(D // w):
        steps.append(up(j))
    steps.append(stream.drain)
    return steps


def attn_filler(ins, more, more_out, scratch):
    parts = ins[0]
    context, grad, normed = more
    (out,) = more_out
    buf, sems, stage, out_sems, turned, ctx_t = scratch
    S, T, width = parts.shape
    D = grad.shape[1]
    Z = out.shape[0]
    d = D // Z
    w = buf.shape[2]
    n = D // w
    stream = Stream(
        [(context, 0)] + [(grad, j) for j in range(n)] + [(normed, j) for j in range(n)],
        buf,
        sems,
        stage,
        out_sems,
    )
    stream.fetch(0).start()
    steps = []

    def dense(j):
        def step():
            if j == 0:
                ctx_t[...] = stream.get(0)[...].T
            right = stream.get(1 + j)

            def make(tile):
                tile[:, :w] = nn(ctx_t[...], right[...]).astype(tile.dtype)

            z, r = (j * w) // d, (j * w) % d
            stream.result(make, [(0, w, out.at[z, pl.ds(0, width), pl.ds(r, w)])])

        return step

    def project(j):
        def step():
            turned[...] = stream.get(1 + n + j)[...].T

            def make(tile):
                for s in range(S):
                    tile[:, s * width : (s + 1) * width] = nn(turned[...], parts[s]).astype(
                        tile.dtype
                    )

            z, r = (j * w) // d, (j * w) % d
            side = pl.ds(r // w * width, width)
            stream.result(
                make,
                [(s * width, width, out.at[z, pl.ds(width + s * w, w), side]) for s in range(S)],
            )

        return step

    for j in range(n):
        steps.append(dense(j))
    for j in range(n):
        steps.append(project(j))
    steps.append(stream.drain)
    return steps


def finish_kernel(plan, n_src, v_ref, u_ref, *refs):
    srcs, refs = refs[:n_src], refs[n_src:]
    v_out, u_out, refs = refs[0], refs[1], refs[2:]
    z_out, refs = (refs[:1], refs[1:]) if plan else ((), refs)
    vs, us, v_in, u_in, send, recv = refs[:6]
    me, core, bx, by, partner, xn, yn = peers()
    z = z_task(plan, srcs, z_out, refs[6:])
    _, z1, z2, _ = z_peers()
    enter(partner, xn, yn, True)
    z.start()
    hops = (({"mp": partner}, False), ({"mp": xn}, False), ({"mp": yn}, False))
    hops += (({"dp": z1}, True), ({"dp": z2}, True))
    vs[0] = v_ref[...]
    us[3] = u_ref[...]
    z.tick()
    for i, (target, both) in enumerate(hops):
        copies = []
        for n, (src, dst) in enumerate(((vs, v_in), (us, u_in))[: 2 if both else 1]):
            c = pltpu.make_async_remote_copy(
                src_ref=src.at[i],
                dst_ref=dst.at[i],
                send_sem=send.at[n, i],
                recv_sem=recv.at[n, i],
                device_id=target,
                device_id_type=MESH,
            )
            c.start()
            copies.append(c)
        z.tick()
        for c in copies:
            c.wait()
        vs[i + 1] = vs[i] + v_in[i]
        if both:
            us[i + 1] = us[i] + u_in[i]
    v_out[...] = vs[5]
    u_out[...] = us[5]
    z.finish()


def finish_call(cid, v, u, z):
    vmem = pl.BlockSpec(memory_space=pltpu.VMEM)
    anywhere = pl.BlockSpec(memory_space=pl.ANY)
    srcs, z_out, more_scratch = z_parts(z)
    plan = tuple(z.plan)
    out = pl.pallas_call(
        functools.partial(finish_kernel, plan, len(srcs)),
        out_shape=(
            jax.ShapeDtypeStruct(v.shape, v.dtype),
            jax.ShapeDtypeStruct(u.shape, u.dtype),
            *z_out,
        ),
        in_specs=[vmem, vmem] + [anywhere] * len(srcs),
        out_specs=(vmem, vmem) + (vmem,) * len(z_out),
        scratch_shapes=[
            pltpu.VMEM((6, *v.shape), v.dtype),
            pltpu.VMEM((6, *u.shape), u.dtype),
            pltpu.VMEM((5, *v.shape), v.dtype),
            pltpu.VMEM((5, *u.shape), u.dtype),
            pltpu.SemaphoreType.DMA((2, 5)),
            pltpu.SemaphoreType.DMA((2, 5)),
            *more_scratch,
        ],
        compiler_params=pltpu.CompilerParams(
            collective_id=cid, has_side_effects=True, vmem_limit_bytes=60 << 20
        ),
        cost_estimate=cost(1 << 20),
        name="finish",
    )(v, u, *srcs)
    if plan:
        z.done(out[2])
    return out[0], out[1]


def layer_norm(values, scale_row, shift_row):
    centre = jnp.mean(values, axis=-1, keepdims=True)
    centred = values - centre
    spread = jnp.mean(centred * centred, axis=-1, keepdims=True)
    return centred * lax.rsqrt(spread + norm_eps) * scale_row + shift_row


def gather_sum(part):
    return lax.psum_scatter(
        part.astype(jnp.bfloat16), "mp", scatter_dimension=0, tiled=True
    ).astype(jnp.float32)


def gather_all(x):
    return lax.all_gather(x, "mp", axis=0, tiled=True)


def side_by_side(w):
    return jnp.concatenate([w[z] for z in range(w.shape[0])], axis=1)


def reduce_dp(part):
    return lax.psum_scatter(part.astype(jnp.bfloat16), "dp", scatter_dimension=0)


class Work:
    def __init__(self, backlog, limit):
        self.plan, self.arrays, self.pieces = [], [], []
        while limit and backlog.queue:
            entry = backlog.queue[0]
            key, array, row = entry
            if not any(a is array for a in self.arrays):
                self.arrays.append(array)
            i = [a is array for a in self.arrays].index(True)
            self.pieces.append((key, len(self.plan)))
            self.plan.append((i, row))
            limit -= 1
            entry[2] += ZR
            if entry[2] == array.shape[1]:
                backlog.queue.pop(0)
        self.backlog = backlog

    def done(self, result):
        for key, n in self.pieces:
            self.backlog.sums.setdefault(key, []).append(result[n * ZR : (n + 1) * ZR])


class Backlog:
    def __init__(self):
        self.queue, self.sums = [], {}

    def add(self, key, array):
        self.queue.append([key, array, 0])

    def take(self, limit):
        return Work(self, limit)

    def total(self, key):
        return jnp.concatenate(self.sums[key], axis=0)


class Fast:
    def __init__(self, T, D):
        self.T, self.D = T, D
        self.backlog = Backlog()

    def project(self, l, normed, w, shift, out_grad):
        T = self.T
        out = jax.ShapeDtypeStruct((T, w.shape[1]), jnp.bfloat16)
        if l == 0:
            full, self.last_grad = gather_only(0, normed, out_grad)
            return full, (nn(full, w) + shift).astype(jnp.bfloat16)
        return gather_call("gather_project", 10 * l, normed, (w, shift[None]), (out,), project_body)

    def dense(self, l, context, w):
        return scatter_call("dense_scatter", 10 * l + 1, self.T, self.D, (context, w), row_split_body)

    def up(self, l, normed, w, shift):
        out = jax.ShapeDtypeStruct((self.T, w.shape[1]), jnp.bfloat16)
        return gather_call("gather_up", 10 * l + 2, normed, (w, shift[None]), (out, out), up_body)

    def down(self, l, last, active, w):
        z = self.backlog.take(5) if last else None
        return scatter_call(
            "down_scatter", 10 * l + 3, self.T, self.D, (active, w), row_split_body, z=z
        )

    def down_back(self, l, last, grad, w, slope):
        if last:
            return self.last_grad, *down_back_here(self.last_grad, w, slope)
        F = slope.shape[1]
        outs = (
            jax.ShapeDtypeStruct((self.T, F), jnp.bfloat16),
            jax.ShapeDtypeStruct((1, F), jnp.float32),
        )
        z = self.backlog.take(5)
        return gather_call("gather_down_back", 10 * l + 4, grad, (w, slope), outs, down_back_body, z)

    def up_back(self, l, grad_hidden, w, active, normed, grad_down):
        T, F = grad_hidden.shape
        Z = lax.axis_size("dp")
        packed = jax.ShapeDtypeStruct((Z, 2 * F, self.D // Z), jnp.bfloat16)
        z = None if l else self.backlog.take(6)
        grad, packed = scatter_call(
            "up_back_scatter",
            10 * l + 5,
            T,
            self.D,
            (grad_hidden, w),
            up_back_body,
            more=(active, normed, grad_down),
            more_out=(packed,),
            scratch=STREAM_SCRATCH
            + (pltpu.VMEM((T, self.D), jnp.bfloat16), pltpu.SemaphoreType.DMA),
            filler=ffn_filler,
            z=z,
        )
        self.backlog.add(("ffn", l), packed)
        return grad

    def ffn_grads(self, l):
        summed = self.backlog.total(("ffn", l))
        d = summed.shape[1]
        F = summed.shape[0] // 2
        up = jnp.concatenate([summed[F + b * d : F + (b + 1) * d] for b in range(F // d)], axis=1)
        return up, summed[:F]

    def dense_back(self, l, grad, w):
        out = jax.ShapeDtypeStruct((self.T, w.shape[1]), jnp.bfloat16)
        z = self.backlog.take(4)
        return gather_call("gather_dense_back", 10 * l + 6, grad, (w,), (out,), dense_back_body, z)

    def project_back(self, l, grad_project, w, context, grad_branch, normed):
        S, T, width = grad_project.shape
        Z = lax.axis_size("dp")
        packed = jax.ShapeDtypeStruct((Z, (S + 1) * width, self.D // Z), jnp.bfloat16)
        grad, packed = scatter_call(
            "project_back_scatter",
            10 * l + 7,
            T,
            self.D,
            (grad_project, w),
            project_back_body,
            more=(context, grad_branch, normed),
            more_out=(packed,),
            scratch=STREAM_SCRATCH + (pltpu.VMEM((width, T), jnp.bfloat16),),
            filler=attn_filler,
            z=self.backlog.take(5),
        )
        self.backlog.add(("attn", l), packed)
        return grad

    def attn_grads(self, l):
        summed = self.backlog.total(("attn", l))
        w = summed.shape[1] // 2
        parts = [summed[(1 + s) * w : (2 + s) * w] for s in range(3)]
        parts = [jnp.concatenate([p[:, :w], p[:, w:]], axis=0) for p in parts]
        return jnp.stack(parts, axis=1), summed[:w]

    def finish(self, copied, split):
        rows = copied.shape[0] * copied.shape[1]
        v = jnp.concatenate([copied.reshape(rows, -1), jnp.zeros((-rows % 8, self.D), jnp.float32)])
        v, u = finish_call(9, v, split.reshape(8, -1), self.backlog.take(1000))
        return v[:rows].reshape(copied.shape), u.reshape(split.shape)


class Plain:
    def __init__(self, T, D):
        self.T, self.D = T, D
        self.ffn, self.attn = {}, {}

    def project(self, l, normed, w, shift, out_grad):
        full = gather_all(normed)
        return full, (nn(full, w) + shift).astype(jnp.bfloat16)

    def dense(self, l, context, w):
        return gather_sum(nn(context, side_by_side(w)))

    def up(self, l, normed, w, shift):
        full = gather_all(normed)
        return full, *gelu_both(nn(full, w) + shift)

    def down(self, l, last, active, w):
        return self.dense(l, active, w)

    def down_back(self, l, last, grad, w, slope):
        full = gather_all(grad)
        g = (nt(full, side_by_side(w)) * slope.astype(jnp.float32)).astype(jnp.bfloat16)
        return full, g, jnp.sum(g.astype(jnp.float32), axis=0, keepdims=True)

    def up_back(self, l, grad_hidden, w, active, normed, grad_down):
        Z = lax.axis_size("dp")
        F = grad_hidden.shape[1]
        d = self.D // Z
        up = jnp.einsum("td,tf->df", normed, grad_hidden, preferred_element_type=jnp.float32)
        down = jnp.einsum(
            "tf,tzd->zfd", active, grad_down.reshape(-1, Z, d), preferred_element_type=jnp.float32
        )
        packed = jnp.concatenate([down, up.reshape(Z, d * F // d, d)], axis=1)
        self.ffn[l] = reduce_dp(packed).astype(jnp.float32)
        return gather_sum(nt(grad_hidden, w))

    def ffn_grads(self, l):
        summed = self.ffn[l]
        d = summed.shape[1]
        F = summed.shape[0] // 2
        return summed[F:].reshape(d, F), summed[:F]

    def dense_back(self, l, grad, w):
        full = gather_all(grad)
        return full, nt(full, side_by_side(w)).astype(jnp.bfloat16)

    def project_back(self, l, grad_project, w, context, grad_branch, normed):
        S, T, width = grad_project.shape
        Z = lax.axis_size("dp")
        d = self.D // Z
        dense = jnp.einsum(
            "ti,tzd->zid", context, grad_branch.reshape(T, Z, d), preferred_element_type=jnp.float32
        )
        project = jnp.einsum(
            "td,sti->dsi", normed, grad_project, preferred_element_type=jnp.float32
        )
        packed = jnp.concatenate(
            [dense.reshape(Z, -1), project.reshape(Z, -1)], axis=1
        ).reshape(Z, -1, width)
        part = sum(nt(grad_project[s], w[:, s * width : (s + 1) * width]) for s in range(S))
        self.attn[l] = reduce_dp(packed).astype(jnp.float32)
        return gather_sum(part)

    def attn_grads(self, l):
        d = self.D // lax.axis_size("dp")
        rows, width = self.attn[l].shape
        flat = self.attn[l].reshape(-1)
        return flat[width * d :].reshape(d, 3, width), flat[: width * d].reshape(width, d)

    def finish(self, copied, split):
        return lax.psum(copied, ("dp", "mp")), lax.psum(split, "dp")


def shards(
    inputs,
    out_grad,
    project_weight,
    dense_weight,
    up_weight,
    down_weight,
    project_bias,
    up_bias,
    norm_gain,
    norm_bias,
    output_bias,
):
    tensor_size = lax.axis_size("mp")
    tensor_rank = lax.axis_index("mp")
    row_count, model_width = inputs.shape
    total_rows = row_count * tensor_size
    inner_width = project_weight.shape[3]
    heads_here = N_HEADS // tensor_size
    layer_count = project_weight.shape[0]
    slopes = 2.0 ** (
        -8.0
        * (tensor_rank * heads_here + lax.iota(jnp.int32, heads_here) + 1).astype(jnp.float32)
        / N_HEADS
    )
    low = jnp.bfloat16
    fast = tensor_size == 8 and lax.axis_size("dp") == 4 and row_count == 256
    ops = (Fast if fast else Plain)(total_rows, model_width)
    gathered = []
    for l in range(layer_count):
        gathered.append(
            (
                lax.all_gather(
                    project_weight[l].reshape(-1, 3 * inner_width).astype(low),
                    "dp",
                    axis=0,
                    tiled=True,
                ),
                lax.all_gather(dense_weight[l].astype(low), "dp", axis=0),
                lax.all_gather(up_weight[l].astype(low), "dp", axis=0, tiled=True),
                lax.all_gather(down_weight[l].astype(low), "dp", axis=0),
            )
        )
    stream = inputs.astype(jnp.float32)
    stored = []
    for l in range(layer_count):
        w_project, w_dense, w_up, w_down = gathered[l]
        normed = layer_norm(stream, norm_gain[l, 0], norm_bias[l, 0]).astype(low)
        shift = jnp.concatenate(
            [project_bias[l, 0], jnp.zeros((inner_width,), jnp.float32), project_bias[l, 1]]
        )
        normed_all, project = ops.project(l, normed, w_project, shift, out_grad)
        context, log_norms = attend_fwd(project, slopes)
        middle = stream + ops.dense(l, context, w_dense) + output_bias[l, 0]
        normed2 = layer_norm(middle, norm_gain[l, 1], norm_bias[l, 1]).astype(low)
        normed2_all, active, slope = ops.up(l, normed2, w_up, up_bias[l])
        stored.append(
            (stream, normed_all, project, log_norms, context, middle, normed2_all, active, slope)
        )
        if l < layer_count - 1:
            stream = middle + ops.down(l, False, active, w_down) + output_bias[l, 1]
    grad = out_grad.astype(jnp.float32)
    copied = [None] * layer_count
    split = [None] * layer_count
    for l in reversed(range(layer_count)):
        last = l == layer_count - 1
        w_project, w_dense, w_up, w_down = gathered[l]
        stream_in, normed_all, project, log_norms, context, middle, normed2_all, active, slope = (
            stored[l]
        )
        down_bias_grad = jnp.sum(grad, axis=0)
        grad_down, grad_hidden, up_bias_part = ops.down_back(l, last, grad.astype(low), w_down, slope)
        grad_normed2 = ops.up_back(l, grad_hidden, w_up, active, normed2_all, grad_down)
        if last:
            rows_out = middle + ops.down(l, True, active, w_down) + output_bias[l, 1]
            outputs = rows_out.astype(low)
        norm_back = jax.vjp(layer_norm, middle, norm_gain[l, 1], norm_bias[l, 1])[1]
        grad_from_norm, gain_second, shift_second = norm_back(grad_normed2)
        grad_middle = grad + grad_from_norm
        dense_bias_grad = jnp.sum(grad_middle, axis=0)
        grad_branch, grad_context = ops.dense_back(l, grad_middle.astype(low), w_dense)
        grad_project, project_bias_part = attend_bwd(
            project, grad_context, context, log_norms, slopes
        )
        grad_normed = ops.project_back(
            l, grad_project, w_project, context, grad_branch, normed_all
        )
        norm_back = jax.vjp(layer_norm, stream_in, norm_gain[l, 0], norm_bias[l, 0])[1]
        grad_from_norm, gain_first, shift_first = norm_back(grad_normed)
        grad = grad_middle + grad_from_norm
        copied[l] = jnp.stack(
            [gain_first, gain_second, shift_first, shift_second, dense_bias_grad, down_bias_grad]
        )
        split[l] = jnp.concatenate([project_bias_part.reshape(-1), up_bias_part.reshape(-1)])
    copied, split = ops.finish(jnp.stack(copied), jnp.stack(split))
    matrix_grads = [(*ops.attn_grads(l), *ops.ffn_grads(l)) for l in range(layer_count)]
    return (
        outputs,
        grad,
        *(jnp.stack(parts) for parts in zip(*matrix_grads)),
        split[:, : 2 * inner_width].reshape(layer_count, 2, inner_width),
        split[:, 2 * inner_width :],
        copied[:, 0:2],
        copied[:, 2:4],
        copied[:, 4:6],
    )


def solution(mesh):
    rows = P(("dp", "mp"), None)
    specs = (P(None, "dp", None, "mp"), P(None, "mp", "dp"), P(None, "dp", "mp"), P(None, "mp", "dp"))
    biases = (P(None, None, "mp"), P(None, "mp"), P(), P(), P())
    return jax.shard_map(
        shards,
        mesh=mesh,
        in_specs=(rows, rows, *specs, *biases),
        out_specs=(rows, rows, *specs, *biases),
        check_vma=False,
    )
```

time: 1660 us -> 1270 us (0.77)
  waiting for transfers between devices: 568 us -> 92.5 us
  Pallas kernels: 815 us -> 1030 us
  matrix products: 92.4 us -> 10.2 us
  local copies, waits for them, and re-layouts: 86.7 us -> 50.8 us
  blocking collectives: 17.5 us -> 0 us
    reduce_scatter x8 -> x0, waiting for transfers between devices: 452 us -> none  [reduce_dp(): lax.psum_scatter(part.astype(low), 'dp', scatter_dimension=0, tiled=True)]
    pallas_call x8 -> x11, Pallas kernels: 362 us -> 650 us  [the longest x8 419 us: scatter_call(): pl.pallas_call(functools.partial(scatter_kernel, C, len(ins), len(more),...]
    dot_general x8 -> x1, matrix products: 92.4 us -> 10.2 us  [nn(): return jnp.dot(a, b, preferred_element_type=jnp.float32)]
    pallas_call x8 -> x6, Pallas kernels: 391 us -> 321 us  [gather_call(): pl.pallas_call(functools.partial(gather_kernel, C, len(ins), len(outs), b...]
    all_gather x2, waiting for transfers between devices: 61.3 us -> 11.5 us  [shards(): lax.all_gather(project_weight[l].reshape(-1, 3 * inner_width).astype(low)...]
    reshape x4, local copies, waits for them, and re-layouts: 48.4 us -> 1.36 us  [the longest x2 0.73 us: finish(): return (v[:rows].reshape(copied.shape), u.reshape(split.shape))]
    psum x1 -> x0, blocking collectives: 17.5 us -> none  [shards(): lax.psum(jnp.concatenate([project_bias_part.reshape(-1), up_bias_part.res...]
  transfers between devices with their start and end apart: 17 -> 8, of which waited for: 12 -> 5; matrix products, arithmetic and copies ran while one was open for 11% -> 3% of each run, Pallas kernels for 22% -> 30%
where the time goes in v2:
time: 1270 us; the launch traced here: 1260 us
  Pallas kernels  1030 us (81%)
  waiting for transfers between devices  92.5 us (7%)
  other arithmetic  56.5 us (4%)
  local copies, waits for them, and re-layouts  50.8 us (4%)
  between operations  15.2 us (1%)
    pallas_call x8, Pallas kernels, scatter_call(): pl.pallas_call(functools.partial(scatter_kernel, C, len(ins), len(more),...  419 us
    pallas_call x6, Pallas kernels, gather_call(): pl.pallas_call(functools.partial(gather_kernel, C, len(ins), len(outs), b...  321 us
    pallas_call x1, Pallas kernels, finish_call(): pl.pallas_call(functools.partial(finish_kernel, plan, len(srcs)), out_sha...  139 us
    pallas_call x1, Pallas kernels, gather_only(): pl.pallas_call(functools.partial(gather_only_kernel, C, n), out_shape=tup...  75.3 us
    all_gather x2, waiting for transfers between devices, shards(): lax.all_gather(down_weight[l].astype(low), 'dp', axis=0)  64 us
    pallas_call x2, Pallas kernels, attend_bwd(): pl.pallas_call(attend_bwd_kernel, grid=(H,), out_shape=(jax.ShapeDtypeStr...  36.2 us
    pallas_call x2, Pallas kernels, attend_fwd(): pl.pallas_call(attend_fwd_kernel, grid=(H,), out_shape=(jax.ShapeDtypeStr...  26.2 us
  transfers between devices with their start and end apart: 8, of which 5 were waited for; matrix products, arithmetic and copies ran while one was open for 3% of the time, Pallas kernels for 30%

profile of v2, /device:TPU:0, one launch (start us, length us, event | category | flops | bytes accessed | tf_op | source)
XLA Modules:
  0.0 1259.6 jit_solution(12146560123113423282)
XLA Ops:
  7.2 2.2 copy.27
  11.9 2.5 convert.18
  14.4 1.5 fusion.41
  16.0 2.5 convert.19
  18.5 1.5 fusion.40
  20.0 1.2 copy.29
  25.4 1.4 fusion.7.refs_0_
  26.8 75.3 %gather_rows.1 = (bf16[2048,2048]{1,0:T(8,128)(2,1)}, bf16[2048,2048]{1,0:T(8,128)(2,1)}) custom-call(bf16[256,2048]{1,0:T(8,128)(2,1)} %fusion.7.refs_0_, bf16[256,2048]{1,0:T(8,128)(2,1)} %refs_1_.1), custom_call_target="tpu_custom_call" | custom-call | flops 1048576 | bytes 65536 | tf_op jit(solution)/shard_map/gather_rows/pallas_call | solution.py:494
  102.1 10.2 add_convert_fusion.q_ref.k_ref.v_ref
  112.4 13.1 %attend_fwd.2 = (bf16[2048,256]{1,0:T(8,128)(2,1)S(1)}, f32[2,8,256]{2,1,0:T(8,128)S(1)}) custom-call(f32[2]{0:T(128)S(1)} %multiply_power_fusion.slope_ref, bf16[2048,768]{1,0:T(8,128)(2,1)S(1)} %add_convert_fusion.q_ref.k_ref.v_ref, bf16[2048,768]{1,0:T(8,128)(2,1)S(1)} %add_convert_fusion.q_ref.k_ref.v_ref, ...), custom_call_target="tpu_custom_call" | custom-call | flops 1048576 | bytes 65536 | tf_op jit(solution)/shard_map/attend_fwd/pallas_call | solution.py:114
  127.1 42.8 %dense_scatter.2 = f32[256,2048]{1,0:T(8,128)} custom-call(bf16[2048,256]{1,0:T(8,128)(2,1)} %copy-done.3, bf16[4,256,512]{2,1,0:T(8,128)(2,1)} %all-gather.13.cloned.1.call-done.refs_1_), custom_call_target="tpu_custom_call" | custom-call | flops 1048576 | bytes 65536 | tf_op jit(solution)/shard_map/dense_scatter/pallas_call | solution.py:756
  169.9 1.9 fusion.37
  172.2 1.4 add_convert_fusion.4.refs_0_
  173.6 13.6 %all-gather.23.cloned.1.call-done = bf16[1,2048,1024]{2,1,0:T(8,128)(2,1)} async-done(((bf16[1,512,1024]{2,1,0:T(8,128)(2,1)}), bf16[1,2048,1024]{2,1,0:T(8,128)(2,1)}) %all-gather.23.cloned.1.call-update) | async-done | bytes 4194320 | tf_op jit(solution)/shard_map/all_gather | solution.py:1347
  187.2 49.4 %gather_up.2 = (bf16[2048,2048]{1,0:T(8,128)(2,1)}, bf16[2048,1024]{1,0:T(8,128)(2,1)}, bf16[2048,1024]{1,0:T(8,128)(2,1)}) custom-call(bf16[256,2048]{1,0:T(8,128)(2,1)} %add_convert_fusion.4.refs_0_, bf16[2048,1024]{1,0:T(8,128)(2,1)} %bitcast.74, f32[1,1024]{1,0:T(1,128)} %get-tuple-element.173.refs_2_), custom_call_target="tpu_custom_call" | custom-call | flops 1048576 | bytes 65536 | tf_op jit(solution)/shard_map/gather_up/pallas_call | solution.py:400
  236.6 32.0 %all-gather.15.cloned.1.call-done.refs_1_ = bf16[4,1024,512]{2,1,0:T(8,128)(2,1)} async-done(((bf16[1,1024,512]{2,1,0:T(8,128)(2,1)}), bf16[4,1024,512]{2,1,0:T(8,128)(2,1)}) %all-gather.15.cloned.1.call-update) | async-done | bytes 4194320 | tf_op jit(solution)/shard_map/all_gather | solution.py:1348
  268.5 47.3 %down_scatter.2 = f32[256,2048]{1,0:T(8,128)} custom-call(bf16[2048,1024]{1,0:T(8,128)(2,1)} %get-tuple-element.59.refs_0_.refs_2_, bf16[4,1024,512]{2,1,0:T(8,128)(2,1)} %all-gather.15.cloned.1.call-done.refs_1_), custom_call_target="tpu_custom_call" | custom-call | flops 1048576 | bytes 65536 | tf_op jit(solution)/shard_map/down_scatter/pallas_call | solution.py:756
  315.8 1.9 fusion.36
  319.1 1.4 add_convert_fusion.3.refs_0_
  320.5 11.5 all-gather.17.cloned.1.call-done.refs_1_
  332.0 44.0 %gather_project.1 = (bf16[2048,2048]{1,0:T(8,128)(2,1)}, bf16[2048,768]{1,0:T(8,128)(2,1)}) custom-call(bf16[256,2048]{1,0:T(8,128)(2,1)} %add_convert_fusion.3.refs_0_, bf16[2048,768]{1,0:T(8,128)(2,1)} %all-gather.17.cloned.1.call-done.refs_1_, f32[1,768]{1,0:T(1,128)} %broadcast_in_dim.18.refs_2_), custom_call_target="tpu_custom_call" | custom-call | flops 1048576 | bytes 65536 | tf_op jit(solution)/shard_map/gather_project/pallas_call | solution.py:400
  376.1 1.9 copy-done.1
  378.0 13.1 %attend_fwd.3 = (bf16[2048,256]{1,0:T(8,128)(2,1)S(1)}, f32[2,8,256]{2,1,0:T(8,128)S(1)}) custom-call(f32[2]{0:T(128)S(1)} %multiply_power_fusion.slope_ref, bf16[2048,768]{1,0:T(8,128)(2,1)S(1)} %copy-done.1, bf16[2048,768]{1,0:T(8,128)(2,1)S(1)} %copy-done.1, bf16[2048,768]{1,0:T(8,128)(2,1)S(1)} %copy-done.1), custom_call_target="tpu_custom_call" | custom-call | flops 1048576 | bytes 65536 | tf_op jit(solution)/shard_map/attend_fwd/pallas_call | solution.py:114
  392.6 43.0 %dense_scatter.3 = f32[256,2048]{1,0:T(8,128)} custom-call(bf16[2048,256]{1,0:T(8,128)(2,1)} %copy-done.4, bf16[4,256,512]{2,1,0:T(8,128)(2,1)} %all-gather.19.cloned.1.call-done.refs_1_), custom_call_target="tpu_custom_call" | custom-call | flops 1048576 | bytes 65536 | tf_op jit(solution)/shard_map/dense_scatter/pallas_call | solution.py:756
  435.7 2.5 fusion.35
  439.6 1.4 add_convert_fusion.2.refs_0_
  441.0 1.5 all-gather.25.cloned.1.call-done
  442.5 49.4 %gather_up.3 = (bf16[2048,2048]{1,0:T(8,128)(2,1)}, bf16[2048,1024]{1,0:T(8,128)(2,1)}, bf16[2048,1024]{1,0:T(8,128)(2,1)}) custom-call(bf16[256,2048]{1,0:T(8,128)(2,1)} %add_convert_fusion.2.refs_0_, bf16[2048,1024]{1,0:T(8,128)(2,1)} %bitcast.72, f32[1,1024]{1,0:T(1,128)} %get-tuple-element.172.refs_2_), custom_call_target="tpu_custom_call" | custom-call | flops 1048576 | bytes 65536 | tf_op jit(solution)/shard_map/gather_up/pallas_call | solution.py:400
  491.9 32.1 %all-gather.21.cloned.1.call-done.w_ref.refs_1_ = bf16[4,1024,512]{2,1,0:T(8,128)(2,1)} async-done(((bf16[1,1024,512]{2,1,0:T(8,128)(2,1)}), bf16[4,1024,512]{2,1,0:T(8,128)(2,1)}) %all-gather.21.cloned.1.call-update) | async-done | bytes 4194320 | tf_op jit(solution)/shard_map/all_gather | solution.py:1348
  524.0 2.2 copy-done.2
  526.2 2.2 copy-done.6
  528.4 17.0 %down_back.1 = (bf16[2048,1024]{1,0:T(8,128)(2,1)S(1)}, f32[1,1024]{1,0:T(1,128)S(1)}) custom-call(bf16[2048,2048]{1,0:T(8,128)(2,1)} %get-tuple-element.63.g_ref.refs_4_, bf16[4,1024,512]{2,1,0:T(8,128)(2,1)S(1)} %copy-done.2, bf16[2048,1024]{1,0:T(8,128)(2,1)S(1)} %copy-done.6), custom_call_target="tpu_custom_call" | custom-call | flops 1048576 | bytes 65536 | tf_op jit(solution)/shard_map/down_back/pallas_call | solution.py:604
  545.4 2.0 copy-done.5
  547.4 59.3 %up_back_scatter.2 = (f32[256,2048]{1,0:T(8,128)}, bf16[4,2048,512]{2,1,0:T(8,128)(2,1)}) custom-call(bf16[2048,1024]{1,0:T(8,128)(2,1)} %copy-done.5, bf16[2048,1024]{1,0:T(8,128)(2,1)} %bitcast.73, bf16[2048,1024]{1,0:T(8,128)(2,1)} %get-tuple-element.62.refs_2_.refs_0_, bf16[2048,2048]{1,0:T(8,128)(2,1)} %get-tuple-element.66.refs_3_, ...), custom_call_target="tpu_custom_call" | custom-call | flops 1048576 | bytes 65536 | tf_op jit(solution)/shard_map/up_back_scatter/pallas_call | solution.py:756
  606.7 2.9 multiply_reduce_fusion
  609.7 51.3 %down_scatter.3 = (f32[256,2048]{1,0:T(8,128)}, f32[640,512]{1,0:T(8,128)}) custom-call(bf16[2048,1024]{1,0:T(8,128)(2,1)} %get-tuple-element.62.refs_2_.refs_0_, bf16[4,1024,512]{2,1,0:T(8,128)(2,1)} %all-gather.21.cloned.1.call-done.w_ref.refs_1_, bf16[4,2048,512]{2,1,0:T(8,128)(2,1)} %get-tuple-element.67.refs_2_.refs_5_.refs_3_), custom_call_target="tpu_custom_call" | custom-call | flops 1048576 | bytes 65536 | tf_op jit(solution)/shard_map/down_scatter/pallas_call | solution.py:756
  661.0 4.6 fusion.34
  665.7 1.3 copy-done.15
  667.0 1.3 fusion.27.refs_0_
  668.3 57.4 %gather_dense_back.2 = (bf16[2048,2048]{1,0:T(8,128)(2,1)}, bf16[2048,256]{1,0:T(8,128)(2,1)}, f32[512,512]{1,0:T(8,128)}) custom-call(bf16[256,2048]{1,0:T(8,128)(2,1)} %fusion.27.refs_0_, bf16[4,256,512]{2,1,0:T(8,128)(2,1)} %all-gather.19.cloned.1.call-done.refs_1_, bf16[4,2048,512]{2,1,0:T(8,128)(2,1)} %get-tuple-element.67.refs_2_.refs_5_.refs_3_), custom_call_target="tpu_custom_call" | custom-call | flops 1048576 | bytes 65536 | tf_op jit(solution)/shard_map/gather_dense_back/pallas_call | solution.py:400
  725.6 18.1 %attend_bwd.2 = (bf16[3,2048,256]{2,1,0:T(8,128)(2,1)}, f32[2,256]{1,0:T(2,128)}) custom-call(f32[2]{0:T(128)} %copy-done.9, bf16[2048,768]{1,0:T(8,128)(2,1)} %get-tuple-element.60.q_ref.k_ref.v_ref, bf16[2048,768]{1,0:T(8,128)(2,1)} %get-tuple-element.60.q_ref.k_ref.v_ref, bf16[2048,768]{1,0:T(8,128)(2,1)} %get-tuple-element.60.q_ref.k_ref.v_ref, ...), custom_call_target="tpu_custom_call" | custom-call | flops 1048576 | bytes 65536 | tf_op jit(solution)/shard_map/attend_bwd/pallas_call | solution.py:128
  743.7 54.2 %project_back_scatter.2 = (f32[256,2048]{1,0:T(8,128)}, bf16[4,1024,512]{2,1,0:T(8,128)(2,1)}, f32[640,512]{1,0:T(8,128)}) custom-call(bf16[3,2048,256]{2,1,0:T(8,128)(2,1)} %get-tuple-element.72.refs_0_, bf16[2048,768]{1,0:T(8,128)(2,1)} %all-gather.17.cloned.1.call-done.refs_1_, bf16[2048,256]{1,0:T(8,128)(2,1)} %copy-done.4, ...), custom_call_target="tpu_custom_call" | custom-call | flops 1048576 | bytes 65536 | tf_op jit(solution)/shard_map/project_back_scatter/pallas_call | solution.py:756
  797.9 3.1 multiply_reduce_fusion.1
  804.1 1.3 copy-done.17
  806.5 64.6 %gather_down_back.1 = (bf16[2048,2048]{1,0:T(8,128)(2,1)}, bf16[2048,1024]{1,0:T(8,128)(2,1)}, f32[1,1024]{1,0:T(1,128)}, f32[640,512]{1,0:T(8,128)}) custom-call(bf16[256,2048]{1,0:T(8,128)(2,1)} %convert_element_type.74.refs_0_, bf16[4,1024,512]{2,1,0:T(8,128)(2,1)} %all-gather.15.cloned.1.call-done.refs_1_, bf16[2048,1024]{1,0:T(8,128)(2,1)} %get-tuple-element.76.refs_2_, ...), custom_call_target="tpu_custom_call" | custom-call | flops 1048576 | bytes 65536 | tf_op jit(solution)/shard_map/gather_down_back/pallas_call | solution.py:400
  871.1 2.2 slice.298
  874.4 64.5 %up_back_scatter.3 = (f32[256,2048]{1,0:T(8,128)}, bf16[4,2048,512]{2,1,0:T(8,128)(2,1)}, f32[640,512]{1,0:T(8,128)}) custom-call(bf16[2048,1024]{1,0:T(8,128)(2,1)} %get-tuple-element.78.refs_0_, bf16[2048,1024]{1,0:T(8,128)(2,1)} %bitcast.75, bf16[2048,1024]{1,0:T(8,128)(2,1)} %get-tuple-element.59.refs_0_.refs_2_, ...), custom_call_target="tpu_custom_call" | custom-call | flops 1048576 | bytes 65536 | tf_op jit(solution)/shard_map/up_back_scatter/pallas_call | solution.py:756
  938.9 2.5 multiply_reduce_fusion.2
  943.3 1.3 copy-done.20
  945.8 56.6 %gather_dense_back.3 = (bf16[2048,2048]{1,0:T(8,128)(2,1)}, bf16[2048,256]{1,0:T(8,128)(2,1)}, f32[512,512]{1,0:T(8,128)}) custom-call(bf16[256,2048]{1,0:T(8,128)(2,1)} %convert_element_type.75.refs_0_, bf16[4,256,512]{2,1,0:T(8,128)(2,1)} %all-gather.13.cloned.1.call-done.refs_1_, bf16[4,2048,512]{2,1,0:T(8,128)(2,1)} %get-tuple-element.82.refs_2_.refs_5_.refs_0_), custom_call_target="tpu_custom_call" | custom-call | flops 1048576 | bytes 65536 | tf_op jit(solution)/shard_map/gather_dense_back/pallas_call | solution.py:400
  1002.3 18.1 %attend_bwd.3 = (bf16[3,2048,256]{2,1,0:T(8,128)(2,1)}, f32[2,256]{1,0:T(2,128)}) custom-call(f32[2]{0:T(128)} %copy-done.9, bf16[2048,768]{1,0:T(8,128)(2,1)} %copy-done, bf16[2048,768]{1,0:T(8,128)(2,1)} %copy-done, bf16[2048,768]{1,0:T(8,128)(2,1)} %copy-done, bf16[2048,256]{1,0:T(8,128)(2,1)} %get-tuple-element.83.g_ref, bf16[2048,256]{1,0:T(8,128)(2,1)} %copy-done.3, ...), custom_call_target="tpu_custom_call" | custom-call | flops 1048576 | bytes 65536 | tf_op jit(solution)/shard_map/attend_bwd/pallas_call | solution.py:128
  1021.8 56.1 %project_back_scatter.3 = (f32[256,2048]{1,0:T(8,128)}, bf16[4,1024,512]{2,1,0:T(8,128)(2,1)}, f32[640,512]{1,0:T(8,128)}) custom-call(bf16[3,2048,256]{2,1,0:T(8,128)(2,1)} %get-tuple-element.85.refs_0_, bf16[2048,768]{1,0:T(8,128)(2,1)} %all-gather.11.cloned.1.call-done.refs_1_, bf16[2048,256]{1,0:T(8,128)(2,1)} %copy-done.3, ...), custom_call_target="tpu_custom_call" | custom-call | flops 1048576 | bytes 65536 | tf_op jit(solution)/shard_map/project_back_scatter/pallas_call | solution.py:756
  1077.9 2.3 fusion.29
  1082.0 139.3 %finish.1 = (f32[16,2048]{1,0:T(8,128)}, f32[8,384]{1,0:T(8,128)}, f32[1920,512]{1,0:T(8,128)}) custom-call(f32[16,2048]{1,0:T(8,128)} %concatenate.66.v_ref, f32[8,384]{1,0:T(8,128)} %reshape.215.u_ref, bf16[4,2048,512]{2,1,0:T(8,128)(2,1)} %get-tuple-element.82.refs_2_.refs_5_.refs_0_, bf16[4,1024,512]{2,1,0:T(8,128)(2,1)} %get-tuple-element.92.refs_1_), custom_call_target="tpu_custom_call" | custom-call | flops 1048576 | bytes 65536 | tf_op jit(solution)/shard_map/finish/pallas_call | solution.py:1040
  1222.7 1.9 slice_bitcast_fusion.1
  1224.6 2.3 slice.309
  1226.8 2.5 fusion.39
  1229.3 3.0 slice.307
  1234.3 2.1 add_add_fusion.4
  1237.7 2.2 pad_maximum_fusion.8
  1240.0 2.1 fusion.12
  1242.1 2.6 pad_maximum_fusion.1
  1246.4 2.5 pad_maximum_fusion
  1250.5 2.1 pad_maximum_fusion.2
  (200 shorter events, 31.9 us)
Async XLA Ops:
  7.2 95.0 %all-gather.11.cloned.1.call-start = ((), (), s32[]{:S(2)}) async-start(), calls=%async_computation | async-start | bytes 3932160 | tf_op jit(solution)/shard_map/all_gather | solution.py:1340
  9.6 1.3 copy-start.36
  10.8 116.3 %all-gather.13.cloned.1.call-start = ((), (), s32[]{:S(2)}) async-start(), calls=%async_computation.1 | async-start | bytes 1310720 | tf_op jit(solution)/shard_map/all_gather | solution.py:1346
  11.8 175.4 %all-gather.23.cloned.1.call-start = ((), (), s32[]{:S(2)}) async-start(), calls=%async_computation.6 | async-start | bytes 5242880 | tf_op jit(solution)/shard_map/all_gather | solution.py:1347
  15.9 252.6 %all-gather.15.cloned.1.call-start = ((), (), s32[]{:S(2)}) async-start(), calls=%async_computation.2 | async-start | bytes 5242880 | tf_op jit(solution)/shard_map/all_gather | solution.py:1348
  19.9 312.1 %all-gather.17.cloned.1.call-start = ((), (), s32[]{:S(2)}) async-start(), calls=%async_computation.3 | async-start | bytes 3932160 | tf_op jit(solution)/shard_map/all_gather | solution.py:1340
  20.0 3.3 copy-start.13
  21.2 371.4 %all-gather.19.cloned.1.call-start = ((), (), s32[]{:S(2)}) async-start(), calls=%async_computation.4 | async-start | bytes 1310720 | tf_op jit(solution)/shard_map/all_gather | solution.py:1346
  21.8 420.7 %all-gather.25.cloned.1.call-start = ((), (), s32[]{:S(2)}) async-start(), calls=%async_computation.7 | async-start | bytes 5242880 | tf_op jit(solution)/shard_map/all_gather | solution.py:1347
  21.8 2.2 copy-start.57
  21.9 2.8 copy-start.55
  21.9 3.4 copy-start.48
  21.9 3.4 copy-start.49
  21.9 3.4 copy-start.50
  22.5 501.4 %all-gather.21.cloned.1.call-start = ((), (), s32[]{:S(2)}) async-start(), calls=%async_computation.5 | async-start | bytes 5242880 | tf_op jit(solution)/shard_map/all_gather | solution.py:1348
  23.3 352.7 %copy-start.9 = (f32[2]{0:T(128)}, f32[2]{0:T(128)S(1)}, u32[]{:S(2)}) copy-start(f32[2]{0:T(128)S(1)} %multiply_power_fusion.slope_ref) | copy-start | bytes 28
  24.0 1056.2 %copy-start.51 = (f32[256]{0:T(256)}, f32[256]{0:T(256)S(1)}, u32[]{:S(2)}) copy-start(f32[256]{0:T(256)S(1)} %fusion.22) | copy-start | bytes 3076
  112.3 13.1 %copy-start = (bf16[2048,768]{1,0:T(8,128)(2,1)}, bf16[2048,768]{1,0:T(8,128)(2,1)S(1)}, u32[]{:S(2)}) copy-start(bf16[2048,768]{1,0:T(8,128)(2,1)S(1)} %add_convert_fusion.q_ref.k_ref.v_ref) | copy-start | bytes 9437188
  127.1 42.8 %copy-start.14 = (bf16[256,2048]{1,0:T(8,128)(2,1)S(1)}, bf16[256,2048]{1,0:T(8,128)(2,1)}, u32[]{:S(2)}) copy-start(bf16[256,2048]{1,0:T(8,128)(2,1)} %param.11) | copy-start | bytes 3145732
  317.8 1.3 copy-start.10
  376.1 1.9 copy-start.1
  438.2 1.3 copy-start.12
  524.0 2.2 copy-start.2
  526.2 2.2 copy-start.6
  545.4 2.0 copy-start.5
  661.0 6.0 copy-start.22
  665.6 1.3 copy-start.15
  797.9 3.1 copy-start.11
  797.9 3.5 copy-start.25
  801.4 1.6 copy-start.16
  801.4 1.9 copy-start.23
  804.0 1.3 copy-start.17
  871.1 2.2 copy-start.32
  871.1 3.2 copy-start.58
  938.9 2.5 copy-start.24
  941.4 1.6 copy-start.18
  943.3 1.3 copy-start.20
  1002.3 18.8 %copy-start.56 = (f32[1,1024]{1,0:T(1,128)S(1)}, f32[1,1024]{1,0:T(1,128)}, u32[]{:S(2)}) copy-start(f32[1,1024]{1,0:T(1,128)} %get-tuple-element.89) | copy-start | bytes 12292
  1077.9 2.3 copy-start.19
  1080.2 1.1 copy-start.53
  1222.1 2.5 copy-start.47
  1229.3 3.0 copy-start.28
  1229.3 4.0 copy-start.31
  1232.3 2.0 copy-start.21
  1232.4 2.0 copy-start.52
  1232.4 2.0 copy-start.54
  1234.3 2.1 copy-start.46
  1234.3 2.8 slice-start
  1236.4 3.5 copy-start.27
  1236.4 3.5 copy-start.29
  1242.0 2.6 copy-start.26
  1242.0 2.7 copy-start.30
  1242.0 3.2 copy-start.33
  1242.0 3.8 copy-start.35
  1246.3 2.6 copy-start.37
  1246.3 2.6 copy-start.42
  1246.4 2.6 copy-start.43
  1246.4 2.6 copy-start.44
  1246.4 2.6 copy-start.45
  1248.9 1.0 copy-start.34
  1249.1 1.0 copy-start.38
  1249.1 1.1 copy-start.39
  1249.1 1.1 copy-start.40
  1249.1 1.2 copy-start.41
  (4 other events, 3.2 us)
Sparse Core Ops, SparseCore 0:
  10.9 66.1 all-gather.10
  78.7 26.5 all-gather.12
  106.9 80.2 all-gather.22
  189.2 79.2 all-gather.14
  269.9 62.0 all-gather.16
  333.4 26.5 all-gather.18
  362.2 80.2 all-gather.24
  444.6 79.3 all-gather.20

commit v3 on v2

v3 whole, which is shorter than its diff:
```python
import functools

import jax
import jax.numpy as jnp
from jax import lax
from jax.experimental import pallas as pl
from jax.experimental.pallas import tpu as pltpu
from jax.sharding import PartitionSpec as P

N_HEADS = 16
BLOCK = 256
HEAD = 128
LOG2E = 1.4426950408889634
MESH = pl.DeviceIdType.MESH
NT_DIMS = (((1,), (1,)), ((), ()))
norm_eps = 1e-05


def nt(a, b):
    return lax.dot_general(a, b, NT_DIMS, preferred_element_type=jnp.float32)


def nn(a, b):
    return jnp.dot(a, b, preferred_element_type=jnp.float32)


def layer_norm(values, scale_row, shift_row):
    centre = jnp.mean(values, axis=-1, keepdims=True)
    centred = values - centre
    spread = jnp.mean(centred * centred, axis=-1, keepdims=True)
    return centred * lax.rsqrt(spread + norm_eps) * scale_row + shift_row


def peers():
    me = lax.axis_index("mp")
    core = me % 2
    bx = (me // 2) % 2
    by = me // 4
    return me, core, bx, by, me + 1 - 2 * core, me + 2 - 4 * bx, me + 4 - 8 * by


def owner(rel, core, bx, by):
    c = core if rel % 2 == 0 else 1 - core
    x = bx if (rel // 2) % 2 == 0 else 1 - bx
    y = by if rel // 4 == 0 else 1 - by
    return y * 4 + x * 2 + c


def z_peers():
    z = lax.axis_index("dp")
    z1 = z + 1 - 2 * (z % 2)
    return z, z1, (z + 2) % 4, (z1 + 2) % 4


def enter(partner, xn, yn, z=False):
    barrier = pltpu.get_barrier_semaphore()
    for n in (partner, xn, yn):
        pl.semaphore_signal(barrier, inc=1, device_id={"mp": n}, device_id_type=MESH)
    if z:
        _, z1, z2, _ = z_peers()
        for n in (z1, z2):
            pl.semaphore_signal(barrier, inc=1, device_id={"dp": n}, device_id_type=MESH)
    pl.semaphore_wait(barrier, 5 if z else 3)


ZR = 128


class ZSum:
    ahead = 3

    def __init__(self, plan, srcs, out, scratch):
        self.plan, self.srcs, self.out = plan, srcs, out[0]
        self.recv, self.own, self.send_sem, self.recv_sem, self.loc = scratch
        self.z, self.z1, self.z2, self.z3 = z_peers()
        self.sent = []
        self.events = [functools.partial(self.event, c) for c in range(len(plan))]

    def block(self, c, z):
        i, row = self.plan[c]
        return self.srcs[i].at[z, pl.ds(row, ZR), :]

    def remote(self, src, kind, c, target):
        return pltpu.make_async_remote_copy(
            src_ref=src,
            dst_ref=self.recv.at[kind, c],
            send_sem=self.send_sem.at[kind, c],
            recv_sem=self.recv_sem.at[kind, c],
            device_id={"dp": target},
            device_id_type=MESH,
        )

    def push(self, *args):
        c = self.remote(*args)
        c.start()
        self.sent.append(c)

    def here(self, kind, c):
        return pltpu.make_async_copy(
            self.block(c, self.z2 if kind else self.z), self.own.at[kind, c], self.loc.at[kind, c]
        )

    def arrive(self, kind, c):
        self.remote(self.own.at[0, c], kind, c, self.z1).wait_recv()

    def start(self):
        for c in range(min(self.ahead, len(self.plan))):
            self.push(self.block(c, self.z3), 1, c, self.z1)
        for c in range(len(self.plan)):
            self.here(1, c).start()
            self.here(0, c).start()

    def event(self, c):
        if c + self.ahead < len(self.plan):
            n = c + self.ahead
            self.push(self.block(n, self.z3), 1, n, self.z1)
        self.arrive(1, c)
        self.here(1, c).wait()

        @pl.loop(0, ZR // 16)
        def _(i):
            rows = pl.ds(pl.multiple_of(i * 16, 16), 16)
            self.own[1, c, rows, :] = (
                self.own[1, c, rows, :].astype(jnp.float32)
                + self.recv[1, c, rows, :].astype(jnp.float32)
            ).astype(jnp.bfloat16)

        self.push(self.own.at[1, c], 2, c, self.z2)
        self.push(self.block(c, self.z1), 0, c, self.z1)

    def tick(self, n=1):
        for _ in range(min(n, len(self.events))):
            self.events.pop(0)()

    def finish(self):
        self.tick(len(self.events))
        for c in range(len(self.plan)):
            self.here(0, c).wait()
            self.arrive(0, c)
            self.arrive(2, c)

            @pl.loop(0, ZR // 16)
            def _(i):
                rows = pl.ds(pl.multiple_of(i * 16, 16), 16)
                to = pl.ds(pl.multiple_of(c * ZR + i * 16, 16), 16)
                self.out[to, :] = (
                    self.own[0, c, rows, :].astype(jnp.float32)
                    + self.recv[0, c, rows, :].astype(jnp.float32)
                    + self.recv[2, c, rows, :].astype(jnp.float32)
                ).astype(jnp.bfloat16)

        for c in self.sent:
            c.wait_send()


class ZGather:
    ahead = 4

    def __init__(self, plan, srcs, outs, scratch):
        self.plan, self.srcs, self.outs = plan, srcs, outs
        self.send_sem, self.recv_sem, self.loc = scratch
        self.z, self.z1, self.z2, self.z3 = z_peers()
        self.sent = []
        self.passed, self.settled = 0, 0

    def place(self, c, z):
        i, row, size, _ = self.plan[c]
        return self.outs[i].at[z, pl.ds(row, size), :]

    def own(self, c):
        i, row, size, layer = self.plan[c]
        return self.srcs[i].at[layer, pl.ds(row, size), :]

    def remote(self, src, z, kind, c, target):
        return pltpu.make_async_remote_copy(
            src_ref=src,
            dst_ref=self.place(c, z),
            send_sem=self.send_sem.at[kind, c],
            recv_sem=self.recv_sem.at[kind, c],
            device_id={"dp": target},
            device_id_type=MESH,
        )

    def push(self, *args):
        c = self.remote(*args)
        c.start()
        self.sent.append(c)

    def here(self, c):
        return pltpu.make_async_copy(self.own(c), self.place(c, self.z), self.loc.at[c])

    def start(self):
        for c in range(len(self.plan)):
            if c < self.ahead:
                self.send_own(c)
            self.here(c).start()

    def send_own(self, c):
        self.push(self.own(c), self.z, 0, c, self.z2)
        self.push(self.own(c), self.z, 1, c, self.z1)

    def event(self, c):
        if c + self.ahead < len(self.plan):
            self.send_own(c + self.ahead)
        self.remote(self.own(c), self.z2, 0, c, self.z2).wait_recv()
        self.push(self.place(c, self.z2), self.z2, 2, c, self.z1)

    def tick(self, n=1):
        for _ in range(min(n, len(self.plan) - self.passed)):
            self.event(self.passed)
            self.passed += 1

    def settle(self, n):
        self.tick(n - self.passed)
        for c in range(self.settled, n):
            self.remote(self.own(c), self.z1, 1, c, self.z1).wait_recv()
            self.remote(self.own(c), self.z3, 2, c, self.z1).wait_recv()
            self.here(c).wait()
        self.settled = n

    def finish(self):
        self.settle(len(self.plan))
        for c in self.sent:
            c.wait_send()


class NoZ:
    ahead = 0

    def start(self):
        pass

    def tick(self, n=1):
        pass

    def finish(self):
        pass


class ZCall:
    plan, arrays, out_shapes, out_space, scratch = (), (), (), pltpu.VMEM, ()

    def make(self, refs):
        return NoZ()

    def done(self, results):
        pass

    def aliases(self, first_in, first_out):
        return {}

    def counts(self):
        return len(self.arrays), len(self.out_shapes), len(self.scratch)

    def in_specs(self):
        return [pl.BlockSpec(memory_space=pl.ANY)] * len(self.arrays)

    def out_specs(self):
        return (pl.BlockSpec(memory_space=self.out_space),) * len(self.out_shapes)


def sum_scratch(n, w):
    return (
        pltpu.VMEM((3, n, ZR, w), jnp.bfloat16),
        pltpu.VMEM((2, n, ZR, w), jnp.bfloat16),
        pltpu.SemaphoreType.DMA((3, n)),
        pltpu.SemaphoreType.DMA((3, n)),
        pltpu.SemaphoreType.DMA((2, n)),
    )


class SumCall(ZCall):
    def __init__(self, backlog, limit):
        self.plan, self.arrays, self.pieces = [], [], []
        while limit and backlog.queue:
            entry = backlog.queue[0]
            key, array, row = entry
            if not any(a is array for a in self.arrays):
                self.arrays.append(array)
            i = [a is array for a in self.arrays].index(True)
            self.pieces.append((key, row))
            self.plan.append((i, row))
            limit -= 1
            entry[2] += ZR
            if entry[2] == array.shape[1]:
                backlog.queue.pop(0)
        self.backlog = backlog
        n = len(self.plan)
        if n:
            w = self.arrays[0].shape[2]
            self.out_shapes = (jax.ShapeDtypeStruct((n * ZR, w), jnp.bfloat16),)
            self.scratch = sum_scratch(n, w)

    def make(self, refs):
        i, o, _ = self.counts()
        return ZSum(self.plan, refs[:i], refs[i : i + o], refs[i + o :]) if self.plan else NoZ()

    def done(self, results):
        for n, (key, row) in enumerate(self.pieces):
            self.backlog.sums.append((key, row, results[0], n * ZR))


class Backlog:
    def __init__(self):
        self.queue, self.sums = [], []

    def add(self, key, array, summed=None):
        done = 0 if summed is None else summed.shape[0]
        self.sums += [(key, row, summed, row) for row in range(0, done, ZR)]
        self.queue.append([key, array, done])

    def take(self, limit):
        return SumCall(self, limit)


class GatherCall(ZCall):
    out_space = pl.ANY

    def __init__(self, queue, limit):
        self.queue, self.keys, self.plan = queue, [], []
        shards, begun, shapes = [], [], []
        while limit and queue.entries:
            entry = queue.entries[0]
            key, shard, row, size, layer = entry
            if key not in self.keys:
                self.keys.append(key)
                shards.append(shard)
                shapes.append(jax.ShapeDtypeStruct((4, *shard.shape[1:]), shard.dtype))
                if key in queue.arrays:
                    begun.append((len(self.keys) - 1, queue.arrays[key]))
            self.plan.append((self.keys.index(key), row, size, layer))
            limit -= 1
            entry[2] += size
            if entry[2] == shard.shape[1]:
                queue.entries.pop(0)
        self.arrays = shards + [x for _, x in begun]
        self.begun = [i for i, _ in begun]
        self.out_shapes = tuple(shapes)
        n = len(self.plan)
        self.scratch = (
            pltpu.SemaphoreType.DMA((3, n)),
            pltpu.SemaphoreType.DMA((3, n)),
            pltpu.SemaphoreType.DMA((n,)),
        )

    def aliases(self, first_in, first_out):
        n = len(self.keys)
        return {first_in + n + j: first_out + i for j, i in enumerate(self.begun)}

    def make(self, refs):
        i, o, _ = self.counts()
        return ZGather(self.plan, refs[:i], refs[i : i + o], refs[i + o :])

    def done(self, results):
        for key, array in zip(self.keys, results):
            self.queue.arrays[key] = array


class GatherQueue:
    def __init__(self):
        self.entries, self.arrays = [], {}

    def add(self, key, shard, layer, size):
        self.entries.append([key, shard, 0, size, layer])

    def take(self, limit):
        return GatherCall(self, limit) if limit and self.entries else NO_Z


NO_Z = ZCall()


def cost(flops):
    return pl.CostEstimate(flops=flops, bytes_accessed=1 << 16, transcendentals=0)


def split_refs(refs, *counts):
    parts = []
    for n in counts:
        parts.append(refs[:n])
        refs = refs[n:]
    return parts


def bias_tile(slope, first_key, first_query, keys, queries):
    kp = first_key + lax.broadcasted_iota(jnp.int32, (keys, queries), 0)
    qp = first_query + lax.broadcasted_iota(jnp.int32, (keys, queries), 1)
    return (jnp.abs(qp - kp).astype(jnp.float32)) * (-slope * LOG2E)

def scores_t(q, k, slope, i, B):
    L = (i+1)*B
    factor = q.shape[1] ** (-0.5) * LOG2E
    st = nt(k, q) * factor
    key = lax.broadcasted_iota(jnp.int32, (L, 1), 0)
    if i > 0:
        m = i * B
        kp = lax.broadcasted_iota(jnp.int32, (m, 1), 0).astype(jnp.float32)
        qp = (m + lax.broadcasted_iota(jnp.int32, (1, B), 1)).astype(jnp.float32)
        head = st[:m] - (qp - kp) * (slope * LOG2E)
        tail = st[m:] + bias_tile(slope, 0, 0, B, B)
        return head, tail
    return None, st + bias_tile(slope, 0, 0, B, B)

def enter_z(zc):
    if zc.plan:
        _, z1, z2, _ = z_peers()
        barrier = pltpu.get_barrier_semaphore()
        for n in (z1, z2):
            pl.semaphore_signal(barrier, inc=1, device_id={"dp": n}, device_id_type=MESH)
        pl.semaphore_wait(barrier, 2)


def attend_fwd_kernel(zc, slope_ref, p_ref, *refs):
    zi, zo, zs = zc.counts()
    z_in, (ctx_ref, lse_ref), z_out, (vt_ref,), z_scratch = split_refs(refs, zi, 2, zo, 1, zs)
    z = zc.make(z_in + z_out + z_scratch)
    enter_z(zc)
    z.start()
    B = BLOCK
    T, W = p_ref.shape
    H = W // (3 * HEAD)
    for h in range(H):
        q, k, v = (pl.ds((part * H + h) * HEAD, HEAD) for part in range(3))
        slope = slope_ref[h]
        vt_ref[...] = p_ref[:, v].T
        for i in range(T // B):
            L = (i + 1) * B
            head, tail = scores_t(p_ref[i * B : L, q], p_ref[:L, k], slope, i, B)
            top = jnp.max(tail, axis=0, keepdims=True)
            if head is not None:
                top = jnp.maximum(top, jnp.max(head, axis=0, keepdims=True))
            pt = jnp.exp2(tail - top)
            den = jnp.sum(pt, axis=0, keepdims=True)
            ct = nn(vt_ref[:, i * B : L], pt.astype(jnp.bfloat16))
            if head is not None:
                ph = jnp.exp2(head - top)
                den = den + jnp.sum(ph, axis=0, keepdims=True)
                ct = ct + nn(vt_ref[:, : i * B], ph.astype(jnp.bfloat16))
            ctx_ref[i * B : L, pl.ds(h * HEAD, HEAD)] = (ct / den).T.astype(ctx_ref.dtype)
            lse_ref[h, i : i + 1, :] = top + jnp.log2(den)
            if i % 4 == 3:
                z.tick()
    z.finish()


def attend_bwd_kernel(zc, slope_ref, p_ref, g_ref, c_ref, lse_ref, *refs):
    zi, zo, zs = zc.counts()
    z_in, (out_ref, sums_ref), z_out, (kt_ref, dk_ref, dv_ref), z_scratch = split_refs(
        refs, zi, 2, zo, 3, zs
    )
    z = zc.make(z_in + z_out + z_scratch)
    enter_z(zc)
    z.start()
    B = BLOCK
    T, W = p_ref.shape
    H = W // (3 * HEAD)
    n = T // B
    factor = HEAD ** (-0.5)
    ones = jnp.ones((8, HEAD), jnp.float32)
    for h in range(H):
        qc, kc, vc = (pl.ds((part * H + h) * HEAD, HEAD) for part in range(3))
        cols = pl.ds(h * HEAD, HEAD)
        slope = slope_ref[h]
        kt_ref[...] = p_ref[:, kc].T
        qsum = jnp.zeros((1, HEAD), jnp.float32)
        for i in reversed(range(n)):
            L = (i + 1) * B
            q = p_ref[i * B : L, qc]
            g = g_ref[i * B : L, cols]
            head, tail = scores_t(q, p_ref[:L, kc], slope, i, B)
            prod = g.astype(jnp.float32) * c_ref[i * B : L, cols].astype(jnp.float32)
            inner = lax.dot_general(
                ones,
                prod,
                NT_DIMS,
                preferred_element_type=jnp.float32,
                precision=lax.Precision.HIGHEST,
            )[:1]
            lse = lse_ref[h, i : i + 1, :]
            dpt = nt(p_ref[:L, vc], g)
            dqt = None
            for part, lo, hi in ((head, 0, i * B), (tail, i * B, L)):
                if part is None:
                    continue
                pt = jnp.exp2(part - lse)
                ds = (pt * (dpt[lo:hi] - inner)).astype(jnp.bfloat16)
                pt = pt.astype(jnp.bfloat16)
                dk = nn(ds, q)
                dv = nn(pt, g)
                if i == n - 1:
                    dk_ref[lo:hi, :] = dk
                    dv_ref[lo:hi, :] = dv
                else:
                    dk_ref[lo:hi, :] += dk
                    dv_ref[lo:hi, :] += dv
                t = nn(kt_ref[:, lo:hi], ds)
                dqt = t if dqt is None else dqt + t
            dq = (dqt * factor).T.astype(jnp.bfloat16)
            out_ref[0, i * B : L, cols] = dq
            qsum += jnp.sum(dq.astype(jnp.float32), axis=0, keepdims=True)
            if i % 4 == 3:
                z.tick()
        out_ref[1, :, cols] = (dk_ref[...] * factor).astype(jnp.bfloat16)
        dv = dv_ref[...].astype(jnp.bfloat16)
        out_ref[2, :, cols] = dv
        sums_ref[0:1, cols] = qsum
        sums_ref[1:2, cols] = jnp.sum(dv.astype(jnp.float32), axis=0, keepdims=True)
    z.finish()


def attend_call(kernel, cid, name, slopes, arrays, outs, scratch, z):
    vmem = pl.BlockSpec(memory_space=pltpu.VMEM)
    out = pl.pallas_call(
        functools.partial(kernel, z),
        out_shape=(*outs, *z.out_shapes),
        in_specs=[pl.BlockSpec(memory_space=pltpu.SMEM)] + [vmem] * len(arrays) + z.in_specs(),
        out_specs=(vmem,) * len(outs) + z.out_specs(),
        scratch_shapes=[*scratch, *z.scratch],
        compiler_params=pltpu.CompilerParams(
            collective_id=cid if z.plan else None,
            has_side_effects=bool(z.plan),
            vmem_limit_bytes=60 << 20,
        ),
        input_output_aliases=z.aliases(1 + len(arrays), len(outs)),
        cost_estimate=cost(1 << 20),
        name=name,
    )(slopes, *arrays, *z.arrays)
    z.done(out[len(outs) :])
    return out[: len(outs)]


def attend_fwd(cid, project, slopes, z):
    T, W = project.shape
    H = W // (3 * HEAD)
    outs = (
        jax.ShapeDtypeStruct((T, H * HEAD), jnp.bfloat16),
        jax.ShapeDtypeStruct((H, T // BLOCK, BLOCK), jnp.float32),
    )
    scratch = (pltpu.VMEM((HEAD, T), jnp.bfloat16),)
    return attend_call(attend_fwd_kernel, cid, "attend_fwd", slopes, (project,), outs, scratch, z)


def attend_bwd(cid, project, grad_context, context, lse, slopes, z):
    T, W = project.shape
    H = W // (3 * HEAD)
    outs = (
        jax.ShapeDtypeStruct((3, T, H * HEAD), jnp.bfloat16),
        jax.ShapeDtypeStruct((2, H * HEAD), jnp.float32),
    )
    scratch = (
        pltpu.VMEM((HEAD, T), jnp.bfloat16),
        pltpu.VMEM((T, HEAD), jnp.float32),
        pltpu.VMEM((T, HEAD), jnp.float32),
    )
    arrays = (project, grad_context, context, lse)
    return attend_call(attend_bwd_kernel, cid, "attend_bwd", slopes, arrays, outs, scratch, z)


def gather_kernel(C, n_in, n_more, n_out, n_more_out, body, filler, zc, n_scratch, *refs):
    zi, zo, zs = zc.counts()
    (x_ref,), ins, more, z_in, (full_ref,), outs, more_out, z_out, own_scratch, scratch, z_scratch = (
        split_refs(refs, 1, n_in, n_more, zi, 1, n_out, n_more_out, zo, 4, n_scratch, zs)
    )
    steps = filler(ins, more, more_out, scratch) if filler else []

    def fill(n):
        for _ in range(min(n, len(steps))):
            steps.pop(0)()

    buf, send, recv, loc = own_scratch
    R, D = x_ref.shape
    rc = R // C
    me, core, bx, by, partner, xn, yn = peers()
    z = zc.make(z_in + z_out + z_scratch)
    enter(partner, xn, yn, bool(zc.plan))
    z.start()
    sent = []

    def copy(src, rel, k, target, sidx):
        return pltpu.make_async_remote_copy(
            src_ref=src,
            dst_ref=buf.at[k, rel],
            send_sem=send.at[sidx, k],
            recv_sem=recv.at[rel, k],
            device_id={"mp": target},
            device_id_type=MESH,
        )

    def push(src, rel, k, target, sidx):
        c = copy(src, rel, k, target, sidx)
        c.start()
        sent.append(c)

    def arrive(rel, k):
        copy(buf.at[k, 0], rel, k, partner, 0).wait_recv()

    kept = []

    def keep(src, start, size, k, rel):
        c = pltpu.make_async_copy(src, full_ref.at[pl.ds(start, size), :], loc.at[k, rel])
        c.start()
        kept.append(c)

    def run(k, lo, hi):
        starts = []
        for rel in range(lo, hi):
            start = pl.multiple_of(owner(rel, core, bx, by) * R + k * rc, rc)
            keep(buf.at[k, rel], start, rc, k, rel)
            starts.append(start)
        body(
            False,
            lambda lo_=lo, hi_=hi: buf[k, lo_:hi_].reshape((hi_ - lo_) * rc, D),
            [pl.ds(s, rc) for s in starts],
            ins,
            outs,
        )

    for k in range(C):
        own = x_ref.at[pl.ds(k * rc, rc), :]
        push(own, 2, k, xn, 1)
        push(own, 4, k, yn, 2)
        push(own, 1, k, partner, 0)
    start = pl.multiple_of(me * R, R)
    keep(x_ref, start, R, 0, 0)
    body(True, lambda: x_ref[...], [pl.ds(start, R)], ins, outs)
    z.tick()
    fill(2)
    across = jnp.where(core == 0, xn, yn)
    for k in range(C + 2):
        if k < C:
            arrive(2, k)
            arrive(4, k)
            push(buf.at[k, 4 - 2 * core], 6, k, across, 3)
            push(buf.at[k, 2], 3, k, partner, 4)
            push(buf.at[k, 4], 5, k, partner, 5)
        if k == 0:
            starts = []
            other = owner(1, core, bx, by) * R
            for j in range(C):
                arrive(1, j)
                starts.append(pl.multiple_of(other + j * rc, rc))
                keep(buf.at[j, 1], starts[-1], rc, j, 1)
            body(
                False,
                lambda: buf[:, 1].reshape(R, D),
                [pl.ds(s, rc) for s in starts],
                ins,
                outs,
            )
        if 1 <= k <= C:
            arrive(3, k - 1)
            arrive(5, k - 1)
            run(k - 1, 2, 6)
            arrive(6, k - 1)
            push(buf.at[k - 1, 6], 7, k - 1, partner, 6)
        if k >= 2:
            arrive(7, k - 2)
            run(k - 2, 6, 8)
        z.tick(-(-(len(zc.plan) - 1) // (C + 1)))
        fill(1)
    fill(len(steps))
    z.finish()
    for c in sent:
        c.wait_send()
    for c in kept:
        c.wait()


def gather_call(
    name, cid, x, ins, outs, body, z=NO_Z, more=(), more_out=(), scratch=(), filler=None, C=4
):
    R, D = x.shape
    vmem = pl.BlockSpec(memory_space=pltpu.VMEM)
    anywhere = pl.BlockSpec(memory_space=pl.ANY)
    spec = lambda inside: vmem if inside else anywhere
    counts = (len(ins), len(more), len(outs), len(more_out))
    out = pl.pallas_call(
        functools.partial(gather_kernel, C, *counts, body, filler, z, len(scratch)),
        out_shape=(
            jax.ShapeDtypeStruct((8 * R, D), x.dtype),
            *outs,
            *(shape for shape, _ in more_out),
            *z.out_shapes,
        ),
        in_specs=[vmem] * (1 + len(ins)) + [spec(i) for _, i in more] + z.in_specs(),
        out_specs=(anywhere,)
        + (vmem,) * len(outs)
        + tuple(spec(i) for _, i in more_out)
        + z.out_specs(),
        scratch_shapes=[
            pltpu.VMEM((C, 8, R // C, D), x.dtype),
            pltpu.SemaphoreType.DMA((7, C)),
            pltpu.SemaphoreType.DMA((8, C)),
            pltpu.SemaphoreType.DMA((C, 8)),
            *scratch,
            *z.scratch,
        ],
        compiler_params=pltpu.CompilerParams(
            collective_id=cid, has_side_effects=True, vmem_limit_bytes=60 << 20
        ),
        input_output_aliases=z.aliases(
            1 + len(ins) + len(more), 1 + len(outs) + len(more_out)
        ),
        cost_estimate=cost(1 << 20),
        name=name,
    )(x, *ins, *(x for x, _ in more), *z.arrays)
    n = 1 + len(outs) + len(more_out)
    z.done(out[n:])
    return out[:n]


def gather_only_kernel(C, n, n_after, zc, *refs):
    zi, zo, zs = zc.counts()
    xs, _, z_in, fulls, z_out, (send, recv, loc), z_scratch = split_refs(
        refs, n, n_after, zi, n, zo, 3, zs
    )
    R, D = xs[0].shape
    rc = R // C
    me, core, bx, by, partner, xn, yn = peers()
    z = zc.make(z_in + z_out + z_scratch)
    enter(partner, xn, yn, bool(zc.plan))
    sent = []

    def copy(src, a, k, target, rel, sidx, whose):
        rows = pl.ds(pl.multiple_of(whose * R + k * rc, rc), rc)
        return pltpu.make_async_remote_copy(
            src_ref=fulls[a].at[rows, :] if src is None else src,
            dst_ref=fulls[a].at[rows, :],
            send_sem=send.at[a, sidx, k],
            recv_sem=recv.at[a, rel, k],
            device_id={"mp": target},
            device_id_type=MESH,
        )

    def push(*args):
        c = copy(*args)
        c.start()
        sent.append(c)

    def arrive(a, k, rel):
        copy(None, a, k, partner, rel, 0, owner(rel, core, bx, by)).wait_recv()

    kept = []
    for a in range(n):
        for k in range(C):
            own = xs[a].at[pl.ds(k * rc, rc), :]
            push(own, a, k, xn, 2, 1, me)
            push(own, a, k, yn, 4, 2, me)
            push(own, a, k, partner, 1, 0, me)
        c = pltpu.make_async_copy(
            xs[a], fulls[a].at[pl.ds(pl.multiple_of(me * R, R), R), :], loc.at[a]
        )
        c.start()
        kept.append(c)
    z.start()
    across = jnp.where(core == 0, xn, yn)
    x_core = owner(2, core, bx, by)
    y_core = owner(4, core, bx, by)
    through = jnp.where(core == 0, y_core, x_core)
    steps = [(a, k) for a in range(n) for k in range(C)]
    for i in range(len(steps) + 1):
        if i < len(steps):
            a, k = steps[i]
            arrive(a, k, 2)
            arrive(a, k, 4)
            push(None, a, k, across, 6, 3, through)
            push(None, a, k, partner, 3, 4, x_core)
            push(None, a, k, partner, 5, 5, y_core)
        if i >= 1:
            a, k = steps[i - 1]
            arrive(a, k, 6)
            push(None, a, k, partner, 7, 6, owner(6, core, bx, by))
        z.tick(-(-len(zc.plan) // (len(steps) + 1)))
    for a, k in steps:
        for rel in (1, 3, 5, 7):
            arrive(a, k, rel)
    z.finish()
    for c in sent:
        c.wait_send()
    for c in kept:
        c.wait()


def gather_only(cid, xs, after=(), z=NO_Z, C=4):
    R, D = xs[0].shape
    n = len(xs)
    anywhere = pl.BlockSpec(memory_space=pl.ANY)
    out = pl.pallas_call(
        functools.partial(gather_only_kernel, C, n, len(after), z),
        out_shape=tuple(jax.ShapeDtypeStruct((8 * R, D), x.dtype) for x in xs) + tuple(z.out_shapes),
        in_specs=[anywhere] * (n + len(after)) + z.in_specs(),
        out_specs=(anywhere,) * n + z.out_specs(),
        scratch_shapes=[
            pltpu.SemaphoreType.DMA((n, 7, C)),
            pltpu.SemaphoreType.DMA((n, 8, C)),
            pltpu.SemaphoreType.DMA((n,)),
            *z.scratch,
        ],
        compiler_params=pltpu.CompilerParams(collective_id=cid, has_side_effects=True),
        input_output_aliases=z.aliases(n + len(after), n),
        cost_estimate=cost(1 << 20),
        name="gather_rows",
    )(*xs, *after, *z.arrays)
    z.done(out[n:])
    return out[:n]


def tiles(n, step, f):
    step = min(step, n)

    @pl.loop(0, n // step)
    def _(j):
        f(pl.ds(pl.multiple_of(j * step, step), step))


def put(ref, pieces, cols, value):
    at = 0
    for rows in pieces:
        ref[rows, cols] = value[at : at + rows.size]
        at += rows.size


def take(ref, pieces, cols):
    parts = [ref[rows, cols] for rows in pieces]
    return parts[0] if len(parts) == 1 else jnp.concatenate(parts, axis=0)


def project_body(first, lhs, pieces, ins, outs):
    w, shift = ins

    def f(cols):
        put(outs[0], pieces, cols, (nn(lhs(), w[:, cols]) + shift[:, cols]).astype(jnp.bfloat16))

    tiles(w.shape[1], 256, f)


def gelu_both(v):
    t = jnp.tanh(0.7978845608028654 * (v + 0.044715 * v * v * v))
    d = 0.5 * (1.0 + t) + 0.5 * v * (1.0 - t * t) * (
        0.7978845608028654 * (1.0 + 3 * 0.044715 * v * v)
    )
    return (0.5 * v * (1.0 + t)).astype(jnp.bfloat16), d.astype(jnp.bfloat16)


def up_body(first, lhs, pieces, ins, outs):
    w, shift = ins

    def f(cols):
        active, slope = gelu_both(nn(lhs(), w[:, cols]) + shift[:, cols])
        put(outs[0], pieces, cols, active)
        put(outs[1], pieces, cols, slope)

    tiles(w.shape[1], 256, f)


def wide_nt(src, w, cols):
    Z, _, d = w.shape
    total = None
    for z in range(Z):
        t = nt(src[:, z * d : (z + 1) * d], w[z, cols, :])
        total = t if total is None else total + t
    return total


def down_back_body(first, lhs, pieces, ins, outs):
    w, slope = ins

    def f(cols):
        g = wide_nt(lhs(), w, cols) * take(slope, pieces, cols).astype(jnp.float32)
        g = g.astype(jnp.bfloat16)
        put(outs[0], pieces, cols, g)
        sums = jnp.sum(g.astype(jnp.float32), axis=0, keepdims=True)
        if first:
            outs[1][:, cols] = sums
        else:
            outs[1][:, cols] += sums

    tiles(w.shape[1], 256, f)


def dense_back_body(first, lhs, pieces, ins, outs):
    (w,) = ins

    def f(cols):
        put(outs[0], pieces, cols, wide_nt(lhs(), w, cols).astype(jnp.bfloat16))

    tiles(w.shape[1], 256, f)


def scatter_kernel(C, n_in, n_more, n_more_out, body, filler, zc, n_scratch, late_n, *refs):
    zi, zo, zs = zc.counts()
    ins, more, z_in, (out_ref,), more_out, z_out, own_scratch, scratch, z_scratch = split_refs(
        refs, n_in, n_more, zi, 1, n_more_out, zo, 4, n_scratch, zs
    )
    pbuf, rbuf, send, recv = own_scratch
    z = zc.make(z_in + z_out + z_scratch)
    z.ahead = max(z.ahead, 6)
    R, D = out_ref.shape
    rc = R // C
    me, core, bx, by, partner, xn, yn = peers()
    steps, late = [], NoZ()
    if late_n:
        scratch, late_out, late_scratch = scratch[:-5], more_out[-1:], scratch[-5:]
        more_out = more_out[:-1]
        plan = [(0, ZR * c) for c in range(late_n)]
        late = ZSum(plan, more_out[:1], late_out, late_scratch)
        steps = filler(ins, more, more_out, scratch, late)
    elif filler:
        steps = filler(ins, more, more_out, scratch)
    enter(partner, xn, yn, bool(zc.plan or late_n))
    z.start()
    dn = jnp.where(core == 0, yn, xn)
    fn = jnp.where(core == 0, xn, yn)
    sent = []

    def fill(n):
        for _ in range(min(n, len(steps))):
            steps.pop(0)()

    def copy(src, slot, k, target):
        rows = pl.ds(k * rc, rc)
        return pltpu.make_async_remote_copy(
            src_ref=src.at[rows, :],
            dst_ref=rbuf.at[slot, rows, :],
            send_sem=send.at[slot, k],
            recv_sem=recv.at[slot, k],
            device_id={"mp": target},
            device_id_type=MESH,
        )

    def push(slot, to, target, k):
        c = copy(pbuf.at[slot], to, k, target)
        c.start()
        sent.append(c)

    def arrive(slot, k):
        copy(pbuf.at[0], slot, k, partner).wait_recv()

    def dest_rank(which, c):
        if which == 0:
            return (1 - by) * 4 + (1 - bx) * 2 + c
        if which == 3:
            return by * 4 + bx * 2 + c
        flip_y = (1 - c) if which == 1 else c
        y = by + flip_y * (1 - 2 * by)
        x = bx + (1 - flip_y) * (1 - 2 * bx)
        return y * 4 + x * 2 + c

    def compute(which, c, slot):
        rows = pl.ds(pl.multiple_of(dest_rank(which, c) * R, R), R)
        body(rows, ins, pbuf.at[slot])

    def theirs(which):
        compute(which, 1 - core, which)
        for k in range(C):
            push(which, which, partner, k)

    def add(slot, rslot, k):
        @pl.loop(0, rc // 16)
        def _(i):
            rows = pl.ds(pl.multiple_of(k * rc + i * 16, 16), 16)
            pbuf[slot, rows, :] = (
                pbuf[slot, rows, :].astype(jnp.float32) + rbuf[rslot, rows, :].astype(jnp.float32)
            ).astype(pbuf.dtype)

    def join(which):
        for k in range(C):
            arrive(which, k)
            add(4 + which, which, k)
            if which < 2:
                push(4 + which, 4 + which, dn, k)

    theirs(0)
    compute(0, core, 4)
    theirs(1)
    join(0)
    compute(1, core, 5)
    theirs(2)
    join(1)
    compute(2, core, 6)
    theirs(3)
    join(2)
    compute(3, core, 7)
    join(3)
    z.tick(3)
    for k in range(C):
        arrive(4, k)
        add(6, 4, k)
        push(6, 6, fn, k)
        z.tick(2)
        fill(2)
    fill(len(steps))
    for k in range(C):
        arrive(5, k)
        arrive(6, k)

        @pl.loop(0, rc // 16)
        def _(i):
            rows = pl.ds(pl.multiple_of(k * rc + i * 16, 16), 16)
            out_ref[rows, :] = (
                pbuf[7, rows, :].astype(jnp.float32)
                + rbuf[5, rows, :].astype(jnp.float32)
                + rbuf[6, rows, :].astype(jnp.float32)
            )
    z.finish()
    late.finish()
    for c in sent:
        c.wait_send()


def scatter_call(
    name, cid, T, D, ins, body, more=(), more_out=(), scratch=(), filler=None, z=NO_Z, late=0, C=4
):
    if late:
        w = more_out[0][0].shape[2]
        more_out = [*more_out, (jax.ShapeDtypeStruct((late * ZR, w), jnp.bfloat16), True)]
        scratch = [*scratch, *sum_scratch(late, w)]
    R = T // 8
    vmem = pl.BlockSpec(memory_space=pltpu.VMEM)
    anywhere = pl.BlockSpec(memory_space=pl.ANY)
    spec = lambda inside: vmem if inside else anywhere
    out = pl.pallas_call(
        functools.partial(
            scatter_kernel, C, len(ins), len(more), len(more_out), body, filler, z, len(scratch), late
        ),
        out_shape=(
            jax.ShapeDtypeStruct((R, D), jnp.float32),
            *(shape for shape, _ in more_out),
            *z.out_shapes,
        ),
        in_specs=[vmem] * len(ins) + [spec(i) for _, i in more] + z.in_specs(),
        out_specs=(vmem,) + tuple(spec(i) for _, i in more_out) + z.out_specs(),
        scratch_shapes=[
            pltpu.VMEM((8, R, D), jnp.bfloat16),
            pltpu.VMEM((7, R, D), jnp.bfloat16),
            pltpu.SemaphoreType.DMA((7, C)),
            pltpu.SemaphoreType.DMA((7, C)),
            *scratch,
            *z.scratch,
        ],
        compiler_params=pltpu.CompilerParams(
            collective_id=cid, has_side_effects=True, vmem_limit_bytes=60 << 20
        ),
        input_output_aliases=z.aliases(len(ins) + len(more), 1 + len(more_out)),
        cost_estimate=cost(1 << 20),
        name=name,
    )(*ins, *(x for x, _ in more), *z.arrays)
    z.done(out[1 + len(more_out) :])
    return out[: 1 + len(more_out)] if more_out else out[0]


def row_split_body(rows, ins, out):
    a, w = ins
    Z, _, d = w.shape
    for z in range(Z):
        out[:, z * d : (z + 1) * d] = nn(a[rows, :], w[z]).astype(out.dtype)


def up_back_body(rows, ins, out):
    a, w = ins

    def f(cols):
        out[:, cols] = nt(a[rows, :], w[cols, :]).astype(out.dtype)

    tiles(w.shape[0], 512, f)


def project_back_body(rows, ins, out):
    a, w = ins
    S, _, width = a.shape

    def f(cols):
        total = None
        for s in range(S):
            t = nt(a[s, rows, :], w[cols, s * width : (s + 1) * width])
            total = t if total is None else total + t
        out[:, cols] = total.astype(out.dtype)

    tiles(w.shape[0], 512, f)


class Stream:
    def __init__(self, chunks, buf, sems, stage, out_sems):
        self.chunks, self.buf, self.sems = chunks, buf, sems
        self.stage, self.out_sems = stage, out_sems
        self.turn, self.flying = 0, [[], []]

    def fetch(self, i):
        src, j = self.chunks[i]
        w = self.buf.shape[2]
        return pltpu.make_async_copy(
            src.at[:, pl.ds(j * w, w)], self.buf.at[i % 2], self.sems.at[i % 2]
        )

    def get(self, i):
        self.fetch(i).wait()
        if i + 1 < len(self.chunks):
            self.fetch(i + 1).start()
        return self.buf.at[i % 2]

    def result(self, make, targets):
        slot = self.turn % 2
        self.turn += 1
        for c in self.flying[slot]:
            c.wait()
        make(self.stage.at[slot])
        self.flying[slot] = []
        for n, (lo, width, dest) in enumerate(targets):
            c = pltpu.make_async_copy(
                self.stage.at[slot, :, pl.ds(lo, width)], dest, self.out_sems.at[slot, n]
            )
            c.start()
            self.flying[slot].append(c)

    def drain(self):
        for slot in range(2):
            for c in self.flying[slot]:
                c.wait()
            self.flying[slot] = []


STREAM_SCRATCH = (
    pltpu.VMEM((2, 2048, 256), jnp.bfloat16),
    pltpu.SemaphoreType.DMA((2,)),
    pltpu.VMEM((2, 256, 1024), jnp.bfloat16),
    pltpu.SemaphoreType.DMA((2, 4)),
    pltpu.VMEM((256, 2048), jnp.bfloat16),
)


def tile_product(turned, right, lo, half):
    def make(tile):
        def f(cols):
            at = pl.ds(pl.multiple_of(lo + cols.start, 256), cols.size)
            tile[:, cols] = nn(turned[...], right[:, at]).astype(tile.dtype)

        tiles(half, 256, f)

    return make


def down_steps(stream, out, turned, held, held_copy, chunk, n, w):
    half = stream.stage.shape[2]
    D = held.shape[1]
    d = out.shape[2]
    steps = []

    def step(j, h):
        if h == 0:
            turned[...] = chunk(j).T
        if j == 0 and h == 0 and held_copy is not None:
            held_copy.wait()
        targets = [
            (b * d, d, out.at[h * (half // d) + b, pl.ds(j * w, w), :]) for b in range(half // d)
        ]
        stream.result(tile_product(turned, held, h * half, half), targets)

    for j in range(n):
        for h in range(D // half):
            steps.append(functools.partial(step, j, h))
    return steps


def up_steps(stream, out, turned, hidden, first, D, w):
    F = hidden.shape[1]
    d = out.shape[2]

    def step(j):
        turned[...] = stream.get(first + j)[...].T
        z, r = (j * w) // d, (j * w) % d
        targets = [(b * d, d, out.at[z, pl.ds(b * d + r, w), :]) for b in range(F // d)]
        stream.result(tile_product(turned, hidden, 0, F), targets)

    return [functools.partial(step, j) for j in range(D // w)]


def down_filler(ins, more, more_out, scratch, late):
    active, grad = more
    (down_out,) = more_out
    buf, sems, stage, out_sems, turned, held, held_sem = scratch
    T, F = active.shape
    D = grad.shape[1]
    w = buf.shape[2]
    n = F // w
    stream = Stream([(active, j) for j in range(n)], buf, sems, stage, out_sems)
    held_copy = pltpu.make_async_copy(grad, held, held_sem)
    stream.fetch(0).start()
    held_copy.start()
    steps = down_steps(
        stream, down_out, turned, held, held_copy, lambda j: stream.get(j)[...], n, w
    )

    def early():
        stream.drain()
        late.start()

    first = len(late.plan) * ZR // w * (D // stage.shape[2])
    steps.insert(first, early)
    for i in range(len(late.plan)):
        steps.insert(first + 2 + 2 * i, late.tick)
    return steps + [stream.drain]


def up_filler(ins, more, more_out, scratch):
    hidden, normed = more
    buf, sems, stage, out_sems, turned = scratch
    D = normed.shape[1]
    w = buf.shape[2]
    stream = Stream([(normed, j) for j in range(D // w)], buf, sems, stage, out_sems)
    stream.fetch(0).start()
    return up_steps(stream, more_out[0], turned, hidden, 0, D, w) + [stream.drain]


def last_filler(ins, more, more_out, scratch):
    active, w_down = ins
    slope, grad = more
    hidden_out, sum_out, down_out = more_out
    stage, out_sems, turned, held, held_sem = scratch
    T, F = active.shape
    w = turned.shape[0]
    stream = Stream([], None, None, stage, out_sems)
    held_copy = pltpu.make_async_copy(grad, held, held_sem)
    held_copy.start()

    def back(i):
        if i == 0:
            held_copy.wait()
        rows = pl.ds(i * BLOCK, BLOCK)
        down_back_body(
            i == 0, lambda: held[rows, :], [rows], (w_down, slope), (hidden_out, sum_out)
        )

    steps = [functools.partial(back, i) for i in range(T // BLOCK)]
    steps += down_steps(
        stream, down_out, turned, held, None, lambda j: active[:, j * w : (j + 1) * w], F // w, w
    )
    return steps + [stream.drain]


def attn_filler(ins, more, more_out, scratch):
    parts = ins[0]
    context, grad, normed = more
    (out,) = more_out
    buf, sems, stage, out_sems, turned, ctx_t = scratch
    S, T, width = parts.shape
    D = grad.shape[1]
    Z = out.shape[0]
    d = D // Z
    w = buf.shape[2]
    n = D // w
    stream = Stream(
        [(context, 0)] + [(grad, j) for j in range(n)] + [(normed, j) for j in range(n)],
        buf,
        sems,
        stage,
        out_sems,
    )
    stream.fetch(0).start()
    steps = []

    def dense(j):
        def step():
            if j == 0:
                ctx_t[...] = stream.get(0)[...].T
            right = stream.get(1 + j)

            def make(tile):
                tile[:, :w] = nn(ctx_t[...], right[...]).astype(tile.dtype)

            z, r = (j * w) // d, (j * w) % d
            stream.result(make, [(0, w, out.at[z, pl.ds(0, width), pl.ds(r, w)])])

        return step

    def project(j):
        def step():
            turned[...] = stream.get(1 + n + j)[...].T

            def make(tile):
                for s in range(S):
                    tile[:, s * width : (s + 1) * width] = nn(turned[...], parts[s]).astype(
                        tile.dtype
                    )

            z, r = (j * w) // d, (j * w) % d
            side = pl.ds(r // w * width, width)
            stream.result(
                make,
                [(s * width, width, out.at[z, pl.ds(width + s * w, w), side]) for s in range(S)],
            )

        return step

    for j in range(n):
        steps.append(dense(j))
    for j in range(n):
        steps.append(project(j))
    steps.append(stream.drain)
    return steps


def finish_kernel(zc, *refs):
    zi, zo, zs = zc.counts()
    (v_ref, u_ref), z_in, (v_out, u_out), z_out, own_scratch, z_scratch = split_refs(
        refs, 2, zi, 2, zo, 6, zs
    )
    vs, us, v_in, u_in, send, recv = own_scratch
    me, core, bx, by, partner, xn, yn = peers()
    z = zc.make(z_in + z_out + z_scratch)
    _, z1, z2, _ = z_peers()
    enter(partner, xn, yn, True)
    z.start()
    hops = (({"mp": partner}, False), ({"mp": xn}, False), ({"mp": yn}, False))
    hops += (({"dp": z1}, True), ({"dp": z2}, True))
    vs[0] = v_ref[...]
    us[3] = u_ref[...]
    for i, (target, both) in enumerate(hops):
        copies = []
        for n, (src, dst) in enumerate(((vs, v_in), (us, u_in))[: 2 if both else 1]):
            c = pltpu.make_async_remote_copy(
                src_ref=src.at[i],
                dst_ref=dst.at[i],
                send_sem=send.at[n, i],
                recv_sem=recv.at[n, i],
                device_id=target,
                device_id_type=MESH,
            )
            c.start()
            copies.append(c)
        z.tick(2)
        for c in copies:
            c.wait()
        vs[i + 1] = vs[i] + v_in[i]
        if both:
            us[i + 1] = us[i] + u_in[i]
    v_out[...] = vs[5]
    u_out[...] = us[5]
    z.finish()


def finish_call(cid, v, u, z):
    vmem = pl.BlockSpec(memory_space=pltpu.VMEM)
    out = pl.pallas_call(
        functools.partial(finish_kernel, z),
        out_shape=(
            jax.ShapeDtypeStruct(v.shape, v.dtype),
            jax.ShapeDtypeStruct(u.shape, u.dtype),
            *z.out_shapes,
        ),
        in_specs=[vmem, vmem] + z.in_specs(),
        out_specs=(vmem, vmem) + z.out_specs(),
        scratch_shapes=[
            pltpu.VMEM((6, *v.shape), v.dtype),
            pltpu.VMEM((6, *u.shape), u.dtype),
            pltpu.VMEM((5, *v.shape), v.dtype),
            pltpu.VMEM((5, *u.shape), u.dtype),
            pltpu.SemaphoreType.DMA((2, 5)),
            pltpu.SemaphoreType.DMA((2, 5)),
            *z.scratch,
        ],
        compiler_params=pltpu.CompilerParams(
            collective_id=cid, has_side_effects=True, vmem_limit_bytes=60 << 20
        ),
        cost_estimate=cost(1 << 20),
        name="finish",
    )(v, u, *z.arrays)
    z.done(out[2:])
    return out[0], out[1]


def place_kernel(moves, n_src, *refs):
    srcs, outs, (low, wide, in_sem, out_sem) = split_refs(refs, n_src, 4, 4)
    depth = low.shape[0]

    def fetch(i):
        s, row, _ = moves[i]
        return pltpu.make_async_copy(
            srcs[s].at[pl.ds(row, ZR), :], low.at[i % depth], in_sem.at[i % depth]
        )

    def store(i):
        _, _, targets = moves[i]
        copies = []
        for n, (o, index, lo, width) in enumerate(targets):
            copies.append(
                pltpu.make_async_copy(
                    wide.at[i % depth, :, pl.ds(lo, width)],
                    outs[o].at[index],
                    out_sem.at[i % depth, n],
                )
            )
        return copies

    for i in range(min(depth, len(moves))):
        fetch(i).start()
    for i in range(len(moves)):
        fetch(i).wait()
        if i >= depth:
            for c in store(i - depth):
                c.wait()
        wide[i % depth] = low[i % depth].astype(jnp.float32)
        for c in store(i):
            c.start()
        if i + depth < len(moves):
            fetch(i + depth).start()
    for i in range(max(0, len(moves) - depth), len(moves)):
        for c in store(i):
            c.wait()


def place_call(sums, out_shapes, targets_of):
    arrays, moves = [], []
    for key, row, array, at in sums:
        if not any(a is array for a in arrays):
            arrays.append(array)
        i = [a is array for a in arrays].index(True)
        moves.append((i, at, targets_of(key, row)))
    w = arrays[0].shape[1]
    depth = 6
    anywhere = pl.BlockSpec(memory_space=pl.ANY)
    return pl.pallas_call(
        functools.partial(place_kernel, moves, len(arrays)),
        out_shape=tuple(out_shapes),
        in_specs=[anywhere] * len(arrays),
        out_specs=(anywhere,) * len(out_shapes),
        scratch_shapes=[
            pltpu.VMEM((depth, ZR, w), jnp.bfloat16),
            pltpu.VMEM((depth, ZR, w), jnp.float32),
            pltpu.SemaphoreType.DMA((depth,)),
            pltpu.SemaphoreType.DMA((depth, 2)),
        ],
        compiler_params=pltpu.CompilerParams(vmem_limit_bytes=40 << 20),
        cost_estimate=cost(1 << 20),
        name="place",
    )(*arrays)


def first_kernel(C, zc, n_project, *refs):
    zi, zo, zs = zc.counts()
    ins, z_in, outs, z_out, scratch, z_scratch = split_refs(refs, 6, zi, 6, zo, 13, zs)
    x_ref, gain_ref, bias_ref, shift_ref, up_ref, down_ref = ins
    full_ref, project_ref, up_out, down_out = *outs[:2], outs[2:4], outs[4:6]
    x_low, w_here, w_sem, wide, low, wide_sem, low_sem, *mine = scratch
    buf, send, recv, loc, wide2, low2 = mine
    R, D = x_ref.shape
    rc = R // C
    me, core, bx, by, partner, xn, yn = peers()
    z = zc.make(z_in + z_out + z_scratch)

    pieces = []
    both = ((up_ref, up_out, wide, low, 0), (down_ref, down_out, wide2, low2, 1))
    for l in range(2):
        for ref, out, w, n, stage in both:
            size = w.shape[1]
            pieces += [
                (ref.at[l, pl.ds(r, size), :], out[l].at[pl.ds(r, size), :], w, n, stage)
                for r in range(0, ref.shape[1], size)
            ]

    def read(i):
        src, _, w, _, stage = pieces[i]
        return pltpu.make_async_copy(src, w.at[i % 2], wide_sem.at[stage, i % 2])

    def write(i):
        _, dst, _, n, stage = pieces[i]
        return pltpu.make_async_copy(n.at[i % 2], dst, low_sem.at[stage, i % 2])

    def cast(i):
        _, _, w, n, _ = pieces[i]
        read(i).wait()
        if i >= 2:
            write(i - 2).wait()
        n[i % 2] = w[i % 2].astype(n.dtype)
        write(i).start()
        if i + 2 < len(pieces):
            read(i + 2).start()

    for i in range(2):
        read(i).start()
    enter(partner, xn, yn, True)
    z.start()

    @pl.loop(0, R // 16)
    def _(i):
        rows = pl.ds(pl.multiple_of(i * 16, 16), 16)
        v = x_ref[rows, :].astype(jnp.float32)
        x_low[rows, :] = layer_norm(v, gain_ref[...], bias_ref[...]).astype(x_low.dtype)

    sent = []

    def copy(src, rel, k, target, sidx):
        return pltpu.make_async_remote_copy(
            src_ref=src,
            dst_ref=buf.at[k, rel],
            send_sem=send.at[sidx, k],
            recv_sem=recv.at[rel, k],
            device_id={"mp": target},
            device_id_type=MESH,
        )

    def push(src, rel, k, target, sidx):
        c = copy(src, rel, k, target, sidx)
        c.start()
        sent.append(c)

    def arrive(rel, k):
        copy(buf.at[k, 0], rel, k, partner, 0).wait_recv()

    for k in range(C):
        own = x_low.at[pl.ds(k * rc, rc), :]
        push(own, 2, k, xn, 1)
        push(own, 4, k, yn, 2)
        push(own, 1, k, partner, 0)
    kept = [
        pltpu.make_async_copy(
            x_low, full_ref.at[pl.ds(pl.multiple_of(me * R, R), R), :], loc.at[0, 0]
        )
    ]
    kept[0].start()
    starts = [pl.multiple_of(owner(rel, core, bx, by) * R, R) for rel in range(8)]
    across = jnp.where(core == 0, xn, yn)
    z.tick()
    for k in range(C + 1):
        if k < C:
            arrive(2, k)
            arrive(4, k)
            push(buf.at[k, 4 - 2 * core], 6, k, across, 3)
            push(buf.at[k, 2], 3, k, partner, 4)
            push(buf.at[k, 4], 5, k, partner, 5)
        if k >= 1:
            arrive(6, k - 1)
            push(buf.at[k - 1, 6], 7, k - 1, partner, 6)
        z.tick()
        for i in range(2 * k, min(2 * k + 2, len(pieces))):
            cast(i)
        z.tick()
    for k in range(C):
        for rel in range(1, 8):
            if rel in (1, 3, 5, 7):
                arrive(rel, k)
            start = pl.multiple_of(starts[rel] + k * rc, rc)
            c = pltpu.make_async_copy(
                buf.at[k, rel], full_ref.at[pl.ds(start, rc), :], loc.at[k, rel]
            )
            c.start()
            kept.append(c)
    for i in range(2 * C + 2, len(pieces)):
        cast(i)
    for i in range(len(pieces) - 2, len(pieces)):
        write(i).wait()
    z.settle(n_project)
    weights = pltpu.make_async_copy(z_out[0], w_here, w_sem)
    weights.start()
    weights.wait()
    for rel in range(8):
        rows = pl.ds(starts[rel], R)

        def f(cols, rel=rel, rows=rows):
            lhs = x_low[...] if rel == 0 else buf[:, rel].reshape(R, D)
            w = w_here[:, :, cols].reshape(D, cols.size)
            project_ref[rows, cols] = (nn(lhs, w) + shift_ref[:, cols]).astype(jnp.bfloat16)

        tiles(project_ref.shape[1], 256, f)
        z.tick()
    z.finish()
    for c in sent:
        c.wait_send()
    for c in kept:
        c.wait()


def first_call(cid, x, gain, bias, shift, up, down, z, n_project, C=4):
    R, D = x.shape
    N = shift.shape[0]
    w = z.arrays[0]
    vmem = pl.BlockSpec(memory_space=pltpu.VMEM)
    anywhere = pl.BlockSpec(memory_space=pl.ANY)
    low = jnp.bfloat16
    out = pl.pallas_call(
        functools.partial(first_kernel, C, z, n_project),
        out_shape=(
            jax.ShapeDtypeStruct((8 * R, D), low),
            jax.ShapeDtypeStruct((8 * R, N), low),
            *[jax.ShapeDtypeStruct(up.shape[1:], low)] * 2,
            *[jax.ShapeDtypeStruct(down.shape[1:], low)] * 2,
            *z.out_shapes,
        ),
        in_specs=[vmem] * 4 + [anywhere] * 2 + z.in_specs(),
        out_specs=(anywhere, vmem) + (anywhere,) * 4 + z.out_specs(),
        scratch_shapes=[
            pltpu.VMEM((R, D), low),
            pltpu.VMEM((4, *w.shape[1:]), low),
            pltpu.SemaphoreType.DMA,
            pltpu.VMEM((2, 256, up.shape[2]), jnp.float32),
            pltpu.VMEM((2, 256, up.shape[2]), low),
            pltpu.SemaphoreType.DMA((2, 2)),
            pltpu.SemaphoreType.DMA((2, 2)),
            pltpu.VMEM((C, 8, R // C, D), low),
            pltpu.SemaphoreType.DMA((7, C)),
            pltpu.SemaphoreType.DMA((8, C)),
            pltpu.SemaphoreType.DMA((C, 8)),
            pltpu.VMEM((2, 512, down.shape[2]), jnp.float32),
            pltpu.VMEM((2, 512, down.shape[2]), low),
            *z.scratch,
        ],
        compiler_params=pltpu.CompilerParams(
            collective_id=cid, has_side_effects=True, vmem_limit_bytes=60 << 20
        ),
        cost_estimate=cost(1 << 20),
        name="first",
    )(x, gain[None], bias[None], shift[None], up, down, *z.arrays)
    z.done(out[6:])
    return out[:6]


def gather_sum(part):
    return lax.psum_scatter(
        part.astype(jnp.bfloat16), "mp", scatter_dimension=0, tiled=True
    ).astype(jnp.float32)


def gather_all(x):
    return lax.all_gather(x, "mp", axis=0, tiled=True)


def side_by_side(w):
    return jnp.concatenate([w[z] for z in range(w.shape[0])], axis=1)


def reduce_dp(part):
    return lax.psum_scatter(part.astype(jnp.bfloat16), "dp", scatter_dimension=0)


class Fast:
    def __init__(self, T, D):
        self.T, self.D = T, D
        self.backlog = Backlog()
        self.grads = None

    def start(self, x, gain, bias, shift, out_grad, weights):
        project, dense, up, down = weights
        low = jnp.bfloat16
        project = project.reshape(*project.shape[:2], -1).astype(low)
        dense = dense.astype(low)
        self.weights = queue = GatherQueue()
        queue.add(("project", 0), project, 0, 64)
        n_project = project.shape[1] // 64
        rows, out, up0, up1, down0, down1 = first_call(
            0, x, gain, bias, shift, up, down, queue.take(n_project), n_project
        )
        self.first = rows, out
        for key, shard in (
            (("up", 0), up0),
            (("down", 0), down0),
            (("project", 1), project[1]),
            (("up", 1), up1),
        ):
            queue.arrays[key] = lax.all_gather(shard, "dp", axis=0)
        queue.add(("dense", 0), dense, 0, 128)
        (self.grad_rows,) = gather_only(8, (out_grad,), z=queue.take(2))
        queue.add(("dense", 1), dense, 1, 128)
        queue.add(("down", 1), down1[None], 0, 128)

    def weight(self, name, l):
        w = self.weights.arrays[name, l]
        return w.reshape(-1, w.shape[2]) if name in ("project", "up") else w

    def project(self, l, normed, shift):
        if l == 0:
            return self.first
        w = self.weight("project", l)
        out = jax.ShapeDtypeStruct((self.T, w.shape[1]), jnp.bfloat16)
        return gather_call(
            "gather_project",
            10 * l,
            normed,
            (w, shift[None]),
            (out,),
            project_body,
            self.weights.take(2),
        )

    def attend(self, l, project, slopes):
        return attend_fwd(20 + l, project, slopes, NO_Z)

    def dense(self, l, context):
        return scatter_call(
            "dense_scatter",
            10 * l + 1,
            self.T,
            self.D,
            (context, self.weight("dense", l)),
            row_split_body,
            z=self.weights.take(3 * l),
        )

    def up(self, l, normed, shift):
        w = self.weight("up", l)
        out = jax.ShapeDtypeStruct((self.T, w.shape[1]), jnp.bfloat16)
        return gather_call(
            "gather_up",
            10 * l + 2,
            normed,
            (w, shift[None]),
            (out, out),
            up_body,
            self.weights.take(5 * l),
        )

    def down(self, l, active):
        return scatter_call(
            "down_scatter",
            10 * l + 3,
            self.T,
            self.D,
            (active, self.weight("down", l)),
            row_split_body,
            more=((self.grad_rows, False),),
        )

    def last_down(self, l, active, slope):
        T, F = active.shape
        Z = lax.axis_size("dp")
        grad = self.grad_rows
        rows, grad_hidden, sums, packed = scatter_call(
            "last_scatter",
            10 * l + 3,
            T,
            self.D,
            (active, self.weight("down", l)),
            row_split_body,
            more=((slope, True), (grad, False)),
            more_out=(
                (jax.ShapeDtypeStruct((T, F), jnp.bfloat16), True),
                (jax.ShapeDtypeStruct((1, F), jnp.float32), True),
                (jax.ShapeDtypeStruct((Z, F, self.D // Z), jnp.bfloat16), False),
            ),
            scratch=(*STREAM_SCRATCH[2:], pltpu.VMEM((T, self.D), jnp.bfloat16), pltpu.SemaphoreType.DMA),
            filler=last_filler,
        )
        self.backlog.add(("down", l), packed)
        return rows, grad, grad_hidden, sums

    def down_back(self, l, grad, slope):
        w = self.weight("down", l)
        F = slope.shape[1]
        outs = (
            jax.ShapeDtypeStruct((self.T, F), jnp.bfloat16),
            jax.ShapeDtypeStruct((1, F), jnp.float32),
        )
        z = self.backlog.take(5)
        return gather_call("gather_down_back", 10 * l + 4, grad, (w, slope), outs, down_back_body, z)

    def up_back(self, l, grad_hidden, active, normed, grad_down):
        T, F = grad_hidden.shape
        packed = jax.ShapeDtypeStruct((4, F, self.D // 4), jnp.bfloat16)
        self.for_up = grad_hidden, normed, packed
        args = (
            "up_back_scatter",
            10 * l + 5,
            T,
            self.D,
            (grad_hidden, self.weight("up", l)),
            up_back_body,
        )
        if l:
            return scatter_call(*args, z=self.backlog.take(5))
        out = scatter_call(
            *args,
            more=((active, False), (grad_down, False)),
            more_out=((packed, False),),
            scratch=STREAM_SCRATCH
            + (pltpu.VMEM((T, self.D), jnp.bfloat16), pltpu.SemaphoreType.DMA),
            filler=down_filler,
            z=self.backlog.take(4),
            late=2,
        )
        self.backlog.add(("down", l), out[1], out[2])
        return out[0]

    def dense_back(self, l, grad):
        w = self.weight("dense", l)
        out = jax.ShapeDtypeStruct((self.T, w.shape[1]), jnp.bfloat16)
        hidden, normed, packed = self.for_up
        full, out, up = gather_call(
            "gather_dense_back",
            10 * l + 6,
            grad,
            (w,),
            (out,),
            dense_back_body,
            self.backlog.take(4),
            more=((hidden, True), (normed, False)),
            more_out=((packed, False),),
            scratch=STREAM_SCRATCH,
            filler=up_filler,
        )
        self.backlog.add(("up", l), up)
        return full, out

    def attend_back(self, l, project, grad_context, context, log_norms, slopes):
        return attend_bwd(
            22 + l, project, grad_context, context, log_norms, slopes, self.backlog.take(2)
        )

    def project_back(self, l, grad_project, context, grad_branch, normed):
        S, T, width = grad_project.shape
        Z = lax.axis_size("dp")
        packed = jax.ShapeDtypeStruct((Z, (S + 1) * width, self.D // Z), jnp.bfloat16)
        grad, packed = scatter_call(
            "project_back_scatter",
            10 * l + 7,
            T,
            self.D,
            (grad_project, self.weight("project", l)),
            project_back_body,
            more=((context, False), (grad_branch, False), (normed, False)),
            more_out=((packed, False),),
            scratch=STREAM_SCRATCH + (pltpu.VMEM((width, T), jnp.bfloat16),),
            filler=attn_filler,
            z=self.backlog.take(5),
        )
        self.backlog.add(("attn", l), packed)
        return grad

    def matrix_grads(self, shapes):
        layers, d, parts, width = shapes[0]
        group = self.D // lax.axis_size("dp")

        def targets(key, row):
            kind, l = key
            if kind == "down":
                return [(3, (l, pl.ds(row, ZR)), 0, group)]
            if kind == "up":
                b, r = divmod(row, group)
                return [(2, (l, pl.ds(r, ZR), pl.ds(b * group, group)), 0, group)]
            if row < width:
                return [(1, (l, pl.ds(row, ZR)), 0, group)]
            s, r = divmod(row - width, width)
            return [(0, (l, s, pl.ds(h * width + r, ZR)), h * width, width) for h in range(2)]

        shapes = [(layers, parts, d, width), *shapes[1:]]
        out = place_call(
            self.backlog.sums, [jax.ShapeDtypeStruct(x, jnp.float32) for x in shapes], targets
        )
        return (out[0].transpose(0, 2, 1, 3), *out[1:])

    def finish(self, copied, split):
        rows = copied.shape[0] * copied.shape[1]
        v = jnp.concatenate([copied.reshape(rows, -1), jnp.zeros((-rows % 8, self.D), jnp.float32)])
        v, u = finish_call(9, v, split.reshape(8, -1), self.backlog.take(1000))
        return v[:rows].reshape(copied.shape), u.reshape(split.shape)


class Plain:
    def __init__(self, T, D):
        self.T, self.D = T, D
        self.ffn, self.attn = {}, {}

    def start(self, x, gain, bias, shift, out_grad, weights):
        self.first = layer_norm(x.astype(jnp.float32), gain, bias).astype(jnp.bfloat16)
        self.out_grad = out_grad
        low = jnp.bfloat16
        gathered = []
        for l in range(weights[0].shape[0]):
            project, dense, up, down = (x[l].astype(low) for x in weights)
            project = project.reshape(project.shape[0], -1)
            gathered.append(
                (
                    lax.all_gather(project, "dp", axis=0, tiled=True),
                    lax.all_gather(dense, "dp", axis=0),
                    lax.all_gather(up, "dp", axis=0, tiled=True),
                    lax.all_gather(down, "dp", axis=0),
                )
            )
        self.weights = gathered

    def project(self, l, normed, shift):
        w = self.weights[l][0]
        full = gather_all(normed if l else self.first)
        return full, (nn(full, w) + shift).astype(jnp.bfloat16)

    def attend(self, l, project, slopes):
        return attend_fwd(0, project, slopes, NO_Z)

    def dense(self, l, context):
        return gather_sum(nn(context, side_by_side(self.weights[l][1])))

    def up(self, l, normed, shift):
        w = self.weights[l][2]
        full = gather_all(normed)
        return full, *gelu_both(nn(full, w) + shift)

    def down(self, l, active):
        return gather_sum(nn(active, side_by_side(self.weights[l][3])))

    def last_down(self, l, active, slope):
        return self.down(l, active), *self.down_back(l, self.out_grad, slope)

    def down_back(self, l, grad, slope):
        full = gather_all(grad)
        g = (nt(full, side_by_side(self.weights[l][3])) * slope.astype(jnp.float32)).astype(jnp.bfloat16)
        return full, g, jnp.sum(g.astype(jnp.float32), axis=0, keepdims=True)

    def up_back(self, l, grad_hidden, active, normed, grad_down):
        Z = lax.axis_size("dp")
        F = grad_hidden.shape[1]
        d = self.D // Z
        up = jnp.einsum("td,tf->df", normed, grad_hidden, preferred_element_type=jnp.float32)
        down = jnp.einsum(
            "tf,tzd->zfd", active, grad_down.reshape(-1, Z, d), preferred_element_type=jnp.float32
        )
        packed = jnp.concatenate([down, up.reshape(Z, d * F // d, d)], axis=1)
        self.ffn[l] = reduce_dp(packed).astype(jnp.float32)
        return gather_sum(nt(grad_hidden, self.weights[l][2]))

    def ffn_grads(self, l):
        summed = self.ffn[l]
        d = summed.shape[1]
        F = summed.shape[0] // 2
        return summed[F:].reshape(d, F), summed[:F]

    def dense_back(self, l, grad):
        full = gather_all(grad)
        return full, nt(full, side_by_side(self.weights[l][1])).astype(jnp.bfloat16)

    def attend_back(self, l, project, grad_context, context, log_norms, slopes):
        return attend_bwd(0, project, grad_context, context, log_norms, slopes, NO_Z)

    def project_back(self, l, grad_project, context, grad_branch, normed):
        w = self.weights[l][0]
        S, T, width = grad_project.shape
        Z = lax.axis_size("dp")
        d = self.D // Z
        dense = jnp.einsum(
            "ti,tzd->zid", context, grad_branch.reshape(T, Z, d), preferred_element_type=jnp.float32
        )
        project = jnp.einsum(
            "td,sti->dsi", normed, grad_project, preferred_element_type=jnp.float32
        )
        packed = jnp.concatenate(
            [dense.reshape(Z, -1), project.reshape(Z, -1)], axis=1
        ).reshape(Z, -1, width)
        part = sum(nt(grad_project[s], w[:, s * width : (s + 1) * width]) for s in range(S))
        self.attn[l] = reduce_dp(packed).astype(jnp.float32)
        return gather_sum(part)

    def attn_grads(self, l):
        d = self.D // lax.axis_size("dp")
        rows, width = self.attn[l].shape
        flat = self.attn[l].reshape(-1)
        return flat[width * d :].reshape(d, 3, width), flat[: width * d].reshape(width, d)

    def matrix_grads(self, shapes):
        grads = [(*self.attn_grads(l), *self.ffn_grads(l)) for l in range(shapes[0][0])]
        return tuple(jnp.stack(parts) for parts in zip(*grads))

    def finish(self, copied, split):
        return lax.psum(copied, ("dp", "mp")), lax.psum(split, "dp")


def shards(
    inputs,
    out_grad,
    project_weight,
    dense_weight,
    up_weight,
    down_weight,
    project_bias,
    up_bias,
    norm_gain,
    norm_bias,
    output_bias,
):
    tensor_size = lax.axis_size("mp")
    tensor_rank = lax.axis_index("mp")
    row_count, model_width = inputs.shape
    total_rows = row_count * tensor_size
    inner_width = project_weight.shape[3]
    heads_here = N_HEADS // tensor_size
    layer_count = project_weight.shape[0]
    slopes = 2.0 ** (
        -8.0
        * (tensor_rank * heads_here + lax.iota(jnp.int32, heads_here) + 1).astype(jnp.float32)
        / N_HEADS
    )
    low = jnp.bfloat16
    fast = tensor_size == 8 and lax.axis_size("dp") == 4 and row_count == 256
    ops = (Fast if fast else Plain)(total_rows, model_width)
    stream = inputs.astype(jnp.float32)
    none = jnp.zeros((inner_width,), jnp.float32)
    shifts = [
        jnp.concatenate([project_bias[l, 0], none, project_bias[l, 1]]) for l in range(layer_count)
    ]
    weights = (project_weight, dense_weight, up_weight, down_weight)
    ops.start(inputs, norm_gain[0, 0], norm_bias[0, 0], shifts[0], out_grad, weights)
    normed = None
    stored = []
    for l in range(layer_count):
        if l:
            normed = layer_norm(stream, norm_gain[l, 0], norm_bias[l, 0]).astype(low)
        normed_all, project = ops.project(l, normed, shifts[l])
        context, log_norms = ops.attend(l, project, slopes)
        middle = stream + ops.dense(l, context) + output_bias[l, 0]
        normed2 = layer_norm(middle, norm_gain[l, 1], norm_bias[l, 1]).astype(low)
        normed2_all, active, slope = ops.up(l, normed2, up_bias[l])
        stored.append(
            (stream, normed_all, project, log_norms, context, middle, normed2_all, active, slope)
        )
        if l < layer_count - 1:
            stream = middle + ops.down(l, active) + output_bias[l, 1]
    grad = out_grad.astype(jnp.float32)
    copied = [None] * layer_count
    split = [None] * layer_count
    for l in reversed(range(layer_count)):
        last = l == layer_count - 1
        stream_in, normed_all, project, log_norms, context, middle, normed2_all, active, slope = (
            stored[l]
        )
        down_bias_grad = jnp.sum(grad, axis=0)
        if last:
            rows_out, grad_down, grad_hidden, up_bias_part = ops.last_down(l, active, slope)
            outputs = (middle + rows_out + output_bias[l, 1]).astype(low)
        else:
            grad_down, grad_hidden, up_bias_part = ops.down_back(l, grad.astype(low), slope)
        grad_normed2 = ops.up_back(l, grad_hidden, active, normed2_all, grad_down)
        norm_back = jax.vjp(layer_norm, middle, norm_gain[l, 1], norm_bias[l, 1])[1]
        grad_from_norm, gain_second, shift_second = norm_back(grad_normed2)
        grad_middle = grad + grad_from_norm
        dense_bias_grad = jnp.sum(grad_middle, axis=0)
        grad_branch, grad_context = ops.dense_back(l, grad_middle.astype(low))
        grad_project, project_bias_part = ops.attend_back(
            l, project, grad_context, context, log_norms, slopes
        )
        grad_normed = ops.project_back(l, grad_project, context, grad_branch, normed_all)
        norm_back = jax.vjp(layer_norm, stream_in, norm_gain[l, 0], norm_bias[l, 0])[1]
        grad_from_norm, gain_first, shift_first = norm_back(grad_normed)
        grad = grad_middle + grad_from_norm
        copied[l] = jnp.stack(
            [gain_first, gain_second, shift_first, shift_second, dense_bias_grad, down_bias_grad]
        )
        split[l] = jnp.concatenate([project_bias_part.reshape(-1), up_bias_part.reshape(-1)])
    copied, split = ops.finish(jnp.stack(copied), jnp.stack(split))
    matrix_grads = ops.matrix_grads([x.shape for x in weights])
    return (
        outputs,
        grad,
        *matrix_grads,
        split[:, : 2 * inner_width].reshape(layer_count, 2, inner_width),
        split[:, 2 * inner_width :],
        copied[:, 0:2],
        copied[:, 2:4],
        copied[:, 4:6],
    )


def solution(mesh):
    rows = P(("dp", "mp"), None)
    specs = (P(None, "dp", None, "mp"), P(None, "mp", "dp"), P(None, "dp", "mp"), P(None, "mp", "dp"))
    biases = (P(None, None, "mp"), P(None, "mp"), P(), P(), P())
    return jax.shard_map(
        shards,
        mesh=mesh,
        in_specs=(rows, rows, *specs, *biases),
        out_specs=(rows, rows, *specs, *biases),
        check_vma=False,
    )
```

time: 1270 us -> 1170 us (0.921)
  waiting for transfers between devices: 92.5 us -> 20.4 us
  Pallas kernels: 1030 us -> 1060 us
  local copies, waits for them, and re-layouts: 50.8 us -> 29.4 us
  other arithmetic: 56.5 us -> 39.8 us
    all_gather x8 -> x4, waiting for transfers between devices: 90.6 us -> 19.4 us  [start(): queue.arrays[key] = lax.all_gather(shard, 'dp', axis=0)]
    pallas_call x13 -> x14, Pallas kernels: 615 us -> 634 us  [the longest x6 309 us: gather_call(): pl.pallas_call(functools.partial(gather_kernel, C, *counts, body, filler,...]
    another operation x15 -> x0, other arithmetic: 18.2 us -> none  [the longest x8 12.1 us: shards(): jnp.stack(parts)]
    slice x14 -> x5, local copies, waits for them, and re-layouts: 16.7 us -> 2.49 us  [the longest x2 1.21 us: start(): project[1]]
  transfers between devices with their start and end apart: 8 -> 4, of which waited for: 5 -> 2; matrix products, arithmetic and copies ran while one was open for 3% -> 1% of each run, Pallas kernels for 30% -> 28%
where the time goes in v3:
time: 1170 us; the launch traced here: 1160 us
  Pallas kernels  1060 us (91%)
  other arithmetic  39.8 us (3%)
  local copies, waits for them, and re-layouts  29.4 us (3%)
  waiting for transfers between devices  20.4 us (2%)
  between operations  14.6 us (1%)
    pallas_call x8, Pallas kernels, scatter_call(): pl.pallas_call(functools.partial(scatter_kernel, C, len(ins), len(more),...  423 us
    pallas_call x6, Pallas kernels, gather_call(): pl.pallas_call(functools.partial(gather_kernel, C, *counts, body, filler,...  309 us
    pallas_call x1, Pallas kernels, finish_call(): pl.pallas_call(functools.partial(finish_kernel, z), out_shape=(jax.ShapeD...  105 us
    pallas_call x4, Pallas kernels, attend_call(): pl.pallas_call(functools.partial(kernel, z), out_shape=(*outs, *z.out_sha...  85 us
    pallas_call x1, Pallas kernels, first_call(): pl.pallas_call(functools.partial(first_kernel, C, z, n_project), out_shap...  74.4 us
    pallas_call x1, Pallas kernels, gather_only(): pl.pallas_call(functools.partial(gather_only_kernel, C, n, len(after), z)...  50 us
  transfers between devices with their start and end apart: 4, of which 2 were waited for; matrix products, arithmetic and copies ran while one was open for 1% of the time, Pallas kernels for 28%

profile of v3, /device:TPU:0, one launch (start us, length us, event | category | flops | bytes accessed | tf_op | source)
XLA Modules:
  0.0 1161.4 jit_solution(4611483695658873855)
XLA Ops:
  7.2 0.8 fusion.33
  8.6 2.2 copy.27
  10.8 1.6 copy.28.refs_6_
  13.0 74.4 %first.1 = (bf16[2048,2048]{1,0:T(8,128)(2,1)}, bf16[2048,768]{1,0:T(8,128)(2,1)}, bf16[512,1024]{1,0:T(8,128)(2,1)}, bf16[512,1024]{1,0:T(8,128)(2,1)}, bf16[10...) custom-call(bf16[256,2048]{1,0:T(8,128)(2,1)} %refs_0_.2, ...), custom_call_target="tpu_custom_call" | custom-call | flops 1048576 | bytes 65536 | tf_op jit(solution)/shard_map/first/pallas_call | solution.py:1579
  87.5 0.7 all-gather.12.cloned.1.call-update
  88.3 1.2 copy.29
  90.7 0.9 convert_element_type.42.refs_1_.refs_3_
  91.5 50.0 %gather_rows.1 = (bf16[2048,2048]{1,0:T(8,128)(2,1)}, bf16[4,256,512]{2,1,0:T(8,128)(2,1)}) custom-call(bf16[256,2048]{1,0:T(8,128)(2,1)} %refs_0_.3, bf16[2,256,512]{2,1,0:T(8,128)(2,1)} %convert_element_type.42.refs_1_.refs_3_), custom_call_target="tpu_custom_call" | custom-call | flops 1048576 | bytes 65536 | tf_op jit(solution)/shard_map/gather_rows/pallas_call | solution.py:788
  142.1 15.1 %attend_fwd.2 = (bf16[2048,256]{1,0:T(8,128)(2,1)}, f32[2,8,256]{2,1,0:T(8,128)}) custom-call(f32[2]{0:T(128)} %multiply_power_fusion.slope_ref, bf16[2048,768]{1,0:T(8,128)(2,1)} %get-tuple-element.77.p_ref), custom_call_target="tpu_custom_call" | custom-call | flops 1048576 | bytes 65536 | tf_op jit(solution)/shard_map/attend_fwd/pallas_call | solution.py:513
  157.2 42.7 %dense_scatter.2 = f32[256,2048]{1,0:T(8,128)} custom-call(bf16[2048,256]{1,0:T(8,128)(2,1)} %get-tuple-element.78.refs_0_.c_ref.refs_2_, bf16[4,256,512]{2,1,0:T(8,128)(2,1)} %get-tuple-element.79.refs_1_), custom_call_target="tpu_custom_call" | custom-call | flops 1048576 | bytes 65536 | tf_op jit(solution)/shard_map/dense_scatter/pallas_call | solution.py:1022
  200.0 2.2 fusion.26
  203.4 1.4 add_convert_fusion.3.refs_0_
  204.9 48.8 %gather_up.2 = (bf16[2048,2048]{1,0:T(8,128)(2,1)}, bf16[2048,1024]{1,0:T(8,128)(2,1)}, bf16[2048,1024]{1,0:T(8,128)(2,1)}) custom-call(bf16[256,2048]{1,0:T(8,128)(2,1)} %add_convert_fusion.3.refs_0_, bf16[2048,1024]{1,0:T(8,128)(2,1)} %all-gather.10.cloned.1.call-done.refs_1_, f32[1,1024]{1,0:T(1,128)} %get-tuple-element.196.refs_2_), custom_call_target="tpu_custom_call" | custom-call | flops 1048576 | bytes 65536 | tf_op jit(solution)/shard_map/gather_up/pallas_call | solution.py:677
  253.6 7.2 all-gather.12.cloned.1.call-done
  260.8 47.3 %down_scatter.1 = f32[256,2048]{1,0:T(8,128)} custom-call(bf16[2048,1024]{1,0:T(8,128)(2,1)} %get-tuple-element.81.refs_0_.refs_2_, bf16[4,1024,512]{2,1,0:T(8,128)(2,1)} %bitcast.47, bf16[2048,2048]{1,0:T(8,128)(2,1)} %get-tuple-element.83.refs_2_.refs_3_), custom_call_target="tpu_custom_call" | custom-call | flops 1048576 | bytes 65536 | tf_op jit(solution)/shard_map/down_scatter/pallas_call | solution.py:1022
  308.1 1.9 fusion.25
  310.4 0.9 copy-done.11
  311.4 1.4 add_convert_fusion.2.refs_0_
  312.8 12.2 %all-gather.8.cloned.1.call-done = bf16[4,512,768]{2,1,0:T(8,128)(2,1)} async-done(((bf16[1,512,768]{2,1,0:T(8,128)(2,1)}), bf16[4,512,768]{2,1,0:T(8,128)(2,1)}) %all-gather.8.cloned.1.call-update) | async-done | bytes 3145744 | tf_op jit(solution)/shard_map/all_gather | solution.py:1658
  325.0 49.8 %gather_project.1 = (bf16[2048,2048]{1,0:T(8,128)(2,1)}, bf16[2048,768]{1,0:T(8,128)(2,1)}, bf16[4,256,512]{2,1,0:T(8,128)(2,1)}) custom-call(bf16[256,2048]{1,0:T(8,128)(2,1)} %add_convert_fusion.2.refs_0_, bf16[2048,768]{1,0:T(8,128)(2,1)} %bitcast.49, f32[1,768]{1,0:T(1,128)} %broadcast_in_dim.26.refs_2_, ...), custom_call_target="tpu_custom_call" | custom-call | flops 1048576 | bytes 65536 | tf_op jit(solution)/shard_map/gather_project/pallas_call | solution.py:677
  374.8 15.1 %attend_fwd.3 = (bf16[2048,256]{1,0:T(8,128)(2,1)}, f32[2,8,256]{2,1,0:T(8,128)}) custom-call(f32[2]{0:T(128)} %multiply_power_fusion.slope_ref, bf16[2048,768]{1,0:T(8,128)(2,1)} %get-tuple-element.84.p_ref), custom_call_target="tpu_custom_call" | custom-call | flops 1048576 | bytes 65536 | tf_op jit(solution)/shard_map/attend_fwd/pallas_call | solution.py:513
  389.8 51.7 %dense_scatter.3 = (f32[256,2048]{1,0:T(8,128)}, bf16[4,1024,512]{2,1,0:T(8,128)(2,1)}) custom-call(bf16[2048,256]{1,0:T(8,128)(2,1)} %get-tuple-element.85.refs_0_.c_ref.refs_2_, bf16[4,256,512]{2,1,0:T(8,128)(2,1)} %get-tuple-element.86.refs_1_, bf16[1,1024,512]{2,1,0:T(8,128)(2,1)} %bitcast.52), custom_call_target="tpu_custom_call" | custom-call | flops 1048576 | bytes 65536 | tf_op jit(solution)/shard_map/dense_scatter/pallas_call | solution.py:1022
  441.5 2.5 fusion.24
  444.5 0.9 copy-done.13
  445.4 1.4 add_convert_fusion.1.refs_0_
  446.8 52.8 %gather_up.3 = (bf16[2048,2048]{1,0:T(8,128)(2,1)}, bf16[2048,1024]{1,0:T(8,128)(2,1)}, bf16[2048,1024]{1,0:T(8,128)(2,1)}, bf16[4,1024,512]{2,1,0:T(8,128)(2,1)}) custom-call(bf16[256,2048]{1,0:T(8,128)(2,1)} %add_convert_fusion.1.refs_0_, bf16[2048,1024]{1,0:T(8,128)(2,1)} %all-gather.14.cloned.1.call-done.refs_1_, ...), custom_call_target="tpu_custom_call", output_to_operand_aliasing={{3}: (4, {})} | custom-call | flops 1048576 | bytes 65536 | tf_op jit(solution)/shard_map/gather_up/pallas_call | solution.py:677
  499.6 54.4 %last_scatter.1 = (f32[256,2048]{1,0:T(8,128)}, bf16[2048,1024]{1,0:T(8,128)(2,1)}, f32[1,1024]{1,0:T(1,128)}, bf16[4,1024,512]{2,1,0:T(8,128)(2,1)}) custom-call(bf16[2048,1024]{1,0:T(8,128)(2,1)} %get-tuple-element.91.refs_0_, bf16[4,1024,512]{2,1,0:T(8,128)(2,1)} %get-tuple-element.92.refs_1_, bf16[2048,1024]{1,0:T(8,128)(2,1)} %get-tuple-element.93.refs_2_, ...), custom_call_target="tpu_custom_call" | custom-call | flops 1048576 | bytes 65536 | tf_op jit(solution)/shard_map/last_scatter/pallas_call | solution.py:1022
  554.1 55.0 %up_back_scatter.2 = (f32[256,2048]{1,0:T(8,128)}, bf16[640,512]{1,0:T(8,128)(2,1)}) custom-call(bf16[2048,1024]{1,0:T(8,128)(2,1)} %get-tuple-element.95.refs_0_.refs_2_, bf16[2048,1024]{1,0:T(8,128)(2,1)} %all-gather.14.cloned.1.call-done.refs_1_, bf16[4,1024,512]{2,1,0:T(8,128)(2,1)} %get-tuple-element.96.refs_2_.refs_4_), custom_call_target="tpu_custom_call" | custom-call | flops 1048576 | bytes 65536 | tf_op jit(solution)/shard_map/up_back_scatter/pallas_call | solution.py:1022
  609.1 3.1 multiply_reduce_fusion
  612.6 3.4 fusion.23
  616.0 1.5 fusion.16.refs_0_
  617.6 51.2 %gather_dense_back.2 = (bf16[2048,2048]{1,0:T(8,128)(2,1)}, bf16[2048,256]{1,0:T(8,128)(2,1)}, bf16[4,1024,512]{2,1,0:T(8,128)(2,1)}, bf16[384,512]{1,0:T(8,128)(2,1)}) custom-call(bf16[256,2048]{1,0:T(8,128)(2,1)} %fusion.16.refs_0_, bf16[4,256,512]{2,1,0:T(8,128)(2,1)} %get-tuple-element.86.refs_1_, bf16[2048,1024]{1,0:T(8,128)(2,1)} %get-tuple-element.95.refs_0_.refs_2_, ...), custom_call_target="tpu_custom_call" | custom-call | flops 1048576 | bytes 65536 | tf_op jit(solution)/shard_map/gather_dense_back/pallas_call | solution.py:677
  668.8 27.6 %attend_bwd.2 = (bf16[3,2048,256]{2,1,0:T(8,128)(2,1)}, f32[2,256]{1,0:T(2,128)}, bf16[256,512]{1,0:T(8,128)(2,1)}) custom-call(f32[2]{0:T(128)} %multiply_power_fusion.slope_ref, bf16[2048,768]{1,0:T(8,128)(2,1)} %get-tuple-element.84.p_ref, bf16[2048,256]{1,0:T(8,128)(2,1)} %get-tuple-element.99.g_ref, ...), custom_call_target="tpu_custom_call" | custom-call | flops 1048576 | bytes 65536 | tf_op jit(solution)/shard_map/attend_bwd/pallas_call | solution.py:513
  696.4 0.7 copy.31
  697.1 52.7 %project_back_scatter.2 = (f32[256,2048]{1,0:T(8,128)}, bf16[4,1024,512]{2,1,0:T(8,128)(2,1)}, bf16[640,512]{1,0:T(8,128)(2,1)}) custom-call(bf16[3,2048,256]{2,1,0:T(8,128)(2,1)} %get-tuple-element.102.refs_0_, bf16[2048,768]{1,0:T(8,128)(2,1)} %bitcast.50, bf16[2048,256]{1,0:T(8,128)(2,1)} %get-tuple-element.85.refs_0_.c_ref.refs_2_, ...), custom_call_target="tpu_custom_call" | custom-call | flops 1048576 | bytes 65536 | tf_op jit(solution)/shard_map/project_back_scatter/pallas_call | solution.py:1022
  749.8 3.1 multiply_reduce_fusion.1
  753.9 0.9 copy-done.17
  755.2 0.8 convert_reduce_fusion.1
  756.0 1.3 copy-done.18
  757.3 1.1 convert_element_type.49.refs_0_
  758.4 54.9 %gather_down_back.1 = (bf16[2048,2048]{1,0:T(8,128)(2,1)}, bf16[2048,1024]{1,0:T(8,128)(2,1)}, f32[1,1024]{1,0:T(1,128)}, bf16[640,512]{1,0:T(8,128)(2,1)}) custom-call(bf16[256,2048]{1,0:T(8,128)(2,1)} %convert_element_type.49.refs_0_, bf16[4,1024,512]{2,1,0:T(8,128)(2,1)} %bitcast.48, bf16[2048,1024]{1,0:T(8,128)(2,1)} %get-tuple-element.106.refs_2_, ...), custom_call_target="tpu_custom_call" | custom-call | flops 1048576 | bytes 65536 | tf_op jit(solution)/shard_map/gather_down_back/pallas_call | solution.py:677
  813.3 66.9 %up_back_scatter.3 = (f32[256,2048]{1,0:T(8,128)}, bf16[4,1024,512]{2,1,0:T(8,128)(2,1)}, bf16[256,512]{1,0:T(8,128)(2,1)}, bf16[512,512]{1,0:T(8,128)(2,1)}) custom-call(bf16[2048,1024]{1,0:T(8,128)(2,1)} %get-tuple-element.108.refs_0_.refs_2_, bf16[2048,1024]{1,0:T(8,128)(2,1)} %all-gather.10.cloned.1.call-done.refs_1_, ...), custom_call_target="tpu_custom_call" | custom-call | flops 1048576 | bytes 65536 | tf_op jit(solution)/shard_map/up_back_scatter/pallas_call | solution.py:1022
  880.2 2.4 multiply_reduce_fusion.2
  883.4 0.9 copy-done.19
  884.6 1.3 copy-done.21
  885.9 1.1 convert_element_type.50.refs_0_
  887.0 51.1 %gather_dense_back.3 = (bf16[2048,2048]{1,0:T(8,128)(2,1)}, bf16[2048,256]{1,0:T(8,128)(2,1)}, bf16[4,1024,512]{2,1,0:T(8,128)(2,1)}, bf16[512,512]{1,0:T(8,128)(2,1)}) custom-call(bf16[256,2048]{1,0:T(8,128)(2,1)} %convert_element_type.50.refs_0_, bf16[4,256,512]{2,1,0:T(8,128)(2,1)} %get-tuple-element.79.refs_1_, ...), custom_call_target="tpu_custom_call" | custom-call | flops 1048576 | bytes 65536 | tf_op jit(solution)/shard_map/gather_dense_back/pallas_call | solution.py:677
  938.2 27.3 %attend_bwd.3 = (bf16[3,2048,256]{2,1,0:T(8,128)(2,1)}, f32[2,256]{1,0:T(2,128)}, bf16[256,512]{1,0:T(8,128)(2,1)}) custom-call(f32[2]{0:T(128)} %multiply_power_fusion.slope_ref, bf16[2048,768]{1,0:T(8,128)(2,1)} %get-tuple-element.77.p_ref, bf16[2048,256]{1,0:T(8,128)(2,1)} %get-tuple-element.113.g_ref, ...), custom_call_target="tpu_custom_call" | custom-call | flops 1048576 | bytes 65536 | tf_op jit(solution)/shard_map/attend_bwd/pallas_call | solution.py:513
  965.5 0.7 copy.30
  966.9 52.5 %project_back_scatter.3 = (f32[256,2048]{1,0:T(8,128)}, bf16[4,1024,512]{2,1,0:T(8,128)(2,1)}, bf16[640,512]{1,0:T(8,128)(2,1)}) custom-call(bf16[3,2048,256]{2,1,0:T(8,128)(2,1)} %get-tuple-element.115.refs_0_, bf16[2048,768]{1,0:T(8,128)(2,1)} %bitcast.54, bf16[2048,256]{1,0:T(8,128)(2,1)} %get-tuple-element.78.refs_0_.c_ref.refs_2_, ...), custom_call_target="tpu_custom_call" | custom-call | flops 1048576 | bytes 65536 | tf_op jit(solution)/shard_map/project_back_scatter/pallas_call | solution.py:1022
  1019.4 2.4 fusion.18
  1021.8 1.0 fusion.7
  1023.7 105.4 %finish.1 = (f32[16,2048]{1,0:T(8,128)}, f32[8,384]{1,0:T(8,128)}, bf16[1408,512]{1,0:T(8,128)(2,1)}) custom-call(f32[16,2048]{1,0:T(8,128)} %concatenate.17.refs_0_, f32[8,384]{1,0:T(8,128)} %reshape.231.refs_1_, bf16[4,1024,512]{2,1,0:T(8,128)(2,1)} %get-tuple-element.119.refs_5_.refs_2_, bf16[4,1024,512]{2,1,0:T(8,128)(2,1)} %get-tuple-element.135.refs_3_), custom_call_target="tpu_custom_call" | custom-call | flops 1048576 | bytes 65536 | tf_op jit(solution)/shard_map/finish/pallas_call | solution.py:1343
  1129.1 0.7 reshape.232
  1130.4 4.7 add_add_fusion.4
  1135.7 0.9 reshape.234
  1137.4 1.1 copy-done.4
  1138.4 1.0 copy-done.5
  1139.5 1.0 copy-done.6
  1140.5 1.0 copy-done.7
  1141.5 0.9 copy-done.8
  1142.5 0.9 copy-done.9
  1143.4 0.9 copy-done.10
  1144.4 10.3 place.1
  (109 shorter events, 11.4 us)
Async XLA Ops:
  7.2 197.7 %all-gather.10.cloned.1.call-start = ((), (), s32[]{:S(2)}) async-start(), calls=%async_computation.1 | async-start | bytes 5242880 | tf_op jit(solution)/shard_map/all_gather | solution.py:1658
  10.8 1.6 copy-start.28
  10.8 1.6 copy-start.29
  87.4 173.4 %all-gather.12.cloned.1.call-start = ((), (), s32[]{:S(2)}) async-start(), calls=%async_computation.2 | async-start | bytes 5242880 | tf_op jit(solution)/shard_map/all_gather | solution.py:1658
  88.2 236.8 %all-gather.8.cloned.1.call-start = ((), (), s32[]{:S(2)}) async-start(), calls=%async_computation | async-start | bytes 3932160 | tf_op jit(solution)/shard_map/all_gather | solution.py:1658
  88.3 2.4 copy-start.27
  89.5 357.3 %all-gather.14.cloned.1.call-start = ((), (), s32[]{:S(2)}) async-start(), calls=%async_computation.3 | async-start | bytes 5242880 | tf_op jit(solution)/shard_map/all_gather | solution.py:1658
  157.2 42.7 %copy-start.30 = (f32[2,2,2048]{2,1,0:T(2,128)S(1)}, f32[2,2,2048]{2,1,0:T(2,128)}, u32[]{:S(2)}) copy-start(f32[2,2,2048]{2,1,0:T(2,128)} %param.21) | copy-start | bytes 98308
  157.2 42.8 %copy-start.15 = (bf16[256,2048]{1,0:T(8,128)(2,1)S(1)}, bf16[256,2048]{1,0:T(8,128)(2,1)}, u32[]{:S(2)}) copy-start(bf16[256,2048]{1,0:T(8,128)(2,1)} %refs_0_.2) | copy-start | bytes 3145732
  202.1 0.7 copy-start.31
  310.1 1.3 copy-start.11
  444.1 1.3 copy-start.13
  609.1 3.1 copy-start.14
  609.1 3.5 copy-start.26
  612.6 3.4 copy-start.22
  616.0 1.7 copy-start.16
  668.8 28.3 %copy-start.33 = (f32[1,1024]{1,0:T(1,128)S(1)}, f32[1,1024]{1,0:T(1,128)}, u32[]{:S(2)}) copy-start(f32[1,1024]{1,0:T(1,128)} %get-tuple-element.134) | copy-start | bytes 12292
  749.8 3.1 copy-start.12
  749.8 3.5 copy-start.24
  753.3 1.6 copy-start.17
  753.3 1.9 copy-start.23
  756.0 1.3 copy-start.18
  880.2 2.5 copy-start.25
  882.7 1.6 copy-start.19
  884.6 1.3 copy-start.21
  938.2 28.0 %copy-start.32 = (f32[1,1024]{1,0:T(1,128)S(1)}, f32[1,1024]{1,0:T(1,128)}, u32[]{:S(2)}) copy-start(f32[1,1024]{1,0:T(1,128)} %get-tuple-element.132) | copy-start | bytes 12292
  1019.4 2.4 copy-start.20
  1130.4 6.9 copy-start
  1130.4 6.9 copy-start.1
  1130.4 6.9 copy-start.2
  1130.4 6.9 copy-start.3
  1137.3 1.1 copy-start.4
  1138.4 1.0 copy-start.5
  1139.5 1.0 copy-start.6
  1140.5 1.0 copy-start.7
  1141.5 0.9 copy-start.8
  1142.5 0.9 copy-start.9
  1143.4 0.9 copy-start.10
Sparse Core Ops, SparseCore 0:
  87.6 91.4 all-gather.9
  180.6 80.1 all-gather.11
  262.9 62.0 all-gather.7
  326.4 109.6 all-gather.13

commit v4 on v3

--- a/solution.py
+++ b/solution.py
@@ -73,7 +73,7 @@
         self.plan, self.srcs, self.out = plan, srcs, out[0]
         self.recv, self.own, self.send_sem, self.recv_sem, self.loc = scratch
         self.z, self.z1, self.z2, self.z3 = z_peers()
-        self.sent = []
+        self.sent, self.begun = [], False
         self.events = [functools.partial(self.event, c) for c in range(len(plan))]
 
     def block(self, c, z):
@@ -104,6 +104,7 @@
         self.remote(self.own.at[0, c], kind, c, self.z1).wait_recv()
 
     def start(self):
+        self.begun = True
         for c in range(min(self.ahead, len(self.plan))):
             self.push(self.block(c, self.z3), 1, c, self.z1)
         for c in range(len(self.plan)):
@@ -129,8 +130,10 @@
         self.push(self.block(c, self.z1), 0, c, self.z1)
 
     def tick(self, n=1):
-        for _ in range(min(n, len(self.events))):
+        n = min(n, len(self.events)) if self.begun else 0
+        for _ in range(n):
             self.events.pop(0)()
+        return n > 0
 
     def finish(self):
         self.tick(len(self.events))
@@ -206,9 +209,11 @@
         self.push(self.place(c, self.z2), self.z2, 2, c, self.z1)
 
     def tick(self, n=1):
-        for _ in range(min(n, len(self.plan) - self.passed)):
+        n = min(n, len(self.plan) - self.passed)
+        for _ in range(n):
             self.event(self.passed)
             self.passed += 1
+        return n > 0
 
     def settle(self, n):
         self.tick(n - self.passed)
@@ -231,7 +236,7 @@
         pass
 
     def tick(self, n=1):
-        pass
+        return False
 
     def finish(self):
         pass
@@ -556,157 +561,441 @@
     return attend_call(attend_bwd_kernel, cid, "attend_bwd", slopes, arrays, outs, scratch, z)
 
 
-def gather_kernel(C, n_in, n_more, n_out, n_more_out, body, filler, zc, n_scratch, *refs):
-    zi, zo, zs = zc.counts()
-    (x_ref,), ins, more, z_in, (full_ref,), outs, more_out, z_out, own_scratch, scratch, z_scratch = (
-        split_refs(refs, 1, n_in, n_more, zi, 1, n_out, n_more_out, zo, 4, n_scratch, zs)
-    )
-    steps = filler(ins, more, more_out, scratch) if filler else []
-
-    def fill(n):
-        for _ in range(min(n, len(steps))):
-            steps.pop(0)()
-
-    buf, send, recv, loc = own_scratch
-    R, D = x_ref.shape
-    rc = R // C
-    me, core, bx, by, partner, xn, yn = peers()
-    z = zc.make(z_in + z_out + z_scratch)
-    enter(partner, xn, yn, bool(zc.plan))
-    z.start()
-    sent = []
-
-    def copy(src, rel, k, target, sidx):
-        return pltpu.make_async_remote_copy(
-            src_ref=src,
-            dst_ref=buf.at[k, rel],
-            send_sem=send.at[sidx, k],
-            recv_sem=recv.at[rel, k],
-            device_id={"mp": target},
-            device_id_type=MESH,
-        )
-
-    def push(src, rel, k, target, sidx):
-        c = copy(src, rel, k, target, sidx)
-        c.start()
-        sent.append(c)
-
-    def arrive(rel, k):
-        copy(buf.at[k, 0], rel, k, partner, 0).wait_recv()
-
-    kept = []
-
-    def keep(src, start, size, k, rel):
-        c = pltpu.make_async_copy(src, full_ref.at[pl.ds(start, size), :], loc.at[k, rel])
-        c.start()
-        kept.append(c)
-
-    def run(k, lo, hi):
-        starts = []
-        for rel in range(lo, hi):
-            start = pl.multiple_of(owner(rel, core, bx, by) * R + k * rc, rc)
-            keep(buf.at[k, rel], start, rc, k, rel)
-            starts.append(start)
-        body(
-            False,
-            lambda lo_=lo, hi_=hi: buf[k, lo_:hi_].reshape((hi_ - lo_) * rc, D),
-            [pl.ds(s, rc) for s in starts],
-            ins,
-            outs,
-        )
-
-    for k in range(C):
-        own = x_ref.at[pl.ds(k * rc, rc), :]
-        push(own, 2, k, xn, 1)
-        push(own, 4, k, yn, 2)
-        push(own, 1, k, partner, 0)
-    start = pl.multiple_of(me * R, R)
-    keep(x_ref, start, R, 0, 0)
-    body(True, lambda: x_ref[...], [pl.ds(start, R)], ins, outs)
-    z.tick()
-    fill(2)
-    across = jnp.where(core == 0, xn, yn)
-    for k in range(C + 2):
-        if k < C:
-            arrive(2, k)
-            arrive(4, k)
-            push(buf.at[k, 4 - 2 * core], 6, k, across, 3)
-            push(buf.at[k, 2], 3, k, partner, 4)
-            push(buf.at[k, 4], 5, k, partner, 5)
-        if k == 0:
-            starts = []
-            other = owner(1, core, bx, by) * R
-            for j in range(C):
-                arrive(1, j)
-                starts.append(pl.multiple_of(other + j * rc, rc))
-                keep(buf.at[j, 1], starts[-1], rc, j, 1)
-            body(
-                False,
-                lambda: buf[:, 1].reshape(R, D),
-                [pl.ds(s, rc) for s in starts],
-                ins,
-                outs,
-            )
-        if 1 <= k <= C:
-            arrive(3, k - 1)
-            arrive(5, k - 1)
-            run(k - 1, 2, 6)
-            arrive(6, k - 1)
-            push(buf.at[k - 1, 6], 7, k - 1, partner, 6)
-        if k >= 2:
-            arrive(7, k - 2)
-            run(k - 2, 6, 8)
-        z.tick(-(-(len(zc.plan) - 1) // (C + 1)))
-        fill(1)
-    fill(len(steps))
-    z.finish()
-    for c in sent:
-        c.wait_send()
-    for c in kept:
-        c.wait()
-
-
-def gather_call(
-    name, cid, x, ins, outs, body, z=NO_Z, more=(), more_out=(), scratch=(), filler=None, C=4
-):
-    R, D = x.shape
-    vmem = pl.BlockSpec(memory_space=pltpu.VMEM)
-    anywhere = pl.BlockSpec(memory_space=pl.ANY)
-    spec = lambda inside: vmem if inside else anywhere
-    counts = (len(ins), len(more), len(outs), len(more_out))
-    out = pl.pallas_call(
-        functools.partial(gather_kernel, C, *counts, body, filler, z, len(scratch)),
-        out_shape=(
-            jax.ShapeDtypeStruct((8 * R, D), x.dtype),
-            *outs,
-            *(shape for shape, _ in more_out),
-            *z.out_shapes,
-        ),
-        in_specs=[vmem] * (1 + len(ins)) + [spec(i) for _, i in more] + z.in_specs(),
-        out_specs=(anywhere,)
-        + (vmem,) * len(outs)
-        + tuple(spec(i) for _, i in more_out)
-        + z.out_specs(),
-        scratch_shapes=[
-            pltpu.VMEM((C, 8, R // C, D), x.dtype),
+class Links:
+    def __init__(self, z):
+        self.me, self.core, self.bx, self.by, self.partner, self.xn, self.yn = peers()
+        self.z, self.late = z, NoZ()
+        self.more, self.made = False, ()
+        self.sent, self.kept = [], []
+
+    def owner(self, rel):
+        return owner(rel, self.core, self.bx, self.by)
+
+    def tick(self, n=1):
+        for _ in range(n):
+            if not self.z.tick():
+                self.late.tick()
+
+    def finish(self):
+        self.z.finish()
+        self.late.finish()
+        for c in self.sent:
+            c.wait_send()
+        for c in self.kept:
+            c.wait()
+
+
+def fill(steps, n):
+    for _ in range(min(n, len(steps))):
+        steps.pop(0)()
+
+
+class Gather:
+    late = 0
+
+    def __init__(
+        self, R, D, x, ins, outs, body, more=(), more_out=(), scratch=(), filler=None, C=4
+    ):
+        self.R, self.D, self.C, self.given = R, D, C, x is not None
+        self.body, self.filler = body, filler
+        self.counts = (len(ins), len(more), len(outs), len(more_out))
+        self.ins = [(x, True)] * self.given + [(a, True) for a in ins] + list(more)
+        low = jnp.bfloat16
+        self.outs = [(jax.ShapeDtypeStruct((8 * R, D), low), False)]
+        self.outs += [(o, True) for o in outs] + list(more_out)
+        self.scratch = [
+            pltpu.VMEM((C, 8, R // C, D), low),
             pltpu.SemaphoreType.DMA((7, C)),
             pltpu.SemaphoreType.DMA((8, C)),
             pltpu.SemaphoreType.DMA((C, 8)),
             *scratch,
-            *z.scratch,
-        ],
+        ]
+
+    def run(self, links, x_ref, ins, outs, scratch):
+        n_in, n_more, n_out, n_more_out = self.counts
+        if self.given:
+            x_ref, ins = ins[0], ins[1:]
+        ins, more = split_refs(ins, n_in, n_more)
+        (full_ref,), outs, more_out = split_refs(outs, 1, n_out, n_more_out)
+        buf, send, recv, loc = scratch[:4]
+        steps = self.filler(ins, more, more_out, scratch[4:]) if self.filler else []
+        R, D, C, body = self.R, self.D, self.C, self.body
+        rc = R // C
+        partner, xn, yn, core = links.partner, links.xn, links.yn, links.core
+
+        def copy(src, rel, k, target, sidx):
+            return pltpu.make_async_remote_copy(
+                src_ref=src,
+                dst_ref=buf.at[k, rel],
+                send_sem=send.at[sidx, k],
+                recv_sem=recv.at[rel, k],
+                device_id={"mp": target},
+                device_id_type=MESH,
+            )
+
+        def push(src, rel, k, target, sidx):
+            c = copy(src, rel, k, target, sidx)
+            c.start()
+            links.sent.append(c)
+
+        def arrive(rel, k):
+            copy(buf.at[k, 0], rel, k, partner, 0).wait_recv()
+
+        def keep(src, start, size, k, rel):
+            c = pltpu.make_async_copy(src, full_ref.at[pl.ds(start, size), :], loc.at[k, rel])
+            c.start()
+            links.kept.append(c)
+
+        def place(rel, k):
+            return pl.multiple_of(links.owner(rel) * R + k * rc, rc)
+
+        def run(k, lo, hi):
+            starts = [place(rel, k) for rel in range(lo, hi)]
+            for rel, start in zip(range(lo, hi), starts):
+                keep(buf.at[k, rel], start, rc, k, rel)
+            body(
+                False,
+                lambda: buf[k, lo:hi].reshape((hi - lo) * rc, D),
+                [pl.ds(start, rc) for start in starts],
+                ins,
+                outs,
+            )
+
+        for k in range(C):
+            own = x_ref.at[pl.ds(k * rc, rc), :]
+            push(own, 2, k, xn, 1)
+            push(own, 4, k, yn, 2)
+            push(own, 1, k, partner, 0)
+        start = pl.multiple_of(links.me * R, R)
+        keep(x_ref, start, R, 0, 0)
+        body(True, lambda: x_ref[...], [pl.ds(start, R)], ins, outs)
+        links.tick()
+        fill(steps, 2)
+        across = jnp.where(core == 0, xn, yn)
+        for k in range(C + 2):
+            if k < C:
+                arrive(2, k)
+                arrive(4, k)
+                push(buf.at[k, 4 - 2 * core], 6, k, across, 3)
+                push(buf.at[k, 2], 3, k, partner, 4)
+                push(buf.at[k, 4], 5, k, partner, 5)
+            if k == 0:
+                starts = [place(1, j) for j in range(C)]
+                for j in range(C):
+                    arrive(1, j)
+                    keep(buf.at[j, 1], starts[j], rc, j, 1)
+                body(
+                    False,
+                    lambda: buf[:, 1].reshape(R, D),
+                    [pl.ds(start, rc) for start in starts],
+                    ins,
+                    outs,
+                )
+            if 1 <= k <= C:
+                arrive(3, k - 1)
+                arrive(5, k - 1)
+                run(k - 1, 2, 6)
+                arrive(6, k - 1)
+                push(buf.at[k - 1, 6], 7, k - 1, partner, 6)
+            if k >= 2:
+                arrive(7, k - 2)
+                run(k - 2, 6, 8)
+            links.tick()
+            fill(steps, 1)
+        fill(steps, len(steps))
+
+
+class Scatter:
+    def __init__(
+        self,
+        T,
+        D,
+        ins,
+        body,
+        epilogue,
+        more=(),
+        more_out=(),
+        scratch=(),
+        filler=None,
+        late=0,
+        C=4,
+    ):
+        R = T // 8
+        self.R, self.D, self.C = R, D, C
+        self.body, self.epilogue, self.filler, self.late = body, epilogue, filler, late
+        self.n_scratch = len(scratch)
+        if late:
+            w = more_out[0][0].shape[2]
+            more_out = [*more_out, (jax.ShapeDtypeStruct((late * ZR, w), jnp.bfloat16), True)]
+            scratch = [*scratch, *sum_scratch(late, w)]
+        self.counts = (len(ins), len(epilogue.ins), len(more)), (len(epilogue.outs), len(more_out))
+        self.ins = [(a, True) for a in ins] + [(a, True) for a in epilogue.ins] + list(more)
+        self.outs = [(o, True) for o in epilogue.outs] + list(more_out)
+        self.scratch = [
+            pltpu.VMEM((8, R, D), jnp.bfloat16),
+            pltpu.VMEM((7, R, D), jnp.bfloat16),
+            pltpu.SemaphoreType.DMA((7, C)),
+            pltpu.SemaphoreType.DMA((7, C)),
+            *epilogue.scratch,
+            *scratch,
+        ]
+
+    def run(self, links, _, ins, outs, scratch):
+        ins, end_ins, more = split_refs(ins, *self.counts[0])
+        end_outs, more_out = split_refs(outs, *self.counts[1])
+        (pbuf, rbuf, send, recv), end_scratch, scratch, late_scratch = split_refs(
+            scratch, 4, len(self.epilogue.scratch), self.n_scratch, 5 if self.late else 0
+        )
+        steps = []
+        if self.late:
+            plan = [(0, ZR * c) for c in range(self.late)]
+            links.late = ZSum(plan, more_out[:1], more_out[-1:], late_scratch)
+            more_out = more_out[:-1]
+        if self.filler:
+            steps = self.filler(ins, more, more_out, scratch) + [links.late.start]
+        R, D, C = self.R, self.D, self.C
+        rc = R // C
+        core, bx, by, partner = links.core, links.bx, links.by, links.partner
+        dn = jnp.where(core == 0, links.yn, links.xn)
+        fn = jnp.where(core == 0, links.xn, links.yn)
+
+        def copy(src, slot, k, target):
+            rows = pl.ds(k * rc, rc)
+            return pltpu.make_async_remote_copy(
+                src_ref=src.at[rows, :],
+                dst_ref=rbuf.at[slot, rows, :],
+                send_sem=send.at[slot, k],
+                recv_sem=recv.at[slot, k],
+                device_id={"mp": target},
+                device_id_type=MESH,
+            )
+
+        def push(slot, to, target, k):
+            c = copy(pbuf.at[slot], to, k, target)
+            c.start()
+            links.sent.append(c)
+
+        def arrive(slot, k):
+            copy(pbuf.at[0], slot, k, partner).wait_recv()
+
+        def dest_rank(which, c):
+            if which == 0:
+                return (1 - by) * 4 + (1 - bx) * 2 + c
+            if which == 3:
+                return by * 4 + bx * 2 + c
+            flip_y = (1 - c) if which == 1 else c
+            y = by + flip_y * (1 - 2 * by)
+            x = bx + (1 - flip_y) * (1 - 2 * bx)
+            return y * 4 + x * 2 + c
+
+        def compute(which, c, slot):
+            rows = pl.ds(pl.multiple_of(dest_rank(which, c) * R, R), R)
+            self.body(rows, ins, pbuf.at[slot])
+
+        def theirs(which):
+            compute(which, 1 - core, which)
+            for k in range(C):
+                push(which, which, partner, k)
+
+        def add(slot, rslot, k):
+            @pl.loop(0, rc // 16)
+            def _(i):
+                rows = pl.ds(pl.multiple_of(k * rc + i * 16, 16), 16)
+                pbuf[slot, rows, :] = (
+                    pbuf[slot, rows, :].astype(jnp.float32)
+                    + rbuf[rslot, rows, :].astype(jnp.float32)
+                ).astype(pbuf.dtype)
+
+        def join(which):
+            for k in range(C):
+                arrive(which, k)
+                add(4 + which, which, k)
+                if which < 2:
+                    push(4 + which, 4 + which, dn, k)
+
+        theirs(0)
+        compute(0, core, 4)
+        theirs(1)
+        join(0)
+        compute(1, core, 5)
+        theirs(2)
+        join(1)
+        compute(2, core, 6)
+        theirs(3)
+        join(2)
+        compute(3, core, 7)
+        join(3)
+        links.tick(2 if links.more else 3)
+        for k in range(C):
+            arrive(4, k)
+            add(6, 4, k)
+            push(6, 6, fn, k)
+            links.tick(1 if links.more else 2)
+            fill(steps, 2)
+        fill(steps, len(steps))
+        self.epilogue.begin(end_outs, end_scratch)
+        for k in range(C):
+            arrive(5, k)
+            arrive(6, k)
+
+            @pl.loop(0, rc // 16)
+            def _(i):
+                rows = pl.ds(pl.multiple_of(k * rc + i * 16, 16), 16)
+                total = (
+                    pbuf[7, rows, :].astype(jnp.float32)
+                    + rbuf[5, rows, :].astype(jnp.float32)
+                    + rbuf[6, rows, :].astype(jnp.float32)
+                )
+                self.epilogue.rows(rows, total, end_ins, end_outs, end_scratch)
+
+        links.made = end_outs
+        return self.epilogue.end(end_outs, end_scratch)
+
+
+class AddNorm:
+    def __init__(self, stream, bias, gain, shift, keep):
+        self.ins = (stream, bias[None], gain[None], shift[None])
+        self.keep = keep
+        low = jax.ShapeDtypeStruct(stream.shape, jnp.bfloat16)
+        self.outs = (jax.ShapeDtypeStruct(stream.shape, jnp.float32),) + (low,) * keep
+        self.scratch = () if keep else (pltpu.VMEM(stream.shape, jnp.bfloat16),)
+
+    def begin(self, outs, scratch):
+        pass
+
+    def rows(self, rows, total, ins, outs, scratch):
+        stream, bias, gain, shift = ins
+        value = stream[rows, :].astype(jnp.float32) + total + bias[...]
+        outs[0][rows, :] = value
+        low = outs[1] if self.keep else scratch[0]
+        low[rows, :] = layer_norm(value, gain[...], shift[...]).astype(low.dtype)
+
+    def end(self, outs, scratch):
+        return None if self.keep else scratch[0]
+
+
+class AddOnly:
+    scratch = ()
+
+    def __init__(self, stream, bias):
+        self.ins = (stream, bias[None])
+        self.outs = (jax.ShapeDtypeStruct(stream.shape, jnp.bfloat16),)
+
+    def begin(self, outs, scratch):
+        pass
+
+    def rows(self, rows, total, ins, outs, scratch):
+        outs[0][rows, :] = (ins[0][rows, :] + total + ins[1][...]).astype(jnp.bfloat16)
+
+    def end(self, outs, scratch):
+        return None
+
+
+class NormBack:
+    def __init__(self, grad, values, gain):
+        R, D = values.shape
+        self.ins = (grad, values, gain[None])
+        self.outs = (
+            jax.ShapeDtypeStruct((R, D), jnp.float32),
+            jax.ShapeDtypeStruct((3, D), jnp.float32),
+        )
+        self.scratch = (pltpu.VMEM((R, D), jnp.bfloat16), pltpu.VMEM((3, 8, D), jnp.float32))
+
+    def begin(self, outs, scratch):
+        scratch[1][...] = jnp.zeros_like(scratch[1])
+
+    def rows(self, rows, total, ins, outs, scratch):
+        grad, values, gain = ins
+        v = values[rows, :].astype(jnp.float32)
+        centred = v - jnp.mean(v, axis=-1, keepdims=True)
+        scale = lax.rsqrt(jnp.mean(centred * centred, axis=-1, keepdims=True) + norm_eps)
+        unit = centred * scale
+        inner = total * gain[...]
+        mean = jnp.mean(inner, axis=-1, keepdims=True)
+        along = jnp.mean(inner * unit, axis=-1, keepdims=True)
+        new = grad[rows, :].astype(jnp.float32) + scale * (inner - mean - unit * along)
+        outs[0][rows, :] = new
+        scratch[0][rows, :] = new.astype(jnp.bfloat16)
+        for i, x in enumerate((total * unit, total, new)):
+            scratch[1][i] += x[:8] + x[8:]
+
+    def end(self, outs, scratch):
+        outs[1][...] = jnp.sum(scratch[1][...], axis=1)
+        return scratch[0]
+
+
+def shared_ins(phases):
+    places = []
+    flat = []
+    for p in phases:
+        mine = []
+        for x, inside in p.ins:
+            at = [i for i, (y, where) in enumerate(flat) if y is x and where == inside]
+            if not at:
+                flat.append((x, inside))
+            mine.append(at[0] if at else len(flat) - 1)
+        places.append(mine)
+    return flat, places
+
+
+def shared_scratch(phases):
+    flat, places = [], []
+    for p in phases:
+        mine = []
+        for x in p.scratch:
+            common = any(x is y for y in STREAM_SCRATCH)
+            at = [i for i, y in enumerate(flat) if y is x] if common else []
+            if not at:
+                flat.append(x)
+            mine.append(at[0] if at else len(flat) - 1)
+        places.append(mine)
+    return flat, places
+
+
+def chain_kernel(phases, zc, n_in, in_places, n_scratch, scratch_places, *refs):
+    zi, zo, zs = zc.counts()
+    ins, z_in, outs, z_out, scratch, z_scratch = split_refs(
+        refs, n_in, zi, sum(len(p.outs) for p in phases), zo, n_scratch, zs
+    )
+    z = zc.make(z_in + z_out + z_scratch)
+    if isinstance(phases[0], Scatter):
+        z.ahead = max(z.ahead, 6)
+    links = Links(z)
+    enter(links.partner, links.xn, links.yn, bool(zc.plan) or any(p.late for p in phases))
+    z.start()
+    rows = None
+    for p, here, there in zip(phases, in_places, scratch_places):
+        links.more = p is not phases[-1]
+        made, outs = outs[: len(p.outs)], outs[len(p.outs) :]
+        mine, held = tuple(ins[i] for i in here), tuple(scratch[i] for i in there)
+        rows = p.run(links, rows, mine, made, held)
+    links.finish()
+
+
+def chain_call(name, cid, phases, z=NO_Z):
+    vmem = pl.BlockSpec(memory_space=pltpu.VMEM)
+    anywhere = pl.BlockSpec(memory_space=pl.ANY)
+    spec = lambda inside: vmem if inside else anywhere
+    ins, in_places = shared_ins(phases)
+    scratch, scratch_places = shared_scratch(phases)
+    outs = [x for p in phases for x in p.outs]
+    out = pl.pallas_call(
+        functools.partial(
+            chain_kernel, phases, z, len(ins), in_places, len(scratch), scratch_places
+        ),
+        out_shape=(*(shape for shape, _ in outs), *z.out_shapes),
+        in_specs=[spec(i) for _, i in ins] + z.in_specs(),
+        out_specs=tuple(spec(i) for _, i in outs) + z.out_specs(),
+        scratch_shapes=[*scratch, *z.scratch],
         compiler_params=pltpu.CompilerParams(
-            collective_id=cid, has_side_effects=True, vmem_limit_bytes=60 << 20
+            collective_id=cid, has_side_effects=True, vmem_limit_bytes=62 << 20
         ),
-        input_output_aliases=z.aliases(
-            1 + len(ins) + len(more), 1 + len(outs) + len(more_out)
-        ),
+        input_output_aliases=z.aliases(len(ins), len(outs)),
         cost_estimate=cost(1 << 20),
         name=name,
-    )(x, *ins, *(x for x, _ in more), *z.arrays)
-    n = 1 + len(outs) + len(more_out)
-    z.done(out[n:])
-    return out[:n]
+    )(*(x for x, _ in ins), *z.arrays)
+    z.done(out[len(outs) :])
+    return split_refs(out, *(len(p.outs) for p in phases))
 
 
 def gather_only_kernel(C, n, n_after, zc, *refs):
@@ -887,168 +1176,6 @@
     tiles(w.shape[1], 256, f)
 
 
-def scatter_kernel(C, n_in, n_more, n_more_out, body, filler, zc, n_scratch, late_n, *refs):
-    zi, zo, zs = zc.counts()
-    ins, more, z_in, (out_ref,), more_out, z_out, own_scratch, scratch, z_scratch = split_refs(
-        refs, n_in, n_more, zi, 1, n_more_out, zo, 4, n_scratch, zs
-    )
-    pbuf, rbuf, send, recv = own_scratch
-    z = zc.make(z_in + z_out + z_scratch)
-    z.ahead = max(z.ahead, 6)
-    R, D = out_ref.shape
-    rc = R // C
-    me, core, bx, by, partner, xn, yn = peers()
-    steps, late = [], NoZ()
-    if late_n:
-        scratch, late_out, late_scratch = scratch[:-5], more_out[-1:], scratch[-5:]
-        more_out = more_out[:-1]
-        plan = [(0, ZR * c) for c in range(late_n)]
-        late = ZSum(plan, more_out[:1], late_out, late_scratch)
-        steps = filler(ins, more, more_out, scratch, late)
-    elif filler:
-        steps = filler(ins, more, more_out, scratch)
-    enter(partner, xn, yn, bool(zc.plan or late_n))
-    z.start()
-    dn = jnp.where(core == 0, yn, xn)
-    fn = jnp.where(core == 0, xn, yn)
-    sent = []
-
-    def fill(n):
-        for _ in range(min(n, len(steps))):
-            steps.pop(0)()
-
-    def copy(src, slot, k, target):
-        rows = pl.ds(k * rc, rc)
-        return pltpu.make_async_remote_copy(
-            src_ref=src.at[rows, :],
-            dst_ref=rbuf.at[slot, rows, :],
-            send_sem=send.at[slot, k],
-            recv_sem=recv.at[slot, k],
-            device_id={"mp": target},
-            device_id_type=MESH,
-        )
-
-    def push(slot, to, target, k):
-        c = copy(pbuf.at[slot], to, k, target)
-        c.start()
-        sent.append(c)
-
-    def arrive(slot, k):
-        copy(pbuf.at[0], slot, k, partner).wait_recv()
-
-    def dest_rank(which, c):
-        if which == 0:
-            return (1 - by) * 4 + (1 - bx) * 2 + c
-        if which == 3:
-            return by * 4 + bx * 2 + c
-        flip_y = (1 - c) if which == 1 else c
-        y = by + flip_y * (1 - 2 * by)
-        x = bx + (1 - flip_y) * (1 - 2 * bx)
-        return y * 4 + x * 2 + c
-
-    def compute(which, c, slot):
-        rows = pl.ds(pl.multiple_of(dest_rank(which, c) * R, R), R)
-        body(rows, ins, pbuf.at[slot])
-
-    def theirs(which):
-        compute(which, 1 - core, which)
-        for k in range(C):
-            push(which, which, partner, k)
-
-    def add(slot, rslot, k):
-        @pl.loop(0, rc // 16)
-        def _(i):
-            rows = pl.ds(pl.multiple_of(k * rc + i * 16, 16), 16)
-            pbuf[slot, rows, :] = (
-                pbuf[slot, rows, :].astype(jnp.float32) + rbuf[rslot, rows, :].astype(jnp.float32)
-            ).astype(pbuf.dtype)
-
-    def join(which):
-        for k in range(C):
-            arrive(which, k)
-            add(4 + which, which, k)
-            if which < 2:
-                push(4 + which, 4 + which, dn, k)
-
-    theirs(0)
-    compute(0, core, 4)
-    theirs(1)
-    join(0)
-    compute(1, core, 5)
-    theirs(2)
-    join(1)
-    compute(2, core, 6)
-    theirs(3)
-    join(2)
-    compute(3, core, 7)
-    join(3)
-    z.tick(3)
-    for k in range(C):
-        arrive(4, k)
-        add(6, 4, k)
-        push(6, 6, fn, k)
-        z.tick(2)
-        fill(2)
-    fill(len(steps))
-    for k in range(C):
-        arrive(5, k)
-        arrive(6, k)
-
-        @pl.loop(0, rc // 16)
-        def _(i):
-            rows = pl.ds(pl.multiple_of(k * rc + i * 16, 16), 16)
-            out_ref[rows, :] = (
-                pbuf[7, rows, :].astype(jnp.float32)
-                + rbuf[5, rows, :].astype(jnp.float32)
-                + rbuf[6, rows, :].astype(jnp.float32)
-            )
-    z.finish()
-    late.finish()
-    for c in sent:
-        c.wait_send()
-
-
-def scatter_call(
-    name, cid, T, D, ins, body, more=(), more_out=(), scratch=(), filler=None, z=NO_Z, late=0, C=4
-):
-    if late:
-        w = more_out[0][0].shape[2]
-        more_out = [*more_out, (jax.ShapeDtypeStruct((late * ZR, w), jnp.bfloat16), True)]
-        scratch = [*scratch, *sum_scratch(late, w)]
-    R = T // 8
-    vmem = pl.BlockSpec(memory_space=pltpu.VMEM)
-    anywhere = pl.BlockSpec(memory_space=pl.ANY)
-    spec = lambda inside: vmem if inside else anywhere
-    out = pl.pallas_call(
-        functools.partial(
-            scatter_kernel, C, len(ins), len(more), len(more_out), body, filler, z, len(scratch), late
-        ),
-        out_shape=(
-            jax.ShapeDtypeStruct((R, D), jnp.float32),
-            *(shape for shape, _ in more_out),
-            *z.out_shapes,
-        ),
-        in_specs=[vmem] * len(ins) + [spec(i) for _, i in more] + z.in_specs(),
-        out_specs=(vmem,) + tuple(spec(i) for _, i in more_out) + z.out_specs(),
-        scratch_shapes=[
-            pltpu.VMEM((8, R, D), jnp.bfloat16),
-            pltpu.VMEM((7, R, D), jnp.bfloat16),
-            pltpu.SemaphoreType.DMA((7, C)),
-            pltpu.SemaphoreType.DMA((7, C)),
-            *scratch,
-            *z.scratch,
-        ],
-        compiler_params=pltpu.CompilerParams(
-            collective_id=cid, has_side_effects=True, vmem_limit_bytes=60 << 20
-        ),
-        input_output_aliases=z.aliases(len(ins) + len(more), 1 + len(more_out)),
-        cost_estimate=cost(1 << 20),
-        name=name,
-    )(*ins, *(x for x, _ in more), *z.arrays)
-    z.done(out[1 + len(more_out) :])
-    return out[: 1 + len(more_out)] if more_out else out[0]
-
-
 def row_split_body(rows, ins, out):
     a, w = ins
     Z, _, d = w.shape
@@ -1174,7 +1301,7 @@
     return [functools.partial(step, j) for j in range(D // w)]
 
 
-def down_filler(ins, more, more_out, scratch, late):
+def down_filler(ins, more, more_out, scratch):
     active, grad = more
     (down_out,) = more_out
     buf, sems, stage, out_sems, turned, held, held_sem = scratch
@@ -1189,15 +1316,6 @@
     steps = down_steps(
         stream, down_out, turned, held, held_copy, lambda j: stream.get(j)[...], n, w
     )
-
-    def early():
-        stream.drain()
-        late.start()
-
-    first = len(late.plan) * ZR // w * (D // stage.shape[2])
-    steps.insert(first, early)
-    for i in range(len(late.plan)):
-        steps.insert(first + 2 + 2 * i, late.tick)
     return steps + [stream.drain]
 
 
@@ -1299,73 +1417,55 @@
     return steps
 
 
-def finish_kernel(zc, *refs):
-    zi, zo, zs = zc.counts()
-    (v_ref, u_ref), z_in, (v_out, u_out), z_out, own_scratch, z_scratch = split_refs(
-        refs, 2, zi, 2, zo, 6, zs
-    )
-    vs, us, v_in, u_in, send, recv = own_scratch
-    me, core, bx, by, partner, xn, yn = peers()
-    z = zc.make(z_in + z_out + z_scratch)
-    _, z1, z2, _ = z_peers()
-    enter(partner, xn, yn, True)
-    z.start()
-    hops = (({"mp": partner}, False), ({"mp": xn}, False), ({"mp": yn}, False))
-    hops += (({"dp": z1}, True), ({"dp": z2}, True))
-    vs[0] = v_ref[...]
-    us[3] = u_ref[...]
-    for i, (target, both) in enumerate(hops):
-        copies = []
-        for n, (src, dst) in enumerate(((vs, v_in), (us, u_in))[: 2 if both else 1]):
-            c = pltpu.make_async_remote_copy(
-                src_ref=src.at[i],
-                dst_ref=dst.at[i],
-                send_sem=send.at[n, i],
-                recv_sem=recv.at[n, i],
-                device_id=target,
-                device_id_type=MESH,
-            )
-            c.start()
-            copies.append(c)
-        z.tick(2)
-        for c in copies:
-            c.wait()
-        vs[i + 1] = vs[i] + v_in[i]
-        if both:
-            us[i + 1] = us[i] + u_in[i]
-    v_out[...] = vs[5]
-    u_out[...] = us[5]
-    z.finish()
-
-
-def finish_call(cid, v, u, z):
-    vmem = pl.BlockSpec(memory_space=pltpu.VMEM)
-    out = pl.pallas_call(
-        functools.partial(finish_kernel, z),
-        out_shape=(
-            jax.ShapeDtypeStruct(v.shape, v.dtype),
-            jax.ShapeDtypeStruct(u.shape, u.dtype),
-            *z.out_shapes,
-        ),
-        in_specs=[vmem, vmem] + z.in_specs(),
-        out_specs=(vmem, vmem) + z.out_specs(),
-        scratch_shapes=[
+class Finish:
+    late = 0
+
+    def __init__(self, v, u):
+        self.ins = [(v, True), (u, True)]
+        self.outs = [
+            (jax.ShapeDtypeStruct(v.shape, v.dtype), True),
+            (jax.ShapeDtypeStruct(u.shape, u.dtype), True),
+        ]
+        self.scratch = [
             pltpu.VMEM((6, *v.shape), v.dtype),
             pltpu.VMEM((6, *u.shape), u.dtype),
             pltpu.VMEM((5, *v.shape), v.dtype),
             pltpu.VMEM((5, *u.shape), u.dtype),
             pltpu.SemaphoreType.DMA((2, 5)),
             pltpu.SemaphoreType.DMA((2, 5)),
-            *z.scratch,
-        ],
-        compiler_params=pltpu.CompilerParams(
-            collective_id=cid, has_side_effects=True, vmem_limit_bytes=60 << 20
-        ),
-        cost_estimate=cost(1 << 20),
-        name="finish",
-    )(v, u, *z.arrays)
-    z.done(out[2:])
-    return out[0], out[1]
+        ]
+
+    def run(self, links, _, ins, outs, scratch):
+        v_ref, u_ref = ins
+        v_out, u_out = outs
+        vs, us, v_in, u_in, send, recv = scratch
+        _, z1, z2, _ = z_peers()
+        hops = [({"mp": n}, False) for n in (links.partner, links.xn, links.yn)]
+        hops += [({"dp": z1}, True), ({"dp": z2}, True)]
+        vs[0] = v_ref[...]
+        vs[0, 0:2, :] = links.made[1][0:2, :]
+        us[3] = u_ref[...]
+        for i, (target, both) in enumerate(hops):
+            copies = []
+            for n, (src, dst) in enumerate(((vs, v_in), (us, u_in))[: 2 if both else 1]):
+                c = pltpu.make_async_remote_copy(
+                    src_ref=src.at[i],
+                    dst_ref=dst.at[i],
+                    send_sem=send.at[n, i],
+                    recv_sem=recv.at[n, i],
+                    device_id=target,
+                    device_id_type=MESH,
+                )
+                c.start()
+                copies.append(c)
+            links.tick(2)
+            for c in copies:
+                c.wait()
+            vs[i + 1] = vs[i] + v_in[i]
+            if both:
+                us[i + 1] = us[i] + u_in[i]
+        v_out[...] = vs[5]
+        u_out[...] = us[5]
 
 
 def place_kernel(moves, n_src, *refs):
@@ -1416,7 +1516,7 @@
         i = [a is array for a in arrays].index(True)
         moves.append((i, at, targets_of(key, row)))
     w = arrays[0].shape[1]
-    depth = 6
+    depth = 12
     anywhere = pl.BlockSpec(memory_space=pl.ANY)
     return pl.pallas_call(
         functools.partial(place_kernel, moves, len(arrays)),
@@ -1429,7 +1529,7 @@
             pltpu.SemaphoreType.DMA((depth,)),
             pltpu.SemaphoreType.DMA((depth, 2)),
         ],
-        compiler_params=pltpu.CompilerParams(vmem_limit_bytes=40 << 20),
+        compiler_params=pltpu.CompilerParams(vmem_limit_bytes=62 << 20),
         cost_estimate=cost(1 << 20),
         name="place",
     )(*arrays)
@@ -1635,7 +1735,7 @@
     def __init__(self, T, D):
         self.T, self.D = T, D
         self.backlog = Backlog()
-        self.grads = None
+        self.rows = None
 
     def start(self, x, gain, bias, shift, out_grad, weights):
         project, dense, up, down = weights
@@ -1665,163 +1765,153 @@
         w = self.weights.arrays[name, l]
         return w.reshape(-1, w.shape[2]) if name in ("project", "up") else w
 
-    def project(self, l, normed, shift):
+    def shape(self, width, dtype=jnp.bfloat16):
+        return jax.ShapeDtypeStruct((self.T, width), dtype)
+
+    def packed(self, rows):
+        return jax.ShapeDtypeStruct((4, rows, self.D // 4), jnp.bfloat16), False
+
+    def scatter(self, ins, body, epilogue, **more):
+        return Scatter(self.T, self.D, ins, body, epilogue, **more)
+
+    def gather(self, x, ins, outs, body, **more):
+        return Gather(self.T // 8, self.D, x, ins, outs, body, **more)
+
+    def project(self, l, shift):
         if l == 0:
             return self.first
         w = self.weight("project", l)
-        out = jax.ShapeDtypeStruct((self.T, w.shape[1]), jnp.bfloat16)
-        return gather_call(
-            "gather_project",
-            10 * l,
-            normed,
-            (w, shift[None]),
-            (out,),
-            project_body,
-            self.weights.take(2),
-        )
+        phase = self.gather(self.rows, (w, shift[None]), (self.shape(w.shape[1]),), project_body)
+        return chain_call("gather_project", 10 * l, [phase], self.weights.take(2))[0]
 
     def attend(self, l, project, slopes):
         return attend_fwd(20 + l, project, slopes, NO_Z)
 
-    def dense(self, l, context):
-        return scatter_call(
-            "dense_scatter",
-            10 * l + 1,
-            self.T,
-            self.D,
-            (context, self.weight("dense", l)),
-            row_split_body,
-            z=self.weights.take(3 * l),
-        )
-
-    def up(self, l, normed, shift):
+    def attn_out(self, l, stream, context, bias, gain, shift, up_shift):
+        phase = self.scatter(
+            (context, self.weight("dense", l)), row_split_body, AddNorm(stream, bias, gain, shift, True)
+        )
+        z = self.weights.take(3 * l)
+        ((middle, rows),) = chain_call("dense_scatter", 10 * l + 1, [phase], z)
         w = self.weight("up", l)
-        out = jax.ShapeDtypeStruct((self.T, w.shape[1]), jnp.bfloat16)
-        return gather_call(
-            "gather_up",
-            10 * l + 2,
-            normed,
-            (w, shift[None]),
-            (out, out),
-            up_body,
-            self.weights.take(5 * l),
-        )
-
-    def down(self, l, active):
-        return scatter_call(
-            "down_scatter",
-            10 * l + 3,
-            self.T,
-            self.D,
+        shape = self.shape(w.shape[1])
+        phase = self.gather(rows, (w, up_shift[None]), (shape, shape), up_body)
+        z = self.weights.take(5 * l)
+        return middle, *chain_call("gather_up", 10 * l + 2, [phase], z)[0]
+
+    def ffn_out(self, l, middle, active, bias, gain, shift):
+        phase = self.scatter(
             (active, self.weight("down", l)),
             row_split_body,
+            AddNorm(middle, bias, gain, shift, True),
             more=((self.grad_rows, False),),
         )
-
-    def last_down(self, l, active, slope):
+        ((stream, self.rows),) = chain_call("down_scatter", 10 * l + 3, [phase])
+        return stream
+
+    def last_out(self, l, middle, active, slope, bias):
         T, F = active.shape
-        Z = lax.axis_size("dp")
         grad = self.grad_rows
-        rows, grad_hidden, sums, packed = scatter_call(
-            "last_scatter",
-            10 * l + 3,
-            T,
-            self.D,
+        phase = self.scatter(
             (active, self.weight("down", l)),
             row_split_body,
+            AddOnly(middle, bias),
             more=((slope, True), (grad, False)),
             more_out=(
-                (jax.ShapeDtypeStruct((T, F), jnp.bfloat16), True),
+                (self.shape(F), True),
                 (jax.ShapeDtypeStruct((1, F), jnp.float32), True),
-                (jax.ShapeDtypeStruct((Z, F, self.D // Z), jnp.bfloat16), False),
+                self.packed(F),
             ),
             scratch=(*STREAM_SCRATCH[2:], pltpu.VMEM((T, self.D), jnp.bfloat16), pltpu.SemaphoreType.DMA),
             filler=last_filler,
         )
+        ((rows, grad_hidden, sums, packed),) = chain_call("last_scatter", 10 * l + 3, [phase])
         self.backlog.add(("down", l), packed)
         return rows, grad, grad_hidden, sums
 
-    def down_back(self, l, grad, slope):
-        w = self.weight("down", l)
-        F = slope.shape[1]
-        outs = (
-            jax.ShapeDtypeStruct((self.T, F), jnp.bfloat16),
-            jax.ShapeDtypeStruct((1, F), jnp.float32),
-        )
-        z = self.backlog.take(5)
-        return gather_call("gather_down_back", 10 * l + 4, grad, (w, slope), outs, down_back_body, z)
-
-    def up_back(self, l, grad_hidden, active, normed, grad_down):
-        T, F = grad_hidden.shape
-        packed = jax.ShapeDtypeStruct((4, F, self.D // 4), jnp.bfloat16)
-        self.for_up = grad_hidden, normed, packed
-        args = (
-            "up_back_scatter",
-            10 * l + 5,
-            T,
-            self.D,
-            (grad_hidden, self.weight("up", l)),
-            up_back_body,
-        )
+    def ffn_back(self, l, grad, middle, gain, grad_hidden, active, normed, grad_down):
+        T, F = active.shape
+        epilogue = NormBack(grad, middle, gain)
+        ins = (grad_hidden, self.weight("up", l))
         if l:
-            return scatter_call(*args, z=self.backlog.take(5))
-        out = scatter_call(
-            *args,
-            more=((active, False), (grad_down, False)),
-            more_out=((packed, False),),
-            scratch=STREAM_SCRATCH
-            + (pltpu.VMEM((T, self.D), jnp.bfloat16), pltpu.SemaphoreType.DMA),
-            filler=down_filler,
-            z=self.backlog.take(4),
-            late=2,
-        )
-        self.backlog.add(("down", l), out[1], out[2])
-        return out[0]
-
-    def dense_back(self, l, grad):
+            first = self.scatter(ins, up_back_body, epilogue)
+        else:
+            first = self.scatter(
+                ins,
+                up_back_body,
+                epilogue,
+                more=((active, False), (grad_down, False)),
+                more_out=(self.packed(F),),
+                scratch=STREAM_SCRATCH
+                + (pltpu.VMEM((T, self.D), jnp.bfloat16), pltpu.SemaphoreType.DMA),
+                filler=down_filler,
+                late=5,
+            )
         w = self.weight("dense", l)
-        out = jax.ShapeDtypeStruct((self.T, w.shape[1]), jnp.bfloat16)
-        hidden, normed, packed = self.for_up
-        full, out, up = gather_call(
-            "gather_dense_back",
-            10 * l + 6,
-            grad,
+        second = self.gather(
+            None,
             (w,),
-            (out,),
+            (self.shape(w.shape[1]),),
             dense_back_body,
-            self.backlog.take(4),
-            more=((hidden, True), (normed, False)),
-            more_out=((packed, False),),
+            more=((grad_hidden, True), (normed, False)),
+            more_out=(self.packed(F),),
             scratch=STREAM_SCRATCH,
             filler=up_filler,
         )
-        self.backlog.add(("up", l), up)
-        return full, out
+        z = self.backlog.take(8 if l else 7)
+        one, two = chain_call("ffn_back", 10 * l + 5, [first, second], z)
+        if not l:
+            self.backlog.add(("down", l), one[2], one[3])
+        self.backlog.add(("up", l), two[2])
+        return one[0], one[1], two[0], two[1]
 
     def attend_back(self, l, project, grad_context, context, log_norms, slopes):
-        return attend_bwd(
-            22 + l, project, grad_context, context, log_norms, slopes, self.backlog.take(2)
-        )
-
-    def project_back(self, l, grad_project, context, grad_branch, normed):
+        z = self.backlog.take(0 if l else 2)
+        return attend_bwd(22 + l, project, grad_context, context, log_norms, slopes, z)
+
+    def project_back(self, grad, stream, gain, grad_project, l, context, grad_branch, normed, late):
         S, T, width = grad_project.shape
-        Z = lax.axis_size("dp")
-        packed = jax.ShapeDtypeStruct((Z, (S + 1) * width, self.D // Z), jnp.bfloat16)
-        grad, packed = scatter_call(
-            "project_back_scatter",
-            10 * l + 7,
-            T,
-            self.D,
+        return self.scatter(
             (grad_project, self.weight("project", l)),
             project_back_body,
+            NormBack(grad, stream, gain),
             more=((context, False), (grad_branch, False), (normed, False)),
-            more_out=((packed, False),),
+            more_out=(self.packed((S + 1) * width),),
             scratch=STREAM_SCRATCH + (pltpu.VMEM((width, T), jnp.bfloat16),),
             filler=attn_filler,
-            z=self.backlog.take(5),
-        )
-        self.backlog.add(("attn", l), packed)
-        return grad
+            late=late,
+        )
+
+    def attn_back(self, l, grad, stream, gain, grad_project, context, grad_branch, normed, slope):
+        first = self.project_back(
+            grad, stream, gain, grad_project, l, context, grad_branch, normed, 4
+        )
+        F = slope.shape[1]
+        w = self.weight("down", l - 1)
+        second = self.gather(
+            None,
+            (w, slope),
+            (self.shape(F), jax.ShapeDtypeStruct((1, F), jnp.float32)),
+            down_back_body,
+        )
+        one, two = chain_call("attn_back", 10 * l + 7, [first, second], self.backlog.take(6))
+        self.backlog.add(("attn", l), one[2], one[3])
+        return one[0], one[1], two
+
+    def first_attn_back(
+        self, grad, stream, gain, grad_project, context, grad_branch, normed, rows, split
+    ):
+        chunks = 4 * grad_project.shape[2] // ZR
+        first = self.project_back(
+            grad, stream, gain, grad_project, 0, context, grad_branch, normed, chunks
+        )
+        n = len(rows)
+        v = jnp.concatenate([jnp.zeros((2, self.D), jnp.float32), jnp.stack(rows)])
+        v = jnp.pad(v, ((0, -v.shape[0] % 8), (0, 0)))
+        second = Finish(v, split.reshape(8, -1))
+        one, two = chain_call("first_attn_back", 7, [first, second], self.backlog.take(1000))
+        self.backlog.add(("attn", 0), one[2], one[3])
+        return one[0], two[0][: 2 + n], two[1].reshape(split.shape)
 
     def matrix_grads(self, shapes):
         layers, d, parts, width = shapes[0]
@@ -1845,12 +1935,6 @@
         )
         return (out[0].transpose(0, 2, 1, 3), *out[1:])
 
-    def finish(self, copied, split):
-        rows = copied.shape[0] * copied.shape[1]
-        v = jnp.concatenate([copied.reshape(rows, -1), jnp.zeros((-rows % 8, self.D), jnp.float32)])
-        v, u = finish_call(9, v, split.reshape(8, -1), self.backlog.take(1000))
-        return v[:rows].reshape(copied.shape), u.reshape(split.shape)
-
 
 class Plain:
     def __init__(self, T, D):
@@ -1858,14 +1942,14 @@
         self.ffn, self.attn = {}, {}
 
     def start(self, x, gain, bias, shift, out_grad, weights):
-        self.first = layer_norm(x.astype(jnp.float32), gain, bias).astype(jnp.bfloat16)
+        self.rows = layer_norm(x.astype(jnp.float32), gain, bias).astype(jnp.bfloat16)
         self.out_grad = out_grad
         low = jnp.bfloat16
-        gathered = []
+        self.weights = []
         for l in range(weights[0].shape[0]):
             project, dense, up, down = (x[l].astype(low) for x in weights)
             project = project.reshape(project.shape[0], -1)
-            gathered.append(
+            self.weights.append(
                 (
                     lax.all_gather(project, "dp", axis=0, tiled=True),
                     lax.all_gather(dense, "dp", axis=0),
@@ -1873,36 +1957,42 @@
                     lax.all_gather(down, "dp", axis=0),
                 )
             )
-        self.weights = gathered
-
-    def project(self, l, normed, shift):
-        w = self.weights[l][0]
-        full = gather_all(normed if l else self.first)
-        return full, (nn(full, w) + shift).astype(jnp.bfloat16)
+
+    def project(self, l, shift):
+        full = gather_all(self.rows)
+        return full, (nn(full, self.weights[l][0]) + shift).astype(jnp.bfloat16)
 
     def attend(self, l, project, slopes):
         return attend_fwd(0, project, slopes, NO_Z)
 
-    def dense(self, l, context):
-        return gather_sum(nn(context, side_by_side(self.weights[l][1])))
-
-    def up(self, l, normed, shift):
-        w = self.weights[l][2]
-        full = gather_all(normed)
-        return full, *gelu_both(nn(full, w) + shift)
-
-    def down(self, l, active):
-        return gather_sum(nn(active, side_by_side(self.weights[l][3])))
-
-    def last_down(self, l, active, slope):
-        return self.down(l, active), *self.down_back(l, self.out_grad, slope)
+    def attn_out(self, l, stream, context, bias, gain, shift, up_shift):
+        middle = stream + gather_sum(nn(context, side_by_side(self.weights[l][1]))) + bias
+        full = gather_all(layer_norm(middle, gain, shift).astype(jnp.bfloat16))
+        return middle, full, *gelu_both(nn(full, self.weights[l][2]) + up_shift)
+
+    def ffn_out(self, l, middle, active, bias, gain, shift):
+        stream = middle + gather_sum(nn(active, side_by_side(self.weights[l][3]))) + bias
+        self.rows = layer_norm(stream, gain, shift).astype(jnp.bfloat16)
+        return stream
 
     def down_back(self, l, grad, slope):
         full = gather_all(grad)
-        g = (nt(full, side_by_side(self.weights[l][3])) * slope.astype(jnp.float32)).astype(jnp.bfloat16)
+        g = (nt(full, side_by_side(self.weights[l][3])) * slope.astype(jnp.float32)).astype(
+            jnp.bfloat16
+        )
         return full, g, jnp.sum(g.astype(jnp.float32), axis=0, keepdims=True)
 
-    def up_back(self, l, grad_hidden, active, normed, grad_down):
+    def last_out(self, l, middle, active, slope, bias):
+        rows = middle + gather_sum(nn(active, side_by_side(self.weights[l][3]))) + bias
+        return rows.astype(jnp.bfloat16), *self.down_back(l, self.out_grad, slope)
+
+    def norm_back(self, grad, values, gain, total):
+        back = jax.vjp(layer_norm, values, gain, gain)[1]
+        step, gain_sum, shift_sum = back(total)
+        grad = grad + step
+        return grad, jnp.stack([gain_sum, shift_sum, jnp.sum(grad, axis=0)])
+
+    def ffn_back(self, l, grad, middle, gain, grad_hidden, active, normed, grad_down):
         Z = lax.axis_size("dp")
         F = grad_hidden.shape[1]
         d = self.D // Z
@@ -1910,26 +2000,18 @@
         down = jnp.einsum(
             "tf,tzd->zfd", active, grad_down.reshape(-1, Z, d), preferred_element_type=jnp.float32
         )
-        packed = jnp.concatenate([down, up.reshape(Z, d * F // d, d)], axis=1)
-        self.ffn[l] = reduce_dp(packed).astype(jnp.float32)
-        return gather_sum(nt(grad_hidden, self.weights[l][2]))
-
-    def ffn_grads(self, l):
-        summed = self.ffn[l]
-        d = summed.shape[1]
-        F = summed.shape[0] // 2
-        return summed[F:].reshape(d, F), summed[:F]
-
-    def dense_back(self, l, grad):
-        full = gather_all(grad)
-        return full, nt(full, side_by_side(self.weights[l][1])).astype(jnp.bfloat16)
+        self.ffn[l] = reduce_dp(up.reshape(Z, d, F)), reduce_dp(down)
+        total = gather_sum(nt(grad_hidden, self.weights[l][2]))
+        grad, sums = self.norm_back(grad, middle, gain, total)
+        full = gather_all(grad.astype(jnp.bfloat16))
+        return grad, sums, full, nt(full, side_by_side(self.weights[l][1])).astype(jnp.bfloat16)
 
     def attend_back(self, l, project, grad_context, context, log_norms, slopes):
         return attend_bwd(0, project, grad_context, context, log_norms, slopes, NO_Z)
 
-    def project_back(self, l, grad_project, context, grad_branch, normed):
+    def project_back(self, l, grad, stream, gain, grad_project, context, grad_branch, normed):
+        S, T, width = grad_project.shape
         w = self.weights[l][0]
-        S, T, width = grad_project.shape
         Z = lax.axis_size("dp")
         d = self.D // Z
         dense = jnp.einsum(
@@ -1938,25 +2020,28 @@
         project = jnp.einsum(
             "td,sti->dsi", normed, grad_project, preferred_element_type=jnp.float32
         )
-        packed = jnp.concatenate(
-            [dense.reshape(Z, -1), project.reshape(Z, -1)], axis=1
-        ).reshape(Z, -1, width)
+        self.attn[l] = reduce_dp(project.reshape(Z, d, S, width)), reduce_dp(dense)
         part = sum(nt(grad_project[s], w[:, s * width : (s + 1) * width]) for s in range(S))
-        self.attn[l] = reduce_dp(packed).astype(jnp.float32)
-        return gather_sum(part)
-
-    def attn_grads(self, l):
-        d = self.D // lax.axis_size("dp")
-        rows, width = self.attn[l].shape
-        flat = self.attn[l].reshape(-1)
-        return flat[width * d :].reshape(d, 3, width), flat[: width * d].reshape(width, d)
+        return self.norm_back(grad, stream, gain, gather_sum(part))
+
+    def attn_back(self, l, grad, stream, gain, grad_project, context, grad_branch, normed, slope):
+        grad, sums = self.project_back(
+            l, grad, stream, gain, grad_project, context, grad_branch, normed
+        )
+        return grad, sums, self.down_back(l - 1, grad.astype(jnp.bfloat16), slope)
+
+    def first_attn_back(
+        self, grad, stream, gain, grad_project, context, grad_branch, normed, rows, split
+    ):
+        grad, sums = self.project_back(
+            0, grad, stream, gain, grad_project, context, grad_branch, normed
+        )
+        rows = jnp.concatenate([sums[:2], jnp.stack(rows)])
+        return grad, lax.psum(rows, ("dp", "mp")), lax.psum(split, "dp")
 
     def matrix_grads(self, shapes):
-        grads = [(*self.attn_grads(l), *self.ffn_grads(l)) for l in range(shapes[0][0])]
-        return tuple(jnp.stack(parts) for parts in zip(*grads))
-
-    def finish(self, copied, split):
-        return lax.psum(copied, ("dp", "mp")), lax.psum(split, "dp")
+        grads = [(*self.attn[l], *self.ffn[l]) for l in range(shapes[0][0])]
+        return tuple(jnp.stack(parts).astype(jnp.float32) for parts in zip(*grads))
 
 
 def shards(
@@ -1984,68 +2069,66 @@
         * (tensor_rank * heads_here + lax.iota(jnp.int32, heads_here) + 1).astype(jnp.float32)
         / N_HEADS
     )
-    low = jnp.bfloat16
     fast = tensor_size == 8 and lax.axis_size("dp") == 4 and row_count == 256
     ops = (Fast if fast else Plain)(total_rows, model_width)
-    stream = inputs.astype(jnp.float32)
     none = jnp.zeros((inner_width,), jnp.float32)
     shifts = [
         jnp.concatenate([project_bias[l, 0], none, project_bias[l, 1]]) for l in range(layer_count)
     ]
     weights = (project_weight, dense_weight, up_weight, down_weight)
     ops.start(inputs, norm_gain[0, 0], norm_bias[0, 0], shifts[0], out_grad, weights)
-    normed = None
+    stream = inputs.astype(jnp.float32)
+    last = layer_count - 1
     stored = []
     for l in range(layer_count):
-        if l:
-            normed = layer_norm(stream, norm_gain[l, 0], norm_bias[l, 0]).astype(low)
-        normed_all, project = ops.project(l, normed, shifts[l])
+        normed_all, project = ops.project(l, shifts[l])
         context, log_norms = ops.attend(l, project, slopes)
-        middle = stream + ops.dense(l, context) + output_bias[l, 0]
-        normed2 = layer_norm(middle, norm_gain[l, 1], norm_bias[l, 1]).astype(low)
-        normed2_all, active, slope = ops.up(l, normed2, up_bias[l])
+        middle, normed2_all, active, slope = ops.attn_out(
+            l,
+            stream,
+            context,
+            output_bias[l, 0],
+            norm_gain[l, 1],
+            norm_bias[l, 1],
+            up_bias[l],
+        )
         stored.append(
             (stream, normed_all, project, log_norms, context, middle, normed2_all, active, slope)
         )
-        if l < layer_count - 1:
-            stream = middle + ops.down(l, active) + output_bias[l, 1]
+        if l < last:
+            stream = ops.ffn_out(
+                l, middle, active, output_bias[l, 1], norm_gain[l + 1, 0], norm_bias[l + 1, 0]
+            )
+    outputs, *step = ops.last_out(last, middle, active, slope, output_bias[last, 1])
     grad = out_grad.astype(jnp.float32)
-    copied = [None] * layer_count
+    down_bias_grad = jnp.sum(grad, axis=0)
+    sums = [None] * layer_count
     split = [None] * layer_count
     for l in reversed(range(layer_count)):
-        last = l == layer_count - 1
-        stream_in, normed_all, project, log_norms, context, middle, normed2_all, active, slope = (
-            stored[l]
-        )
-        down_bias_grad = jnp.sum(grad, axis=0)
-        if last:
-            rows_out, grad_down, grad_hidden, up_bias_part = ops.last_down(l, active, slope)
-            outputs = (middle + rows_out + output_bias[l, 1]).astype(low)
-        else:
-            grad_down, grad_hidden, up_bias_part = ops.down_back(l, grad.astype(low), slope)
-        grad_normed2 = ops.up_back(l, grad_hidden, active, normed2_all, grad_down)
-        norm_back = jax.vjp(layer_norm, middle, norm_gain[l, 1], norm_bias[l, 1])[1]
-        grad_from_norm, gain_second, shift_second = norm_back(grad_normed2)
-        grad_middle = grad + grad_from_norm
-        dense_bias_grad = jnp.sum(grad_middle, axis=0)
-        grad_branch, grad_context = ops.dense_back(l, grad_middle.astype(low))
+        stream, normed_all, project, log_norms, context, middle, normed2_all, active, _ = stored[l]
+        grad_down, grad_hidden, up_bias_part = step
+        grad, second, grad_branch, grad_context = ops.ffn_back(
+            l, grad, middle, norm_gain[l, 1], grad_hidden, active, normed2_all, grad_down
+        )
         grad_project, project_bias_part = ops.attend_back(
             l, project, grad_context, context, log_norms, slopes
         )
-        grad_normed = ops.project_back(l, grad_project, context, grad_branch, normed_all)
-        norm_back = jax.vjp(layer_norm, stream_in, norm_gain[l, 0], norm_bias[l, 0])[1]
-        grad_from_norm, gain_first, shift_first = norm_back(grad_normed)
-        grad = grad_middle + grad_from_norm
-        copied[l] = jnp.stack(
-            [gain_first, gain_second, shift_first, shift_second, dense_bias_grad, down_bias_grad]
-        )
+        sums[l] = [second[0], second[1], second[2], down_bias_grad]
         split[l] = jnp.concatenate([project_bias_part.reshape(-1), up_bias_part.reshape(-1)])
-    copied, split = ops.finish(jnp.stack(copied), jnp.stack(split))
-    matrix_grads = ops.matrix_grads([x.shape for x in weights])
+        args = (grad, stream, norm_gain[l, 0], grad_project, context, grad_branch, normed_all)
+        if l:
+            grad, first, step = ops.attn_back(l, *args, stored[l - 1][-1])
+            sums[l] += [first[0], first[1]]
+            down_bias_grad = first[2]
+    rows = sums[0] + [x for parts in sums[1:] for x in parts]
+    grad, total, split = ops.first_attn_back(*args, rows, jnp.stack(split))
+    parts = [jnp.concatenate([total[2:6], total[:2]])]
+    parts += [total[6 * l : 6 * l + 6] for l in range(1, layer_count)]
+    copied = jnp.stack([jnp.stack([p[4], p[0], p[5], p[1], p[2], p[3]]) for p in parts])
     return (
         outputs,
         grad,
-        *matrix_grads,
+        *ops.matrix_grads([x.shape for x in weights]),
         split[:, : 2 * inner_width].reshape(layer_count, 2, inner_width),
         split[:, 2 * inner_width :],
         copied[:, 0:2],

time: 1170 us -> 1100 us (0.940)
  other arithmetic: 39.8 us -> 5.53 us
  Pallas kernels: 1060 us -> 1030 us
    reduce_sum x15 -> x0, other arithmetic: 24.7 us -> none  [the longest x5 12 us: layer_norm(): return centred * lax.rsqrt(spread + norm_eps) * scale_row + shift_row]
    pallas_call x15 -> x11, Pallas kernels: 837 us -> 818 us  [chain_call(): pl.pallas_call(functools.partial(chain_kernel, phases, z, len(ins), in_pl...]
  transfers between devices with their start and end apart: 4 -> 4, of which waited for: 2 -> 2; matrix products, arithmetic and copies ran while one was open for 1% -> 1% of each run, Pallas kernels for 28% -> 30%
where the time goes in v4:
time: 1100 us; the launch traced here: 1090 us
  Pallas kernels  1030 us (94%)
  waiting for transfers between devices  22.7 us (2%)
  local copies, waits for them, and re-layouts  20.7 us (2%)
  between operations  14.3 us (1%)
    pallas_call x11, Pallas kernels, chain_call(): pl.pallas_call(functools.partial(chain_kernel, phases, z, len(ins), in_pl...  818 us
    pallas_call x4, Pallas kernels, attend_call(): pl.pallas_call(functools.partial(kernel, z), out_shape=(*outs, *z.out_sha...  75.4 us
    pallas_call x1, Pallas kernels, first_call(): pl.pallas_call(functools.partial(first_kernel, C, z, n_project), out_shap...  74.4 us
    pallas_call x1, Pallas kernels, gather_only(): pl.pallas_call(functools.partial(gather_only_kernel, C, n, len(after), z)...  51.6 us
  transfers between devices with their start and end apart: 4, of which 2 were waited for; matrix products, arithmetic and copies ran while one was open for 1% of the time, Pallas kernels for 30%

profile of v4, /device:TPU:0, one launch (start us, length us, event | category | flops | bytes accessed | tf_op | source)
XLA Modules:
  0.0 1091.2 jit_solution(5507370332460236664)
XLA Ops:
  7.2 0.0 all-gather.10.cloned.1.call-start
  7.2 0.8 fusion.5
  8.0 0.6 broadcast_in_dim.16.refs_3_
  8.6 2.2 copy.27
  10.8 1.6 copy.28.refs_6_
  12.4 0.6 slice_bitcast_fusion.1
  13.0 74.4 %first.1 = (bf16[2048,2048]{1,0:T(8,128)(2,1)}, bf16[2048,768]{1,0:T(8,128)(2,1)}, bf16[512,1024]{1,0:T(8,128)(2,1)}, bf16[512,1024]{1,0:T(8,128)(2,1)}, bf16[10...) custom-call(bf16[256,2048]{1,0:T(8,128)(2,1)} %refs_0_.2, ...), custom_call_target="tpu_custom_call" | custom-call | flops 1048576 | bytes 65536 | tf_op jit(solution)/shard_map/first/pallas_call | solution.py:1679
  87.4 0.0 copy-start.2
  87.4 0.0 all-gather.10.cloned.1.call-update
  87.4 0.0 all-gather.12.cloned.1.call-start
  87.5 0.7 all-gather.12.cloned.1.call-update
  88.2 0.0 all-gather.8.cloned.1.call-start
  88.2 0.1 slice.179
  88.3 0.0 copy-start
  88.3 1.2 copy.29
  89.5 0.0 all-gather.8.cloned.1.call-update
  89.5 0.5 all-gather.14.cloned.1.call-start
  90.0 0.1 all-gather.14.cloned.1.call-update
  90.1 1.6 convert_element_type.23.refs_2_.refs_3_
  91.6 0.9 convert_element_type.22.refs_1_.refs_3_
  92.5 0.6 broadcast_in_dim.17.refs_2_
  93.1 0.0 copy-done
  93.1 1.6 convert_element_type.24.refs_2_
  94.6 51.6 %gather_rows.1 = (bf16[2048,2048]{1,0:T(8,128)(2,1)}, bf16[4,256,512]{2,1,0:T(8,128)(2,1)}) custom-call(bf16[256,2048]{1,0:T(8,128)(2,1)} %refs_0_.3, bf16[2,256,512]{2,1,0:T(8,128)(2,1)} %convert_element_type.22.refs_1_.refs_3_), custom_call_target="tpu_custom_call" | custom-call | flops 1048576 | bytes 65536 | tf_op jit(solution)/shard_map/gather_rows/pallas_call | solution.py:1077
  146.3 0.6 multiply_power_fusion.slope_ref
  146.9 15.1 %attend_fwd.2 = (bf16[2048,256]{1,0:T(8,128)(2,1)}, f32[2,8,256]{2,1,0:T(8,128)}) custom-call(f32[2]{0:T(128)} %multiply_power_fusion.slope_ref, bf16[2048,768]{1,0:T(8,128)(2,1)} %get-tuple-element.81.p_ref), custom_call_target="tpu_custom_call" | custom-call | flops 1048576 | bytes 65536 | tf_op jit(solution)/shard_map/attend_fwd/pallas_call | solution.py:518
  161.9 0.0 copy-done.7
  161.9 0.6 slice_bitcast_fusion
  162.6 44.7 %dense_scatter.2 = (f32[256,2048]{1,0:T(8,128)}, bf16[256,2048]{1,0:T(8,128)(2,1)}) custom-call(bf16[2048,256]{1,0:T(8,128)(2,1)} %get-tuple-element.82.refs_0_.c_ref.refs_5_, bf16[4,256,512]{2,1,0:T(8,128)(2,1)} %get-tuple-element.83.refs_1_.refs_7_, f32[256,2048]{1,0:T(8,128)} %convert_element_type.23.refs_2_.refs_3_, ...), custom_call_target="tpu_custom_call" | custom-call | flops 1048576 | bytes 65536 | tf_op jit(solution)/shard_map/dense_scatter/pallas_call | solution.py:982
  207.2 0.0 copy-done.1
  207.2 0.2 convert_reduce_fusion
  207.4 0.6 fusion.4
  208.0 49.0 %gather_up.2 = (bf16[2048,2048]{1,0:T(8,128)(2,1)}, bf16[2048,1024]{1,0:T(8,128)(2,1)}, bf16[2048,1024]{1,0:T(8,128)(2,1)}) custom-call(bf16[256,2048]{1,0:T(8,128)(2,1)} %get-tuple-element.84.refs_0_, bf16[2048,1024]{1,0:T(8,128)(2,1)} %all-gather.10.cloned.1.call-done.refs_1_, f32[1,1024]{1,0:T(1,128)} %get-tuple-element.175.refs_2_), custom_call_target="tpu_custom_call" | custom-call | flops 1048576 | bytes 65536 | tf_op jit(solution)/shard_map/gather_up/pallas_call | solution.py:982
  257.0 6.9 all-gather.12.cloned.1.call-done
  263.9 49.1 %down_scatter.1 = (f32[256,2048]{1,0:T(8,128)}, bf16[256,2048]{1,0:T(8,128)(2,1)}) custom-call(bf16[2048,1024]{1,0:T(8,128)(2,1)} %get-tuple-element.86.refs_0_.refs_5_, bf16[4,1024,512]{2,1,0:T(8,128)(2,1)} %bitcast.46, f32[256,2048]{1,0:T(8,128)} %get-tuple-element.88.refs_2_.refs_3_, f32[1,2048]{1,0:T(1,128)} %get-tuple-element.163.refs_3_, ...), custom_call_target="tpu_custom_call" | custom-call | flops 1048576 | bytes 65536 | tf_op jit(solution)/shard_map/down_scatter/pallas_call | solution.py:982
  313.0 15.1 %all-gather.8.cloned.1.call-done = bf16[4,512,768]{2,1,0:T(8,128)(2,1)} async-done(((bf16[1,512,768]{2,1,0:T(8,128)(2,1)}), bf16[4,512,768]{2,1,0:T(8,128)(2,1)}) %all-gather.8.cloned.1.call-update) | async-done | bytes 3145744 | tf_op jit(solution)/shard_map/all_gather | solution.py:1758
  328.1 49.8 %gather_project.1 = (bf16[2048,2048]{1,0:T(8,128)(2,1)}, bf16[2048,768]{1,0:T(8,128)(2,1)}, bf16[4,256,512]{2,1,0:T(8,128)(2,1)}) custom-call(bf16[256,2048]{1,0:T(8,128)(2,1)} %get-tuple-element.90.refs_0_, bf16[2048,768]{1,0:T(8,128)(2,1)} %bitcast.48, f32[1,768]{1,0:T(1,128)} %broadcast_in_dim.17.refs_2_, ...), custom_call_target="tpu_custom_call" | custom-call | flops 1048576 | bytes 65536 | tf_op jit(solution)/shard_map/gather_project/pallas_call | solution.py:982
  378.0 15.1 %attend_fwd.3 = (bf16[2048,256]{1,0:T(8,128)(2,1)}, f32[2,8,256]{2,1,0:T(8,128)}) custom-call(f32[2]{0:T(128)} %multiply_power_fusion.slope_ref, bf16[2048,768]{1,0:T(8,128)(2,1)} %get-tuple-element.91.p_ref), custom_call_target="tpu_custom_call" | custom-call | flops 1048576 | bytes 65536 | tf_op jit(solution)/shard_map/attend_fwd/pallas_call | solution.py:518
  393.0 52.0 %dense_scatter.3 = (f32[256,2048]{1,0:T(8,128)}, bf16[256,2048]{1,0:T(8,128)(2,1)}, bf16[4,1024,512]{2,1,0:T(8,128)(2,1)}) custom-call(bf16[2048,256]{1,0:T(8,128)(2,1)} %get-tuple-element.92.refs_0_.c_ref.refs_5_, bf16[4,256,512]{2,1,0:T(8,128)(2,1)} %get-tuple-element.93.refs_1_.refs_5_, f32[256,2048]{1,0:T(8,128)} %get-tuple-element.94.refs_2_.refs_3_, ...), custom_call_target="tpu_custom_call" | custom-call | flops 1048576 | bytes 65536 | tf_op jit(solution)/shard_map/dense_scatter/pallas_call | solution.py:982
  445.0 0.0 all-gather.14.cloned.1.call-done.refs_1_
  445.1 53.1 %gather_up.3 = (bf16[2048,2048]{1,0:T(8,128)(2,1)}, bf16[2048,1024]{1,0:T(8,128)(2,1)}, bf16[2048,1024]{1,0:T(8,128)(2,1)}, bf16[4,1024,512]{2,1,0:T(8,128)(2,1)}) custom-call(bf16[256,2048]{1,0:T(8,128)(2,1)} %get-tuple-element.96.refs_0_, bf16[2048,1024]{1,0:T(8,128)(2,1)} %all-gather.14.cloned.1.call-done.refs_1_, ...), custom_call_target="tpu_custom_call", output_to_operand_aliasing={{3}: (4, {})} | custom-call | flops 1048576 | bytes 65536 | tf_op jit(solution)/shard_map/gather_up/pallas_call | solution.py:982
  498.2 54.7 %last_scatter.1 = (bf16[256,2048]{1,0:T(8,128)(2,1)}, bf16[2048,1024]{1,0:T(8,128)(2,1)}, f32[1,1024]{1,0:T(1,128)}, bf16[4,1024,512]{2,1,0:T(8,128)(2,1)}) custom-call(bf16[2048,1024]{1,0:T(8,128)(2,1)} %get-tuple-element.99.refs_0_, bf16[4,1024,512]{2,1,0:T(8,128)(2,1)} %get-tuple-element.100.refs_1_, f32[256,2048]{1,0:T(8,128)} %get-tuple-element.101.refs_2_.refs_3_, ...), custom_call_target="tpu_custom_call" | custom-call | flops 1048576 | bytes 65536 | tf_op jit(solution)/shard_map/last_scatter/pallas_call | solution.py:982
  552.9 99.7 %ffn_back.2 = (f32[256,2048]{1,0:T(8,128)}, f32[3,2048]{1,0:T(4,128)}, bf16[2048,2048]{1,0:T(8,128)(2,1)}, bf16[2048,256]{1,0:T(8,128)(2,1)}, bf16[4,1024,512]{2,1,0:T(8,128)(2,1)}, /*index=5*/bf16[1024,512]{1,0:T(8,128)(2,1)}) custom-call(bf16[2048,1024]{1,0:T(8,128)(2,1)} %get-tuple-element.104.refs_0_, ...), custom_call_target="tpu_custom_call" | custom-call | flops 1048576 | bytes 65536 | tf_op jit(solution)/shard_map/ffn_back/pallas_call | solution.py:982
  652.6 18.9 %attend_bwd.2 = (bf16[3,2048,256]{2,1,0:T(8,128)(2,1)}, f32[2,256]{1,0:T(2,128)}) custom-call(f32[2]{0:T(128)} %multiply_power_fusion.slope_ref, bf16[2048,768]{1,0:T(8,128)(2,1)} %get-tuple-element.91.p_ref, bf16[2048,256]{1,0:T(8,128)(2,1)} %get-tuple-element.107.g_ref, bf16[2048,256]{1,0:T(8,128)(2,1)} %get-tuple-element.92.refs_0_.c_ref.refs_5_, ...), custom_call_target="tpu_custom_call" | custom-call | flops 1048576 | bytes 65536 | tf_op jit(solution)/shard_map/attend_bwd/pallas_call | solution.py:518
  671.6 100.6 %attn_back.1 = (f32[256,2048]{1,0:T(8,128)}, f32[3,2048]{1,0:T(4,128)}, bf16[4,1024,512]{2,1,0:T(8,128)(2,1)}, bf16[512,512]{1,0:T(8,128)(2,1)}, bf16[2048,2048]...) custom-call(bf16[3,2048,256]{2,1,0:T(8,128)(2,1)} %get-tuple-element.109.refs_0_, ...), custom_call_target="tpu_custom_call" | custom-call | flops 1048576 | bytes 65536 | tf_op jit(solution)/shard_map/attn_back/pallas_call | solution.py:982
  772.2 0.8 slice.165
  772.9 0.8 slice.164
  773.7 105.3 %ffn_back.3 = (f32[256,2048]{1,0:T(8,128)}, f32[3,2048]{1,0:T(4,128)}, bf16[4,1024,512]{2,1,0:T(8,128)(2,1)}, bf16[640,512]{1,0:T(8,128)(2,1)}, bf16[2048,2048]{...) custom-call(bf16[2048,1024]{1,0:T(8,128)(2,1)} %get-tuple-element.115.refs_0_,, ...), custom_call_target="tpu_custom_call" | custom-call | flops 1048576 | bytes 65536 | tf_op jit(solution)/shard_map/ffn_back/pallas_call | solution.py:982
  879.1 0.0 copy-start.13
  879.1 26.3 %attend_bwd.3 = (bf16[3,2048,256]{2,1,0:T(8,128)(2,1)}, f32[2,256]{1,0:T(2,128)}, bf16[256,512]{1,0:T(8,128)(2,1)}) custom-call(f32[2]{0:T(128)} %multiply_power_fusion.slope_ref, bf16[2048,768]{1,0:T(8,128)(2,1)} %get-tuple-element.81.p_ref, bf16[2048,256]{1,0:T(8,128)(2,1)} %get-tuple-element.120.g_ref, ...), custom_call_target="tpu_custom_call" | custom-call | flops 1048576 | bytes 65536 | tf_op jit(solution)/shard_map/attend_bwd/pallas_call | solution.py:518
  905.4 0.7 copy.30
  906.2 0.6 reshape.69.refs_9_
  906.8 0.2 concatenate.18
  907.0 0.7 pad.4.refs_8_
  907.7 160.3 %first_attn_back.1 = (f32[256,2048]{1,0:T(8,128)}, f32[3,2048]{1,0:T(4,128)}, bf16[4,1024,512]{2,1,0:T(8,128)(2,1)}, bf16[1024,512]{1,0:T(8,128)(2,1)}, f32[16,2...) custom-call(bf16[3,2048,256]{2,1,0:T(8,128)(2,1)} %get-tuple-element.123.refs_0_, ...), custom_call_target="tpu_custom_call" | custom-call | flops 1048576 | bytes 65536 | tf_op jit(solution)/shard_map/first_attn_back/pallas_call | solution.py:982
  1068.0 1.0 fusion.3
  1069.1 1.1 fusion.2
  1070.1 0.7 reshape.70
  1070.8 0.6 slice.181
  1071.4 0.6 reshape.71
  1072.1 0.7 pad_maximum_fusion
  1072.8 7.6 place.1
  1080.4 1.0 copy.35
  1081.4 3.1 copy.36
  (35 shorter events, 0.2 us)
Async XLA Ops:
  7.2 5.2 copy-start.9
  7.2 5.2 copy-start.8
  7.2 200.8 %all-gather.10.cloned.1.call-start = ((), (), s32[]{:S(2)}) async-start(), calls=%async_computation.1 | async-start | bytes 5242880 | tf_op jit(solution)/shard_map/all_gather | solution.py:1758
  87.4 2.7 copy-start.2
  87.4 176.5 %all-gather.12.cloned.1.call-start = ((), (), s32[]{:S(2)}) async-start(), calls=%async_computation.2 | async-start | bytes 5242880 | tf_op jit(solution)/shard_map/all_gather | solution.py:1758
  88.2 239.9 %all-gather.8.cloned.1.call-start = ((), (), s32[]{:S(2)}) async-start(), calls=%async_computation | async-start | bytes 3932160 | tf_op jit(solution)/shard_map/all_gather | solution.py:1758
  88.3 4.8 copy-start
  89.5 2.2 copy-start.3
  89.5 355.6 %all-gather.14.cloned.1.call-start = ((), (), s32[]{:S(2)}) async-start(), calls=%async_computation.3 | async-start | bytes 5242880 | tf_op jit(solution)/shard_map/all_gather | solution.py:1758
  92.5 69.4 %copy-start.7 = (f32[2,2,2048]{2,1,0:T(2,128)S(1)}, f32[2,2,2048]{2,1,0:T(2,128)}, u32[]{:S(2)}) copy-start(f32[2,2,2048]{2,1,0:T(2,128)} %param.21) | copy-start | bytes 98308
  94.6 112.6 %copy-start.1 = (bf16[256,2048]{1,0:T(8,128)(2,1)S(1)}, bf16[256,2048]{1,0:T(8,128)(2,1)}, u32[]{:S(2)}) copy-start(bf16[256,2048]{1,0:T(8,128)(2,1)} %refs_0_.3) | copy-start | bytes 3145732
  146.9 60.6 %copy-start.10 = (f32[2,1024]{1,0:T(2,128)S(1)}, f32[2,1024]{1,0:T(2,128)}, u32[]{:S(2)}) copy-start(f32[2,1024]{1,0:T(2,128)} %param.18) | copy-start | bytes 24580
  879.1 27.0 %copy-start.12 = (f32[1,1024]{1,0:T(1,128)S(1)}, f32[1,1024]{1,0:T(1,128)}, u32[]{:S(2)}) copy-start(f32[1,1024]{1,0:T(1,128)} %get-tuple-element.132) | copy-start | bytes 12292
  879.1 27.0 %copy-start.13 = (f32[2,256]{1,0:T(2,128)S(1)}, f32[2,256]{1,0:T(2,128)}, u32[]{:S(2)}) copy-start(f32[2,256]{1,0:T(2,128)} %get-tuple-element.133) | copy-start | bytes 6148
  879.1 27.0 %copy-start.11 = (f32[1,1024]{1,0:T(1,128)S(1)}, f32[1,1024]{1,0:T(1,128)}, u32[]{:S(2)}) copy-start(f32[1,1024]{1,0:T(1,128)} %get-tuple-element.134) | copy-start | bytes 12292
  879.1 27.7 %copy-start.5 = (f32[3,2048]{1,0:T(4,128)S(1)}, f32[3,2048]{1,0:T(4,128)}, u32[]{:S(2)}) copy-start(f32[3,2048]{1,0:T(4,128)} %get-tuple-element.130) | copy-start | bytes 73732
  879.1 27.7 %copy-start.6 = (f32[3,2048]{1,0:T(4,128)S(1)}, f32[3,2048]{1,0:T(4,128)}, u32[]{:S(2)}) copy-start(f32[3,2048]{1,0:T(4,128)} %get-tuple-element.128) | copy-start | bytes 73732
  1068.0 12.4 %copy-start.4 = (bf16[256,2048]{1,0:T(8,128)(2,1)S(1)}, bf16[256,2048]{1,0:T(8,128)(2,1)}, u32[]{:S(2)}) copy-start(bf16[256,2048]{1,0:T(8,128)(2,1)} %get-tuple-element.197) | copy-start | bytes 3145732
Sparse Core Ops, SparseCore 0:
  87.6 94.5 all-gather.9
  183.7 80.1 all-gather.11
  266.0 62.0 all-gather.7
  329.5 109.4 all-gather.13

commit v5 on v4

--- a/solution.py
+++ b/solution.py
@@ -573,8 +573,8 @@
 
     def tick(self, n=1):
         for _ in range(n):
-            if not self.z.tick():
-                self.late.tick()
+            if not self.z.tick() and not self.late.tick():
+                break
 
     def finish(self):
         self.z.finish()
@@ -583,6 +583,27 @@
             c.wait_send()
         for c in self.kept:
             c.wait()
+
+
+class Fetched:
+    def __init__(self, src, ref, sem):
+        self.ref, self.copy, self.here = ref, pltpu.make_async_copy(src, ref, sem), False
+
+    def wait(self):
+        if not self.here:
+            self.copy.wait()
+        self.here = True
+
+
+def need(operands):
+    for x in operands:
+        if isinstance(x, Fetched):
+            x.wait()
+    return refs_of(operands)
+
+
+def refs_of(operands):
+    return tuple(x.ref if isinstance(x, Fetched) else x for x in operands)
 
 
 def fill(steps, n):
@@ -614,11 +635,14 @@
     def run(self, links, x_ref, ins, outs, scratch):
         n_in, n_more, n_out, n_more_out = self.counts
         if self.given:
-            x_ref, ins = ins[0], ins[1:]
+            (x_ref,), ins = need(ins[:1]), ins[1:]
         ins, more = split_refs(ins, n_in, n_more)
         (full_ref,), outs, more_out = split_refs(outs, 1, n_out, n_more_out)
         buf, send, recv, loc = scratch[:4]
-        steps = self.filler(ins, more, more_out, scratch[4:]) if self.filler else []
+        steps = []
+        if self.filler:
+            steps = self.filler(refs_of(ins), refs_of(more), more_out, scratch[4:])
+            steps = [functools.partial(need, more)] + steps
         R, D, C, body = self.R, self.D, self.C, self.body
         rc = R // C
         partner, xn, yn, core = links.partner, links.xn, links.yn, links.core
@@ -668,6 +692,7 @@
             push(own, 1, k, partner, 0)
         start = pl.multiple_of(links.me * R, R)
         keep(x_ref, start, R, 0, 0)
+        ins = need(ins)
         body(True, lambda: x_ref[...], [pl.ds(start, R)], ins, outs)
         links.tick()
         fill(steps, 2)
@@ -752,7 +777,9 @@
             links.late = ZSum(plan, more_out[:1], more_out[-1:], late_scratch)
             more_out = more_out[:-1]
         if self.filler:
-            steps = self.filler(ins, more, more_out, scratch) + [links.late.start]
+            steps = self.filler(refs_of(ins), refs_of(more), more_out, scratch)
+            steps = [functools.partial(need, more)] + steps + [links.late.start]
+        ins = need(ins)
         R, D, C = self.R, self.D, self.C
         rc = R // C
         core, bx, by, partner = links.core, links.bx, links.by, links.partner
@@ -788,13 +815,14 @@
             x = bx + (1 - flip_y) * (1 - 2 * bx)
             return y * 4 + x * 2 + c
 
-        def compute(which, c, slot):
-            rows = pl.ds(pl.multiple_of(dest_rank(which, c) * R, R), R)
-            self.body(rows, ins, pbuf.at[slot])
-
-        def theirs(which):
-            compute(which, 1 - core, which)
-            for k in range(C):
+        def compute(which, c, slot, part=0, parts=1):
+            n = R // parts
+            rows = pl.ds(pl.multiple_of(dest_rank(which, c) * R + part * n, n), n)
+            self.body(rows, ins, pbuf.at[slot, pl.ds(part * n, n), :])
+
+        def theirs(which, part=0, parts=1):
+            compute(which, 1 - core, which, part, parts)
+            for k in range(part * C // parts, (part + 1) * C // parts):
                 push(which, which, partner, k)
 
         def add(slot, rslot, k):
@@ -806,17 +834,20 @@
                     + rbuf[rslot, rows, :].astype(jnp.float32)
                 ).astype(pbuf.dtype)
 
-        def join(which):
-            for k in range(C):
+        def join(which, part=0, parts=1):
+            for k in range(part * C // parts, (part + 1) * C // parts):
                 arrive(which, k)
                 add(4 + which, which, k)
                 if which < 2:
                     push(4 + which, 4 + which, dn, k)
 
-        theirs(0)
-        compute(0, core, 4)
+        theirs(0, 0, 2)
+        theirs(0, 1, 2)
+        compute(0, core, 4, 0, 2)
+        compute(0, core, 4, 1, 2)
+        join(0, 0, 2)
         theirs(1)
-        join(0)
+        join(0, 1, 2)
         compute(1, core, 5)
         theirs(2)
         join(1)
@@ -833,6 +864,7 @@
             links.tick(1 if links.more else 2)
             fill(steps, 2)
         fill(steps, len(steps))
+        end_ins = need(end_ins)
         self.epilogue.begin(end_outs, end_scratch)
         for k in range(C):
             arrive(5, k)
@@ -952,11 +984,27 @@
     return flat, places
 
 
-def chain_kernel(phases, zc, n_in, in_places, n_scratch, scratch_places, *refs):
+def chain_kernel(phases, zc, inside, in_places, n_scratch, scratch_places, *refs):
     zi, zo, zs = zc.counts()
-    ins, z_in, outs, z_out, scratch, z_scratch = split_refs(
-        refs, n_in, zi, sum(len(p.outs) for p in phases), zo, n_scratch, zs
+    n_fetch = sum(inside)
+    ins, z_in, outs, z_out, scratch, z_scratch, held, sems = split_refs(
+        refs,
+        len(inside),
+        zi,
+        sum(len(p.outs) for p in phases),
+        zo,
+        n_scratch,
+        zs,
+        n_fetch,
+        1,
     )
+    operands, n = [], 0
+    for ref, fetch in zip(ins, inside):
+        operands.append(Fetched(ref, held[n], sems[0].at[n]) if fetch else ref)
+        n += fetch
+    for x in operands:
+        if isinstance(x, Fetched):
+            x.copy.start()
     z = zc.make(z_in + z_out + z_scratch)
     if isinstance(phases[0], Scatter):
         z.ahead = max(z.ahead, 6)
@@ -967,9 +1015,10 @@
     for p, here, there in zip(phases, in_places, scratch_places):
         links.more = p is not phases[-1]
         made, outs = outs[: len(p.outs)], outs[len(p.outs) :]
-        mine, held = tuple(ins[i] for i in here), tuple(scratch[i] for i in there)
-        rows = p.run(links, rows, mine, made, held)
+        mine, room = tuple(operands[i] for i in here), tuple(scratch[i] for i in there)
+        rows = p.run(links, rows, mine, made, room)
     links.finish()
+    need(operands)
 
 
 def chain_call(name, cid, phases, z=NO_Z):
@@ -981,12 +1030,23 @@
     outs = [x for p in phases for x in p.outs]
     out = pl.pallas_call(
         functools.partial(
-            chain_kernel, phases, z, len(ins), in_places, len(scratch), scratch_places
+            chain_kernel,
+            phases,
+            z,
+            [i for _, i in ins],
+            in_places,
+            len(scratch),
+            scratch_places,
         ),
         out_shape=(*(shape for shape, _ in outs), *z.out_shapes),
-        in_specs=[spec(i) for _, i in ins] + z.in_specs(),
+        in_specs=[anywhere] * len(ins) + z.in_specs(),
         out_specs=tuple(spec(i) for _, i in outs) + z.out_specs(),
-        scratch_shapes=[*scratch, *z.scratch],
+        scratch_shapes=[
+            *scratch,
+            *z.scratch,
+            *(pltpu.VMEM(x.shape, x.dtype) for x, i in ins if i),
+            pltpu.SemaphoreType.DMA((max(1, sum(i for _, i in ins)),)),
+        ],
         compiler_params=pltpu.CompilerParams(
             collective_id=cid, has_side_effects=True, vmem_limit_bytes=62 << 20
         ),
@@ -1436,7 +1496,7 @@
         ]
 
     def run(self, links, _, ins, outs, scratch):
-        v_ref, u_ref = ins
+        v_ref, u_ref = need(ins)
         v_out, u_out = outs
         vs, us, v_in, u_in, send, recv = scratch
         _, z1, z2, _ = z_peers()
@@ -1469,7 +1529,19 @@
 
 
 def place_kernel(moves, n_src, *refs):
-    srcs, outs, (low, wide, in_sem, out_sem) = split_refs(refs, n_src, 4, 4)
+    (v, u), srcs, outs, small, (low, wide, in_sem, out_sem) = split_refs(refs, 2, n_src, 4, 5, 4)
+    gain, shift, bias, of_project, of_up = small
+    for l in range(gain.shape[0]):
+        at = 6 * l
+        order = (0, 2, 1, 3, 4, 5) if l == 0 else (at + 4, at, at + 5, at + 1, at + 2, at + 3)
+        for i, ref in enumerate((gain, shift, bias)):
+            for j in range(2):
+                r = order[2 * i + j]
+                ref[l, j : j + 1, :] = v[r : r + 1, :]
+        width = of_project.shape[2]
+        for j in range(2):
+            of_project[l, j : j + 1, :] = u[l : l + 1, j * width : (j + 1) * width]
+        of_up[l : l + 1, :] = u[l : l + 1, 2 * width :]
     depth = low.shape[0]
 
     def fetch(i):
@@ -1508,7 +1580,8 @@
             c.wait()
 
 
-def place_call(sums, out_shapes, targets_of):
+def place_call(sums, out_shapes, targets_of, v, u, small):
+    vmem = pl.BlockSpec(memory_space=pltpu.VMEM)
     arrays, moves = [], []
     for key, row, array, at in sums:
         if not any(a is array for a in arrays):
@@ -1520,9 +1593,9 @@
     anywhere = pl.BlockSpec(memory_space=pl.ANY)
     return pl.pallas_call(
         functools.partial(place_kernel, moves, len(arrays)),
-        out_shape=tuple(out_shapes),
-        in_specs=[anywhere] * len(arrays),
-        out_specs=(anywhere,) * len(out_shapes),
+        out_shape=tuple(out_shapes) + tuple(small),
+        in_specs=[vmem] * 2 + [anywhere] * len(arrays),
+        out_specs=(anywhere,) * len(out_shapes) + (vmem,) * len(small),
         scratch_shapes=[
             pltpu.VMEM((depth, ZR, w), jnp.bfloat16),
             pltpu.VMEM((depth, ZR, w), jnp.float32),
@@ -1532,16 +1605,16 @@
         compiler_params=pltpu.CompilerParams(vmem_limit_bytes=62 << 20),
         cost_estimate=cost(1 << 20),
         name="place",
-    )(*arrays)
+    )(v, u, *arrays)
 
 
 def first_kernel(C, zc, n_project, *refs):
     zi, zo, zs = zc.counts()
-    ins, z_in, outs, z_out, scratch, z_scratch = split_refs(refs, 6, zi, 6, zo, 13, zs)
+    ins, z_in, outs, z_out, scratch, z_scratch = split_refs(refs, 6, zi, 6, zo, 14, zs)
     x_ref, gain_ref, bias_ref, shift_ref, up_ref, down_ref = ins
     full_ref, project_ref, up_out, down_out = *outs[:2], outs[2:4], outs[4:6]
     x_low, w_here, w_sem, wide, low, wide_sem, low_sem, *mine = scratch
-    buf, send, recv, loc, wide2, low2 = mine
+    buf, send, recv, loc, wide2, low2, total_ref = mine
     R, D = x_ref.shape
     rc = R // C
     me, core, bx, by, partner, xn, yn = peers()
@@ -1577,6 +1650,7 @@
 
     for i in range(2):
         read(i).start()
+    z.ahead = n_project
     enter(partner, xn, yn, True)
     z.start()
 
@@ -1619,7 +1693,6 @@
     kept[0].start()
     starts = [pl.multiple_of(owner(rel, core, bx, by) * R, R) for rel in range(8)]
     across = jnp.where(core == 0, xn, yn)
-    z.tick()
     for k in range(C + 1):
         if k < C:
             arrive(2, k)
@@ -1630,10 +1703,9 @@
         if k >= 1:
             arrive(6, k - 1)
             push(buf.at[k - 1, 6], 7, k - 1, partner, 6)
-        z.tick()
         for i in range(2 * k, min(2 * k + 2, len(pieces))):
             cast(i)
-        z.tick()
+        z.tick((0, 0, 3, 2, 1)[k])
     for k in range(C):
         for rel in range(1, 8):
             if rel in (1, 3, 5, 7):
@@ -1648,20 +1720,36 @@
         cast(i)
     for i in range(len(pieces) - 2, len(pieces)):
         write(i).wait()
-    z.settle(n_project)
-    weights = pltpu.make_async_copy(z_out[0], w_here, w_sem)
-    weights.start()
-    weights.wait()
-    for rel in range(8):
-        rows = pl.ds(starts[rel], R)
-
-        def f(cols, rel=rel, rows=rows):
-            lhs = x_low[...] if rel == 0 else buf[:, rel].reshape(R, D)
-            w = w_here[:, :, cols].reshape(D, cols.size)
-            project_ref[rows, cols] = (nn(lhs, w) + shift_ref[:, cols]).astype(jnp.bfloat16)
-
-        tiles(project_ref.shape[1], 256, f)
-        z.tick()
+    z.tick(n_project)
+    Z, per, _ = w_here.shape
+    parts = w_sem.shape[0]
+    size = per // parts
+    for p in range(parts):
+        z.settle((p + 1) * n_project // parts)
+        here = pl.ds(p * size, size)
+        weights = pltpu.make_async_copy(z_out[0].at[:, here, :], w_here.at[:, here, :], w_sem.at[p])
+        weights.start()
+        weights.wait()
+        for rel in range(8):
+            rows = pl.ds(starts[rel], R)
+
+            def f(cols, rel=rel, rows=rows):
+                lhs = []
+                for i in range(Z):
+                    depth = pl.ds(i * per + p * size, size)
+                    x = x_low[:, depth] if rel == 0 else buf[:, rel, :, depth].reshape(R, size)
+                    lhs.append(x)
+                w = w_here[:, here, cols].reshape(Z * size, cols.size)
+                term = nn(jnp.concatenate(lhs, axis=1), w)
+                if p > 0:
+                    term = term + total_ref[rows, cols]
+                if p < parts - 1:
+                    total_ref[rows, cols] = term
+                else:
+                    project_ref[rows, cols] = (term + shift_ref[:, cols]).astype(jnp.bfloat16)
+
+            tiles(project_ref.shape[1], 256, f)
+            z.tick()
     z.finish()
     for c in sent:
         c.wait_send()
@@ -1690,7 +1778,7 @@
         scratch_shapes=[
             pltpu.VMEM((R, D), low),
             pltpu.VMEM((4, *w.shape[1:]), low),
-            pltpu.SemaphoreType.DMA,
+            pltpu.SemaphoreType.DMA((2,)),
             pltpu.VMEM((2, 256, up.shape[2]), jnp.float32),
             pltpu.VMEM((2, 256, up.shape[2]), low),
             pltpu.SemaphoreType.DMA((2, 2)),
@@ -1701,6 +1789,7 @@
             pltpu.SemaphoreType.DMA((C, 8)),
             pltpu.VMEM((2, 512, down.shape[2]), jnp.float32),
             pltpu.VMEM((2, 512, down.shape[2]), low),
+            pltpu.VMEM((8 * R, N), jnp.float32),
             *z.scratch,
         ],
         compiler_params=pltpu.CompilerParams(
@@ -1833,36 +1922,29 @@
         T, F = active.shape
         epilogue = NormBack(grad, middle, gain)
         ins = (grad_hidden, self.weight("up", l))
-        if l:
-            first = self.scatter(ins, up_back_body, epilogue)
-        else:
-            first = self.scatter(
-                ins,
-                up_back_body,
-                epilogue,
-                more=((active, False), (grad_down, False)),
-                more_out=(self.packed(F),),
-                scratch=STREAM_SCRATCH
-                + (pltpu.VMEM((T, self.D), jnp.bfloat16), pltpu.SemaphoreType.DMA),
-                filler=down_filler,
-                late=5,
-            )
-        w = self.weight("dense", l)
-        second = self.gather(
-            None,
-            (w,),
-            (self.shape(w.shape[1]),),
-            dense_back_body,
+        up = dict(
             more=((grad_hidden, True), (normed, False)),
             more_out=(self.packed(F),),
             scratch=STREAM_SCRATCH,
             filler=up_filler,
         )
-        z = self.backlog.take(8 if l else 7)
+        down = dict(
+            more=((active, False), (grad_down, False)),
+            more_out=(self.packed(F),),
+            scratch=STREAM_SCRATCH
+            + (pltpu.VMEM((T, self.D), jnp.bfloat16), pltpu.SemaphoreType.DMA),
+            filler=down_filler,
+        )
+        beside = dict(up, late=1) if l else dict(down, late=5)
+        first = self.scatter(ins, up_back_body, epilogue, **beside)
+        w = self.weight("dense", l)
+        beside = {} if l else up
+        second = self.gather(None, (w,), (self.shape(w.shape[1]),), dense_back_body, **beside)
+        z = self.backlog.take(8 if l else 6)
         one, two = chain_call("ffn_back", 10 * l + 5, [first, second], z)
+        self.backlog.add(("up" if l else "down", l), one[2], one[3])
         if not l:
-            self.backlog.add(("down", l), one[2], one[3])
-        self.backlog.add(("up", l), two[2])
+            self.backlog.add(("up", l), two[2])
         return one[0], one[1], two[0], two[1]
 
     def attend_back(self, l, project, grad_context, context, log_norms, slopes):
@@ -1884,7 +1966,7 @@
 
     def attn_back(self, l, grad, stream, gain, grad_project, context, grad_branch, normed, slope):
         first = self.project_back(
-            grad, stream, gain, grad_project, l, context, grad_branch, normed, 4
+            grad, stream, gain, grad_project, l, context, grad_branch, normed, 2
         )
         F = slope.shape[1]
         w = self.weight("down", l - 1)
@@ -1894,7 +1976,7 @@
             (self.shape(F), jax.ShapeDtypeStruct((1, F), jnp.float32)),
             down_back_body,
         )
-        one, two = chain_call("attn_back", 10 * l + 7, [first, second], self.backlog.take(6))
+        one, two = chain_call("attn_back", 10 * l + 7, [first, second], self.backlog.take(7))
         self.backlog.add(("attn", l), one[2], one[3])
         return one[0], one[1], two
 
@@ -1905,15 +1987,14 @@
         first = self.project_back(
             grad, stream, gain, grad_project, 0, context, grad_branch, normed, chunks
         )
-        n = len(rows)
         v = jnp.concatenate([jnp.zeros((2, self.D), jnp.float32), jnp.stack(rows)])
-        v = jnp.pad(v, ((0, -v.shape[0] % 8), (0, 0)))
-        second = Finish(v, split.reshape(8, -1))
+        u = jnp.pad(split, ((0, -split.shape[0] % 8), (0, 0)))
+        second = Finish(jnp.pad(v, ((0, -v.shape[0] % 8), (0, 0))), u)
         one, two = chain_call("first_attn_back", 7, [first, second], self.backlog.take(1000))
         self.backlog.add(("attn", 0), one[2], one[3])
-        return one[0], two[0][: 2 + n], two[1].reshape(split.shape)
-
-    def matrix_grads(self, shapes):
+        return one[0], two[0], two[1]
+
+    def results(self, shapes, small, v, u):
         layers, d, parts, width = shapes[0]
         group = self.D // lax.axis_size("dp")
 
@@ -1930,9 +2011,16 @@
             return [(0, (l, s, pl.ds(h * width + r, ZR)), h * width, width) for h in range(2)]
 
         shapes = [(layers, parts, d, width), *shapes[1:]]
+        shape = lambda x: jax.ShapeDtypeStruct(x, jnp.float32)
         out = place_call(
-            self.backlog.sums, [jax.ShapeDtypeStruct(x, jnp.float32) for x in shapes], targets
-        )
+            self.backlog.sums,
+            [shape(x) for x in shapes],
+            targets,
+            v,
+            u,
+            [shape(x) for x in (small[2], small[2], small[2], small[0], small[1])],
+        )
+        out = (*out[:4], out[7], out[8], *out[4:7])
         return (out[0].transpose(0, 2, 1, 3), *out[1:])
 
 
@@ -1987,7 +2075,7 @@
         return rows.astype(jnp.bfloat16), *self.down_back(l, self.out_grad, slope)
 
     def norm_back(self, grad, values, gain, total):
-        back = jax.vjp(layer_norm, values, gain, gain)[1]
+        back = jax.vjp(layer_norm, values.astype(jnp.float32), gain, gain)[1]
         step, gain_sum, shift_sum = back(total)
         grad = grad + step
         return grad, jnp.stack([gain_sum, shift_sum, jnp.sum(grad, axis=0)])
@@ -2039,9 +2127,15 @@
         rows = jnp.concatenate([sums[:2], jnp.stack(rows)])
         return grad, lax.psum(rows, ("dp", "mp")), lax.psum(split, "dp")
 
-    def matrix_grads(self, shapes):
+    def results(self, shapes, small, total, split):
         grads = [(*self.attn[l], *self.ffn[l]) for l in range(shapes[0][0])]
-        return tuple(jnp.stack(parts).astype(jnp.float32) for parts in zip(*grads))
+        matrices = tuple(jnp.stack(parts).astype(jnp.float32) for parts in zip(*grads))
+        parts = [jnp.concatenate([total[2:6], total[:2]])]
+        parts += [total[6 * l : 6 * l + 6] for l in range(1, len(grads))]
+        pick = lambda i, j: jnp.stack([jnp.stack([p[i], p[j]]) for p in parts])
+        n = small[0][1] * small[0][2]
+        split = split[:, :n].reshape(small[0]), split[:, n:]
+        return (*matrices, *split, pick(4, 0), pick(5, 1), pick(2, 3))
 
 
 def shards(
@@ -2077,7 +2171,7 @@
     ]
     weights = (project_weight, dense_weight, up_weight, down_weight)
     ops.start(inputs, norm_gain[0, 0], norm_bias[0, 0], shifts[0], out_grad, weights)
-    stream = inputs.astype(jnp.float32)
+    stream = inputs
     last = layer_count - 1
     stored = []
     for l in range(layer_count):
@@ -2100,8 +2194,8 @@
                 l, middle, active, output_bias[l, 1], norm_gain[l + 1, 0], norm_bias[l + 1, 0]
             )
     outputs, *step = ops.last_out(last, middle, active, slope, output_bias[last, 1])
-    grad = out_grad.astype(jnp.float32)
-    down_bias_grad = jnp.sum(grad, axis=0)
+    grad = out_grad
+    down_bias_grad = jnp.sum(grad.astype(jnp.float32), axis=0)
     sums = [None] * layer_count
     split = [None] * layer_count
     for l in reversed(range(layer_count)):
@@ -2122,19 +2216,9 @@
             down_bias_grad = first[2]
     rows = sums[0] + [x for parts in sums[1:] for x in parts]
     grad, total, split = ops.first_attn_back(*args, rows, jnp.stack(split))
-    parts = [jnp.concatenate([total[2:6], total[:2]])]
-    parts += [total[6 * l : 6 * l + 6] for l in range(1, layer_count)]
-    copied = jnp.stack([jnp.stack([p[4], p[0], p[5], p[1], p[2], p[3]]) for p in parts])
-    return (
-        outputs,
-        grad,
-        *ops.matrix_grads([x.shape for x in weights]),
-        split[:, : 2 * inner_width].reshape(layer_count, 2, inner_width),
-        split[:, 2 * inner_width :],
-        copied[:, 0:2],
-        copied[:, 2:4],
-        copied[:, 4:6],
-    )
+    shapes = [x.shape for x in weights]
+    small = [x.shape for x in (project_bias, up_bias, norm_gain)]
+    return outputs, grad, *ops.results(shapes, small, total, split)
 
 
 def solution(mesh):

time: 1100 us -> 1080 us (0.982)
  Pallas kernels: 1030 us -> 1010 us
    pallas_call x11, Pallas kernels: 818 us -> 797 us  [chain_call(): pl.pallas_call(functools.partial(chain_kernel, phases, z, [i for _, i in...]
  transfers between devices with their start and end apart: 4 -> 4, of which waited for: 2 -> 2; matrix products, arithmetic and copies ran while one was open for 1% -> 0% of each run, Pallas kernels for 30% -> 30%
where the time goes in v5:
time: 1080 us; the launch traced here: 1070 us
  Pallas kernels  1010 us (94%)
  waiting for transfers between devices  30.6 us (3%)
  local copies, waits for them, and re-layouts  16.1 us (1%)
  between operations  14.3 us (1%)
    pallas_call x11, Pallas kernels, chain_call(): pl.pallas_call(functools.partial(chain_kernel, phases, z, [i for _, i in...  797 us
    pallas_call x4, Pallas kernels, attend_call(): pl.pallas_call(functools.partial(kernel, z), out_shape=(*outs, *z.out_sha...  75.7 us
    pallas_call x1, Pallas kernels, first_call(): pl.pallas_call(functools.partial(first_kernel, C, z, n_project), out_shap...  71.7 us
    pallas_call x1, Pallas kernels, gather_only(): pl.pallas_call(functools.partial(gather_only_kernel, C, n, len(after), z)...  54.8 us
    all_gather x4, waiting for transfers between devices, start(): queue.arrays[key] = lax.all_gather(shard, 'dp', axis=0)  29.8 us
  transfers between devices with their start and end apart: 4, of which 2 were waited for; matrix products, arithmetic and copies ran while one was open for 0% of the time, Pallas kernels for 30%

profile of v5, /device:TPU:0, one launch (start us, length us, event | category | flops | bytes accessed | tf_op | source)
XLA Modules:
  0.0 1072.5 jit_solution(16661654710997287693)
XLA Ops:
  7.2 0.0 copy-start.7
  7.2 0.0 copy-start.6
  7.2 0.0 all-gather.10.cloned.1.call-start
  7.2 0.8 fusion.3
  8.0 0.6 broadcast_in_dim.16.refs_3_
  8.6 2.2 copy.27
  10.8 1.6 copy.28.refs_6_
  12.4 0.0 copy-done.7
  12.4 0.0 copy-done.6
  12.4 0.7 slice_bitcast_fusion.1
  13.0 71.7 %first.1 = (bf16[2048,2048]{1,0:T(8,128)(2,1)}, bf16[2048,768]{1,0:T(8,128)(2,1)}, bf16[512,1024]{1,0:T(8,128)(2,1)}, bf16[512,1024]{1,0:T(8,128)(2,1)}, bf16[10...) custom-call(bf16[256,2048]{1,0:T(8,128)(2,1)} %refs_3_.1, ...), custom_call_target="tpu_custom_call" | custom-call | flops 1048576 | bytes 65536 | tf_op jit(solution)/shard_map/first/pallas_call | solution.py:1767
  84.7 0.0 copy-start.1
  84.7 0.0 all-gather.10.cloned.1.call-update
  84.8 0.0 all-gather.12.cloned.1.call-start
  84.8 0.7 all-gather.12.cloned.1.call-update
  85.5 0.0 all-gather.8.cloned.1.call-start
  85.6 0.1 slice.102
  85.6 1.2 copy.29
  86.8 0.0 all-gather.8.cloned.1.call-update
  86.8 0.5 all-gather.14.cloned.1.call-start
  87.3 0.1 all-gather.14.cloned.1.call-update
  87.4 0.0 copy-done.1
  87.4 0.9 convert_element_type.21.refs_1_.refs_3_
  88.3 0.6 broadcast_in_dim.17.refs_2_
  88.8 0.5 multiply_power_fusion.slope_ref
  89.4 15.4 %attend_fwd.2 = (bf16[2048,256]{1,0:T(8,128)(2,1)}, f32[2,8,256]{2,1,0:T(8,128)}) custom-call(f32[2]{0:T(128)} %multiply_power_fusion.slope_ref, bf16[2048,768]{1,0:T(8,128)(2,1)} %get-tuple-element.87.p_ref), custom_call_target="tpu_custom_call" | custom-call | flops 1048576 | bytes 65536 | tf_op jit(solution)/shard_map/attend_fwd/pallas_call | solution.py:518
  104.7 54.8 %gather_rows.1 = (bf16[2048,2048]{1,0:T(8,128)(2,1)}, bf16[4,256,512]{2,1,0:T(8,128)(2,1)}) custom-call(bf16[256,2048]{1,0:T(8,128)(2,1)} %refs_2_.3, bf16[2,256,512]{2,1,0:T(8,128)(2,1)} %convert_element_type.21.refs_1_.refs_3_), custom_call_target="tpu_custom_call" | custom-call | flops 1048576 | bytes 65536 | tf_op jit(solution)/shard_map/gather_rows/pallas_call | solution.py:1137
  159.6 0.0 copy-done.5
  159.6 0.6 slice_bitcast_fusion
  160.2 43.1 %dense_scatter.2 = (f32[256,2048]{1,0:T(8,128)}, bf16[256,2048]{1,0:T(8,128)(2,1)}) custom-call(bf16[2048,256]{1,0:T(8,128)(2,1)} %get-tuple-element.88.refs_0_.c_ref.refs_5_, bf16[4,256,512]{2,1,0:T(8,128)(2,1)} %get-tuple-element.89.refs_1_.refs_7_, bf16[256,2048]{1,0:T(8,128)(2,1)} %refs_3_.1, f32[1,2048]{1,0:T(1,128)} %get-tuple-element.165.refs_3_, ...), custom_call_target="tpu_custom_call" | custom-call | flops 1048576 | bytes 65536 | tf_op jit(solution)/shard_map/dense_scatter/pallas_call | solution.py:1031
  203.3 0.0 copy-done
  203.3 0.2 convert_reduce_fusion
  203.5 0.6 fusion.2
  204.1 46.3 %gather_up.2 = (bf16[2048,2048]{1,0:T(8,128)(2,1)}, bf16[2048,1024]{1,0:T(8,128)(2,1)}, bf16[2048,1024]{1,0:T(8,128)(2,1)}) custom-call(bf16[256,2048]{1,0:T(8,128)(2,1)} %get-tuple-element.90.refs_0_, bf16[2048,1024]{1,0:T(8,128)(2,1)} %all-gather.10.cloned.1.call-done.refs_1_, f32[1,1024]{1,0:T(1,128)} %get-tuple-element.176.refs_2_), custom_call_target="tpu_custom_call" | custom-call | flops 1048576 | bytes 65536 | tf_op jit(solution)/shard_map/gather_up/pallas_call | solution.py:1031
  250.4 11.8 %all-gather.12.cloned.1.call-done = bf16[4096,512]{1,0:T(8,128)(2,1)} async-done(((bf16[1024,512]{1,0:T(8,128)(2,1)}), bf16[4096,512]{1,0:T(8,128)(2,1)}) %all-gather.12.cloned.1.call-update) | async-done | bytes 4194320 | tf_op jit(solution)/shard_map/all_gather | solution.py:1847
  262.3 46.2 %down_scatter.1 = (f32[256,2048]{1,0:T(8,128)}, bf16[256,2048]{1,0:T(8,128)(2,1)}) custom-call(bf16[2048,1024]{1,0:T(8,128)(2,1)} %get-tuple-element.92.refs_0_.refs_5_, bf16[4,1024,512]{2,1,0:T(8,128)(2,1)} %bitcast.42, f32[256,2048]{1,0:T(8,128)} %get-tuple-element.94.refs_2_.refs_3_, f32[1,2048]{1,0:T(1,128)} %get-tuple-element.164.refs_3_, ...), custom_call_target="tpu_custom_call" | custom-call | flops 1048576 | bytes 65536 | tf_op jit(solution)/shard_map/down_scatter/pallas_call | solution.py:1031
  308.5 18.0 %all-gather.8.cloned.1.call-done = bf16[4,512,768]{2,1,0:T(8,128)(2,1)} async-done(((bf16[1,512,768]{2,1,0:T(8,128)(2,1)}), bf16[4,512,768]{2,1,0:T(8,128)(2,1)}) %all-gather.8.cloned.1.call-update) | async-done | bytes 3145744 | tf_op jit(solution)/shard_map/all_gather | solution.py:1847
  326.5 46.2 %gather_project.1 = (bf16[2048,2048]{1,0:T(8,128)(2,1)}, bf16[2048,768]{1,0:T(8,128)(2,1)}, bf16[4,256,512]{2,1,0:T(8,128)(2,1)}) custom-call(bf16[256,2048]{1,0:T(8,128)(2,1)} %get-tuple-element.96.refs_0_, bf16[2048,768]{1,0:T(8,128)(2,1)} %bitcast.44, f32[1,768]{1,0:T(1,128)} %broadcast_in_dim.17.refs_2_, ...), custom_call_target="tpu_custom_call" | custom-call | flops 1048576 | bytes 65536 | tf_op jit(solution)/shard_map/gather_project/pallas_call | solution.py:1031
  372.7 15.1 %attend_fwd.3 = (bf16[2048,256]{1,0:T(8,128)(2,1)}, f32[2,8,256]{2,1,0:T(8,128)}) custom-call(f32[2]{0:T(128)} %multiply_power_fusion.slope_ref, bf16[2048,768]{1,0:T(8,128)(2,1)} %get-tuple-element.97.p_ref), custom_call_target="tpu_custom_call" | custom-call | flops 1048576 | bytes 65536 | tf_op jit(solution)/shard_map/attend_fwd/pallas_call | solution.py:518
  387.8 53.5 %dense_scatter.3 = (f32[256,2048]{1,0:T(8,128)}, bf16[256,2048]{1,0:T(8,128)(2,1)}, bf16[4,1024,512]{2,1,0:T(8,128)(2,1)}) custom-call(bf16[2048,256]{1,0:T(8,128)(2,1)} %get-tuple-element.98.refs_0_.c_ref.refs_5_, bf16[4,256,512]{2,1,0:T(8,128)(2,1)} %get-tuple-element.99.refs_1_.refs_6_, f32[256,2048]{1,0:T(8,128)} %get-tuple-element.100.refs_2_.refs_3_, ...), custom_call_target="tpu_custom_call" | custom-call | flops 1048576 | bytes 65536 | tf_op jit(solution)/shard_map/dense_scatter/pallas_call | solution.py:1031
  441.3 0.0 all-gather.14.cloned.1.call-done.refs_1_
  441.3 50.5 %gather_up.3 = (bf16[2048,2048]{1,0:T(8,128)(2,1)}, bf16[2048,1024]{1,0:T(8,128)(2,1)}, bf16[2048,1024]{1,0:T(8,128)(2,1)}, bf16[4,1024,512]{2,1,0:T(8,128)(2,1)}) custom-call(bf16[256,2048]{1,0:T(8,128)(2,1)} %get-tuple-element.102.refs_0_, bf16[2048,1024]{1,0:T(8,128)(2,1)} %all-gather.14.cloned.1.call-done.refs_1_, ...), custom_call_target="tpu_custom_call", output_to_operand_aliasing={{3}: (4, {})} | custom-call | flops 1048576 | bytes 65536 | tf_op jit(solution)/shard_map/gather_up/pallas_call | solution.py:1031
  491.8 51.9 %last_scatter.1 = (bf16[256,2048]{1,0:T(8,128)(2,1)}, bf16[2048,1024]{1,0:T(8,128)(2,1)}, f32[1,1024]{1,0:T(1,128)}, bf16[4,1024,512]{2,1,0:T(8,128)(2,1)}) custom-call(bf16[2048,1024]{1,0:T(8,128)(2,1)} %get-tuple-element.105.refs_0_, bf16[4,1024,512]{2,1,0:T(8,128)(2,1)} %get-tuple-element.106.refs_1_, f32[256,2048]{1,0:T(8,128)} %get-tuple-element.107.refs_2_.refs_3_, ...), custom_call_target="tpu_custom_call" | custom-call | flops 1048576 | bytes 65536 | tf_op jit(solution)/shard_map/last_scatter/pallas_call | solution.py:1031
  543.7 92.8 %ffn_back.2 = (f32[256,2048]{1,0:T(8,128)}, f32[3,2048]{1,0:T(4,128)}, bf16[4,1024,512]{2,1,0:T(8,128)(2,1)}, bf16[128,512]{1,0:T(8,128)(2,1)}, bf16[2048,2048]{...) custom-call(bf16[2048,1024]{1,0:T(8,128)(2,1)} %get-tuple-element.110.refs_0_, ...), custom_call_target="tpu_custom_call" | custom-call | flops 1048576 | bytes 65536 | tf_op jit(solution)/shard_map/ffn_back/pallas_call | solution.py:1031
  636.5 18.9 %attend_bwd.2 = (bf16[3,2048,256]{2,1,0:T(8,128)(2,1)}, f32[2,256]{1,0:T(2,128)}) custom-call(f32[2]{0:T(128)} %multiply_power_fusion.slope_ref, bf16[2048,768]{1,0:T(8,128)(2,1)} %get-tuple-element.97.p_ref, bf16[2048,256]{1,0:T(8,128)(2,1)} %get-tuple-element.113.g_ref, bf16[2048,256]{1,0:T(8,128)(2,1)} %get-tuple-element.98.refs_0_.c_ref.refs_5_, ...), custom_call_target="tpu_custom_call" | custom-call | flops 1048576 | bytes 65536 | tf_op jit(solution)/shard_map/attend_bwd/pallas_call | solution.py:518
  655.4 99.4 %attn_back.1 = (f32[256,2048]{1,0:T(8,128)}, f32[3,2048]{1,0:T(4,128)}, bf16[4,1024,512]{2,1,0:T(8,128)(2,1)}, bf16[256,512]{1,0:T(8,128)(2,1)}, bf16[2048,2048]...) custom-call(bf16[3,2048,256]{2,1,0:T(8,128)(2,1)} %get-tuple-element.115.refs_0_, ...), custom_call_target="tpu_custom_call" | custom-call | flops 1048576 | bytes 65536 | tf_op jit(solution)/shard_map/attn_back/pallas_call | solution.py:1031
  754.8 0.8 slice.101
  755.6 0.8 slice.100
  756.3 106.1 %ffn_back.3 = (f32[256,2048]{1,0:T(8,128)}, f32[3,2048]{1,0:T(4,128)}, bf16[4,1024,512]{2,1,0:T(8,128)(2,1)}, bf16[640,512]{1,0:T(8,128)(2,1)}, bf16[2048,2048]{...) custom-call(bf16[2048,1024]{1,0:T(8,128)(2,1)} %get-tuple-element.121.refs_0_,, ...), custom_call_target="tpu_custom_call" | custom-call | flops 1048576 | bytes 65536 | tf_op jit(solution)/shard_map/ffn_back/pallas_call | solution.py:1031
  862.4 0.0 copy-start.11
  862.4 0.0 copy-start.9
  862.4 0.0 copy-start.3
  862.4 0.0 copy-start.4
  862.4 26.3 %attend_bwd.3 = (bf16[3,2048,256]{2,1,0:T(8,128)(2,1)}, f32[2,256]{1,0:T(2,128)}, bf16[256,512]{1,0:T(8,128)(2,1)}) custom-call(f32[2]{0:T(128)} %multiply_power_fusion.slope_ref, bf16[2048,768]{1,0:T(8,128)(2,1)} %get-tuple-element.87.p_ref, bf16[2048,256]{1,0:T(8,128)(2,1)} %get-tuple-element.126.g_ref, ...), custom_call_target="tpu_custom_call" | custom-call | flops 1048576 | bytes 65536 | tf_op jit(solution)/shard_map/attend_bwd/pallas_call | solution.py:518
  888.8 0.7 copy.30
  889.5 0.0 copy-done.11
  889.5 0.2 concatenate.18
  889.8 0.7 pad.8.refs_8_
  890.4 0.6 select_maximum_fusion.refs_9_
  891.1 161.4 %first_attn_back.1 = (f32[256,2048]{1,0:T(8,128)}, f32[3,2048]{1,0:T(4,128)}, bf16[4,1024,512]{2,1,0:T(8,128)(2,1)}, bf16[1024,512]{1,0:T(8,128)(2,1)}, f32[16,2...) custom-call(bf16[3,2048,256]{2,1,0:T(8,128)(2,1)} %get-tuple-element.129.refs_0_, ...), custom_call_target="tpu_custom_call" | custom-call | flops 1048576 | bytes 65536 | tf_op jit(solution)/shard_map/first_attn_back/pallas_call | solution.py:1031
  1052.5 9.2 place.1
  1061.7 0.0 copy-done.2
  1061.7 1.0 copy.35
  1062.7 3.1 copy.36
  (19 shorter events, 0.1 us)
Async XLA Ops:
  7.2 5.2 copy-start.7
  7.2 5.2 copy-start.6
  7.2 196.9 %all-gather.10.cloned.1.call-start = ((), (), s32[]{:S(2)}) async-start(), calls=%async_computation.1 | async-start | bytes 5242880 | tf_op jit(solution)/shard_map/all_gather | solution.py:1847
  84.7 2.7 copy-start.1
  84.8 177.5 %all-gather.12.cloned.1.call-start = ((), (), s32[]{:S(2)}) async-start(), calls=%async_computation.2 | async-start | bytes 5242880 | tf_op jit(solution)/shard_map/all_gather | solution.py:1847
  85.5 241.0 %all-gather.8.cloned.1.call-start = ((), (), s32[]{:S(2)}) async-start(), calls=%async_computation | async-start | bytes 3932160 | tf_op jit(solution)/shard_map/all_gather | solution.py:1847
  86.8 72.8 %copy-start.5 = (f32[2,2,2048]{2,1,0:T(2,128)S(1)}, f32[2,2,2048]{2,1,0:T(2,128)}, u32[]{:S(2)}) copy-start(f32[2,2,2048]{2,1,0:T(2,128)} %param.21) | copy-start | bytes 98308
  86.8 354.5 %all-gather.14.cloned.1.call-start = ((), (), s32[]{:S(2)}) async-start(), calls=%async_computation.3 | async-start | bytes 5242880 | tf_op jit(solution)/shard_map/all_gather | solution.py:1847
  88.2 115.1 %copy-start = (bf16[256,2048]{1,0:T(8,128)(2,1)S(1)}, bf16[256,2048]{1,0:T(8,128)(2,1)}, u32[]{:S(2)}) copy-start(bf16[256,2048]{1,0:T(8,128)(2,1)} %refs_2_.3) | copy-start | bytes 3145732
  89.4 114.2 %copy-start.8 = (f32[2,1024]{1,0:T(2,128)S(1)}, f32[2,1024]{1,0:T(2,128)}, u32[]{:S(2)}) copy-start(f32[2,1024]{1,0:T(2,128)} %param.18) | copy-start | bytes 24580
  862.4 27.0 %copy-start.10 = (f32[1,1024]{1,0:T(1,128)S(1)}, f32[1,1024]{1,0:T(1,128)}, u32[]{:S(2)}) copy-start(f32[1,1024]{1,0:T(1,128)} %get-tuple-element.138) | copy-start | bytes 12292
  862.4 27.1 %copy-start.11 = (f32[2,256]{1,0:T(2,128)S(1)}, f32[2,256]{1,0:T(2,128)}, u32[]{:S(2)}) copy-start(f32[2,256]{1,0:T(2,128)} %get-tuple-element.139) | copy-start | bytes 6148
  862.4 27.1 %copy-start.9 = (f32[1,1024]{1,0:T(1,128)S(1)}, f32[1,1024]{1,0:T(1,128)}, u32[]{:S(2)}) copy-start(f32[1,1024]{1,0:T(1,128)} %get-tuple-element.140) | copy-start | bytes 12292
  862.4 27.1 %copy-start.3 = (f32[3,2048]{1,0:T(4,128)S(1)}, f32[3,2048]{1,0:T(4,128)}, u32[]{:S(2)}) copy-start(f32[3,2048]{1,0:T(4,128)} %get-tuple-element.136) | copy-start | bytes 73732
  862.4 27.1 %copy-start.4 = (f32[3,2048]{1,0:T(4,128)S(1)}, f32[3,2048]{1,0:T(4,128)}, u32[]{:S(2)}) copy-start(f32[3,2048]{1,0:T(4,128)} %get-tuple-element.134) | copy-start | bytes 73732
  1052.4 9.2 copy-start.2
Sparse Core Ops, SparseCore 0:
  84.9 94.6 all-gather.9
  181.2 81.0 all-gather.11
  264.4 62.0 all-gather.7
  327.9 109.8 all-gather.13

commit v6 on v5

--- a/solution.py
+++ b/solution.py
@@ -857,12 +857,13 @@
         compute(3, core, 7)
         join(3)
         links.tick(2 if links.more else 3)
+        share = -(-len(steps) // C) if self.late else 2
         for k in range(C):
             arrive(4, k)
             add(6, 4, k)
             push(6, 6, fn, k)
             links.tick(1 if links.more else 2)
-            fill(steps, 2)
+            fill(steps, share)
         fill(steps, len(steps))
         end_ins = need(end_ins)
         self.epilogue.begin(end_outs, end_scratch)
@@ -1935,12 +1936,12 @@
             + (pltpu.VMEM((T, self.D), jnp.bfloat16), pltpu.SemaphoreType.DMA),
             filler=down_filler,
         )
-        beside = dict(up, late=1) if l else dict(down, late=5)
+        beside = dict(up, late=1) if l else dict(down, late=6)
         first = self.scatter(ins, up_back_body, epilogue, **beside)
         w = self.weight("dense", l)
         beside = {} if l else up
         second = self.gather(None, (w,), (self.shape(w.shape[1]),), dense_back_body, **beside)
-        z = self.backlog.take(8 if l else 6)
+        z = self.backlog.take(8 if l else 5)
         one, two = chain_call("ffn_back", 10 * l + 5, [first, second], z)
         self.backlog.add(("up" if l else "down", l), one[2], one[3])
         if not l:
@@ -1966,7 +1967,7 @@
 
     def attn_back(self, l, grad, stream, gain, grad_project, context, grad_branch, normed, slope):
         first = self.project_back(
-            grad, stream, gain, grad_project, l, context, grad_branch, normed, 2
+            grad, stream, gain, grad_project, l, context, grad_branch, normed, 3
         )
         F = slope.shape[1]
         w = self.weight("down", l - 1)

time: 1080 us -> 1070 us (level)
  no operation moved by 1% of the time
where the time goes in v6:
time: 1070 us
  Pallas kernels  1000 us (93%)
  waiting for transfers between devices  30.8 us (3%)
  local copies, waits for them, and re-layouts  16.1 us (2%)
  between operations  14.3 us (1%)
    pallas_call x11, Pallas kernels, chain_call(): pl.pallas_call(functools.partial(chain_kernel, phases, z, [i for _, i in...  793 us
    pallas_call x4, Pallas kernels, attend_call(): pl.pallas_call(functools.partial(kernel, z), out_shape=(*outs, *z.out_sha...  75.4 us
    pallas_call x1, Pallas kernels, first_call(): pl.pallas_call(functools.partial(first_kernel, C, z, n_project), out_shap...  71.7 us
    pallas_call x1, Pallas kernels, gather_only(): pl.pallas_call(functools.partial(gather_only_kernel, C, n, len(after), z)...  54.8 us
    all_gather x4, waiting for transfers between devices, start(): queue.arrays[key] = lax.all_gather(shard, 'dp', axis=0)  29.8 us
  transfers between devices with their start and end apart: 4, of which 2 were waited for; matrix products, arithmetic and copies ran while one was open for 0% of the time, Pallas kernels for 30%

profile of v6, /device:TPU:0, one launch (start us, length us, event | category | flops | bytes accessed | tf_op | source)
XLA Modules:
  0.0 1067.9 jit_solution(5409475065707852833)
XLA Ops:
  7.2 0.0 copy-start.7
  7.2 0.0 copy-start.6
  7.2 0.0 all-gather.10.cloned.1.call-start
  7.2 0.8 fusion.3
  8.0 0.6 broadcast_in_dim.16.refs_3_
  8.6 2.2 copy.27
  10.8 1.6 copy.28.refs_6_
  12.4 0.0 copy-done.7
  12.4 0.0 copy-done.6
  12.4 0.7 slice_bitcast_fusion.1
  13.0 71.7 %first.1 = (bf16[2048,2048]{1,0:T(8,128)(2,1)}, bf16[2048,768]{1,0:T(8,128)(2,1)}, bf16[512,1024]{1,0:T(8,128)(2,1)}, bf16[512,1024]{1,0:T(8,128)(2,1)}, bf16[10...) custom-call(bf16[256,2048]{1,0:T(8,128)(2,1)} %refs_3_.1, ...), custom_call_target="tpu_custom_call" | custom-call | flops 1048576 | bytes 65536 | tf_op jit(solution)/shard_map/first/pallas_call | solution.py:1768
  84.7 0.0 copy-start.1
  84.7 0.0 all-gather.10.cloned.1.call-update
  84.8 0.0 all-gather.12.cloned.1.call-start
  84.8 0.7 all-gather.12.cloned.1.call-update
  85.5 0.0 all-gather.8.cloned.1.call-start
  85.6 0.1 slice.102
  85.6 1.2 copy.29
  86.8 0.0 all-gather.8.cloned.1.call-update
  86.8 0.3 all-gather.14.cloned.1.call-start
  87.1 0.2 all-gather.14.cloned.1.call-update
  87.4 0.0 copy-done.1
  87.4 0.9 convert_element_type.21.refs_1_.refs_3_
  88.3 0.6 broadcast_in_dim.17.refs_2_
  88.8 0.5 multiply_power_fusion.slope_ref
  89.4 15.4 %attend_fwd.2 = (bf16[2048,256]{1,0:T(8,128)(2,1)}, f32[2,8,256]{2,1,0:T(8,128)}) custom-call(f32[2]{0:T(128)} %multiply_power_fusion.slope_ref, bf16[2048,768]{1,0:T(8,128)(2,1)} %get-tuple-element.87.p_ref), custom_call_target="tpu_custom_call" | custom-call | flops 1048576 | bytes 65536 | tf_op jit(solution)/shard_map/attend_fwd/pallas_call | solution.py:518
  104.7 54.8 %gather_rows.1 = (bf16[2048,2048]{1,0:T(8,128)(2,1)}, bf16[4,256,512]{2,1,0:T(8,128)(2,1)}) custom-call(bf16[256,2048]{1,0:T(8,128)(2,1)} %refs_2_.3, bf16[2,256,512]{2,1,0:T(8,128)(2,1)} %convert_element_type.21.refs_1_.refs_3_), custom_call_target="tpu_custom_call" | custom-call | flops 1048576 | bytes 65536 | tf_op jit(solution)/shard_map/gather_rows/pallas_call | solution.py:1138
  159.6 0.0 copy-done.5
  159.6 0.6 slice_bitcast_fusion
  160.2 43.5 %dense_scatter.2 = (f32[256,2048]{1,0:T(8,128)}, bf16[256,2048]{1,0:T(8,128)(2,1)}) custom-call(bf16[2048,256]{1,0:T(8,128)(2,1)} %get-tuple-element.88.refs_0_.c_ref.refs_5_, bf16[4,256,512]{2,1,0:T(8,128)(2,1)} %get-tuple-element.89.refs_1_.refs_7_, bf16[256,2048]{1,0:T(8,128)(2,1)} %refs_3_.1, f32[1,2048]{1,0:T(1,128)} %get-tuple-element.165.refs_3_, ...), custom_call_target="tpu_custom_call" | custom-call | flops 1048576 | bytes 65536 | tf_op jit(solution)/shard_map/dense_scatter/pallas_call | solution.py:1032
  203.7 0.0 copy-done
  203.7 0.2 convert_reduce_fusion
  203.9 0.0 copy-done.8
  203.9 0.6 fusion.2
  204.5 45.9 %gather_up.2 = (bf16[2048,2048]{1,0:T(8,128)(2,1)}, bf16[2048,1024]{1,0:T(8,128)(2,1)}, bf16[2048,1024]{1,0:T(8,128)(2,1)}) custom-call(bf16[256,2048]{1,0:T(8,128)(2,1)} %get-tuple-element.90.refs_0_, bf16[2048,1024]{1,0:T(8,128)(2,1)} %all-gather.10.cloned.1.call-done.refs_1_, f32[1,1024]{1,0:T(1,128)} %get-tuple-element.176.refs_2_), custom_call_target="tpu_custom_call" | custom-call | flops 1048576 | bytes 65536 | tf_op jit(solution)/shard_map/gather_up/pallas_call | solution.py:1032
  250.4 11.8 %all-gather.12.cloned.1.call-done = bf16[4096,512]{1,0:T(8,128)(2,1)} async-done(((bf16[1024,512]{1,0:T(8,128)(2,1)}), bf16[4096,512]{1,0:T(8,128)(2,1)}) %all-gather.12.cloned.1.call-update) | async-done | bytes 4194320 | tf_op jit(solution)/shard_map/all_gather | solution.py:1848
  262.3 46.2 %down_scatter.1 = (f32[256,2048]{1,0:T(8,128)}, bf16[256,2048]{1,0:T(8,128)(2,1)}) custom-call(bf16[2048,1024]{1,0:T(8,128)(2,1)} %get-tuple-element.92.refs_0_.refs_5_, bf16[4,1024,512]{2,1,0:T(8,128)(2,1)} %bitcast.42, f32[256,2048]{1,0:T(8,128)} %get-tuple-element.94.refs_2_.refs_3_, f32[1,2048]{1,0:T(1,128)} %get-tuple-element.164.refs_3_, ...), custom_call_target="tpu_custom_call" | custom-call | flops 1048576 | bytes 65536 | tf_op jit(solution)/shard_map/down_scatter/pallas_call | solution.py:1032
  308.5 18.0 %all-gather.8.cloned.1.call-done = bf16[4,512,768]{2,1,0:T(8,128)(2,1)} async-done(((bf16[1,512,768]{2,1,0:T(8,128)(2,1)}), bf16[4,512,768]{2,1,0:T(8,128)(2,1)}) %all-gather.8.cloned.1.call-update) | async-done | bytes 3145744 | tf_op jit(solution)/shard_map/all_gather | solution.py:1848
  326.5 46.2 %gather_project.1 = (bf16[2048,2048]{1,0:T(8,128)(2,1)}, bf16[2048,768]{1,0:T(8,128)(2,1)}, bf16[4,256,512]{2,1,0:T(8,128)(2,1)}) custom-call(bf16[256,2048]{1,0:T(8,128)(2,1)} %get-tuple-element.96.refs_0_, bf16[2048,768]{1,0:T(8,128)(2,1)} %bitcast.44, f32[1,768]{1,0:T(1,128)} %broadcast_in_dim.17.refs_2_, ...), custom_call_target="tpu_custom_call" | custom-call | flops 1048576 | bytes 65536 | tf_op jit(solution)/shard_map/gather_project/pallas_call | solution.py:1032
  372.7 15.1 %attend_fwd.3 = (bf16[2048,256]{1,0:T(8,128)(2,1)}, f32[2,8,256]{2,1,0:T(8,128)}) custom-call(f32[2]{0:T(128)} %multiply_power_fusion.slope_ref, bf16[2048,768]{1,0:T(8,128)(2,1)} %get-tuple-element.97.p_ref), custom_call_target="tpu_custom_call" | custom-call | flops 1048576 | bytes 65536 | tf_op jit(solution)/shard_map/attend_fwd/pallas_call | solution.py:518
  387.8 53.5 %dense_scatter.3 = (f32[256,2048]{1,0:T(8,128)}, bf16[256,2048]{1,0:T(8,128)(2,1)}, bf16[4,1024,512]{2,1,0:T(8,128)(2,1)}) custom-call(bf16[2048,256]{1,0:T(8,128)(2,1)} %get-tuple-element.98.refs_0_.c_ref.refs_5_, bf16[4,256,512]{2,1,0:T(8,128)(2,1)} %get-tuple-element.99.refs_1_.refs_6_, f32[256,2048]{1,0:T(8,128)} %get-tuple-element.100.refs_2_.refs_3_, ...), custom_call_target="tpu_custom_call" | custom-call | flops 1048576 | bytes 65536 | tf_op jit(solution)/shard_map/dense_scatter/pallas_call | solution.py:1032
  441.3 0.0 all-gather.14.cloned.1.call-done.refs_1_
  441.3 50.5 %gather_up.3 = (bf16[2048,2048]{1,0:T(8,128)(2,1)}, bf16[2048,1024]{1,0:T(8,128)(2,1)}, bf16[2048,1024]{1,0:T(8,128)(2,1)}, bf16[4,1024,512]{2,1,0:T(8,128)(2,1)}) custom-call(bf16[256,2048]{1,0:T(8,128)(2,1)} %get-tuple-element.102.refs_0_, bf16[2048,1024]{1,0:T(8,128)(2,1)} %all-gather.14.cloned.1.call-done.refs_1_, ...), custom_call_target="tpu_custom_call", output_to_operand_aliasing={{3}: (4, {})} | custom-call | flops 1048576 | bytes 65536 | tf_op jit(solution)/shard_map/gather_up/pallas_call | solution.py:1032
  491.8 51.8 %last_scatter.1 = (bf16[256,2048]{1,0:T(8,128)(2,1)}, bf16[2048,1024]{1,0:T(8,128)(2,1)}, f32[1,1024]{1,0:T(1,128)}, bf16[4,1024,512]{2,1,0:T(8,128)(2,1)}) custom-call(bf16[2048,1024]{1,0:T(8,128)(2,1)} %get-tuple-element.105.refs_0_, bf16[4,1024,512]{2,1,0:T(8,128)(2,1)} %get-tuple-element.106.refs_1_, f32[256,2048]{1,0:T(8,128)} %get-tuple-element.107.refs_2_.refs_3_, ...), custom_call_target="tpu_custom_call" | custom-call | flops 1048576 | bytes 65536 | tf_op jit(solution)/shard_map/last_scatter/pallas_call | solution.py:1032
  543.7 92.9 %ffn_back.2 = (f32[256,2048]{1,0:T(8,128)}, f32[3,2048]{1,0:T(4,128)}, bf16[4,1024,512]{2,1,0:T(8,128)(2,1)}, bf16[128,512]{1,0:T(8,128)(2,1)}, bf16[2048,2048]{...) custom-call(bf16[2048,1024]{1,0:T(8,128)(2,1)} %get-tuple-element.110.refs_0_, ...), custom_call_target="tpu_custom_call" | custom-call | flops 1048576 | bytes 65536 | tf_op jit(solution)/shard_map/ffn_back/pallas_call | solution.py:1032
  636.5 18.9 %attend_bwd.2 = (bf16[3,2048,256]{2,1,0:T(8,128)(2,1)}, f32[2,256]{1,0:T(2,128)}) custom-call(f32[2]{0:T(128)} %multiply_power_fusion.slope_ref, bf16[2048,768]{1,0:T(8,128)(2,1)} %get-tuple-element.97.p_ref, bf16[2048,256]{1,0:T(8,128)(2,1)} %get-tuple-element.113.g_ref, bf16[2048,256]{1,0:T(8,128)(2,1)} %get-tuple-element.98.refs_0_.c_ref.refs_5_, ...), custom_call_target="tpu_custom_call" | custom-call | flops 1048576 | bytes 65536 | tf_op jit(solution)/shard_map/attend_bwd/pallas_call | solution.py:518
  655.4 100.4 %attn_back.1 = (f32[256,2048]{1,0:T(8,128)}, f32[3,2048]{1,0:T(4,128)}, bf16[4,1024,512]{2,1,0:T(8,128)(2,1)}, bf16[384,512]{1,0:T(8,128)(2,1)}, bf16[2048,2048]...) custom-call(bf16[3,2048,256]{2,1,0:T(8,128)(2,1)} %get-tuple-element.115.refs_0_, ...), custom_call_target="tpu_custom_call" | custom-call | flops 1048576 | bytes 65536 | tf_op jit(solution)/shard_map/attn_back/pallas_call | solution.py:1032
  755.8 0.8 slice.101
  756.6 0.8 slice.100
  757.3 109.3 %ffn_back.3 = (f32[256,2048]{1,0:T(8,128)}, f32[3,2048]{1,0:T(4,128)}, bf16[4,1024,512]{2,1,0:T(8,128)(2,1)}, bf16[768,512]{1,0:T(8,128)(2,1)}, bf16[2048,2048]{...) custom-call(bf16[2048,1024]{1,0:T(8,128)(2,1)} %get-tuple-element.121.refs_0_,, ...), custom_call_target="tpu_custom_call" | custom-call | flops 1048576 | bytes 65536 | tf_op jit(solution)/shard_map/ffn_back/pallas_call | solution.py:1032
  866.6 0.0 copy-start.10
  866.6 0.0 copy-start.11
  866.6 0.0 copy-start.9
  866.6 0.0 copy-start.3
  866.6 26.1 %attend_bwd.3 = (bf16[3,2048,256]{2,1,0:T(8,128)(2,1)}, f32[2,256]{1,0:T(2,128)}, bf16[256,512]{1,0:T(8,128)(2,1)}) custom-call(f32[2]{0:T(128)} %multiply_power_fusion.slope_ref, bf16[2048,768]{1,0:T(8,128)(2,1)} %get-tuple-element.87.p_ref, bf16[2048,256]{1,0:T(8,128)(2,1)} %get-tuple-element.126.g_ref, ...), custom_call_target="tpu_custom_call" | custom-call | flops 1048576 | bytes 65536 | tf_op jit(solution)/shard_map/attend_bwd/pallas_call | solution.py:518
  892.7 0.7 copy.30
  893.4 0.0 copy-done.11
  893.5 0.2 concatenate.18
  893.7 0.7 pad.8.refs_8_
  894.4 0.6 select_maximum_fusion.refs_9_
  895.0 152.8 %first_attn_back.1 = (f32[256,2048]{1,0:T(8,128)}, f32[3,2048]{1,0:T(4,128)}, bf16[4,1024,512]{2,1,0:T(8,128)(2,1)}, bf16[1024,512]{1,0:T(8,128)(2,1)}, f32[16,2...) custom-call(bf16[3,2048,256]{2,1,0:T(8,128)(2,1)} %get-tuple-element.129.refs_0_, ...), custom_call_target="tpu_custom_call" | custom-call | flops 1048576 | bytes 65536 | tf_op jit(solution)/shard_map/first_attn_back/pallas_call | solution.py:1032
  1047.8 9.2 place.1
  1057.1 1.0 copy.35
  1058.0 3.1 copy.36
  (19 shorter events, 0.1 us)
Async XLA Ops:
  7.2 5.2 copy-start.7
  7.2 5.2 copy-start.6
  7.2 197.3 %all-gather.10.cloned.1.call-start = ((), (), s32[]{:S(2)}) async-start(), calls=%async_computation.1 | async-start | bytes 5242880 | tf_op jit(solution)/shard_map/all_gather | solution.py:1848
  84.7 2.7 copy-start.1
  84.8 177.5 %all-gather.12.cloned.1.call-start = ((), (), s32[]{:S(2)}) async-start(), calls=%async_computation.2 | async-start | bytes 5242880 | tf_op jit(solution)/shard_map/all_gather | solution.py:1848
  85.5 241.0 %all-gather.8.cloned.1.call-start = ((), (), s32[]{:S(2)}) async-start(), calls=%async_computation | async-start | bytes 3932160 | tf_op jit(solution)/shard_map/all_gather | solution.py:1848
  86.8 72.8 %copy-start.5 = (f32[2,2,2048]{2,1,0:T(2,128)S(1)}, f32[2,2,2048]{2,1,0:T(2,128)}, u32[]{:S(2)}) copy-start(f32[2,2,2048]{2,1,0:T(2,128)} %param.21) | copy-start | bytes 98308
  86.8 354.5 %all-gather.14.cloned.1.call-start = ((), (), s32[]{:S(2)}) async-start(), calls=%async_computation.3 | async-start | bytes 5242880 | tf_op jit(solution)/shard_map/all_gather | solution.py:1848
  88.2 115.4 %copy-start = (bf16[256,2048]{1,0:T(8,128)(2,1)S(1)}, bf16[256,2048]{1,0:T(8,128)(2,1)}, u32[]{:S(2)}) copy-start(bf16[256,2048]{1,0:T(8,128)(2,1)} %refs_2_.3) | copy-start | bytes 3145732
  89.4 114.5 %copy-start.8 = (f32[2,1024]{1,0:T(2,128)S(1)}, f32[2,1024]{1,0:T(2,128)}, u32[]{:S(2)}) copy-start(f32[2,1024]{1,0:T(2,128)} %param.18) | copy-start | bytes 24580
  866.6 26.8 %copy-start.10 = (f32[1,1024]{1,0:T(1,128)S(1)}, f32[1,1024]{1,0:T(1,128)}, u32[]{:S(2)}) copy-start(f32[1,1024]{1,0:T(1,128)} %get-tuple-element.138) | copy-start | bytes 12292
  866.6 26.8 %copy-start.11 = (f32[2,256]{1,0:T(2,128)S(1)}, f32[2,256]{1,0:T(2,128)}, u32[]{:S(2)}) copy-start(f32[2,256]{1,0:T(2,128)} %get-tuple-element.139) | copy-start | bytes 6148
  866.6 26.8 %copy-start.9 = (f32[1,1024]{1,0:T(1,128)S(1)}, f32[1,1024]{1,0:T(1,128)}, u32[]{:S(2)}) copy-start(f32[1,1024]{1,0:T(1,128)} %get-tuple-element.140) | copy-start | bytes 12292
  866.6 26.9 %copy-start.3 = (f32[3,2048]{1,0:T(4,128)S(1)}, f32[3,2048]{1,0:T(4,128)}, u32[]{:S(2)}) copy-start(f32[3,2048]{1,0:T(4,128)} %get-tuple-element.136) | copy-start | bytes 73732
  866.6 26.9 %copy-start.4 = (f32[3,2048]{1,0:T(4,128)S(1)}, f32[3,2048]{1,0:T(4,128)}, u32[]{:S(2)}) copy-start(f32[3,2048]{1,0:T(4,128)} %get-tuple-element.134) | copy-start | bytes 73732
  1047.8 9.2 copy-start.2
Sparse Core Ops, SparseCore 0:
  84.9 94.6 all-gather.9
  181.2 81.0 all-gather.11
  264.4 62.0 all-gather.7
  327.9 109.8 all-gather.13

commit v7 on v6

--- a/solution.py
+++ b/solution.py
@@ -856,13 +856,14 @@
         join(2)
         compute(3, core, 7)
         join(3)
-        links.tick(2 if links.more else 3)
+        weights = isinstance(links.z, ZGather)
+        links.tick(0 if weights else 2 if links.more else 3)
         share = -(-len(steps) // C) if self.late else 2
         for k in range(C):
             arrive(4, k)
             add(6, 4, k)
             push(6, 6, fn, k)
-            links.tick(1 if links.more else 2)
+            links.tick(k // 2 if weights else 1 if links.more else 2)
             fill(steps, share)
         fill(steps, len(steps))
         end_ins = need(end_ins)
@@ -1881,12 +1882,12 @@
         phase = self.scatter(
             (context, self.weight("dense", l)), row_split_body, AddNorm(stream, bias, gain, shift, True)
         )
-        z = self.weights.take(3 * l)
+        z = self.weights.take(2 * l)
         ((middle, rows),) = chain_call("dense_scatter", 10 * l + 1, [phase], z)
         w = self.weight("up", l)
         shape = self.shape(w.shape[1])
         phase = self.gather(rows, (w, up_shift[None]), (shape, shape), up_body)
-        z = self.weights.take(5 * l)
+        z = self.weights.take(6 * l)
         return middle, *chain_call("gather_up", 10 * l + 2, [phase], z)[0]
 
     def ffn_out(self, l, middle, active, bias, gain, shift):

time: 1070 us -> 1070 us (level)
  transfers between devices with their start and end apart: 4 -> 4, of which waited for: 2 -> 2; matrix products, arithmetic and copies ran while one was open for 0% -> 0% of each run, Pallas kernels for 30% -> 29%
where the time goes in v7:
time: 1070 us
  Pallas kernels  1000 us (93%)
  waiting for transfers between devices  30.8 us (3%)
  local copies, waits for them, and re-layouts  16.1 us (2%)
  between operations  14.3 us (1%)
    pallas_call x11, Pallas kernels, chain_call(): pl.pallas_call(functools.partial(chain_kernel, phases, z, [i for _, i in...  791 us
    pallas_call x4, Pallas kernels, attend_call(): pl.pallas_call(functools.partial(kernel, z), out_shape=(*outs, *z.out_sha...  75.6 us
    pallas_call x1, Pallas kernels, first_call(): pl.pallas_call(functools.partial(first_kernel, C, z, n_project), out_shap...  71.7 us
    pallas_call x1, Pallas kernels, gather_only(): pl.pallas_call(functools.partial(gather_only_kernel, C, n, len(after), z)...  54.8 us
    all_gather x4, waiting for transfers between devices, start(): queue.arrays[key] = lax.all_gather(shard, 'dp', axis=0)  29.8 us
  transfers between devices with their start and end apart: 4, of which 2 were waited for; matrix products, arithmetic and copies ran while one was open for 0% of the time, Pallas kernels for 29%

profile of v7, /device:TPU:0, one launch (start us, length us, event | category | flops | bytes accessed | tf_op | source)
XLA Modules:
  0.0 1065.9 jit_solution(948913554187605920)
XLA Ops:
  7.2 0.0 copy-start.7
  7.2 0.0 copy-start.6
  7.2 0.0 all-gather.10.cloned.1.call-start
  7.2 0.8 fusion.3
  8.0 0.6 broadcast_in_dim.16.refs_3_
  8.6 2.2 copy.27
  10.8 1.6 copy.28.refs_6_
  12.4 0.0 copy-done.7
  12.4 0.0 copy-done.6
  12.4 0.7 slice_bitcast_fusion.1
  13.0 71.7 %first.1 = (bf16[2048,2048]{1,0:T(8,128)(2,1)}, bf16[2048,768]{1,0:T(8,128)(2,1)}, bf16[512,1024]{1,0:T(8,128)(2,1)}, bf16[512,1024]{1,0:T(8,128)(2,1)}, bf16[10...) custom-call(bf16[256,2048]{1,0:T(8,128)(2,1)} %refs_3_.1, ...), custom_call_target="tpu_custom_call" | custom-call | flops 1048576 | bytes 65536 | tf_op jit(solution)/shard_map/first/pallas_call | solution.py:1769
  84.7 0.0 copy-start.1
  84.7 0.0 all-gather.10.cloned.1.call-update
  84.8 0.0 all-gather.12.cloned.1.call-start
  84.8 0.7 all-gather.12.cloned.1.call-update
  85.5 0.0 all-gather.8.cloned.1.call-start
  85.6 0.1 slice.102
  85.6 1.2 copy.29
  86.8 0.0 all-gather.8.cloned.1.call-update
  86.8 0.3 all-gather.14.cloned.1.call-start
  87.1 0.2 all-gather.14.cloned.1.call-update
  87.4 0.9 convert_element_type.21.refs_1_.refs_3_
  88.3 0.6 broadcast_in_dim.17.refs_2_
  88.8 0.5 multiply_power_fusion.slope_ref
  89.4 15.4 %attend_fwd.2 = (bf16[2048,256]{1,0:T(8,128)(2,1)}, f32[2,8,256]{2,1,0:T(8,128)}) custom-call(f32[2]{0:T(128)} %multiply_power_fusion.slope_ref, bf16[2048,768]{1,0:T(8,128)(2,1)} %get-tuple-element.87.p_ref), custom_call_target="tpu_custom_call" | custom-call | flops 1048576 | bytes 65536 | tf_op jit(solution)/shard_map/attend_fwd/pallas_call | solution.py:518
  104.7 54.8 %gather_rows.1 = (bf16[2048,2048]{1,0:T(8,128)(2,1)}, bf16[4,256,512]{2,1,0:T(8,128)(2,1)}) custom-call(bf16[256,2048]{1,0:T(8,128)(2,1)} %refs_2_.3, bf16[2,256,512]{2,1,0:T(8,128)(2,1)} %convert_element_type.21.refs_1_.refs_3_), custom_call_target="tpu_custom_call" | custom-call | flops 1048576 | bytes 65536 | tf_op jit(solution)/shard_map/gather_rows/pallas_call | solution.py:1139
  159.6 0.6 slice_bitcast_fusion
  160.2 43.5 %dense_scatter.2 = (f32[256,2048]{1,0:T(8,128)}, bf16[256,2048]{1,0:T(8,128)(2,1)}) custom-call(bf16[2048,256]{1,0:T(8,128)(2,1)} %get-tuple-element.88.refs_0_.c_ref.refs_5_, bf16[4,256,512]{2,1,0:T(8,128)(2,1)} %get-tuple-element.89.refs_1_.refs_7_, bf16[256,2048]{1,0:T(8,128)(2,1)} %refs_3_.1, f32[1,2048]{1,0:T(1,128)} %get-tuple-element.165.refs_3_, ...), custom_call_target="tpu_custom_call" | custom-call | flops 1048576 | bytes 65536 | tf_op jit(solution)/shard_map/dense_scatter/pallas_call | solution.py:1033
  203.7 0.0 copy-done
  203.7 0.2 convert_reduce_fusion
  203.9 0.6 fusion.2
  204.5 45.9 %gather_up.2 = (bf16[2048,2048]{1,0:T(8,128)(2,1)}, bf16[2048,1024]{1,0:T(8,128)(2,1)}, bf16[2048,1024]{1,0:T(8,128)(2,1)}) custom-call(bf16[256,2048]{1,0:T(8,128)(2,1)} %get-tuple-element.90.refs_0_, bf16[2048,1024]{1,0:T(8,128)(2,1)} %all-gather.10.cloned.1.call-done.refs_1_, f32[1,1024]{1,0:T(1,128)} %get-tuple-element.176.refs_2_), custom_call_target="tpu_custom_call" | custom-call | flops 1048576 | bytes 65536 | tf_op jit(solution)/shard_map/gather_up/pallas_call | solution.py:1033
  250.4 11.8 %all-gather.12.cloned.1.call-done = bf16[4096,512]{1,0:T(8,128)(2,1)} async-done(((bf16[1024,512]{1,0:T(8,128)(2,1)}), bf16[4096,512]{1,0:T(8,128)(2,1)}) %all-gather.12.cloned.1.call-update) | async-done | bytes 4194320 | tf_op jit(solution)/shard_map/all_gather | solution.py:1849
  262.3 46.2 %down_scatter.1 = (f32[256,2048]{1,0:T(8,128)}, bf16[256,2048]{1,0:T(8,128)(2,1)}) custom-call(bf16[2048,1024]{1,0:T(8,128)(2,1)} %get-tuple-element.92.refs_0_.refs_5_, bf16[4,1024,512]{2,1,0:T(8,128)(2,1)} %bitcast.42, f32[256,2048]{1,0:T(8,128)} %get-tuple-element.94.refs_2_.refs_3_, f32[1,2048]{1,0:T(1,128)} %get-tuple-element.164.refs_3_, ...), custom_call_target="tpu_custom_call" | custom-call | flops 1048576 | bytes 65536 | tf_op jit(solution)/shard_map/down_scatter/pallas_call | solution.py:1033
  308.5 18.0 %all-gather.8.cloned.1.call-done = bf16[4,512,768]{2,1,0:T(8,128)(2,1)} async-done(((bf16[1,512,768]{2,1,0:T(8,128)(2,1)}), bf16[4,512,768]{2,1,0:T(8,128)(2,1)}) %all-gather.8.cloned.1.call-update) | async-done | bytes 3145744 | tf_op jit(solution)/shard_map/all_gather | solution.py:1849
  326.5 46.2 %gather_project.1 = (bf16[2048,2048]{1,0:T(8,128)(2,1)}, bf16[2048,768]{1,0:T(8,128)(2,1)}, bf16[4,256,512]{2,1,0:T(8,128)(2,1)}) custom-call(bf16[256,2048]{1,0:T(8,128)(2,1)} %get-tuple-element.96.refs_0_, bf16[2048,768]{1,0:T(8,128)(2,1)} %bitcast.44, f32[1,768]{1,0:T(1,128)} %broadcast_in_dim.17.refs_2_, ...), custom_call_target="tpu_custom_call" | custom-call | flops 1048576 | bytes 65536 | tf_op jit(solution)/shard_map/gather_project/pallas_call | solution.py:1033
  372.7 15.1 %attend_fwd.3 = (bf16[2048,256]{1,0:T(8,128)(2,1)}, f32[2,8,256]{2,1,0:T(8,128)}) custom-call(f32[2]{0:T(128)} %multiply_power_fusion.slope_ref, bf16[2048,768]{1,0:T(8,128)(2,1)} %get-tuple-element.97.p_ref), custom_call_target="tpu_custom_call" | custom-call | flops 1048576 | bytes 65536 | tf_op jit(solution)/shard_map/attend_fwd/pallas_call | solution.py:518
  387.8 43.2 %dense_scatter.3 = (f32[256,2048]{1,0:T(8,128)}, bf16[256,2048]{1,0:T(8,128)(2,1)}, bf16[4,1024,512]{2,1,0:T(8,128)(2,1)}) custom-call(bf16[2048,256]{1,0:T(8,128)(2,1)} %get-tuple-element.98.refs_0_.c_ref.refs_5_, bf16[4,256,512]{2,1,0:T(8,128)(2,1)} %get-tuple-element.99.refs_1_.refs_6_, f32[256,2048]{1,0:T(8,128)} %get-tuple-element.100.refs_2_.refs_3_, ...), custom_call_target="tpu_custom_call" | custom-call | flops 1048576 | bytes 65536 | tf_op jit(solution)/shard_map/dense_scatter/pallas_call | solution.py:1033
  431.0 0.0 all-gather.14.cloned.1.call-done.refs_1_
  431.0 59.7 %gather_up.3 = (bf16[2048,2048]{1,0:T(8,128)(2,1)}, bf16[2048,1024]{1,0:T(8,128)(2,1)}, bf16[2048,1024]{1,0:T(8,128)(2,1)}, bf16[4,1024,512]{2,1,0:T(8,128)(2,1)}) custom-call(bf16[256,2048]{1,0:T(8,128)(2,1)} %get-tuple-element.102.refs_0_, bf16[2048,1024]{1,0:T(8,128)(2,1)} %all-gather.14.cloned.1.call-done.refs_1_, ...), custom_call_target="tpu_custom_call", output_to_operand_aliasing={{3}: (4, {})} | custom-call | flops 1048576 | bytes 65536 | tf_op jit(solution)/shard_map/gather_up/pallas_call | solution.py:1033
  490.7 51.9 %last_scatter.1 = (bf16[256,2048]{1,0:T(8,128)(2,1)}, bf16[2048,1024]{1,0:T(8,128)(2,1)}, f32[1,1024]{1,0:T(1,128)}, bf16[4,1024,512]{2,1,0:T(8,128)(2,1)}) custom-call(bf16[2048,1024]{1,0:T(8,128)(2,1)} %get-tuple-element.105.refs_0_, bf16[4,1024,512]{2,1,0:T(8,128)(2,1)} %get-tuple-element.106.refs_1_, f32[256,2048]{1,0:T(8,128)} %get-tuple-element.107.refs_2_.refs_3_, ...), custom_call_target="tpu_custom_call" | custom-call | flops 1048576 | bytes 65536 | tf_op jit(solution)/shard_map/last_scatter/pallas_call | solution.py:1033
  542.7 92.6 %ffn_back.2 = (f32[256,2048]{1,0:T(8,128)}, f32[3,2048]{1,0:T(4,128)}, bf16[4,1024,512]{2,1,0:T(8,128)(2,1)}, bf16[128,512]{1,0:T(8,128)(2,1)}, bf16[2048,2048]{...) custom-call(bf16[2048,1024]{1,0:T(8,128)(2,1)} %get-tuple-element.110.refs_0_, ...), custom_call_target="tpu_custom_call" | custom-call | flops 1048576 | bytes 65536 | tf_op jit(solution)/shard_map/ffn_back/pallas_call | solution.py:1033
  635.3 18.9 %attend_bwd.2 = (bf16[3,2048,256]{2,1,0:T(8,128)(2,1)}, f32[2,256]{1,0:T(2,128)}) custom-call(f32[2]{0:T(128)} %multiply_power_fusion.slope_ref, bf16[2048,768]{1,0:T(8,128)(2,1)} %get-tuple-element.97.p_ref, bf16[2048,256]{1,0:T(8,128)(2,1)} %get-tuple-element.113.g_ref, bf16[2048,256]{1,0:T(8,128)(2,1)} %get-tuple-element.98.refs_0_.c_ref.refs_5_, ...), custom_call_target="tpu_custom_call" | custom-call | flops 1048576 | bytes 65536 | tf_op jit(solution)/shard_map/attend_bwd/pallas_call | solution.py:518
  654.2 99.6 %attn_back.1 = (f32[256,2048]{1,0:T(8,128)}, f32[3,2048]{1,0:T(4,128)}, bf16[4,1024,512]{2,1,0:T(8,128)(2,1)}, bf16[384,512]{1,0:T(8,128)(2,1)}, bf16[2048,2048]...) custom-call(bf16[3,2048,256]{2,1,0:T(8,128)(2,1)} %get-tuple-element.115.refs_0_, ...), custom_call_target="tpu_custom_call" | custom-call | flops 1048576 | bytes 65536 | tf_op jit(solution)/shard_map/attn_back/pallas_call | solution.py:1033
  753.8 0.8 slice.101
  754.5 0.8 slice.100
  755.3 109.6 %ffn_back.3 = (f32[256,2048]{1,0:T(8,128)}, f32[3,2048]{1,0:T(4,128)}, bf16[4,1024,512]{2,1,0:T(8,128)(2,1)}, bf16[768,512]{1,0:T(8,128)(2,1)}, bf16[2048,2048]{...) custom-call(bf16[2048,1024]{1,0:T(8,128)(2,1)} %get-tuple-element.121.refs_0_,, ...), custom_call_target="tpu_custom_call" | custom-call | flops 1048576 | bytes 65536 | tf_op jit(solution)/shard_map/ffn_back/pallas_call | solution.py:1033
  865.0 0.0 copy-start.11
  865.0 0.0 copy-start.9
  865.0 0.0 copy-start.3
  865.0 0.0 copy-start.4
  865.0 26.3 %attend_bwd.3 = (bf16[3,2048,256]{2,1,0:T(8,128)(2,1)}, f32[2,256]{1,0:T(2,128)}, bf16[256,512]{1,0:T(8,128)(2,1)}) custom-call(f32[2]{0:T(128)} %multiply_power_fusion.slope_ref, bf16[2048,768]{1,0:T(8,128)(2,1)} %get-tuple-element.87.p_ref, bf16[2048,256]{1,0:T(8,128)(2,1)} %get-tuple-element.126.g_ref, ...), custom_call_target="tpu_custom_call" | custom-call | flops 1048576 | bytes 65536 | tf_op jit(solution)/shard_map/attend_bwd/pallas_call | solution.py:518
  891.3 0.7 copy.30
  892.1 0.0 copy-done.9
  892.1 0.0 copy-done.3
  892.1 0.0 copy-done.4
  892.1 0.2 concatenate.18
  892.4 0.7 pad.8.refs_8_
  893.0 0.6 select_maximum_fusion.refs_9_
  893.7 152.1 %first_attn_back.1 = (f32[256,2048]{1,0:T(8,128)}, f32[3,2048]{1,0:T(4,128)}, bf16[4,1024,512]{2,1,0:T(8,128)(2,1)}, bf16[1024,512]{1,0:T(8,128)(2,1)}, f32[16,2...) custom-call(bf16[3,2048,256]{2,1,0:T(8,128)(2,1)} %get-tuple-element.129.refs_0_, ...), custom_call_target="tpu_custom_call" | custom-call | flops 1048576 | bytes 65536 | tf_op jit(solution)/shard_map/first_attn_back/pallas_call | solution.py:1033
  1045.8 9.2 place.1
  1055.1 0.0 copy-done.2
  1055.1 1.0 copy.35
  1056.0 3.1 copy.36
  (19 shorter events, 0.1 us)
Async XLA Ops:
  7.2 5.2 copy-start.7
  7.2 5.2 copy-start.6
  7.2 197.3 %all-gather.10.cloned.1.call-start = ((), (), s32[]{:S(2)}) async-start(), calls=%async_computation.1 | async-start | bytes 5242880 | tf_op jit(solution)/shard_map/all_gather | solution.py:1849
  84.7 2.7 copy-start.1
  84.8 177.5 %all-gather.12.cloned.1.call-start = ((), (), s32[]{:S(2)}) async-start(), calls=%async_computation.2 | async-start | bytes 5242880 | tf_op jit(solution)/shard_map/all_gather | solution.py:1849
  85.5 241.0 %all-gather.8.cloned.1.call-start = ((), (), s32[]{:S(2)}) async-start(), calls=%async_computation | async-start | bytes 3932160 | tf_op jit(solution)/shard_map/all_gather | solution.py:1849
  86.8 72.8 %copy-start.5 = (f32[2,2,2048]{2,1,0:T(2,128)S(1)}, f32[2,2,2048]{2,1,0:T(2,128)}, u32[]{:S(2)}) copy-start(f32[2,2,2048]{2,1,0:T(2,128)} %param.21) | copy-start | bytes 98308
  86.8 344.2 %all-gather.14.cloned.1.call-start = ((), (), s32[]{:S(2)}) async-start(), calls=%async_computation.3 | async-start | bytes 5242880 | tf_op jit(solution)/shard_map/all_gather | solution.py:1849
  88.2 115.4 %copy-start = (bf16[256,2048]{1,0:T(8,128)(2,1)S(1)}, bf16[256,2048]{1,0:T(8,128)(2,1)}, u32[]{:S(2)}) copy-start(bf16[256,2048]{1,0:T(8,128)(2,1)} %refs_2_.3) | copy-start | bytes 3145732
  89.4 114.5 %copy-start.8 = (f32[2,1024]{1,0:T(2,128)S(1)}, f32[2,1024]{1,0:T(2,128)}, u32[]{:S(2)}) copy-start(f32[2,1024]{1,0:T(2,128)} %param.18) | copy-start | bytes 24580
  865.0 27.1 %copy-start.10 = (f32[1,1024]{1,0:T(1,128)S(1)}, f32[1,1024]{1,0:T(1,128)}, u32[]{:S(2)}) copy-start(f32[1,1024]{1,0:T(1,128)} %get-tuple-element.138) | copy-start | bytes 12292
  865.0 27.1 %copy-start.11 = (f32[2,256]{1,0:T(2,128)S(1)}, f32[2,256]{1,0:T(2,128)}, u32[]{:S(2)}) copy-start(f32[2,256]{1,0:T(2,128)} %get-tuple-element.139) | copy-start | bytes 6148
  865.0 27.1 %copy-start.9 = (f32[1,1024]{1,0:T(1,128)S(1)}, f32[1,1024]{1,0:T(1,128)}, u32[]{:S(2)}) copy-start(f32[1,1024]{1,0:T(1,128)} %get-tuple-element.140) | copy-start | bytes 12292
  865.0 27.1 %copy-start.3 = (f32[3,2048]{1,0:T(4,128)S(1)}, f32[3,2048]{1,0:T(4,128)}, u32[]{:S(2)}) copy-start(f32[3,2048]{1,0:T(4,128)} %get-tuple-element.136) | copy-start | bytes 73732
  865.0 27.1 %copy-start.4 = (f32[3,2048]{1,0:T(4,128)S(1)}, f32[3,2048]{1,0:T(4,128)}, u32[]{:S(2)}) copy-start(f32[3,2048]{1,0:T(4,128)} %get-tuple-element.134) | copy-start | bytes 73732
  1045.8 9.2 copy-start.2
Sparse Core Ops, SparseCore 0:
  84.9 94.6 all-gather.9
  181.2 81.0 all-gather.11
  264.4 62.0 all-gather.7
  327.9 102.6 all-gather.13
